TPU v7x, 32 devices: a whole 2x2x4 slice. The times are simulated.
32 devices in a mesh: expert: 8 (over z, y), hidden: 4 (over x, core).
Axes of the slice: x: 2, y: 2, z: 4, core: 2. Of those that a mesh axis runs over, the one named last changes fastest.
Arguments:
- tokens: bfloat16 [1024, 2048], P('expert', 'hidden'), may hold values from -6 to 6
- cotangent: bfloat16 [1024, 2048], P('expert', 'hidden'), may hold values from -6 to 6
- gate_weight: bfloat16 [16, 2048, 1408], P('expert', 'hidden'), may hold values from -0.125 to 0.125
- up_weight: bfloat16 [16, 2048, 1408], P('expert', 'hidden'), may hold values from -0.125 to 0.125
- down_weight: bfloat16 [16, 2048, 1408], P('expert', 'hidden'), may hold values from -0.15625 to 0.15625
- routing: int32 [1024, 6], P('expert'), may hold values from 0 to 15, all different within a row; in each aligned block of 128 rows (0 to 127, 128 to 255, ...) at most 64 rows name the same one
- route_weight: float32 [1024, 6], P('expert'), may hold values from 0.05 to 1
- merge_source: int32 [4], replicated, may hold values from 2 to 13, as said below
- merge_target: int32 [4], replicated, may hold values from 0 to 15, as said below
- neuron_perm: int32 [4, 1408], replicated, may hold values from 0 to 1407, as said below
Outputs:
- mixed: bfloat16 [1024, 2048], P('expert', 'hidden')
- grad_gate: bfloat16 [16, 2048, 1408], P('expert', 'hidden')
- grad_up: bfloat16 [16, 2048, 1408], P('expert', 'hidden')
- grad_down: bfloat16 [16, 2048, 1408], P('expert', 'hidden')
Inputs may be any that keep to these rules, and one draw needn't show every extreme that they name: `routing`: in each aligned block of 128 tokens no expert is named more than 64 times, a bound that some block reaches. `merge_source`: 4 distinct experts, always including expert 2 and expert 16 - 3; merge_source and merge_target together hold exactly one expert of each aligned group of 2 consecutive expert numbers. `merge_target`: distinct experts, none of them a source, always including expert 0 and expert 16 - 1; see merge_source. `neuron_perm`: each row is a permutation of 0 to 1407.
All inputs are finite; a program needn't handle non-finite values.
Results may differ from a plain program's by a relative error of at most 0.019.
Values may be sent and summed in bfloat16 or wider, within the bound.
No kernel may reach another device: no remote copies, remote signals or barrier semaphores. Data moves between devices by JAX's collectives and lax.ppermute only.
A program may use at most 128 MiB of HBM per device.

v0:
```python
import jax
import jax.numpy as jnp
from jax import lax
from jax.sharding import PartitionSpec as P


def silu_parts(values):
    sigma = jax.nn.sigmoid(values)
    return (values * sigma, sigma * (1.0 + values * (1.0 - sigma)))


def shards(
    tokens,
    cotangent,
    gate_weight,
    up_weight,
    down_weight,
    routing,
    route_weight,
    merge_source,
    merge_target,
    neuron_perm,
):
    devices_n = lax.axis_size("expert")
    my_index = lax.axis_index("expert")
    exp_local, width_local, neurons = gate_weight.shape
    experts = exp_local * devices_n
    groups = exp_local + 1
    tok_local, top_count = routing.shape
    slot_depth = max(2, tok_local * top_count * 4 // (3 * experts))
    group_rows = devices_n * slot_depth
    slot_total = groups * group_rows
    assign_n = tok_local * top_count
    expert_ids = jnp.arange(experts, dtype=jnp.int32)
    source_hit = merge_source[:, None] == expert_ids[None, :]
    is_source = jnp.any(source_hit, axis=0)
    mapped = jnp.where(
        is_source, jnp.sum(jnp.where(source_hit, merge_target[:, None], 0), axis=0), expert_ids
    )
    group_of = jnp.where(is_source, exp_local, mapped % exp_local)
    slot_base = group_of * group_rows + mapped // exp_local * slot_depth
    flat_ids = routing.reshape(-1)
    flat_weight = route_weight.reshape(-1)
    expert_hot = (flat_ids[:, None] == expert_ids[None, :]).astype(jnp.int32)
    rank_in = jnp.sum(jnp.cumsum(expert_hot, axis=0) * expert_hot, axis=1) - 1
    slot_index = jnp.sum(expert_hot * slot_base[None, :], axis=1) + rank_in
    slot_hot = jnp.arange(slot_total, dtype=jnp.int32)[:, None] == slot_index[None, :]
    token_hot = (
        jnp.arange(assign_n, dtype=jnp.int32)[:, None] // top_count
        == jnp.arange(tok_local, dtype=jnp.int32)[None, :]
    )
    placing = jnp.dot(
        slot_hot.astype(jnp.bfloat16),
        token_hot.astype(jnp.bfloat16),
        preferred_element_type=jnp.float32,
    ).astype(jnp.bfloat16)
    slot_weight = jnp.sum(jnp.where(slot_hot, flat_weight[None, :], 0.0), axis=1)
    send_tokens = jnp.dot(placing, tokens, preferred_element_type=jnp.float32).astype(jnp.bfloat16)
    placed_grads = jnp.dot(placing, cotangent, preferred_element_type=jnp.float32)
    send_grads = (placed_grads * slot_weight[:, None]).astype(jnp.bfloat16)
    slot_shape = (groups, devices_n, slot_depth, width_local)
    inputs_x, inputs_dy = (
        lax.all_to_all(
            send_tokens.reshape(slot_shape), "expert", split_axis=1, concat_axis=1, tiled=True
        ),
        lax.all_to_all(
            send_grads.reshape(slot_shape), "expert", split_axis=1, concat_axis=1, tiled=True
        ),
    )
    inputs_x = inputs_x.reshape(groups, group_rows, width_local)
    inputs_dy = inputs_dy.reshape(groups, group_rows, width_local)
    source_dev = merge_source // exp_local
    target_dev = merge_target // exp_local
    source_slot = jnp.sum(jnp.where(source_dev == my_index, merge_source % exp_local, 0))
    piece_shape = (devices_n, width_local // devices_n, neurons)
    out_gate = lax.dynamic_index_in_dim(gate_weight, source_slot, 0, keepdims=False).reshape(
        piece_shape
    )
    out_up = lax.dynamic_index_in_dim(up_weight, source_slot, 0, keepdims=False).reshape(
        piece_shape
    )
    out_down = lax.dynamic_index_in_dim(down_weight, source_slot, 0, keepdims=False).reshape(
        piece_shape
    )
    spread_gate, spread_up, spread_down = (
        lax.all_to_all(out_gate, "expert", split_axis=0, concat_axis=0, tiled=True),
        lax.all_to_all(out_up, "expert", split_axis=0, concat_axis=0, tiled=True),
        lax.all_to_all(out_down, "expert", split_axis=0, concat_axis=0, tiled=True),
    )
    device_ids = jnp.arange(devices_n, dtype=jnp.int32)
    pair_hit = target_dev[:, None] == device_ids[None, :]
    source_for = jnp.sum(jnp.where(pair_hit, source_dev[:, None], 0), axis=0)
    relay_gate = jnp.take(spread_gate, source_for, axis=0)
    relay_up = jnp.take(spread_up, source_for, axis=0)
    relay_down = jnp.take(spread_down, source_for, axis=0)
    got_gate, got_up, got_down = (
        lax.all_to_all(relay_gate, "expert", split_axis=0, concat_axis=0, tiled=True),
        lax.all_to_all(relay_up, "expert", split_axis=0, concat_axis=0, tiled=True),
        lax.all_to_all(relay_down, "expert", split_axis=0, concat_axis=0, tiled=True),
    )
    own_target = target_dev == my_index
    has_target = jnp.any(own_target)
    target_slot = jnp.sum(jnp.where(own_target, merge_target % exp_local, 0))
    order_perm = jnp.sum(jnp.where(own_target[:, None], neuron_perm, 0), axis=0)

    def merged_groups(weight, arrived):
        local_one = lax.dynamic_index_in_dim(weight, target_slot, 0, keepdims=False)
        permuted = jnp.take(arrived.reshape(width_local, neurons), order_perm, axis=1)
        blended = (0.5 * (local_one.astype(jnp.float32) + permuted.astype(jnp.float32))).astype(
            jnp.bfloat16
        )
        chosen = jnp.where(has_target, blended, local_one)
        updated = lax.dynamic_update_index_in_dim(weight, chosen, target_slot, 0)
        return jnp.concatenate([updated, chosen[None]], axis=0)

    group_gate = merged_groups(gate_weight, got_gate)
    group_up = merged_groups(up_weight, got_up)
    group_down = merged_groups(down_weight, got_down)
    gate_part = jnp.einsum("grd,gdf->grf", inputs_x, group_gate, preferred_element_type=jnp.float32)
    up_part = jnp.einsum("grd,gdf->grf", inputs_x, group_up, preferred_element_type=jnp.float32)
    gate_sum, up_sum = (
        lax.psum_scatter(
            gate_part.astype(jnp.bfloat16), "hidden", scatter_dimension=2, tiled=True
        ).astype(jnp.float32),
        lax.psum_scatter(
            up_part.astype(jnp.bfloat16), "hidden", scatter_dimension=2, tiled=True
        ).astype(jnp.float32),
    )
    active, slope = silu_parts(gate_sum)
    hidden_act = lax.all_gather(
        (active * up_sum).astype(jnp.bfloat16), "hidden", axis=2, tiled=True
    )
    outputs_y = jnp.einsum(
        "grf,gdf->grd", hidden_act, group_down, preferred_element_type=jnp.float32
    ).astype(jnp.bfloat16)
    returned = lax.all_to_all(
        outputs_y.reshape(slot_shape), "expert", split_axis=1, concat_axis=1, tiled=True
    )
    picked = (
        jnp.take(returned.reshape(slot_total, width_local), slot_index, axis=0).astype(jnp.float32)
        * flat_weight[:, None]
    )
    mixed = jnp.sum(picked.reshape(tok_local, top_count, width_local), axis=1).astype(jnp.bfloat16)
    grad_down = jnp.einsum(
        "grd,grf->gdf", inputs_dy, hidden_act, preferred_element_type=jnp.float32
    )
    back_part = jnp.einsum(
        "grd,gdf->grf", inputs_dy, group_down, preferred_element_type=jnp.float32
    )
    back_sum = lax.psum_scatter(
        back_part.astype(jnp.bfloat16), "hidden", scatter_dimension=2, tiled=True
    ).astype(jnp.float32)
    grad_gate_act, grad_up_act = (
        lax.all_gather(
            (back_sum * up_sum * slope).astype(jnp.bfloat16), "hidden", axis=2, tiled=True
        ),
        lax.all_gather((back_sum * active).astype(jnp.bfloat16), "hidden", axis=2, tiled=True),
    )
    grad_gate = jnp.einsum(
        "grd,grf->gdf", inputs_x, grad_gate_act, preferred_element_type=jnp.float32
    )
    grad_up = jnp.einsum("grd,grf->gdf", inputs_x, grad_up_act, preferred_element_type=jnp.float32)

    def fold(grad):
        base = grad[:exp_local]
        extra = lax.dynamic_index_in_dim(base, target_slot, 0, keepdims=False) + grad[exp_local]
        return lax.dynamic_update_index_in_dim(base, extra, target_slot, 0).astype(jnp.bfloat16)

    return (mixed, fold(grad_gate), fold(grad_up), fold(grad_down))


def solution(mesh):
    placed = (
        P("expert", "hidden"),
        P("expert", "hidden"),
        P("expert", "hidden", None),
        P("expert", "hidden", None),
        P("expert", "hidden", None),
        P("expert", None),
        P("expert", None),
        P(),
        P(),
        P(),
    )
    return jax.shard_map(
        shards,
        mesh=mesh,
        in_specs=placed,
        out_specs=(
            P("expert", "hidden"),
            P("expert", "hidden", None),
            P("expert", "hidden", None),
            P("expert", "hidden", None),
        ),
        check_vma=False,
    )
```

profile of v0, /device:TPU:0, one launch (start us, length us, event | category | flops | bytes accessed | tf_op | source)
XLA Modules:
  0.0 588.1 jit_solution(5720240870110106808)
XLA Ops:
  20.8 41.7 %all_to_all.45 = bf16[8,64,1408]{2,1,0:T(8,128)(2,1)} all-to-all(bf16[8,64,1408]{2,1,0:T(8,128)(2,1)S(1)} %bitcast.78), channel_id=1, replica_groups=mesh['expert'=8,'hidden'=4] {'expert'}, dimensions={0} | all-to-all | bytes 2883584 | tf_op jit(solution)/shard_map/all_to_all | solution.py:88
  69.0 31.4 %all-to-all-done.3 = bf16[8,64,1408]{2,1,0:T(8,128)(2,1)} async-done(((bf16[8,64,1408]{2,1,0:T(8,128)(2,1)}), bf16[8,64,1408]{2,1,0:T(8,128)(2,1)}, u32[]{:S(2)}, u32[]{:S(2)}) %all-to-all-start.3) | async-done | bytes 1441824 | tf_op jit(solution)/shard_map/all_to_all | solution.py:87
  110.4 27.7 %all-to-all-done.1 = bf16[8,64,1408]{2,1,0:T(8,128)(2,1)S(1)} async-done(((bf16[8,64,1408]{2,1,0:T(8,128)(2,1)}), bf16[8,64,1408]{2,1,0:T(8,128)(2,1)S(1)}, u32[]{:S(2)}, u32[]{:S(2)}) %all-to-all-start.1) | async-done | bytes 1441824 | tf_op jit(solution)/shard_map/all_to_all | solution.py:86
  154.4 25.6 %all-to-all-done.8 = bf16[3,8,64,512]{3,2,0,1:T(8,128)(2,1)S(1)} async-done(((bf16[3,8,64,512]{3,2,0,1:T(8,128)(2,1)}), bf16[3,8,64,512]{3,2,0,1:T(8,128)(2,1)S(1)}, u32[]{:S(2)}, u32[]{:S(2)}) %all-to-all-start.8) | async-done | bytes 1572896 | tf_op jit(solution)/shard_map/all_to_all | solution.py:66
  189.2 29.0 %all-to-all-done.6 = bf16[8,64,1408]{2,1,0:T(8,128)(2,1)} async-done(((bf16[8,64,1408]{2,1,0:T(8,128)(2,1)}), bf16[8,64,1408]{2,1,0:T(8,128)(2,1)}, u32[]{:S(2)}, u32[]{:S(2)}) %all-to-all-start.6) | async-done | bytes 1441824 | tf_op jit(solution)/shard_map/all_to_all | solution.py:99
  224.4 5.4 gather_fusion.6
  238.1 6.7 %convolution_convert_fusion = bf16[3,512,1408]{1,2,0:T(8,128)(2,1)} fusion(bf16[3,512,512]{2,1,0:T(8,128)(2,1)S(1)} %bitcast.71, bf16[1,512,1408]{2,1,0:T(8,128)(2,1)} %copy.83, bf16[2,512,1408]{2,1,0:T(8,128)(2,1)S(1)} %constant_dynamic-update-slice_fusion), kind=kOutput, calls=%fused_computation.10 | convolution fusion | flops 2218917888 | bytes 10223616 | tf_op jit(solution)/shard_map/grd,gdf->grf/dot_general | solution.py:147
  244.9 14.2 %all-to-all-done = bf16[3,8,64,512]{3,2,0,1:T(8,128)(2,1)} async-done(((bf16[3,8,64,512]{3,2,0,1:T(8,128)(2,1)}), bf16[3,8,64,512]{3,2,0,1:T(8,128)(2,1)}, u32[]{:S(2)}, u32[]{:S(2)}) %all-to-all-start) | async-done | bytes 1572896 | tf_op jit(solution)/shard_map/all_to_all | solution.py:63
  259.1 38.2 %all_to_all.46 = bf16[8,64,1408]{2,1,0:T(8,128)(2,1)} all-to-all(bf16[8,64,1408]{2,1,0:T(8,128)(2,1)S(1)} %copy-done.17), channel_id=1, replica_groups=mesh['expert'=8,'hidden'=4] {'expert'}, dimensions={0} | all-to-all | bytes 2883584 | tf_op jit(solution)/shard_map/all_to_all | solution.py:97
  315.8 5.4 gather_fusion.2
  321.2 14.0 %all-to-all-done.4 = bf16[8,64,1408]{2,1,0:T(8,128)(2,1)} async-done(((bf16[8,64,1408]{2,1,0:T(8,128)(2,1)}), bf16[8,64,1408]{2,1,0:T(8,128)(2,1)}, u32[]{:S(2)}, u32[]{:S(2)}) %all-to-all-start.4) | async-done | bytes 1441824 | tf_op jit(solution)/shard_map/all_to_all | solution.py:98
  336.9 5.4 gather_fusion.4
  342.3 5.2 constant_dynamic-update-slice_fusion.2
  347.5 6.3 %convolution_convert_fusion.2 = bf16[3,512,1408]{1,2,0:T(8,128)(2,1)} fusion(bf16[3,512,512]{2,1,0:T(8,128)(2,1)S(1)} %bitcast.67, bf16[1,512,1408]{1,2,0:T(8,128)(2,1)S(1)} %get-tuple-element.9, bf16[2,512,1408]{1,2,0:T(8,128)(2,1)} %get-tuple-element.8), kind=kOutput, calls=%fused_computation.12 | convolution fusion | flops 2218917888 | bytes 10223616 | tf_op jit(solution)/shard_map/grd,gdf->grf/dot_general | solution.py:119
  354.1 6.3 %convolution_convert_fusion.1 = bf16[3,512,1408]{1,2,0:T(8,128)(2,1)} fusion(bf16[3,512,512]{2,1,0:T(8,128)(2,1)S(1)} %bitcast.68, bf16[1,512,1408]{1,2,0:T(8,128)(2,1)S(1)} %get-tuple-element.27, bf16[2,512,1408]{1,2,0:T(8,128)(2,1)} %get-tuple-element.26), kind=kOutput, calls=%fused_computation.11 | convolution fusion | flops 2218917888 | bytes 10223616 | tf_op jit(solution)/shard_map/grd,gdf->grf/dot_general | solution.py:120
  360.5 37.6 %reduce-scatter.4.cloned.1.call-done = bf16[3,512,352]{1,2,0:T(8,128)(2,1)} async-done(((bf16[3,512,1408]{1,2,0:T(8,128)(2,1)}), bf16[3,512,352]{1,2,0:T(8,128)(2,1)}) %reduce-scatter.4.cloned.1.call-update) | async-done | bytes 1081360 | tf_op jit(solution)/shard_map/reduce_scatter | solution.py:122
  398.1 47.9 %reduce-scatter.6.cloned.1.call-done = bf16[3,512,352]{1,2,0:T(8,128)(2,1)} async-done(((bf16[3,512,1408]{1,2,0:T(8,128)(2,1)}), bf16[3,512,352]{1,2,0:T(8,128)(2,1)}) %reduce-scatter.6.cloned.1.call-update) | async-done | bytes 1081360 | tf_op jit(solution)/shard_map/reduce_scatter | solution.py:125
  446.0 5.2 fusion.17
  452.6 34.0 %all-gather.4.cloned.1.call-done = bf16[3,512,1408]{1,2,0:T(8,128)(2,1)} async-done(((bf16[3,512,352]{1,2,0:T(8,128)(2,1)}), bf16[3,512,1408]{1,2,0:T(8,128)(2,1)}) %all-gather.4.cloned.1.call-update) | async-done | bytes 4325392 | tf_op jit(solution)/shard_map/all_gather | solution.py:130
  486.6 6.2 %fusion.26 = bf16[3,512,512]{2,1,0:T(8,128)(2,1)S(1)} fusion(bf16[3,512,1408]{1,2,0:T(8,128)(2,1)} %all-gather.4.cloned.1.call-done, bf16[1,512,1408]{2,1,0:T(8,128)(2,1)S(1)} %copy-done.11, bf16[2,512,1408]{2,1,0:T(8,128)(2,1)} %copy-done.6), kind=kOutput, calls=%fused_computation.54 | convolution fusion | flops 2217541632 | bytes 10223616 | tf_op jit(solution)/shard_map/grf,gdf->grd/dot_general | solution.py:133
  494.1 5.7 all-to-all-start.7
  499.9 24.1 %all-gather.6.cloned.1.call-done = bf16[3,512,1408]{1,2,0:T(8,128)(2,1)} async-done(((bf16[3,512,352]{1,2,0:T(8,128)(2,1)}), bf16[3,512,1408]{1,2,0:T(8,128)(2,1)}) %all-gather.6.cloned.1.call-update) | async-done | bytes 4325392 | tf_op jit(solution)/shard_map/all_gather | solution.py:154
  524.0 5.0 fusion.50
  531.7 29.6 %all-gather.8.cloned.1.call-done = bf16[3,512,1408]{1,2,0:T(8,128)(2,1)} async-done(((bf16[3,512,352]{1,2,0:T(8,128)(2,1)}), bf16[3,512,1408]{1,2,0:T(8,128)(2,1)}) %all-gather.8.cloned.1.call-update) | async-done | bytes 4325392 | tf_op jit(solution)/shard_map/all_gather | solution.py:157
  (148 shorter events, 111.1 us)
Async XLA Ops:
  7.2 101.4 %copy-start = (bf16[128,512]{1,0:T(8,128)(2,1)S(1)}, bf16[128,512]{1,0:T(8,128)(2,1)}, u32[]{:S(2)}) copy-start(bf16[128,512]{1,0:T(8,128)(2,1)} %param.15) | copy-start | bytes 393220
  7.2 9.6 %copy-start.4 = (bf16[2,512,1408]{2,1,0:T(8,128)(2,1)S(1)}, bf16[2,512,1408]{2,1,0:T(8,128)(2,1)}, u32[]{:S(2)}) copy-start(bf16[2,512,1408]{2,1,0:T(8,128)(2,1)} %param.17) | copy-start | bytes 8650756
  7.2 5.7 copy-start.24
  62.6 37.9 %all-to-all-start.3 = ((bf16[8,64,1408]{2,1,0:T(8,128)(2,1)}), bf16[8,64,1408]{2,1,0:T(8,128)(2,1)}, u32[]{:S(2)}, u32[]{:S(2)}) async-start(bf16[8,64,1408]{2,1,0:T(8,128)(2,1)} %bitcast.77), calls=%async_computation.4 | async-start | bytes 2883584 | tf_op jit(solution)/shard_map/all_to_all | solution.py:87
  69.0 35.0 %copy-start.22 = (s32[128,6]{0,1:T(8,128)S(1)}, s32[128,6]{0,1:T(8,128)}, u32[]{:S(2)}) copy-start(s32[128,6]{0,1:T(8,128)} %param.19) | copy-start | bytes 9220
  69.0 35.4 %copy-start.23 = (f32[128,6]{0,1:T(8,128)S(1)}, f32[128,6]{0,1:T(8,128)}, u32[]{:S(2)}) copy-start(f32[128,6]{0,1:T(8,128)} %param.20) | copy-start | bytes 9220
  100.4 37.7 %all-to-all-start.1 = ((bf16[8,64,1408]{2,1,0:T(8,128)(2,1)}), bf16[8,64,1408]{2,1,0:T(8,128)(2,1)S(1)}, u32[]{:S(2)}, u32[]{:S(2)}) async-start(bf16[8,64,1408]{2,1,0:T(8,128)(2,1)} %bitcast.80), calls=%async_computation.1 | async-start | bytes 2883584 | tf_op jit(solution)/shard_map/all_to_all | solution.py:86
  110.4 32.6 %copy-start.12 = (bf16[8,64,1408]{2,1,0:T(8,128)(2,1)S(1)}, bf16[8,64,1408]{2,1,0:T(8,128)(2,1)}, u32[]{:S(2)}) copy-start(bf16[8,64,1408]{2,1,0:T(8,128)(2,1)} %all_to_all.45) | copy-start | bytes 4325380
  139.2 40.8 %all-to-all-start.8 = ((bf16[3,8,64,512]{3,2,0,1:T(8,128)(2,1)}), bf16[3,8,64,512]{3,2,0,1:T(8,128)(2,1)S(1)}, u32[]{:S(2)}, u32[]{:S(2)}) async-start(bf16[3,8,64,512]{3,2,0,1:T(8,128)(2,1)} %copy.89), calls=%async_computation.10 | async-start | bytes 3145728 | tf_op jit(solution)/shard_map/all_to_all | solution.py:66
  154.4 30.0 %copy-start.10 = (bf16[1,512,1408]{2,1,0:T(8,128)(2,1)S(1)}, bf16[1,512,1408]{2,1,0:T(8,128)(2,1)}, u32[]{:S(2)}) copy-start(bf16[1,512,1408]{2,1,0:T(8,128)(2,1)} %get-tuple-element.18) | copy-start | bytes 4325380
  180.1 38.1 %all-to-all-start.6 = ((bf16[8,64,1408]{2,1,0:T(8,128)(2,1)}), bf16[8,64,1408]{2,1,0:T(8,128)(2,1)}, u32[]{:S(2)}, u32[]{:S(2)}) async-start(bf16[8,64,1408]{2,1,0:T(8,128)(2,1)} %get-tuple-element.28), calls=%async_computation.8 | async-start | bytes 2883584 | tf_op jit(solution)/shard_map/all_to_all | solution.py:99
  218.2 40.9 %all-to-all-start = ((bf16[3,8,64,512]{3,2,0,1:T(8,128)(2,1)}), bf16[3,8,64,512]{3,2,0,1:T(8,128)(2,1)}, u32[]{:S(2)}, u32[]{:S(2)}) async-start(bf16[3,8,64,512]{3,2,0,1:T(8,128)(2,1)} %copy.73), calls=%async_computation | async-start | bytes 3145728 | tf_op jit(solution)/shard_map/all_to_all | solution.py:63
  222.5 138.0 %reduce-scatter.8.cloned.1.call-start = ((), (), s32[]{:S(2)}) async-start(), calls=%async_computation.15 | async-start | bytes 5406720 | tf_op jit(solution)/shard_map/reduce_scatter | solution.py:150
  224.4 5.4 copy-start.15
  238.0 6.9 %copy-start.6 = (bf16[2,512,1408]{2,1,0:T(8,128)(2,1)}, bf16[2,512,1408]{2,1,0:T(8,128)(2,1)S(1)}, u32[]{:S(2)}) copy-start(bf16[2,512,1408]{2,1,0:T(8,128)(2,1)S(1)} %constant_dynamic-update-slice_fusion) | copy-start | bytes 8650756
  244.8 14.3 %copy-start.17 = (bf16[8,64,1408]{2,1,0:T(8,128)(2,1)S(1)}, bf16[8,64,1408]{2,1,0:T(8,128)(2,1)}, u32[]{:S(2)}) copy-start(bf16[8,64,1408]{2,1,0:T(8,128)(2,1)} %get-tuple-element.30) | copy-start | bytes 4325380
  297.3 37.9 %all-to-all-start.4 = ((bf16[8,64,1408]{2,1,0:T(8,128)(2,1)}), bf16[8,64,1408]{2,1,0:T(8,128)(2,1)}, u32[]{:S(2)}, u32[]{:S(2)}) async-start(bf16[8,64,1408]{2,1,0:T(8,128)(2,1)} %get-tuple-element.29), calls=%async_computation.5 | async-start | bytes 2883584 | tf_op jit(solution)/shard_map/all_to_all | solution.py:98
  301.9 96.1 %reduce-scatter.4.cloned.1.call-start = ((), (), s32[]{:S(2)}) async-start(), calls=%async_computation.12 | async-start | bytes 5406720 | tf_op jit(solution)/shard_map/reduce_scatter | solution.py:122
  353.8 92.2 %reduce-scatter.6.cloned.1.call-start = ((), (), s32[]{:S(2)}) async-start(), calls=%async_computation.13 | async-start | bytes 5406720 | tf_op jit(solution)/shard_map/reduce_scatter | solution.py:125
  360.4 126.2 %all-gather.4.cloned.1.call-start = ((), (), s32[]{:S(2)}) async-start(), calls=%async_computation.14 | async-start | bytes 5406720 | tf_op jit(solution)/shard_map/all_gather | solution.py:130
  451.2 35.4 %copy-start.11 = (bf16[1,512,1408]{2,1,0:T(8,128)(2,1)S(1)}, bf16[1,512,1408]{2,1,0:T(8,128)(2,1)}, u32[]{:S(2)}) copy-start(bf16[1,512,1408]{2,1,0:T(8,128)(2,1)} %copy.83) | copy-start | bytes 4325380
  451.2 72.7 %all-gather.6.cloned.1.call-start = ((), (), s32[]{:S(2)}) async-start(), calls=%async_computation.16 | async-start | bytes 5406720 | tf_op jit(solution)/shard_map/all_gather | solution.py:154
  451.8 109.5 %all-gather.8.cloned.1.call-start = ((), (), s32[]{:S(2)}) async-start(), calls=%async_computation.17 | async-start | bytes 5406720 | tf_op jit(solution)/shard_map/all_gather | solution.py:157
  494.1 82.0 %all-to-all-start.7 = ((bf16[3,8,64,512]{3,2,0,1:T(8,128)(2,1)}), bf16[3,8,64,512]{3,2,0,1:T(8,128)(2,1)S(1)}, u32[]{:S(2)}, u32[]{:S(2)}) async-start(bf16[3,8,64,512]{3,2,0,1:T(8,128)(2,1)} %copy.85), calls=%async_computation.9 | async-start | bytes 3145728 | tf_op jit(solution)/shard_map/all_to_all | solution.py:136
  (17 other events, 51.4 us)
Sparse Core Ops, SparseCore 0:
  245.0 46.5 reduce-scatter.7
  353.9 44.0 reduce-scatter.3
  400.6 45.3 reduce-scatter.5
  451.4 35.2 all-gather.3
  488.7 35.2 all-gather.5
  526.0 35.2 all-gather.7
where the time goes:
time: 595 us; the launch traced here: 588 us
  waiting for transfers between devices  316 us (53%)
  blocking collectives  80 us (13%)
  local copies, waits for them, and re-layouts  68.6 us (12%)
  matrix products  40.6 us (7%)
  other arithmetic  32.2 us (5%)
  starting transfers between devices  31.3 us (5%)
  between operations  19 us (3%)
    reduce_scatter x1, waiting for transfers between devices, shards(): lax.psum_scatter(up_part.astype(jnp.bfloat16), 'hidden', scatter_dimensio...  47.9 us
    all_to_all x1, blocking collectives, shards(): lax.all_to_all(out_down, 'expert', split_axis=0, concat_axis=0, tiled=True)  41.7 us
    all_to_all x1, blocking collectives, shards(): lax.all_to_all(relay_gate, 'expert', split_axis=0, concat_axis=0, tiled=T...  38.2 us
    reduce_scatter x1, waiting for transfers between devices, shards(): lax.psum_scatter(gate_part.astype(jnp.bfloat16), 'hidden', scatter_dimens...  37.6 us
    all_gather x1, waiting for transfers between devices, shards(): lax.all_gather((active * up_sum).astype(jnp.bfloat16), 'hidden', axis=2,...  34 us
    all_to_all x1, waiting for transfers between devices, shards(): lax.all_to_all(out_up, 'expert', split_axis=0, concat_axis=0, tiled=True)  31.4 us
    all_gather x1, waiting for transfers between devices, shards(): lax.all_gather((back_sum * active).astype(jnp.bfloat16), 'hidden', axis=2...  29.6 us
    all_to_all x1, waiting for transfers between devices, shards(): lax.all_to_all(relay_down, 'expert', split_axis=0, concat_axis=0, tiled=T...  29 us
  transfers between devices with their start and end apart: 13, of which 11 were waited for; matrix products, arithmetic and copies ran while one was open for 20% of the time, Pallas kernels for 0%

commit v1 on v0

v1 whole, which is shorter than its diff:
```python
import functools

import jax
import jax.numpy as jnp
from jax import lax
from jax.sharding import PartitionSpec as P

F32 = jnp.float32
INLINE = 8
BF16 = jnp.bfloat16


def dot(a, b, ca, cb):
    return lax.dot_general(a, b, (((ca,), (cb,)), ((), ())), preferred_element_type=F32)


def xor_pairs(count, bits):
    return [(i, i ^ bits) for i in range(count)]


def with_partner(count, apart, run, *args):
    def exchange(bits, values):
        return [lax.ppermute(v, "expert", xor_pairs(count, bits)) for v in values]

    choices = range(1, count)
    if count <= INLINE:
        branches = [functools.partial(run, functools.partial(exchange, b)) for b in choices]
        return lax.switch(apart - 1, branches, *args)
    branches = [functools.partial(exchange, b) for b in choices]
    return run(lambda values: lax.switch(apart - 1, branches, values), *args)


def activations(gate_sum, up_sum, back_sum):
    sigma = jax.nn.sigmoid(gate_sum)
    active = gate_sum * sigma
    slope = sigma * (1.0 + gate_sum * (1.0 - sigma))
    return (
        (active * up_sum).astype(BF16),
        (back_sum * up_sum * slope).astype(BF16),
        (back_sum * active).astype(BF16),
    )


def shards(
    tokens,
    cotangent,
    gate_weight,
    up_weight,
    down_weight,
    routing,
    route_weight,
    merge_source,
    merge_target,
    neuron_perm,
):
    devices_n = lax.axis_size("expert")
    hidden_n = lax.axis_size("hidden")
    me = lax.axis_index("expert")
    low_bit = lax.axis_index("hidden") % 2
    exp_local, width, neurons = gate_weight.shape
    experts = exp_local * devices_n
    tok_local, top_count = routing.shape
    tok_all = tok_local * devices_n
    depth = max(2, tok_local * top_count * 4 // (3 * experts))
    slots = devices_n * depth
    half = neurons // 2
    weights = (gate_weight, up_weight, down_weight)

    source_dev = merge_source // exp_local
    target_dev = merge_target // exp_local
    is_source = source_dev == me
    is_target = target_dev == me
    mine = is_source | is_target
    am_target = jnp.any(is_target)
    partner = jnp.sum(jnp.where(is_source, target_dev, 0) + jnp.where(is_target, source_dev, 0))
    source_e = jnp.sum(jnp.where(mine, merge_source, 0))
    target_e = jnp.sum(jnp.where(mine, merge_target, 0))
    merged_slot = jnp.where(am_target, target_e, source_e) % exp_local
    other_slot = exp_local - 1 - merged_slot
    other_e = me * exp_local + other_slot
    perm = jnp.sum(jnp.where(mine[:, None], neuron_perm, 0), axis=0)

    expert_ids = jnp.arange(experts, dtype=jnp.int32)
    route = jnp.sum(
        jnp.where(routing[:, :, None] == expert_ids, route_weight[:, :, None], 0.0), axis=1
    )
    high = lax.reduce_precision(route, 8, 7)
    middle = lax.reduce_precision(route - high, 8, 7)
    low = route - high - middle
    pieces = jnp.concatenate([high, middle, low], axis=1).astype(BF16)
    pad = -pieces.shape[1] % 128
    payload = jnp.concatenate(
        [tokens, cotangent, jnp.pad(pieces, ((0, 0), (0, pad)))], axis=1
    )
    gathered = lax.all_gather(payload, "expert", axis=0, tiled=True)

    order = jnp.where(am_target, jnp.arange(neurons, dtype=jnp.int32), perm)
    keep_order = jnp.where(am_target, order[:half], order[half:])
    send_order = jnp.where(am_target, order[half:], order[:half])
    columns = jnp.arange(neurons, dtype=jnp.int32)
    keep_hot = (keep_order[:, None] == columns[None, :]).astype(BF16)
    send_hot = (send_order[:, None] == columns[None, :]).astype(BF16)
    chosen = [lax.dynamic_index_in_dim(w, merged_slot, 0, keepdims=False) for w in weights]
    others = [lax.dynamic_index_in_dim(w, other_slot, 0, keepdims=False) for w in weights]
    sends = [dot(send_hot, w, 1, 1).astype(BF16) for w in chosen]
    keeps = [dot(keep_hot, w, 1, 1).astype(BF16) for w in chosen]

    inputs_x = gathered[:, :width]
    inputs_c = gathered[:, width : 2 * width]
    parts = gathered[:, 2 * width : 2 * width + 3 * experts].astype(F32)
    route_all = parts[:, :experts] + parts[:, experts : 2 * experts] + parts[:, 2 * experts :]
    merged_hit = (expert_ids == source_e) | (expert_ids == target_e)
    merged_p = jnp.sum(jnp.where(merged_hit, route_all, 0.0), axis=1)
    other_p = jnp.sum(jnp.where(expert_ids == other_e, route_all, 0.0), axis=1)
    merged_dy = (merged_p[:, None] * inputs_c.astype(F32)).astype(BF16)

    named = (other_p > 0.0).reshape(devices_n, tok_local)
    upper = jnp.arange(tok_local)[:, None] <= jnp.arange(tok_local)[None, :]
    rank = dot(named.astype(BF16), upper.astype(BF16), 1, 0).astype(jnp.int32) - 1
    block = (jnp.arange(devices_n, dtype=jnp.int32) + (1 - low_bit) * (devices_n // 2)) % devices_n
    place = jnp.where(named, block[:, None] * depth + rank, -1).reshape(tok_all)
    slot_hot = jnp.arange(slots, dtype=jnp.int32)[:, None] == place[None, :]
    slot_p = jnp.sum(jnp.where(slot_hot, other_p[None, :], 0.0), axis=1)
    slot_hot = slot_hot.astype(BF16)
    other_x = dot(slot_hot, inputs_x, 1, 0).astype(BF16)
    other_dy = (dot(slot_hot, inputs_c, 1, 0) * slot_p[:, None]).astype(BF16)

    def reduced(send_part, keep_part):
        total = keep_part
        if hidden_n > 1:
            total = total + lax.ppermute(send_part.astype(BF16), "hidden", xor_pairs(hidden_n, 1))
        bit = 2
        while bit < hidden_n:
            rounded = total.astype(BF16)
            total = rounded.astype(F32) + lax.ppermute(
                rounded, "hidden", xor_pairs(hidden_n, bit)
            ).astype(F32)
            bit *= 2
        return total

    def swapped(value):
        return lax.ppermute(value, "hidden", xor_pairs(hidden_n, 1))

    slots_half = slots // 2
    quarter = half // 2

    def forward(
        exchange, sends, keeps, others, inputs_x, merged_dy, other_x, other_dy, slot_p, merged_p
    ):
        arrived = exchange(sends)
        sums = [
            reduced(dot(value[:slots_half], w, 1, 0), dot(value[slots_half:], w, 1, 0))
            for value, w in zip((other_x, other_x, other_dy), others)
        ]
        acts = activations(*sums)
        other_acts = [jnp.concatenate([swapped(a), a], axis=0) for a in acts]
        other_y = dot(other_acts[0], others[2], 1, 1)
        other_y = (other_y * slot_p[:, None]).astype(BF16)

        merged = [
            (0.5 * (k.astype(F32) + a.astype(F32))).astype(BF16)
            for k, a in zip(keeps, arrived)
        ]
        sums = []
        for value, w in zip((inputs_x, inputs_x, merged_dy), merged):
            w_send = lax.dynamic_slice_in_dim(w, (1 - low_bit) * quarter, quarter, 0)
            w_keep = lax.dynamic_slice_in_dim(w, low_bit * quarter, quarter, 0)
            sums.append(reduced(dot(w_send, value, 1, 1), dot(w_keep, value, 1, 1)))
        acts = activations(*sums)
        merged_acts = []
        for a in acts:
            b = swapped(a)
            merged_acts.append(
                jnp.concatenate(
                    [jnp.where(low_bit == 0, a, b), jnp.where(low_bit == 0, b, a)], axis=0
                )
            )
        merged_y = dot(merged_acts[0], merged[2], 0, 0)
        mixed = dot(slot_hot, other_y, 0, 0) + merged_p[:, None] * merged_y
        return mixed.astype(BF16), other_acts, merged_acts

    mixed, other_acts, merged_acts = with_partner(
        devices_n,
        me ^ partner,
        forward,
        sends,
        keeps,
        others,
        inputs_x,
        merged_dy,
        other_x,
        other_dy,
        slot_p,
        merged_p,
    )
    mixed = lax.psum_scatter(mixed, "expert", scatter_dimension=0, tiled=True)

    def backward(exchange, inputs_x, merged_dy, merged_acts):
        h, dg, du = merged_acts
        own = [
            dot(value, a, 0, 1).astype(BF16)
            for value, a in ((merged_dy, h), (inputs_x, dg), (inputs_x, du))
        ]
        return own, exchange(own)

    own, returned = with_partner(
        devices_n, me ^ partner, backward, inputs_x, merged_dy, merged_acts
    )
    h, dg, du = other_acts
    outs = []
    for value, a, mine_half, far_half in zip(
        (other_dy, other_x, other_x), (h, dg, du), own, returned
    ):
        other_grad = dot(value, a, 0, 0).astype(BF16)
        merged_grad = jnp.where(
            am_target, jnp.concatenate([mine_half, far_half], axis=1), jnp.zeros((), BF16)
        )
        outs.append(
            jnp.where(
                merged_slot == 0,
                jnp.stack([merged_grad, other_grad]),
                jnp.stack([other_grad, merged_grad]),
            )
        )
    grad_down, grad_gate, grad_up = outs
    return mixed, grad_gate, grad_up, grad_down


def solution(mesh):
    placed = (
        P("expert", "hidden"),
        P("expert", "hidden"),
        P("expert", "hidden", None),
        P("expert", "hidden", None),
        P("expert", "hidden", None),
        P("expert", None),
        P("expert", None),
        P(),
        P(),
        P(),
    )
    return jax.shard_map(
        shards,
        mesh=mesh,
        in_specs=placed,
        out_specs=(
            P("expert", "hidden"),
            P("expert", "hidden", None),
            P("expert", "hidden", None),
            P("expert", "hidden", None),
        ),
        check_vma=False,
    )
```

time: 595 us -> 406 us (0.68)
  waiting for transfers between devices: 316 us -> 201 us
  blocking collectives: 80 us -> 0 us
  loops' own time: 0 us -> 50.9 us
  local copies, waits for them, and re-layouts: 68.6 us -> 22.4 us
  starting transfers between devices: 31.3 us -> 14.5 us
  other arithmetic: 32.2 us -> 45.2 us
  matrix products: 40.6 us -> 47.2 us
    all_to_all x7 -> x0, waiting for transfers between devices: 142 us -> none  [the longest x1 31.4 us: shards(): lax.all_to_all(out_up, 'expert', split_axis=0, concat_axis=0, tiled=True)]
    ppermute x0 -> x24, waiting for transfers between devices: none -> 129 us  [the longest x6 75.4 us: exchange(): return [lax.ppermute(v, 'expert', xor_pairs(count, bits)) for v in values]]
    all_to_all x2 -> x0, blocking collectives: 80 us -> none  [the longest x1 41.7 us: shards(): lax.all_to_all(out_down, 'expert', split_axis=0, concat_axis=0, tiled=True)]
    all_gather x3 -> x1, waiting for transfers between devices: 87.7 us -> 26.1 us  [shards(): gathered = lax.all_gather(payload, 'expert', axis=0, tiled=True)]
    unnamed x0 -> x2, loops' own time: none -> 50.9 us
    reduce_scatter x3 -> x1, waiting for transfers between devices: 85.5 us -> 45.2 us  [shards(): mixed = lax.psum_scatter(mixed, 'expert', scatter_dimension=0, tiled=True)]
    all_to_all x7 -> x0, starting transfers between devices: 30.7 us -> none  [the longest x1 5.74 us: shards(): lax.all_to_all(outputs_y.reshape(slot_shape), 'expert', split_axis=1, con...]
    gather x8 -> x0, local copies, waits for them, and re-layouts: 26 us -> none  [the longest x3 16.1 us: merged_groups(): jnp.take(arrived.reshape(width_local, neurons), order_perm, axis=1)]
  transfers between devices with their start and end apart: 13 -> 26, of which waited for: 11 -> 12; matrix products, arithmetic and copies ran while one was open for 20% -> 22% of each run, Pallas kernels for 0% -> 0%
where the time goes in v1:
time: 406 us; the launch traced here: 398 us
  waiting for transfers between devices  201 us (50%)
  loops' own time  50.9 us (13%)
  matrix products  47.2 us (12%)
  other arithmetic  45.2 us (11%)
  local copies, waits for them, and re-layouts  22.4 us (6%)
  between operations  17.3 us (4%)
  starting transfers between devices  14.5 us (4%)
    ppermute x6, waiting for transfers between devices, exchange(): return [lax.ppermute(v, 'expert', xor_pairs(count, bits)) for v in values]  75.4 us
    ppermute x6, waiting for transfers between devices, reduced(): lax.ppermute(rounded, 'hidden', xor_pairs(hidden_n, bit)).astype(F32)  53.8 us
    unnamed x2, loops' own time  50.9 us
    dot_general x29, matrix products, dot(): lax.dot_general(a, b, (((ca,), (cb,)), ((), ())), preferred_element_type=...  47.2 us
    reduce_scatter x1, waiting for transfers between devices, shards(): mixed = lax.psum_scatter(mixed, 'expert', scatter_dimension=0, tiled=True)  45.2 us
    all_gather x1, waiting for transfers between devices, shards(): gathered = lax.all_gather(payload, 'expert', axis=0, tiled=True)  26.1 us
    another operation x41, local copies, waits for them, and re-layouts  11.8 us
  transfers between devices with their start and end apart: 26, of which 12 were waited for; matrix products, arithmetic and copies ran while one was open for 22% of the time, Pallas kernels for 0%

profile of v1, /device:TPU:0, one launch (start us, length us, event | category | flops | bytes accessed | tf_op | source)
XLA Modules:
  0.0 398.1 jit_solution(4977003809712363943)
XLA Ops:
  27.7 2.3 fusion.316
  34.3 2.3 fusion.307
  38.8 26.1 %all-gather.2.cloned.1.call-done = bf16[1024,1152]{1,0:T(8,128)(2,1)} async-done(((bf16[128,1152]{1,0:T(8,128)(2,1)}), bf16[1024,1152]{1,0:T(8,128)(2,1)}) %all-gather.2.cloned.1.call-update) | async-done | bytes 2359312 | tf_op jit(solution)/shard_map/all_gather | solution.py:95
  72.1 194.3 %conditional.4 = (bf16[512,1408]{1,0:T(8,128)(2,1)}, bf16[512,1408]{1,0:T(8,128)(2,1)S(1)}, bf16[512,1408]{1,0:T(8,128)(2,1)S(1)}, bf16[512,1408]{1,0:T(8,128)(2...) conditional(s32[]{:T(128)} %clamp.4, ...), branch_computations={%region_9.10_spmd, %region_10.11_spmd, %region_11.12_spmd, %region... | conditional | flops 6493798400 | bytes 211094912
  72.4 2.6 convolution_convert_fusion
  86.1 10.2 %collective-permute-done.30 = bf16[704,512]{1,0:T(8,128)(2,1)} collective-permute-done((bf16[704,512]{1,0:T(8,128)(2,1)}, bf16[704,512]{1,0:T(8,128)(2,1)}, u32[]{:S(2)}, u32[]{:S(2)}) %collective-permute-start.30) | collective-permute-done | bytes 720928 | tf_op jit(solution)/shard_map/cond/branch_0_fun/ppermute | solution.py:23
  99.7 12.1 %collective-permute-done.33 = bf16[704,512]{1,0:T(8,128)(2,1)} collective-permute-done((bf16[704,512]{1,0:T(8,128)(2,1)}, bf16[704,512]{1,0:T(8,128)(2,1)}, u32[]{:S(2)}, u32[]{:S(2)}) %collective-permute-start.33) | collective-permute-done | bytes 720928 | tf_op jit(solution)/shard_map/cond/branch_0_fun/ppermute | solution.py:23
  113.7 12.5 %collective-permute-done.37 = bf16[704,512]{1,0:T(8,128)(2,1)S(1)} collective-permute-done((bf16[704,512]{1,0:T(8,128)(2,1)}, bf16[704,512]{1,0:T(8,128)(2,1)S(1)}, u32[]{:S(2)}, u32[]{:S(2)}) %collective-permute-start.37) | collective-permute-done | bytes 720928 | tf_op jit(solution)/shard_map/cond/branch_0_fun/ppermute | solution.py:23
  138.1 10.5 %collective-permute-done.22 = bf16[256,1408]{1,0:T(8,128)(2,1)S(1)} collective-permute-done((bf16[256,1408]{1,0:T(8,128)(2,1)S(1)}, bf16[256,1408]{1,0:T(8,128)(2,1)S(1)}, u32[]{:S(2)}, u32[]{:S(2)}) %collective-permute-start.22) | collective-permute-done | bytes 720928 | tf_op jit(solution)/shard_map/cond/branch_0_fun/ppermute | solution.py:135
  148.7 2.3 multiply_convert_fusion.6
  151.5 12.7 %collective-permute-done.32 = bf16[352,1024]{1,0:T(8,128)(2,1)} collective-permute-done((bf16[352,1024]{1,0:T(8,128)(2,1)}, bf16[352,1024]{1,0:T(8,128)(2,1)}, u32[]{:S(2)}, u32[]{:S(2)}) %collective-permute-start.32) | collective-permute-done | bytes 720928 | tf_op jit(solution)/shard_map/cond/branch_0_fun/ppermute | solution.py:135
  164.2 15.4 %collective-permute-done.35 = bf16[352,1024]{1,0:T(8,128)(2,1)} collective-permute-done((bf16[352,1024]{1,0:T(8,128)(2,1)}, bf16[352,1024]{1,0:T(8,128)(2,1)}, u32[]{:S(2)}, u32[]{:S(2)}) %collective-permute-start.35) | collective-permute-done | bytes 720928 | tf_op jit(solution)/shard_map/cond/branch_0_fun/ppermute | solution.py:135
  179.7 15.1 %collective-permute-done.39 = bf16[352,1024]{1,0:T(8,128)(2,1)} collective-permute-done((bf16[352,1024]{1,0:T(8,128)(2,1)}, bf16[352,1024]{1,0:T(8,128)(2,1)}, u32[]{:S(2)}, u32[]{:S(2)}) %collective-permute-start.39) | collective-permute-done | bytes 720928 | tf_op jit(solution)/shard_map/cond/branch_0_fun/ppermute | solution.py:135
  194.7 4.9 %multiply_convert_fusion = (bf16[352,1024]{1,0:T(8,128)(2,1)}, bf16[352,1024]{1,0:T(8,128)(2,1)}, bf16[352,1024]{1,0:T(8,128)(2,1)}) fusion(bf16[352,1024]{1,0:T(8,128)(2,1)} %collective-permute-done.39, bf16[352,1024]{1,0:T(8,128)(2,1)} %add_convert_fusion, bf16[352,1024]{1,0:T(8,128)(2,1)} %collective-permute-done.32, ...), kind=kLoop, calls=%fused_computation.10 | loop fusion | flops 8650752 | bytes 6488064 | tf_op jit(solution)/shard_map/cond/branch_0_fun/convert_element_type | solution.py:40
  199.7 2.5 pad_maximum_fusion
  202.2 4.7 %convolution_bitcast_fusion = f32[1024,512]{0,1:T(8,128)} fusion(bf16[512,1024]{1,0:T(8,128)(2,1)} %get-tuple-element.354, bf16[512,1408]{1,0:T(8,128)(2,1)} %pad_maximum_fusion, bf16[512,1408]{1,0:T(8,128)(2,1)S(1)} %get-tuple-element.343, f32[512]{0:T(512)S(1)} %get-tuple-element.353), kind=kOutput, calls=%fused_computation.3 | convolution fusion | flops 1275592704 | bytes 6031360 | tf_op jit(solution)/shard_map/cond/branch_0_fun/dot_general | solution.py:14
  206.9 2.9 copy.41
  269.3 55.6 %conditional.5 = (bf16[512,704]{0,1:T(8,128)(2,1)}, bf16[512,704]{0,1:T(8,128)(2,1)}, bf16[512,704]{0,1:T(8,128)(2,1)}, bf16[1,512,704]{2,1,0:T(8,128)(2,1)S(1)}...) conditional(s32[]{:T(128)} %clamp.4, ...), branch_computations={%region_17.18_spmd, %region_18.19_spmd, %region_19.20_spmd, %regio... | conditional | flops 2214592512 | bytes 31260924
  276.4 12.8 %collective-permute-done.2 = bf16[512,704]{0,1:T(8,128)(2,1)S(1)} collective-permute-done((bf16[512,704]{0,1:T(8,128)(2,1)S(1)}, bf16[512,704]{0,1:T(8,128)(2,1)S(1)}, u32[]{:S(2)}, u32[]{:S(2)}) %collective-permute-start.2) | collective-permute-done | bytes 720928 | tf_op jit(solution)/shard_map/cond/branch_0_fun/ppermute | solution.py:23
  291.4 13.2 %collective-permute-done.1 = bf16[512,704]{0,1:T(8,128)(2,1)S(1)} collective-permute-done((bf16[512,704]{0,1:T(8,128)(2,1)}, bf16[512,704]{0,1:T(8,128)(2,1)S(1)}, u32[]{:S(2)}, u32[]{:S(2)}) %collective-permute-start.1) | collective-permute-done | bytes 720928 | tf_op jit(solution)/shard_map/cond/branch_0_fun/ppermute | solution.py:23
  304.9 14.7 %collective-permute-done = bf16[512,704]{0,1:T(8,128)(2,1)S(1)} collective-permute-done((bf16[512,704]{0,1:T(8,128)(2,1)}, bf16[512,704]{0,1:T(8,128)(2,1)S(1)}, u32[]{:S(2)}, u32[]{:S(2)}) %collective-permute-start) | collective-permute-done | bytes 720928 | tf_op jit(solution)/shard_map/cond/branch_0_fun/ppermute | solution.py:23
  324.9 4.0 %add_convert_fusion.42 = bf16[1024,512]{1,0:T(8,128)(2,1)} fusion(f32[1024,512]{1,0:T(8,128)} %get-tuple-element.527, f32[1024,512]{1,0:T(8,128)} %copy-done.110, f32[1024]{0:T(1024)S(1)} %get-tuple-element.513), kind=kLoop, calls=%fused_computation.514 | loop fusion | flops 1572864 | bytes 5246976 | tf_op jit(solution)/shard_map/cond/branch_0_fun/convert_element_type | solution.py:180
  332.1 2.7 fusion.288
  345.8 45.2 %reduce-scatter.2.cloned.1.call-done = bf16[128,512]{1,0:T(8,128)(2,1)} async-done(((bf16[1024,512]{1,0:T(8,128)(2,1)}), bf16[128,512]{1,0:T(8,128)(2,1)}) %reduce-scatter.2.cloned.1.call-update) | async-done | bytes 131088 | tf_op jit(solution)/shard_map/reduce_scatter | solution.py:196
  (187 shorter events, 98.3 us)
Async XLA Ops:
  7.2 57.7 %all-gather.2.cloned.1.call-start = ((), (), s32[]{:S(2)}) async-start(), calls=%async_computation.1 | async-start | bytes 2654208 | tf_op jit(solution)/shard_map/all_gather | solution.py:95
  10.0 381.0 %reduce-scatter.2.cloned.1.call-start = ((), (), s32[]{:S(2)}) async-start(), calls=%async_computation.2 | async-start | bytes 1179648 | tf_op jit(solution)/shard_map/reduce_scatter | solution.py:196
  76.5 6.4 %collective-permute-start.23 = (bf16[256,1408]{1,0:T(8,128)(2,1)}, bf16[256,1408]{1,0:T(8,128)(2,1)}, u32[]{:S(2)}, u32[]{:S(2)}) collective-permute-start(bf16[256,1408]{1,0:T(8,128)(2,1)} %convolution_convert_fusion.1), channel_id=1, source_target_pairs={{0,1},{1,0},{2,3},{3,2},{4,5},{5,4},{6,7},{7,6},{8,9},{9,8},{10,11... | collective-permute-start | bytes 2162696 | tf_op jit(solution)/shard_map/cond/branch_0_fun/ppermute | solution.py:131
  77.0 19.3 %collective-permute-start.30 = (bf16[704,512]{1,0:T(8,128)(2,1)}, bf16[704,512]{1,0:T(8,128)(2,1)}, u32[]{:S(2)}, u32[]{:S(2)}) collective-permute-start(bf16[704,512]{1,0:T(8,128)(2,1)} %get-tuple-element.346), channel_id=1, source_target_pairs={{0,4},{4,0},{8,12},{12,8},{16,20},{20,16},{24,28},{28,24},{1,5},{5... | collective-permute-start | bytes 2162696 | tf_op jit(solution)/shard_map/cond/branch_0_fun/ppermute | solution.py:23
  79.0 48.0 %collective-permute-start.21 = (bf16[256,1408]{1,0:T(8,128)(2,1)}, bf16[256,1408]{1,0:T(8,128)(2,1)}, u32[]{:S(2)}, u32[]{:S(2)}) collective-permute-start(bf16[256,1408]{1,0:T(8,128)(2,1)} %convolution_convert_fusion.2), channel_id=1, source_target_pairs={{0,1},{1,0},{2,3},{3,2},{4,5},{5,4},{6,7},{7,6},{8,9},{9,8},{10,11... | collective-permute-start | bytes 2162696 | tf_op jit(solution)/shard_map/cond/branch_0_fun/ppermute | solution.py:131
  79.0 32.7 %collective-permute-start.33 = (bf16[704,512]{1,0:T(8,128)(2,1)}, bf16[704,512]{1,0:T(8,128)(2,1)}, u32[]{:S(2)}, u32[]{:S(2)}) collective-permute-start(bf16[704,512]{1,0:T(8,128)(2,1)} %get-tuple-element.349), channel_id=1, source_target_pairs={{0,4},{4,0},{8,12},{12,8},{16,20},{20,16},{24,28},{28,24},{1,5},{5... | collective-permute-start | bytes 2162696 | tf_op jit(solution)/shard_map/cond/branch_0_fun/ppermute | solution.py:23
  80.5 45.6 %collective-permute-start.37 = (bf16[704,512]{1,0:T(8,128)(2,1)}, bf16[704,512]{1,0:T(8,128)(2,1)S(1)}, u32[]{:S(2)}, u32[]{:S(2)}) collective-permute-start(bf16[704,512]{1,0:T(8,128)(2,1)} %get-tuple-element.351), channel_id=1, source_target_pairs={{0,4},{4,0},{8,12},{12,8},{16,20},{20,16},{24,28},{28,24},{1,5},{5... | collective-permute-start | bytes 2162696 | tf_op jit(solution)/shard_map/cond/branch_0_fun/ppermute | solution.py:23
  82.9 54.7 %collective-permute-start.27 = (bf16[256,1408]{1,0:T(8,128)(2,1)S(1)}, bf16[256,1408]{1,0:T(8,128)(2,1)S(1)}, u32[]{:S(2)}, u32[]{:S(2)}) collective-permute-start(bf16[256,1408]{1,0:T(8,128)(2,1)S(1)} %add_convert_fusion.3), channel_id=1, source_target_pairs={{0,2},{1,3},{2,0},{3,1},{4,6},{5,7},{6,4},{7,5},{8,10},{9,11},{10,... | collective-permute-start | bytes 2162696 | tf_op jit(solution)/shard_map/cond/branch_0_fun/ppermute | solution.py:135
  96.3 41.9 %collective-permute-start.24 = (bf16[256,1408]{1,0:T(8,128)(2,1)S(1)}, bf16[256,1408]{1,0:T(8,128)(2,1)S(1)}, u32[]{:S(2)}, u32[]{:S(2)}) collective-permute-start(bf16[256,1408]{1,0:T(8,128)(2,1)S(1)} %add_convert_fusion.4), channel_id=1, source_target_pairs={{0,2},{1,3},{2,0},{3,1},{4,6},{5,7},{6,4},{7,5},{8,10},{9,11},{10,... | collective-permute-start | bytes 2162696 | tf_op jit(solution)/shard_map/cond/branch_0_fun/ppermute | solution.py:135
  111.7 17.9 %collective-permute-start.31 = (bf16[352,1024]{1,0:T(8,128)(2,1)S(1)}, bf16[352,1024]{1,0:T(8,128)(2,1)S(1)}, u32[]{:S(2)}, u32[]{:S(2)}) collective-permute-start(bf16[352,1024]{1,0:T(8,128)(2,1)S(1)} %convolution_convert_fusion.5), channel_id=1, source_target_pairs={{0,1},{1,0},{2,3},{3,2},{4,5},{5,4},{6,7},{7,6},{8,9},{9,8},{10,11... | collective-permute-start | bytes 2162696 | tf_op jit(solution)/shard_map/cond/branch_0_fun/ppermute | solution.py:131
  126.1 6.5 %collective-permute-start.34 = (bf16[352,1024]{1,0:T(8,128)(2,1)S(1)}, bf16[352,1024]{1,0:T(8,128)(2,1)S(1)}, u32[]{:S(2)}, u32[]{:S(2)}) collective-permute-start(bf16[352,1024]{1,0:T(8,128)(2,1)S(1)} %convolution_convert_fusion.4), channel_id=1, source_target_pairs={{0,1},{1,0},{2,3},{3,2},{4,5},{5,4},{6,7},{7,6},{8,9},{9,8},{10,11... | collective-permute-start | bytes 2162696 | tf_op jit(solution)/shard_map/cond/branch_0_fun/ppermute | solution.py:131
  127.0 7.7 %collective-permute-start.38 = (bf16[352,1024]{1,0:T(8,128)(2,1)S(1)}, bf16[352,1024]{1,0:T(8,128)(2,1)S(1)}, u32[]{:S(2)}, u32[]{:S(2)}) collective-permute-start(bf16[352,1024]{1,0:T(8,128)(2,1)S(1)} %convolution_convert_fusion.3), channel_id=1, source_target_pairs={{0,1},{1,0},{2,3},{3,2},{4,5},{5,4},{6,7},{7,6},{8,9},{9,8},{10,11... | collective-permute-start | bytes 2162696 | tf_op jit(solution)/shard_map/cond/branch_0_fun/ppermute | solution.py:131
  129.7 19.0 %collective-permute-start.22 = (bf16[256,1408]{1,0:T(8,128)(2,1)S(1)}, bf16[256,1408]{1,0:T(8,128)(2,1)S(1)}, u32[]{:S(2)}, u32[]{:S(2)}) collective-permute-start(bf16[256,1408]{1,0:T(8,128)(2,1)S(1)} %add_convert_fusion.5), channel_id=1, source_target_pairs={{0,2},{1,3},{2,0},{3,1},{4,6},{5,7},{6,4},{7,5},{8,10},{9,11},{10,... | collective-permute-start | bytes 2162696 | tf_op jit(solution)/shard_map/cond/branch_0_fun/ppermute | solution.py:135
  132.6 31.6 %collective-permute-start.32 = (bf16[352,1024]{1,0:T(8,128)(2,1)}, bf16[352,1024]{1,0:T(8,128)(2,1)}, u32[]{:S(2)}, u32[]{:S(2)}) collective-permute-start(bf16[352,1024]{1,0:T(8,128)(2,1)} %add_convert_fusion.2), channel_id=1, source_target_pairs={{0,2},{1,3},{2,0},{3,1},{4,6},{5,7},{6,4},{7,5},{8,10},{9,11},{10,... | collective-permute-start | bytes 2162696 | tf_op jit(solution)/shard_map/cond/branch_0_fun/ppermute | solution.py:135
  134.7 45.0 %collective-permute-start.35 = (bf16[352,1024]{1,0:T(8,128)(2,1)}, bf16[352,1024]{1,0:T(8,128)(2,1)}, u32[]{:S(2)}, u32[]{:S(2)}) collective-permute-start(bf16[352,1024]{1,0:T(8,128)(2,1)} %add_convert_fusion.1), channel_id=1, source_target_pairs={{0,2},{1,3},{2,0},{3,1},{4,6},{5,7},{6,4},{7,5},{8,10},{9,11},{10,... | collective-permute-start | bytes 2162696 | tf_op jit(solution)/shard_map/cond/branch_0_fun/ppermute | solution.py:135
  137.6 57.2 %collective-permute-start.39 = (bf16[352,1024]{1,0:T(8,128)(2,1)}, bf16[352,1024]{1,0:T(8,128)(2,1)}, u32[]{:S(2)}, u32[]{:S(2)}) collective-permute-start(bf16[352,1024]{1,0:T(8,128)(2,1)} %add_convert_fusion), channel_id=1, source_target_pairs={{0,2},{1,3},{2,0},{3,1},{4,6},{5,7},{6,4},{7,5},{8,10},{9,11},{10,... | collective-permute-start | bytes 2162696 | tf_op jit(solution)/shard_map/cond/branch_0_fun/ppermute | solution.py:135
  151.0 48.7 %collective-permute-start.25 = (bf16[256,1408]{1,0:T(8,128)(2,1)}, bf16[256,1408]{1,0:T(8,128)(2,1)}, u32[]{:S(2)}, u32[]{:S(2)}) collective-permute-start(bf16[256,1408]{1,0:T(8,128)(2,1)} %get-tuple-element.544), channel_id=1, source_target_pairs={{0,1},{1,0},{2,3},{3,2},{4,5},{5,4},{6,7},{7,6},{8,9},{9,8},{10,11... | collective-permute-start | bytes 2162696 | tf_op jit(solution)/shard_map/cond/branch_0_fun/ppermute | solution.py:142
  151.0 59.3 %collective-permute-start.29 = (bf16[256,1408]{1,0:T(8,128)(2,1)}, bf16[256,1408]{1,0:T(8,128)(2,1)}, u32[]{:S(2)}, u32[]{:S(2)}) collective-permute-start(bf16[256,1408]{1,0:T(8,128)(2,1)} %get-tuple-element.542), channel_id=1, source_target_pairs={{0,1},{1,0},{2,3},{3,2},{4,5},{5,4},{6,7},{7,6},{8,9},{9,8},{10,11... | collective-permute-start | bytes 2162696 | tf_op jit(solution)/shard_map/cond/branch_0_fun/ppermute | solution.py:142
  164.2 47.4 %collective-permute-start.28 = (bf16[256,1408]{1,0:T(8,128)(2,1)}, bf16[256,1408]{1,0:T(8,128)(2,1)}, u32[]{:S(2)}, u32[]{:S(2)}) collective-permute-start(bf16[256,1408]{1,0:T(8,128)(2,1)} %get-tuple-element.543), channel_id=1, source_target_pairs={{0,1},{1,0},{2,3},{3,2},{4,5},{5,4},{6,7},{7,6},{8,9},{9,8},{10,11... | collective-permute-start | bytes 2162696 | tf_op jit(solution)/shard_map/cond/branch_0_fun/ppermute | solution.py:142
  199.7 13.2 %collective-permute-start.36 = (bf16[352,1024]{1,0:T(8,128)(2,1)}, bf16[352,1024]{1,0:T(8,128)(2,1)}, u32[]{:S(2)}, u32[]{:S(2)}) collective-permute-start(bf16[352,1024]{1,0:T(8,128)(2,1)} %get-tuple-element.541), channel_id=1, source_target_pairs={{0,1},{1,0},{2,3},{3,2},{4,5},{5,4},{6,7},{7,6},{8,9},{9,8},{10,11... | collective-permute-start | bytes 2162696 | tf_op jit(solution)/shard_map/cond/branch_0_fun/ppermute | solution.py:142
  210.3 8.0 %collective-permute-start.40 = (bf16[352,1024]{1,0:T(8,128)(2,1)}, bf16[352,1024]{1,0:T(8,128)(2,1)S(1)}, u32[]{:S(2)}, u32[]{:S(2)}) collective-permute-start(bf16[352,1024]{1,0:T(8,128)(2,1)} %get-tuple-element.540), channel_id=1, source_target_pairs={{0,1},{1,0},{2,3},{3,2},{4,5},{5,4},{6,7},{7,6},{8,9},{9,8},{10,11... | collective-permute-start | bytes 2162696 | tf_op jit(solution)/shard_map/cond/branch_0_fun/ppermute | solution.py:142
  270.2 19.0 %collective-permute-start.2 = (bf16[512,704]{0,1:T(8,128)(2,1)S(1)}, bf16[512,704]{0,1:T(8,128)(2,1)S(1)}, u32[]{:S(2)}, u32[]{:S(2)}) collective-permute-start(bf16[512,704]{0,1:T(8,128)(2,1)S(1)} %fusion.359), channel_id=1, source_target_pairs={{0,4},{4,0},{8,12},{12,8},{16,20},{20,16},{24,28},{28,24},{1,5},{5... | collective-permute-start | bytes 2162696 | tf_op jit(solution)/shard_map/cond/branch_0_fun/ppermute | solution.py:23
  272.6 32.1 %collective-permute-start.1 = (bf16[512,704]{0,1:T(8,128)(2,1)}, bf16[512,704]{0,1:T(8,128)(2,1)S(1)}, u32[]{:S(2)}, u32[]{:S(2)}) collective-permute-start(bf16[512,704]{0,1:T(8,128)(2,1)} %fusion.358), channel_id=1, source_target_pairs={{0,4},{4,0},{8,12},{12,8},{16,20},{20,16},{24,28},{28,24},{1,5},{5... | collective-permute-start | bytes 2162696 | tf_op jit(solution)/shard_map/cond/branch_0_fun/ppermute | solution.py:23
  275.8 43.8 %collective-permute-start = (bf16[512,704]{0,1:T(8,128)(2,1)}, bf16[512,704]{0,1:T(8,128)(2,1)S(1)}, u32[]{:S(2)}, u32[]{:S(2)}) collective-permute-start(bf16[512,704]{0,1:T(8,128)(2,1)} %fusion.357), channel_id=1, source_target_pairs={{0,4},{4,0},{8,12},{12,8},{16,20},{20,16},{24,28},{28,24},{1,5},{5... | collective-permute-start | bytes 2162696 | tf_op jit(solution)/shard_map/cond/branch_0_fun/ppermute | solution.py:23
  (39 other events, 197.4 us)
Sparse Core Ops, SparseCore 0:
  10.2 54.6 all-gather.1
  329.0 61.9 reduce-scatter.1

commit v2 on v1

--- a/solution.py
+++ b/solution.py
@@ -6,7 +6,6 @@
 from jax.sharding import PartitionSpec as P
 
 F32 = jnp.float32
-INLINE = 8
 BF16 = jnp.bfloat16
 
 
@@ -18,16 +17,45 @@
     return [(i, i ^ bits) for i in range(count)]
 
 
-def with_partner(count, apart, run, *args):
-    def exchange(bits, values):
-        return [lax.ppermute(v, "expert", xor_pairs(count, bits)) for v in values]
-
-    choices = range(1, count)
-    if count <= INLINE:
-        branches = [functools.partial(run, functools.partial(exchange, b)) for b in choices]
-        return lax.switch(apart - 1, branches, *args)
-    branches = [functools.partial(exchange, b) for b in choices]
-    return run(lambda values: lax.switch(apart - 1, branches, values), *args)
+def with_partner(count, apart, value):
+    branches = [
+        functools.partial(lax.ppermute, axis_name="expert", perm=xor_pairs(count, bits))
+        for bits in range(1, count)
+    ]
+    return lax.switch(apart - 1, branches, value)
+
+
+def ring_gather(value, count, me):
+    rows = value.shape[0]
+    ring = [(i, (i + 2) % count) for i in range(count)]
+    result = jnp.zeros((rows * count, value.shape[1]), value.dtype)
+    for step in range(count // 2):
+        if step > 0:
+            value = lax.ppermute(value, "expert", ring)
+        twin = lax.ppermute(value, "expert", xor_pairs(count, 1))
+        for block, owner in ((value, me), (twin, me ^ 1)):
+            at = (owner - 2 * step) % count * rows
+            result = lax.dynamic_update_slice_in_dim(result, block, at, 0)
+    return result
+
+
+def ring_scatter(partial, count, me):
+    rows = partial.shape[0] // count
+    ring = [(i, (i + 2) % count) for i in range(count)]
+
+    def block(owner):
+        return lax.dynamic_slice_in_dim(partial, owner % count * rows, rows, 0)
+
+    total = None
+    for step in range(count // 2):
+        twin = lax.ppermute(
+            block((me ^ 1) - 2 * (step + 1)).astype(BF16), "expert", xor_pairs(count, 1)
+        )
+        own = block(me - 2 * (step + 1)).astype(F32) + twin.astype(F32)
+        if step > 0:
+            own = own + lax.ppermute(total, "expert", ring).astype(F32)
+        total = own.astype(BF16)
+    return total
 
 
 def activations(gate_sum, up_sum, back_sum):
@@ -89,10 +117,9 @@
     low = route - high - middle
     pieces = jnp.concatenate([high, middle, low], axis=1).astype(BF16)
     pad = -pieces.shape[1] % 128
-    payload = jnp.concatenate(
-        [tokens, cotangent, jnp.pad(pieces, ((0, 0), (0, pad)))], axis=1
-    )
-    gathered = lax.all_gather(payload, "expert", axis=0, tiled=True)
+    payload = jnp.concatenate([tokens, jnp.pad(pieces, ((0, 0), (0, pad)))], axis=1)
+    gathered = ring_gather(payload, devices_n, me)
+    inputs_c = ring_gather(cotangent, devices_n, me)
 
     order = jnp.where(am_target, jnp.arange(neurons, dtype=jnp.int32), perm)
     keep_order = jnp.where(am_target, order[:half], order[half:])
@@ -106,8 +133,7 @@
     keeps = [dot(keep_hot, w, 1, 1).astype(BF16) for w in chosen]
 
     inputs_x = gathered[:, :width]
-    inputs_c = gathered[:, width : 2 * width]
-    parts = gathered[:, 2 * width : 2 * width + 3 * experts].astype(F32)
+    parts = gathered[:, width : width + 3 * experts].astype(F32)
     route_all = parts[:, :experts] + parts[:, experts : 2 * experts] + parts[:, 2 * experts :]
     merged_hit = (expert_ids == source_e) | (expert_ids == target_e)
     merged_p = jnp.sum(jnp.where(merged_hit, route_all, 0.0), axis=1)
@@ -144,86 +170,61 @@
     slots_half = slots // 2
     quarter = half // 2
 
-    def forward(
-        exchange, sends, keeps, others, inputs_x, merged_dy, other_x, other_dy, slot_p, merged_p
-    ):
-        arrived = exchange(sends)
-        sums = [
-            reduced(dot(value[:slots_half], w, 1, 0), dot(value[slots_half:], w, 1, 0))
-            for value, w in zip((other_x, other_x, other_dy), others)
-        ]
-        acts = activations(*sums)
-        other_acts = [jnp.concatenate([swapped(a), a], axis=0) for a in acts]
-        other_y = dot(other_acts[0], others[2], 1, 1)
-        other_y = (other_y * slot_p[:, None]).astype(BF16)
-
-        merged = [
-            (0.5 * (k.astype(F32) + a.astype(F32))).astype(BF16)
-            for k, a in zip(keeps, arrived)
-        ]
-        sums = []
-        for value, w in zip((inputs_x, inputs_x, merged_dy), merged):
-            w_send = lax.dynamic_slice_in_dim(w, (1 - low_bit) * quarter, quarter, 0)
-            w_keep = lax.dynamic_slice_in_dim(w, low_bit * quarter, quarter, 0)
-            sums.append(reduced(dot(w_send, value, 1, 1), dot(w_keep, value, 1, 1)))
-        acts = activations(*sums)
-        merged_acts = []
-        for a in acts:
-            b = swapped(a)
-            merged_acts.append(
-                jnp.concatenate(
-                    [jnp.where(low_bit == 0, a, b), jnp.where(low_bit == 0, b, a)], axis=0
-                )
-            )
-        merged_y = dot(merged_acts[0], merged[2], 0, 0)
-        mixed = dot(slot_hot, other_y, 0, 0) + merged_p[:, None] * merged_y
-        return mixed.astype(BF16), other_acts, merged_acts
-
-    mixed, other_acts, merged_acts = with_partner(
-        devices_n,
-        me ^ partner,
-        forward,
-        sends,
-        keeps,
-        others,
-        inputs_x,
-        merged_dy,
-        other_x,
-        other_dy,
-        slot_p,
-        merged_p,
-    )
-    mixed = lax.psum_scatter(mixed, "expert", scatter_dimension=0, tiled=True)
-
-    def backward(exchange, inputs_x, merged_dy, merged_acts):
-        h, dg, du = merged_acts
-        own = [
-            dot(value, a, 0, 1).astype(BF16)
-            for value, a in ((merged_dy, h), (inputs_x, dg), (inputs_x, du))
-        ]
-        return own, exchange(own)
-
-    own, returned = with_partner(
-        devices_n, me ^ partner, backward, inputs_x, merged_dy, merged_acts
-    )
-    h, dg, du = other_acts
-    outs = []
-    for value, a, mine_half, far_half in zip(
-        (other_dy, other_x, other_x), (h, dg, du), own, returned
-    ):
-        other_grad = dot(value, a, 0, 0).astype(BF16)
-        merged_grad = jnp.where(
-            am_target, jnp.concatenate([mine_half, far_half], axis=1), jnp.zeros((), BF16)
-        )
-        outs.append(
-            jnp.where(
-                merged_slot == 0,
-                jnp.stack([merged_grad, other_grad]),
-                jnp.stack([other_grad, merged_grad]),
+    apart = me ^ partner
+    arrived = [with_partner(devices_n, apart, value) for value in sends]
+
+    sums = [
+        reduced(dot(value[:slots_half], w, 1, 0), dot(value[slots_half:], w, 1, 0))
+        for value, w in zip((other_x, other_x, other_dy), others)
+    ]
+    other_h, other_dg, other_du = [
+        jnp.concatenate([swapped(a), a], axis=0) for a in activations(*sums)
+    ]
+    other_y = (dot(other_h, others[2], 1, 1) * slot_p[:, None]).astype(BF16)
+    other_grads = [
+        dot(value, a, 0, 0).astype(BF16)
+        for value, a in ((other_x, other_dg), (other_x, other_du), (other_dy, other_h))
+    ]
+
+    merged = [
+        (0.5 * (k.astype(F32) + a.astype(F32))).astype(BF16) for k, a in zip(keeps, arrived)
+    ]
+    sums = []
+    for value, w in zip((inputs_x, inputs_x, merged_dy), merged):
+        w_send = lax.dynamic_slice_in_dim(w, (1 - low_bit) * quarter, quarter, 0)
+        w_keep = lax.dynamic_slice_in_dim(w, low_bit * quarter, quarter, 0)
+        sums.append(reduced(dot(w_send, value, 1, 1), dot(w_keep, value, 1, 1)))
+    merged_acts = []
+    for a in activations(*sums):
+        b = swapped(a)
+        merged_acts.append(
+            jnp.concatenate(
+                [jnp.where(low_bit == 0, a, b), jnp.where(low_bit == 0, b, a)], axis=0
             )
         )
-    grad_down, grad_gate, grad_up = outs
-    return mixed, grad_gate, grad_up, grad_down
+    merged_h, merged_dg, merged_du = merged_acts
+    merged_y = dot(merged_h, merged[2], 0, 0)
+    mixed = dot(slot_hot, other_y, 0, 0) + merged_p[:, None] * merged_y
+    mixed = ring_scatter(mixed.astype(BF16), devices_n, me)
+
+    down_half = dot(merged_dy, merged_h, 0, 1).astype(BF16)
+    gate_half = dot(inputs_x, merged_dg, 0, 1).astype(BF16)
+    up_half = dot(inputs_x, merged_du, 0, 1).astype(BF16)
+    far_down = with_partner(devices_n, apart, down_half)
+    far_gate = with_partner(devices_n, apart, gate_half)
+    far_up = with_partner(devices_n, apart, up_half)
+
+    outs = []
+    for other_grad, own_half, far_half in zip(
+        other_grads, (gate_half, up_half, down_half), (far_gate, far_up, far_down)
+    ):
+        merged_grad = jnp.where(
+            am_target, jnp.concatenate([own_half, far_half], axis=1), jnp.zeros((), BF16)
+        )
+        out = jnp.zeros((exp_local, width, neurons), BF16)
+        out = lax.dynamic_update_slice_in_dim(out, other_grad[None], other_slot, 0)
+        outs.append(lax.dynamic_update_slice_in_dim(out, merged_grad[None], merged_slot, 0))
+    return (mixed, *outs)
 
 
 def solution(mesh):

time: 406 us -> 370 us (0.911)
  loops' own time: 50.9 us -> 0.03 us
  starting transfers between devices: 14.5 us -> 38.1 us
  between operations: 17.3 us -> 4.31 us
  matrix products: 47.2 us -> 59 us
  waiting for transfers between devices: 201 us -> 191 us
  local copies, waits for them, and re-layouts: 22.4 us -> 31.4 us
    unnamed x2 -> x3, loops' own time: 50.9 us -> 0.02 us
    reduce_scatter x1 -> x0, waiting for transfers between devices: 45.2 us -> none  [shards(): mixed = lax.psum_scatter(mixed, 'expert', scatter_dimension=0, tiled=True)]
    ppermute x6 -> x27, waiting for transfers between devices: 75.4 us -> 117 us  [the longest x6 97.8 us: with_partner(): return lax.switch(apart - 1, branches, value)]
    all_gather x1 -> x0, waiting for transfers between devices: 26.1 us -> none  [shards(): gathered = lax.all_gather(payload, 'expert', axis=0, tiled=True)]
    ppermute x6 -> x27, starting transfers between devices: 5.22 us -> 28.2 us  [the longest x6 10.4 us: ring_gather(): value = lax.ppermute(value, 'expert', ring)]
    ppermute x6, waiting for transfers between devices: 53.8 us -> 73.8 us  [reduced(): lax.ppermute(rounded, 'hidden', xor_pairs(hidden_n, bit)).astype(F32)]
    dynamic_update_slice x0 -> x18, local copies, waits for them, and re-layouts: none -> 12 us  [the longest x15 6.69 us: ring_gather(): result = lax.dynamic_update_slice_in_dim(result, block, at, 0)]
    dot_general x29, matrix products: 47.2 us -> 59 us  [dot(): lax.dot_general(a, b, (((ca,), (cb,)), ((), ())), preferred_element_type=...]
  transfers between devices with their start and end apart: 26 -> 45, of which waited for: 12 -> 18; matrix products, arithmetic and copies ran while one was open for 22% -> 32% of each run, Pallas kernels for 0% -> 0%
where the time goes in v2:
time: 370 us; the launch traced here: 365 us
  waiting for transfers between devices  191 us (52%)
  matrix products  59 us (16%)
  other arithmetic  41.5 us (11%)
  starting transfers between devices  38.1 us (10%)
  local copies, waits for them, and re-layouts  31.4 us (8%)
  between operations  4.31 us (1%)
    ppermute x6, waiting for transfers between devices, with_partner(): return lax.switch(apart - 1, branches, value)  97.8 us
    ppermute x6, waiting for transfers between devices, reduced(): lax.ppermute(rounded, 'hidden', xor_pairs(hidden_n, bit)).astype(F32)  73.8 us
    dot_general x29, matrix products, dot(): lax.dot_general(a, b, (((ca,), (cb,)), ((), ())), preferred_element_type=...  59 us
    select_n x3, other arithmetic, shards(): jnp.where(low_bit == 0, a, b)  12.2 us
    ppermute x6, starting transfers between devices, ring_gather(): value = lax.ppermute(value, 'expert', ring)  10.4 us
    convert_element_type x2, other arithmetic, activations(): (back_sum * active).astype(BF16)  9.12 us
    select_n x3, local copies, waits for them, and re-layouts, shards(): jnp.where(am_target, jnp.concatenate([own_half, far_half], axis=1), jnp.z...  7.63 us
    ppermute x6, waiting for transfers between devices, ring_gather(): value = lax.ppermute(value, 'expert', ring)  7.52 us
  transfers between devices with their start and end apart: 45, of which 18 were waited for; matrix products, arithmetic and copies ran while one was open for 32% of the time, Pallas kernels for 0%

profile of v2, /device:TPU:0, one launch (start us, length us, event | category | flops | bytes accessed | tf_op | source)
XLA Modules:
  0.0 364.9 jit_solution(5938509056890867942)
XLA Ops:
  22.0 17.1 %conditional.17 = (bf16[704,512]{1,0:T(8,128)(2,1)}) conditional(s32[]{:T(128)} %clamp.2, bf16[704,512]{1,0:T(8,128)(2,1)} %fusion.72, bf16[704,512]{1,0:T(8,128)(2,1)} %fusion.72, bf16[704,512]{1,0:T(8,128)(2,1)} %fusion.72, bf16[704,512]{1,0:T(8,128)(2,1)} %fusion.72, bf16[704,512]{1,0:T(8,128)(2,1)} %fusion.72, ...), branch_computations={%region_23.24_spmd, %region_24.25_spmd, %region_25.26_spmd, %regio... | conditional | bytes 2883632
  23.5 15.5 %collective-permute-done.14 = bf16[704,512]{1,0:T(8,128)(2,1)} collective-permute-done((bf16[704,512]{1,0:T(8,128)(2,1)}, bf16[704,512]{1,0:T(8,128)(2,1)}, u32[]{:S(2)}, u32[]{:S(2)}) %collective-permute-start.14) | collective-permute-done | bytes 720928 | tf_op jit(solution)/shard_map/cond/branch_0_fun/ppermute | solution.py:25
  39.1 16.1 %conditional.16 = (bf16[704,512]{1,0:T(8,128)(2,1)}) conditional(s32[]{:T(128)} %clamp.2, bf16[704,512]{1,0:T(8,128)(2,1)} %fusion.69, bf16[704,512]{1,0:T(8,128)(2,1)} %fusion.69, bf16[704,512]{1,0:T(8,128)(2,1)} %fusion.69, bf16[704,512]{1,0:T(8,128)(2,1)} %fusion.69, bf16[704,512]{1,0:T(8,128)(2,1)} %fusion.69, ...), branch_computations={%region_16.17_spmd, %region_17.18_spmd, %region_18.19_spmd, %regio... | conditional | bytes 2883632
  40.6 14.6 %collective-permute-done.7 = bf16[704,512]{1,0:T(8,128)(2,1)} collective-permute-done((bf16[704,512]{1,0:T(8,128)(2,1)}, bf16[704,512]{1,0:T(8,128)(2,1)}, u32[]{:S(2)}, u32[]{:S(2)}) %collective-permute-start.7) | collective-permute-done | bytes 720928 | tf_op jit(solution)/shard_map/cond/branch_0_fun/ppermute | solution.py:25
  63.5 15.1 %conditional.15 = (bf16[704,512]{1,0:T(8,128)(2,1)}) conditional(s32[]{:T(128)} %clamp.2, bf16[704,512]{1,0:T(8,128)(2,1)S(1)} %fusion.66, bf16[704,512]{1,0:T(8,128)(2,1)S(1)} %fusion.66, bf16[704,512]{1,0:T(8,128)(2,1)S(1)} %fusion.66, bf16[704,512]{1,0:T(8,128)(2,1)S(1)} %fusion.66, ...), branch_computations={%region_9.10_spmd, %region_10.11_spmd, %region_11.12_spmd, %region... | conditional | bytes 2883632
  65.1 13.5 %collective-permute-done = bf16[704,512]{1,0:T(8,128)(2,1)} collective-permute-done((bf16[704,512]{1,0:T(8,128)(2,1)S(1)}, bf16[704,512]{1,0:T(8,128)(2,1)}, u32[]{:S(2)}, u32[]{:S(2)}) %collective-permute-start) | collective-permute-done | bytes 720928 | tf_op jit(solution)/shard_map/cond/branch_0_fun/ppermute | solution.py:25
  82.6 4.4 %collective-permute-start.69 = (bf16[128,512]{1,0:T(8,128)(2,1)}, bf16[128,512]{1,0:T(8,128)(2,1)S(1)}, u32[]{:S(2)}, u32[]{:S(2)}) collective-permute-start(bf16[128,512]{1,0:T(8,128)(2,1)} %collective-permute-done.67), channel_id=1, source_target_pairs={{0,8},{4,12},{8,16},{12,20},{16,24},{20,28},{24,0},{28,4},{1,9},{5... | collective-permute-start | bytes 393224 | tf_op jit(solution)/shard_map/ppermute | solution.py:34
  141.8 4.7 %collective-permute-done.57 = bf16[352,1024]{1,0:T(8,128)(2,1)S(1)} collective-permute-done((bf16[352,1024]{1,0:T(8,128)(2,1)S(1)}, bf16[352,1024]{1,0:T(8,128)(2,1)S(1)}, u32[]{:S(2)}, u32[]{:S(2)}) %collective-permute-start.57) | collective-permute-done | bytes 720928 | tf_op jit(solution)/shard_map/ppermute | solution.py:161
  148.8 13.2 %collective-permute-done.55 = bf16[352,1024]{1,0:T(8,128)(2,1)} collective-permute-done((bf16[352,1024]{1,0:T(8,128)(2,1)}, bf16[352,1024]{1,0:T(8,128)(2,1)}, u32[]{:S(2)}, u32[]{:S(2)}) %collective-permute-start.55) | collective-permute-done | bytes 720928 | tf_op jit(solution)/shard_map/ppermute | solution.py:161
  162.0 15.4 %collective-permute-done.77 = bf16[352,1024]{1,0:T(8,128)(2,1)} collective-permute-done((bf16[352,1024]{1,0:T(8,128)(2,1)}, bf16[352,1024]{1,0:T(8,128)(2,1)}, u32[]{:S(2)}, u32[]{:S(2)}) %collective-permute-start.77) | collective-permute-done | bytes 720928 | tf_op jit(solution)/shard_map/ppermute | solution.py:161
  177.4 4.5 %multiply_convert_fusion.1 = (bf16[352,1024]{1,0:T(8,128)(2,1)S(1)}, bf16[352,1024]{1,0:T(8,128)(2,1)}, bf16[352,1024]{1,0:T(8,128)(2,1)}) fusion(bf16[352,1024]{1,0:T(8,128)(2,1)} %collective-permute-done.77, bf16[352,1024]{1,0:T(8,128)(2,1)} %fusion.56, bf16[352,1024]{1,0:T(8,128)(2,1)} %collective-permute-done.55, bf16[352,1024]{1,0:T(8,128)(2,1)} %fusion.54, ...), kind=kLoop, calls=%fused_computation.72 | loop fusion | flops 8650752 | bytes 6488064 | tf_op jit(solution)/shard_map/convert_element_type | solution.py:68
  182.4 10.4 %collective-permute-done.50 = bf16[256,1408]{1,0:T(8,128)(2,1)} collective-permute-done((bf16[256,1408]{1,0:T(8,128)(2,1)}, bf16[256,1408]{1,0:T(8,128)(2,1)}, u32[]{:S(2)}, u32[]{:S(2)}) %collective-permute-start.50) | collective-permute-done | bytes 720928 | tf_op jit(solution)/shard_map/ppermute | solution.py:161
  192.9 15.4 %collective-permute-done.52 = bf16[256,1408]{1,0:T(8,128)(2,1)} collective-permute-done((bf16[256,1408]{1,0:T(8,128)(2,1)}, bf16[256,1408]{1,0:T(8,128)(2,1)}, u32[]{:S(2)}, u32[]{:S(2)}) %collective-permute-start.52) | collective-permute-done | bytes 720928 | tf_op jit(solution)/shard_map/ppermute | solution.py:161
  208.3 14.6 %collective-permute-done.74 = bf16[256,1408]{1,0:T(8,128)(2,1)} collective-permute-done((bf16[256,1408]{1,0:T(8,128)(2,1)}, bf16[256,1408]{1,0:T(8,128)(2,1)}, u32[]{:S(2)}, u32[]{:S(2)}) %collective-permute-start.74) | collective-permute-done | bytes 720928 | tf_op jit(solution)/shard_map/ppermute | solution.py:161
  222.9 4.6 %multiply_convert_fusion.2 = (bf16[256,1408]{1,0:T(8,128)(2,1)}, bf16[256,1408]{1,0:T(8,128)(2,1)}, bf16[256,1408]{1,0:T(8,128)(2,1)}) fusion(bf16[256,1408]{1,0:T(8,128)(2,1)} %collective-permute-done.74, bf16[256,1408]{1,0:T(8,128)(2,1)} %add_convert_fusion.1, bf16[256,1408]{1,0:T(8,128)(2,1)} %collective-permute-done.50, ...), kind=kLoop, calls=%fused_computation.73 | loop fusion | flops 8650752 | bytes 6488064 | tf_op jit(solution)/shard_map/convert_element_type | solution.py:68
  228.0 9.3 %broadcast_select_fusion.1 = (bf16[352,1024]{1,0:T(8,128)(2,1)S(1)}, bf16[352,1024]{1,0:T(8,128)(2,1)S(1)}) fusion(bf16[352,1024]{1,0:T(8,128)(2,1)S(1)} %get-tuple-element.123, bf16[352,1024]{1,0:T(8,128)(2,1)S(1)} %collective-permute-done.80, pred[]{:T(512)S(6)} %eq.135), kind=kLoop, calls=%fused_computation.136 | loop fusion | flops 720896 | bytes 2883585 | tf_op jit(solution)/shard_map/jit(_where)/select_n | solution.py:202
  240.4 18.9 %conditional.19 = (bf16[1,512,704]{1,2,0:T(8,128)(2,1)}) conditional(s32[]{:T(128)} %clamp.2, bf16[512,704]{0,1:T(8,128)(2,1)S(1)} %fusion.75, bf16[512,704]{0,1:T(8,128)(2,1)S(1)} %fusion.75, bf16[512,704]{0,1:T(8,128)(2,1)S(1)} %fusion.75, bf16[512,704]{0,1:T(8,128)(2,1)S(1)} %fusion.75, ...), branch_computations={%region_37.38_spmd, %region_38.39_spmd, %region_39.40_spmd, %regio... | conditional | bytes 5767244 | solution.py:25
  240.4 18.0 %collective-permute-done.28 = bf16[512,704]{0,1:T(8,128)(2,1)S(1)} collective-permute-done((bf16[512,704]{0,1:T(8,128)(2,1)S(1)}, bf16[512,704]{0,1:T(8,128)(2,1)S(1)}, u32[]{:S(2)}, u32[]{:S(2)}) %collective-permute-start.28) | collective-permute-done | bytes 720928 | tf_op jit(solution)/shard_map/cond/branch_0_fun/ppermute | solution.py:25
  268.4 18.9 %conditional.18 = (bf16[1,512,704]{1,2,0:T(8,128)(2,1)}) conditional(s32[]{:T(128)} %clamp.2, bf16[512,704]{0,1:T(8,128)(2,1)} %fusion.78, bf16[512,704]{0,1:T(8,128)(2,1)} %fusion.78, bf16[512,704]{0,1:T(8,128)(2,1)} %fusion.78, bf16[512,704]{0,1:T(8,128)(2,1)} %fusion.78, bf16[512,704]{0,1:T(8,128)(2,1)} %fusion.78, ...), branch_computations={%region_30.31_spmd, %region_31.32_spmd, %region_32.33_spmd, %regio... | conditional | bytes 2883632 | solution.py:25
  268.7 18.6 %collective-permute-done.21 = bf16[512,704]{0,1:T(8,128)(2,1)} collective-permute-done((bf16[512,704]{0,1:T(8,128)(2,1)}, bf16[512,704]{0,1:T(8,128)(2,1)}, u32[]{:S(2)}, u32[]{:S(2)}) %collective-permute-start.21) | collective-permute-done | bytes 720928 | tf_op jit(solution)/shard_map/cond/branch_0_fun/ppermute | solution.py:25
  290.9 18.6 %conditional.20 = (bf16[1,512,704]{1,2,0:T(8,128)(2,1)}) conditional(s32[]{:T(128)} %clamp.2, bf16[512,704]{0,1:T(8,128)(2,1)S(1)} %convolution_convert_fusion.6, bf16[512,704]{0,1:T(8,128)(2,1)S(1)} %convolution_convert_fusion.6, bf16[512,704]{0,1:T(8,128)(2,1)S(1)} %convolution_convert_fusion.6, ...), branch_computations={%region_44.45_spmd, %region_45.46_spmd, %region_46.47_spmd, %regio... | conditional | bytes 5767244 | solution.py:25
  291.1 17.5 %collective-permute-done.35 = bf16[512,704]{0,1:T(8,128)(2,1)S(1)} collective-permute-done((bf16[512,704]{0,1:T(8,128)(2,1)S(1)}, bf16[512,704]{0,1:T(8,128)(2,1)S(1)}, u32[]{:S(2)}, u32[]{:S(2)}) %collective-permute-start.35) | collective-permute-done | bytes 720928 | tf_op jit(solution)/shard_map/cond/branch_0_fun/ppermute | solution.py:25
  309.5 4.3 %fusion.13 = f32[1024,512]{1,0:T(8,128)} fusion(bf16[2,512,1408]{2,1,0:T(8,128)(2,1)S(1)} %copy-done, s32[]{:T(128)S(6)} %select_n.319, s32[1024]{0:T(1024)S(1)} %fusion.113, bf16[256,1408]{1,0:T(8,128)(2,1)} %get-tuple-element.128, bf16[256,1408]{1,0:T(8,128)(2,1)} %collective-permute-done.53, f32[512]{0:T(512)S(1)} %select_reduce_fusion), kind=kOutput, calls=%fused_computation.25 | convolution fusion | flops 1279000576 | bytes 4986884 | tf_op jit(solution)/shard_map/dot_general | solution.py:13
  358.9 4.2 %collective-permute-done.65 = bf16[128,512]{1,0:T(8,128)(2,1)S(1)} collective-permute-done((bf16[128,512]{1,0:T(8,128)(2,1)S(1)}, bf16[128,512]{1,0:T(8,128)(2,1)S(1)}, u32[]{:S(2)}, u32[]{:S(2)}) %collective-permute-start.65) | collective-permute-done | bytes 131104 | tf_op jit(solution)/shard_map/ppermute | solution.py:56
  (226 shorter events, 157.8 us)
Async XLA Ops:
  0.7 81.9 %collective-permute-start.67 = (bf16[128,512]{1,0:T(8,128)(2,1)}, bf16[128,512]{1,0:T(8,128)(2,1)}, u32[]{:S(2)}, u32[]{:S(2)}) collective-permute-start(bf16[128,512]{1,0:T(8,128)(2,1)} %param.53), channel_id=1, source_target_pairs={{0,8},{4,12},{8,16},{12,20},{16,24},{20,28},{24,0},{28,4},{1,9},{5... | collective-permute-start | bytes 393224 | tf_op jit(solution)/shard_map/ppermute | solution.py:34
  3.8 84.7 %collective-permute-start.66 = (bf16[128,512]{1,0:T(8,128)(2,1)}, bf16[128,512]{1,0:T(8,128)(2,1)}, u32[]{:S(2)}, u32[]{:S(2)}) collective-permute-start(bf16[128,512]{1,0:T(8,128)(2,1)} %param.53), channel_id=1, source_target_pairs={{0,4},{4,0},{8,12},{12,8},{16,20},{20,16},{24,28},{28,24},{1,5},{5... | collective-permute-start | bytes 393224 | tf_op jit(solution)/shard_map/ppermute | solution.py:35
  8.0 83.7 %collective-permute-start.42 = (bf16[128,640]{1,0:T(8,128)(2,1)S(1)}, bf16[128,640]{1,0:T(8,128)(2,1)S(1)}, u32[]{:S(2)}, u32[]{:S(2)}) collective-permute-start(bf16[128,640]{1,0:T(8,128)(2,1)S(1)} %get-tuple-element.139), channel_id=1, source_target_pairs={{0,4},{4,0},{8,12},{12,8},{16,20},{20,16},{24,28},{28,24},{1,5},{5... | collective-permute-start | bytes 491528 | tf_op jit(solution)/shard_map/ppermute | solution.py:35
  8.5 81.8 %collective-permute-start.43 = (bf16[128,640]{1,0:T(8,128)(2,1)S(1)}, bf16[128,640]{1,0:T(8,128)(2,1)S(1)}, u32[]{:S(2)}, u32[]{:S(2)}) collective-permute-start(bf16[128,640]{1,0:T(8,128)(2,1)S(1)} %get-tuple-element.139), channel_id=1, source_target_pairs={{0,8},{4,12},{8,16},{12,20},{16,24},{20,28},{24,0},{28,4},{1,9},{5... | collective-permute-start | bytes 491528 | tf_op jit(solution)/shard_map/ppermute | solution.py:34
  22.0 17.1 %collective-permute-start.14 = (bf16[704,512]{1,0:T(8,128)(2,1)}, bf16[704,512]{1,0:T(8,128)(2,1)}, u32[]{:S(2)}, u32[]{:S(2)}) collective-permute-start(bf16[704,512]{1,0:T(8,128)(2,1)} %param.14), channel_id=1, source_target_pairs={{0,4},{4,0},{8,12},{12,8},{16,20},{20,16},{24,28},{28,24},{1,5},{5... | collective-permute-start | bytes 2162696 | tf_op jit(solution)/shard_map/cond/branch_0_fun/ppermute | solution.py:25
  127.4 19.1 %collective-permute-start.57 = (bf16[352,1024]{1,0:T(8,128)(2,1)S(1)}, bf16[352,1024]{1,0:T(8,128)(2,1)S(1)}, u32[]{:S(2)}, u32[]{:S(2)}) collective-permute-start(bf16[352,1024]{1,0:T(8,128)(2,1)S(1)} %fusion.55), channel_id=1, source_target_pairs={{0,2},{1,3},{2,0},{3,1},{4,6},{5,7},{6,4},{7,5},{8,10},{9,11},{10,... | collective-permute-start | bytes 2162696 | tf_op jit(solution)/shard_map/ppermute | solution.py:161
  131.6 30.4 %collective-permute-start.55 = (bf16[352,1024]{1,0:T(8,128)(2,1)}, bf16[352,1024]{1,0:T(8,128)(2,1)}, u32[]{:S(2)}, u32[]{:S(2)}) collective-permute-start(bf16[352,1024]{1,0:T(8,128)(2,1)} %fusion.54), channel_id=1, source_target_pairs={{0,2},{1,3},{2,0},{3,1},{4,6},{5,7},{6,4},{7,5},{8,10},{9,11},{10,... | collective-permute-start | bytes 2162696 | tf_op jit(solution)/shard_map/ppermute | solution.py:161
  133.7 43.7 %collective-permute-start.77 = (bf16[352,1024]{1,0:T(8,128)(2,1)}, bf16[352,1024]{1,0:T(8,128)(2,1)}, u32[]{:S(2)}, u32[]{:S(2)}) collective-permute-start(bf16[352,1024]{1,0:T(8,128)(2,1)} %fusion.56), channel_id=1, source_target_pairs={{0,2},{1,3},{2,0},{3,1},{4,6},{5,7},{6,4},{7,5},{8,10},{9,11},{10,... | collective-permute-start | bytes 2162696 | tf_op jit(solution)/shard_map/ppermute | solution.py:161
  136.7 56.1 %collective-permute-start.50 = (bf16[256,1408]{1,0:T(8,128)(2,1)}, bf16[256,1408]{1,0:T(8,128)(2,1)}, u32[]{:S(2)}, u32[]{:S(2)}) collective-permute-start(bf16[256,1408]{1,0:T(8,128)(2,1)} %add_convert_fusion.3), channel_id=1, source_target_pairs={{0,2},{1,3},{2,0},{3,1},{4,6},{5,7},{6,4},{7,5},{8,10},{9,11},{10,... | collective-permute-start | bytes 2162696 | tf_op jit(solution)/shard_map/ppermute | solution.py:161
  138.8 69.5 %collective-permute-start.52 = (bf16[256,1408]{1,0:T(8,128)(2,1)}, bf16[256,1408]{1,0:T(8,128)(2,1)}, u32[]{:S(2)}, u32[]{:S(2)}) collective-permute-start(bf16[256,1408]{1,0:T(8,128)(2,1)} %add_convert_fusion.2), channel_id=1, source_target_pairs={{0,2},{1,3},{2,0},{3,1},{4,6},{5,7},{6,4},{7,5},{8,10},{9,11},{10,... | collective-permute-start | bytes 2162696 | tf_op jit(solution)/shard_map/ppermute | solution.py:161
  147.3 75.6 %collective-permute-start.74 = (bf16[256,1408]{1,0:T(8,128)(2,1)}, bf16[256,1408]{1,0:T(8,128)(2,1)}, u32[]{:S(2)}, u32[]{:S(2)}) collective-permute-start(bf16[256,1408]{1,0:T(8,128)(2,1)} %add_convert_fusion.1), channel_id=1, source_target_pairs={{0,2},{1,3},{2,0},{3,1},{4,6},{5,7},{6,4},{7,5},{8,10},{9,11},{10,... | collective-permute-start | bytes 2162696 | tf_op jit(solution)/shard_map/ppermute | solution.py:161
  181.9 46.1 %collective-permute-start.80 = (bf16[352,1024]{1,0:T(8,128)(2,1)S(1)}, bf16[352,1024]{1,0:T(8,128)(2,1)S(1)}, u32[]{:S(2)}, u32[]{:S(2)}) collective-permute-start(bf16[352,1024]{1,0:T(8,128)(2,1)S(1)} %get-tuple-element.123), channel_id=1, source_target_pairs={{0,1},{1,0},{2,3},{3,2},{4,5},{5,4},{6,7},{7,6},{8,9},{9,8},{10,11... | collective-permute-start | bytes 2162696 | tf_op jit(solution)/shard_map/ppermute | solution.py:168
  181.9 77.3 %collective-permute-start.78 = (bf16[352,1024]{1,0:T(8,128)(2,1)}, bf16[352,1024]{1,0:T(8,128)(2,1)}, u32[]{:S(2)}, u32[]{:S(2)}) collective-permute-start(bf16[352,1024]{1,0:T(8,128)(2,1)} %get-tuple-element.124), channel_id=1, source_target_pairs={{0,1},{1,0},{2,3},{3,2},{4,5},{5,4},{6,7},{7,6},{8,9},{9,8},{10,11... | collective-permute-start | bytes 2162696 | tf_op jit(solution)/shard_map/ppermute | solution.py:168
  192.9 94.4 %collective-permute-start.58 = (bf16[352,1024]{1,0:T(8,128)(2,1)}, bf16[352,1024]{1,0:T(8,128)(2,1)}, u32[]{:S(2)}, u32[]{:S(2)}) collective-permute-start(bf16[352,1024]{1,0:T(8,128)(2,1)} %get-tuple-element.125), channel_id=1, source_target_pairs={{0,1},{1,0},{2,3},{3,2},{4,5},{5,4},{6,7},{7,6},{8,9},{9,8},{10,11... | collective-permute-start | bytes 2162696 | tf_op jit(solution)/shard_map/ppermute | solution.py:168
  227.5 95.8 %collective-permute-start.79 = (bf16[256,1408]{1,0:T(8,128)(2,1)}, bf16[256,1408]{1,0:T(8,128)(2,1)}, u32[]{:S(2)}, u32[]{:S(2)}) collective-permute-start(bf16[256,1408]{1,0:T(8,128)(2,1)} %get-tuple-element.126), channel_id=1, source_target_pairs={{0,1},{1,0},{2,3},{3,2},{4,5},{5,4},{6,7},{7,6},{8,9},{9,8},{10,11... | collective-permute-start | bytes 2162696 | tf_op jit(solution)/shard_map/ppermute | solution.py:168
  227.5 102.7 %collective-permute-start.75 = (bf16[256,1408]{1,0:T(8,128)(2,1)}, bf16[256,1408]{1,0:T(8,128)(2,1)}, u32[]{:S(2)}, u32[]{:S(2)}) collective-permute-start(bf16[256,1408]{1,0:T(8,128)(2,1)} %get-tuple-element.127), channel_id=1, source_target_pairs={{0,1},{1,0},{2,3},{3,2},{4,5},{5,4},{6,7},{7,6},{8,9},{9,8},{10,11... | collective-permute-start | bytes 2162696 | tf_op jit(solution)/shard_map/ppermute | solution.py:168
  240.4 18.0 %collective-permute-start.28 = (bf16[512,704]{0,1:T(8,128)(2,1)S(1)}, bf16[512,704]{0,1:T(8,128)(2,1)S(1)}, u32[]{:S(2)}, u32[]{:S(2)}) collective-permute-start(bf16[512,704]{0,1:T(8,128)(2,1)S(1)} %param.28), channel_id=1, source_target_pairs={{0,4},{4,0},{8,12},{12,8},{16,20},{20,16},{24,28},{28,24},{1,5},{5... | collective-permute-start | bytes 2162696 | tf_op jit(solution)/shard_map/cond/branch_0_fun/ppermute | solution.py:25
  259.3 50.2 %collective-permute-start.53 = (bf16[256,1408]{1,0:T(8,128)(2,1)}, bf16[256,1408]{1,0:T(8,128)(2,1)}, u32[]{:S(2)}, u32[]{:S(2)}) collective-permute-start(bf16[256,1408]{1,0:T(8,128)(2,1)} %get-tuple-element.128), channel_id=1, source_target_pairs={{0,1},{1,0},{2,3},{3,2},{4,5},{5,4},{6,7},{7,6},{8,9},{9,8},{10,11... | collective-permute-start | bytes 2162696 | tf_op jit(solution)/shard_map/ppermute | solution.py:168
  268.4 18.9 %collective-permute-start.21 = (bf16[512,704]{0,1:T(8,128)(2,1)}, bf16[512,704]{0,1:T(8,128)(2,1)}, u32[]{:S(2)}, u32[]{:S(2)}) collective-permute-start(bf16[512,704]{0,1:T(8,128)(2,1)} %param.21), channel_id=1, source_target_pairs={{0,4},{4,0},{8,12},{12,8},{16,20},{20,16},{24,28},{28,24},{1,5},{5... | collective-permute-start | bytes 2162696 | tf_op jit(solution)/shard_map/cond/branch_0_fun/ppermute | solution.py:25
  290.9 17.8 %collective-permute-start.35 = (bf16[512,704]{0,1:T(8,128)(2,1)S(1)}, bf16[512,704]{0,1:T(8,128)(2,1)S(1)}, u32[]{:S(2)}, u32[]{:S(2)}) collective-permute-start(bf16[512,704]{0,1:T(8,128)(2,1)S(1)} %param.35), channel_id=1, source_target_pairs={{0,4},{4,0},{8,12},{12,8},{16,20},{20,16},{24,28},{28,24},{1,5},{5... | collective-permute-start | bytes 2162696 | tf_op jit(solution)/shard_map/cond/branch_0_fun/ppermute | solution.py:25
  317.9 41.0 %collective-permute-start.59 = (bf16[128,512]{1,0:T(8,128)(2,1)}, bf16[128,512]{1,0:T(8,128)(2,1)S(1)}, u32[]{:S(2)}, u32[]{:S(2)}) collective-permute-start(bf16[128,512]{1,0:T(8,128)(2,1)} %get-tuple-element.135), channel_id=1, source_target_pairs={{0,4},{4,0},{8,12},{12,8},{16,20},{20,16},{24,28},{28,24},{1,5},{5... | collective-permute-start | bytes 393224 | tf_op jit(solution)/shard_map/ppermute | solution.py:51
  318.2 20.6 %collective-permute-start.62 = (bf16[128,512]{1,0:T(8,128)(2,1)}, bf16[128,512]{1,0:T(8,128)(2,1)}, u32[]{:S(2)}, u32[]{:S(2)}) collective-permute-start(bf16[128,512]{1,0:T(8,128)(2,1)} %get-tuple-element.136), channel_id=1, source_target_pairs={{0,4},{4,0},{8,12},{12,8},{16,20},{20,16},{24,28},{28,24},{1,5},{5... | collective-permute-start | bytes 393224 | tf_op jit(solution)/shard_map/ppermute | solution.py:51
  319.9 23.4 %collective-permute-start.61 = (bf16[128,512]{1,0:T(8,128)(2,1)}, bf16[128,512]{1,0:T(8,128)(2,1)}, u32[]{:S(2)}, u32[]{:S(2)}) collective-permute-start(bf16[128,512]{1,0:T(8,128)(2,1)} %get-tuple-element.137), channel_id=1, source_target_pairs={{0,4},{4,0},{8,12},{12,8},{16,20},{20,16},{24,28},{28,24},{1,5},{5... | collective-permute-start | bytes 393224 | tf_op jit(solution)/shard_map/ppermute | solution.py:51
  323.3 31.9 %collective-permute-start.60 = (bf16[128,512]{1,0:T(8,128)(2,1)}, bf16[128,512]{1,0:T(8,128)(2,1)}, u32[]{:S(2)}, u32[]{:S(2)}) collective-permute-start(bf16[128,512]{1,0:T(8,128)(2,1)} %get-tuple-element.138), channel_id=1, source_target_pairs={{0,4},{4,0},{8,12},{12,8},{16,20},{20,16},{24,28},{28,24},{1,5},{5... | collective-permute-start | bytes 393224 | tf_op jit(solution)/shard_map/ppermute | solution.py:51
  (56 other events, 350.9 us)

commit v3 on v2

--- a/solution.py
+++ b/solution.py
@@ -3,6 +3,8 @@
 import jax
 import jax.numpy as jnp
 from jax import lax
+from jax.experimental import pallas as pl
+from jax.experimental.pallas import tpu as pltpu
 from jax.sharding import PartitionSpec as P
 
 F32 = jnp.float32
@@ -25,37 +27,99 @@
     return lax.switch(apart - 1, branches, value)
 
 
-def ring_gather(value, count, me):
-    rows = value.shape[0]
+def ring_gather(value, count):
     ring = [(i, (i + 2) % count) for i in range(count)]
-    result = jnp.zeros((rows * count, value.shape[1]), value.dtype)
+    blocks = []
     for step in range(count // 2):
         if step > 0:
             value = lax.ppermute(value, "expert", ring)
-        twin = lax.ppermute(value, "expert", xor_pairs(count, 1))
-        for block, owner in ((value, me), (twin, me ^ 1)):
-            at = (owner - 2 * step) % count * rows
-            result = lax.dynamic_update_slice_in_dim(result, block, at, 0)
-    return result
-
-
-def ring_scatter(partial, count, me):
+        blocks += [value, lax.ppermute(value, "expert", xor_pairs(count, 1))]
+    return jnp.concatenate(blocks, axis=0)
+
+
+def ring_scatter(partial, count):
     rows = partial.shape[0] // count
     ring = [(i, (i + 2) % count) for i in range(count)]
-
-    def block(owner):
-        return lax.dynamic_slice_in_dim(partial, owner % count * rows, rows, 0)
-
+    steps = count // 2
+    twins = []
+    for step in range(steps):
+        at = ((step + 1) % steps * 2 + 1) * rows
+        twins.append(lax.ppermute(partial[at : at + rows], "expert", xor_pairs(count, 1)))
     total = None
-    for step in range(count // 2):
-        twin = lax.ppermute(
-            block((me ^ 1) - 2 * (step + 1)).astype(BF16), "expert", xor_pairs(count, 1)
-        )
-        own = block(me - 2 * (step + 1)).astype(F32) + twin.astype(F32)
+    for step in range(steps):
+        at = (step + 1) % steps * 2 * rows
+        own = partial[at : at + rows].astype(F32) + twins[step].astype(F32)
         if step > 0:
             own = own + lax.ppermute(total, "expert", ring).astype(F32)
         total = own.astype(BF16)
     return total
+
+
+def after(value, *others):
+    return lax.optimization_barrier((value, *others))[0]
+
+
+def tile_of(extent, most):
+    return max(t for t in range(128, most + 1, 128) if extent % t == 0)
+
+
+def slot_matmul(slot, left, right, slots):
+    rows, width = left.shape
+    neurons = right.shape[1]
+    tile = tile_of(width, 256)
+
+    def kernel(slot_ref, left_ref, right_ref, out_ref):
+        out_ref[0] = dot(left_ref[...], right_ref[...], 0, 0).astype(BF16)
+
+    return pl.pallas_call(
+        kernel,
+        out_shape=jax.ShapeDtypeStruct((slots, width, neurons), BF16),
+        grid_spec=pltpu.PrefetchScalarGridSpec(
+            num_scalar_prefetch=1,
+            grid=(width // tile,),
+            in_specs=[
+                pl.BlockSpec((rows, tile), lambda i, s: (0, i)),
+                pl.BlockSpec((rows, neurons), lambda i, s: (0, 0)),
+            ],
+            out_specs=pl.BlockSpec((1, tile, neurons), lambda i, s: (s[0], i, 0)),
+        ),
+        compiler_params=pltpu.CompilerParams(vmem_limit_bytes=32 << 20),
+        cost_estimate=pl.CostEstimate(
+            flops=2 * rows * width * neurons,
+            bytes_accessed=2 * (rows * width + rows * neurons + width * neurons),
+            transcendentals=0,
+        ),
+    )(slot.reshape(1), left, right)
+
+
+def slot_place(slot, keep, first, second, into):
+    half, width = first.shape
+    tile = tile_of(width, 256)
+
+    def kernel(slot_ref, keep_ref, first_ref, second_ref, into_ref, out_ref):
+        whole = jnp.concatenate([first_ref[...], second_ref[...]], axis=0).astype(F32)
+        whole = jnp.where(keep_ref[0] > 0, whole, 0.0)
+        out_ref[0] = whole.T.astype(BF16)
+
+    return pl.pallas_call(
+        kernel,
+        out_shape=jax.ShapeDtypeStruct(into.shape, BF16),
+        grid_spec=pltpu.PrefetchScalarGridSpec(
+            num_scalar_prefetch=2,
+            grid=(width // tile,),
+            in_specs=[
+                pl.BlockSpec((half, tile), lambda i, s, k: (0, i)),
+                pl.BlockSpec((half, tile), lambda i, s, k: (0, i)),
+                pl.BlockSpec(memory_space=pl.ANY),
+            ],
+            out_specs=pl.BlockSpec((1, tile, 2 * half), lambda i, s, k: (s[0], i, 0)),
+        ),
+        input_output_aliases={4: 0},
+        compiler_params=pltpu.CompilerParams(vmem_limit_bytes=32 << 20),
+        cost_estimate=pl.CostEstimate(
+            flops=0, bytes_accessed=8 * half * width, transcendentals=0
+        ),
+    )(slot.reshape(1), keep.reshape(1), first, second, into)
 
 
 def activations(gate_sum, up_sum, back_sum):
@@ -118,8 +182,8 @@
     pieces = jnp.concatenate([high, middle, low], axis=1).astype(BF16)
     pad = -pieces.shape[1] % 128
     payload = jnp.concatenate([tokens, jnp.pad(pieces, ((0, 0), (0, pad)))], axis=1)
-    gathered = ring_gather(payload, devices_n, me)
-    inputs_c = ring_gather(cotangent, devices_n, me)
+    gathered = ring_gather(payload, devices_n)
+    inputs_c = ring_gather(cotangent, devices_n)
 
     order = jnp.where(am_target, jnp.arange(neurons, dtype=jnp.int32), perm)
     keep_order = jnp.where(am_target, order[:half], order[half:])
@@ -151,17 +215,19 @@
     other_x = dot(slot_hot, inputs_x, 1, 0).astype(BF16)
     other_dy = (dot(slot_hot, inputs_c, 1, 0) * slot_p[:, None]).astype(BF16)
 
-    def reduced(send_part, keep_part):
-        total = keep_part
-        if hidden_n > 1:
-            total = total + lax.ppermute(send_part.astype(BF16), "hidden", xor_pairs(hidden_n, 1))
-        bit = 2
+    def core_sum(send_part, keep_part):
+        if hidden_n == 1:
+            return keep_part.astype(BF16)
+        arrived = lax.ppermute(send_part.astype(BF16), "hidden", xor_pairs(hidden_n, 1))
+        return (keep_part + arrived.astype(F32)).astype(BF16)
+
+    def far_sum(part):
+        total, bit = part.astype(F32), 2
         while bit < hidden_n:
-            rounded = total.astype(BF16)
-            total = rounded.astype(F32) + lax.ppermute(
-                rounded, "hidden", xor_pairs(hidden_n, bit)
-            ).astype(F32)
-            bit *= 2
+            if bit > 2:
+                part = total.astype(BF16)
+            arrived = lax.ppermute(part, "hidden", xor_pairs(hidden_n, bit))
+            total, bit = part.astype(F32) + arrived.astype(F32), bit * 2
         return total
 
     def swapped(value):
@@ -169,61 +235,69 @@
 
     slots_half = slots // 2
     quarter = half // 2
-
     apart = me ^ partner
-    arrived = [with_partner(devices_n, apart, value) for value in sends]
-
-    sums = [
-        reduced(dot(value[:slots_half], w, 1, 0), dot(value[slots_half:], w, 1, 0))
+
+    other_parts = [
+        core_sum(dot(value[:slots_half], w, 1, 0), dot(value[slots_half:], w, 1, 0))
         for value, w in zip((other_x, other_x, other_dy), others)
     ]
-    other_h, other_dg, other_du = [
-        jnp.concatenate([swapped(a), a], axis=0) for a in activations(*sums)
-    ]
-    other_y = (dot(other_h, others[2], 1, 1) * slot_p[:, None]).astype(BF16)
-    other_grads = [
-        dot(value, a, 0, 0).astype(BF16)
-        for value, a in ((other_x, other_dg), (other_x, other_du), (other_dy, other_h))
-    ]
-
-    merged = [
-        (0.5 * (k.astype(F32) + a.astype(F32))).astype(BF16) for k, a in zip(keeps, arrived)
-    ]
-    sums = []
-    for value, w in zip((inputs_x, inputs_x, merged_dy), merged):
+    other_sums = [far_sum(part) for part in other_parts]
+
+    last = other_parts
+    merged, merged_sums = [], []
+    for value, send, keep in zip((inputs_x, inputs_x, merged_dy), sends, keeps):
+        arrived = with_partner(devices_n, apart, after(send, *last))
+        w = (0.5 * (keep.astype(F32) + arrived.astype(F32))).astype(BF16)
+        merged.append(w)
         w_send = lax.dynamic_slice_in_dim(w, (1 - low_bit) * quarter, quarter, 0)
         w_keep = lax.dynamic_slice_in_dim(w, low_bit * quarter, quarter, 0)
-        sums.append(reduced(dot(w_send, value, 1, 1), dot(w_keep, value, 1, 1)))
-    merged_acts = []
-    for a in activations(*sums):
+        part = core_sum(dot(w_send, value, 1, 1), dot(w_keep, value, 1, 1))
+        merged_sums.append(far_sum(part))
+        last = [part]
+
+    other_h, other_dg, other_du = [
+        jnp.concatenate([swapped(a), a], axis=0) for a in activations(*other_sums)
+    ]
+    other_y = (dot(other_h, others[2], 1, 1) * slot_p[:, None]).astype(BF16)
+    other_mixed = dot(slot_hot, other_y, 0, 0)
+    other_grads = [
+        slot_matmul(other_slot, value, a, exp_local)
+        for value, a in ((other_x, other_dg), (other_x, other_du), (other_dy, other_h))
+    ]
+
+    def ordered(a):
         b = swapped(a)
-        merged_acts.append(
-            jnp.concatenate(
-                [jnp.where(low_bit == 0, a, b), jnp.where(low_bit == 0, b, a)], axis=0
-            )
+        return jnp.concatenate(
+            [jnp.where(low_bit == 0, a, b), jnp.where(low_bit == 0, b, a)], axis=0
         )
-    merged_h, merged_dg, merged_du = merged_acts
-    merged_y = dot(merged_h, merged[2], 0, 0)
-    mixed = dot(slot_hot, other_y, 0, 0) + merged_p[:, None] * merged_y
-    mixed = ring_scatter(mixed.astype(BF16), devices_n, me)
-
-    down_half = dot(merged_dy, merged_h, 0, 1).astype(BF16)
-    gate_half = dot(inputs_x, merged_dg, 0, 1).astype(BF16)
-    up_half = dot(inputs_x, merged_du, 0, 1).astype(BF16)
-    far_down = with_partner(devices_n, apart, down_half)
-    far_gate = with_partner(devices_n, apart, gate_half)
-    far_up = with_partner(devices_n, apart, up_half)
-
-    outs = []
-    for other_grad, own_half, far_half in zip(
-        other_grads, (gate_half, up_half, down_half), (far_gate, far_up, far_down)
-    ):
-        merged_grad = jnp.where(
-            am_target, jnp.concatenate([own_half, far_half], axis=1), jnp.zeros((), BF16)
+
+    gate_sum, up_sum, back_sum = merged_sums
+    sigma = jax.nn.sigmoid(gate_sum)
+    active = gate_sum * sigma
+    inner = up_sum * sigma * (1.0 + gate_sum * (1.0 - sigma))
+    merged_h = ordered((active * up_sum).astype(BF16))
+    mixed = other_mixed + merged_p[:, None] * dot(merged_h, merged[2], 0, 0)
+    mixed = mixed.astype(BF16)
+    down_half = dot(merged_h, merged_dy, 1, 0).astype(BF16)
+    far_down = with_partner(devices_n, apart, after(down_half, mixed))
+    mixed = ring_scatter(mixed, devices_n)
+    gate_half = dot(ordered((back_sum * inner).astype(BF16)), inputs_x, 1, 0).astype(BF16)
+    up_half = dot(ordered((back_sum * active).astype(BF16)), inputs_x, 1, 0).astype(BF16)
+    far_gate, far_up = with_partner(devices_n, apart, (gate_half, up_half))
+
+    keep_flag = am_target.astype(jnp.int32)
+    outs = [
+        slot_place(
+            merged_slot,
+            keep_flag,
+            own,
+            far,
+            into,
         )
-        out = jnp.zeros((exp_local, width, neurons), BF16)
-        out = lax.dynamic_update_slice_in_dim(out, other_grad[None], other_slot, 0)
-        outs.append(lax.dynamic_update_slice_in_dim(out, merged_grad[None], merged_slot, 0))
+        for into, own, far in zip(
+            other_grads, (gate_half, up_half, down_half), (far_gate, far_up, far_down)
+        )
+    ]
     return (mixed, *outs)
 
 

time: 370 us -> 312 us (0.84)
  local copies, waits for them, and re-layouts: 31.4 us -> 7.87 us
  matrix products: 59 us -> 39.8 us
  other arithmetic: 41.5 us -> 27.3 us
  Pallas kernels: 0 us -> 14 us
  waiting for transfers between devices: 191 us -> 185 us
  starting transfers between devices: 38.1 us -> 32.2 us
    dot_general x29 -> x26, matrix products: 59 us -> 39.8 us  [dot(): lax.dot_general(a, b, (((ca,), (cb,)), ((), ())), preferred_element_type=...]
    select_n x6 -> x3, other arithmetic: 19.6 us -> 1.77 us  [ordered(): jnp.where(low_bit == 0, a, b)]
    pallas_call x0 -> x6, Pallas kernels: none -> 14 us  [the longest x3 7.55 us: slot_place(): pl.pallas_call(kernel, out_shape=jax.ShapeDtypeStruct(into.shape, BF16),...]
    dynamic_update_slice x18 -> x0, local copies, waits for them, and re-layouts: 12 us -> none  [the longest x15 6.69 us: ring_gather(): result = lax.dynamic_update_slice_in_dim(result, block, at, 0)]
    select_n x3 -> x0, local copies, waits for them, and re-layouts: 7.63 us -> none  [shards(): jnp.where(am_target, jnp.concatenate([own_half, far_half], axis=1), jnp.z...]
    ppermute x24, waiting for transfers between devices: 77.7 us -> 71.8 us  [the longest x6 62 us: far_sum(): arrived = lax.ppermute(part, 'hidden', xor_pairs(hidden_n, bit))]
    ppermute x6, starting transfers between devices: 10.4 us -> 5.05 us  [ring_gather(): value = lax.ppermute(value, 'expert', ring)]
    convert_element_type x0 -> x1, other arithmetic: none -> 4.9 us  [shards(): (back_sum * active).astype(BF16)]
  transfers between devices with their start and end apart: 45 -> 45, of which waited for: 18 -> 20; matrix products, arithmetic and copies ran while one was open for 32% -> 17% of each run, Pallas kernels for 0% -> 5%
where the time goes in v3:
time: 312 us; the launch traced here: 310 us
  waiting for transfers between devices  185 us (59%)
  matrix products  39.8 us (13%)
  starting transfers between devices  32.2 us (10%)
  other arithmetic  27.3 us (9%)
  Pallas kernels  14 us (4%)
  local copies, waits for them, and re-layouts  7.87 us (3%)
  between operations  4.5 us (1%)
    ppermute x6, waiting for transfers between devices, with_partner(): return lax.switch(apart - 1, branches, value)  95.4 us
    ppermute x6, waiting for transfers between devices, far_sum(): arrived = lax.ppermute(part, 'hidden', xor_pairs(hidden_n, bit))  62 us
    dot_general x26, matrix products, dot(): lax.dot_general(a, b, (((ca,), (cb,)), ((), ())), preferred_element_type=...  39.8 us
    ppermute x6, waiting for transfers between devices, ring_gather(): value = lax.ppermute(value, 'expert', ring)  11.1 us
    ppermute x8, starting transfers between devices, ring_gather(): blocks += [value, lax.ppermute(value, 'expert', xor_pairs(count, 1))]  9.15 us
    pallas_call x3, Pallas kernels, slot_place(): pl.pallas_call(kernel, out_shape=jax.ShapeDtypeStruct(into.shape, BF16),...  7.55 us
    unnamed x64, local copies, waits for them, and re-layouts  7.14 us
    ppermute x6, starting transfers between devices, far_sum(): arrived = lax.ppermute(part, 'hidden', xor_pairs(hidden_n, bit))  7.11 us
  transfers between devices with their start and end apart: 45, of which 20 were waited for; matrix products, arithmetic and copies ran while one was open for 17% of the time, Pallas kernels for 5%

profile of v3, /device:TPU:0, one launch (start us, length us, event | category | flops | bytes accessed | tf_op | source)
XLA Modules:
  0.0 310.2 jit_solution(5008744674321240204)
XLA Ops:
  26.3 3.7 %collective-permute-done.57 = bf16[128,512]{1,0:T(8,128)(2,1)S(1)} collective-permute-done((bf16[128,512]{1,0:T(8,128)(2,1)S(1)}, bf16[128,512]{1,0:T(8,128)(2,1)S(1)}, u32[]{:S(2)}, u32[]{:S(2)}) %collective-permute-start.57) | collective-permute-done | bytes 131104 | tf_op jit(solution)/shard_map/ppermute | solution.py:35
  30.3 3.2 %collective-permute-done.45 = bf16[128,640]{1,0:T(8,128)(2,1)S(1)} collective-permute-done((bf16[128,640]{1,0:T(8,128)(2,1)S(1)}, bf16[128,640]{1,0:T(8,128)(2,1)S(1)}, u32[]{:S(2)}, u32[]{:S(2)}) %collective-permute-start.45) | collective-permute-done | bytes 163872 | tf_op jit(solution)/shard_map/ppermute | solution.py:35
  44.0 3.3 %collective-permute-done.48 = bf16[128,640]{1,0:T(8,128)(2,1)S(1)} collective-permute-done((bf16[128,640]{1,0:T(8,128)(2,1)S(1)}, bf16[128,640]{1,0:T(8,128)(2,1)S(1)}, u32[]{:S(2)}, u32[]{:S(2)}) %collective-permute-start.48) | collective-permute-done | bytes 163872 | tf_op jit(solution)/shard_map/ppermute | solution.py:36
  60.3 18.3 %conditional.14 = (bf16[704,512]{1,0:T(8,128)(2,1)}) conditional(s32[]{:T(128)} %clamp.2, bf16[704,512]{1,0:T(8,128)(2,1)S(1)} %fusion.54, bf16[704,512]{1,0:T(8,128)(2,1)S(1)} %fusion.54, bf16[704,512]{1,0:T(8,128)(2,1)S(1)} %fusion.54, bf16[704,512]{1,0:T(8,128)(2,1)S(1)} %fusion.54, ...), branch_computations={%region_9.10_spmd, %region_10.11_spmd, %region_11.12_spmd, %region... | conditional | bytes 2883632
  60.8 17.7 %collective-permute-done = bf16[704,512]{1,0:T(8,128)(2,1)} collective-permute-done((bf16[704,512]{1,0:T(8,128)(2,1)S(1)}, bf16[704,512]{1,0:T(8,128)(2,1)}, u32[]{:S(2)}, u32[]{:S(2)}) %collective-permute-start) | collective-permute-done | bytes 720928 | tf_op jit(solution)/shard_map/cond/branch_0_fun/ppermute | solution.py:27
  88.5 18.6 %conditional.15 = (bf16[704,512]{1,0:T(8,128)(2,1)}) conditional(s32[]{:T(128)} %clamp.2, bf16[704,512]{1,0:T(8,128)(2,1)S(1)} %fusion.57, bf16[704,512]{1,0:T(8,128)(2,1)S(1)} %fusion.57, bf16[704,512]{1,0:T(8,128)(2,1)S(1)} %fusion.57, bf16[704,512]{1,0:T(8,128)(2,1)S(1)} %fusion.57, ...), branch_computations={%region_16.17_spmd, %region_17.18_spmd, %region_18.19_spmd, %regio... | conditional | bytes 2883632
  89.1 18.1 %collective-permute-done.7 = bf16[704,512]{1,0:T(8,128)(2,1)} collective-permute-done((bf16[704,512]{1,0:T(8,128)(2,1)S(1)}, bf16[704,512]{1,0:T(8,128)(2,1)}, u32[]{:S(2)}, u32[]{:S(2)}) %collective-permute-start.7) | collective-permute-done | bytes 720928 | tf_op jit(solution)/shard_map/cond/branch_0_fun/ppermute | solution.py:27
  117.2 17.8 %conditional.16 = (bf16[704,512]{1,0:T(8,128)(2,1)}) conditional(s32[]{:T(128)} %clamp.2, bf16[704,512]{1,0:T(8,128)(2,1)S(1)} %fusion.60, bf16[704,512]{1,0:T(8,128)(2,1)S(1)} %fusion.60, bf16[704,512]{1,0:T(8,128)(2,1)S(1)} %fusion.60, bf16[704,512]{1,0:T(8,128)(2,1)S(1)} %fusion.60, ...), branch_computations={%region_23.24_spmd, %region_24.25_spmd, %region_25.26_spmd, %regio... | conditional | bytes 2883632
  117.7 17.2 %collective-permute-done.14 = bf16[704,512]{1,0:T(8,128)(2,1)} collective-permute-done((bf16[704,512]{1,0:T(8,128)(2,1)S(1)}, bf16[704,512]{1,0:T(8,128)(2,1)}, u32[]{:S(2)}, u32[]{:S(2)}) %collective-permute-start.14) | collective-permute-done | bytes 720928 | tf_op jit(solution)/shard_map/cond/branch_0_fun/ppermute | solution.py:27
  138.3 8.6 %collective-permute-done.50 = bf16[256,1408]{1,0:T(8,128)(2,1)} collective-permute-done((bf16[256,1408]{1,0:T(8,128)(2,1)}, bf16[256,1408]{1,0:T(8,128)(2,1)}, u32[]{:S(2)}, u32[]{:S(2)}) %collective-permute-start.50) | collective-permute-done | bytes 720928 | tf_op jit(solution)/shard_map/ppermute | solution.py:229
  146.9 15.1 %collective-permute-done.78 = bf16[256,1408]{1,0:T(8,128)(2,1)} collective-permute-done((bf16[256,1408]{1,0:T(8,128)(2,1)}, bf16[256,1408]{1,0:T(8,128)(2,1)}, u32[]{:S(2)}, u32[]{:S(2)}) %collective-permute-start.78) | collective-permute-done | bytes 720928 | tf_op jit(solution)/shard_map/ppermute | solution.py:229
  161.9 4.6 %multiply_convert_fusion.1 = (bf16[256,1408]{1,0:T(8,128)(2,1)}, bf16[256,1408]{1,0:T(8,128)(2,1)}, bf16[256,1408]{1,0:T(8,128)(2,1)}) fusion(bf16[256,1408]{1,0:T(8,128)(2,1)} %collective-permute-done.78, bf16[256,1408]{1,0:T(8,128)(2,1)} %add_convert_fusion.1, bf16[256,1408]{1,0:T(8,128)(2,1)} %collective-permute-done.50, ...), kind=kLoop, calls=%fused_computation.56 | loop fusion | flops 8650752 | bytes 6488064 | tf_op jit(solution)/shard_map/convert_element_type | solution.py:132
  178.0 8.4 %collective-permute-done.63 = bf16[352,1024]{1,0:T(8,128)(2,1)} collective-permute-done((bf16[352,1024]{1,0:T(8,128)(2,1)}, bf16[352,1024]{1,0:T(8,128)(2,1)}, u32[]{:S(2)}, u32[]{:S(2)}) %collective-permute-start.63) | collective-permute-done | bytes 720928 | tf_op jit(solution)/shard_map/ppermute | solution.py:229
  186.4 15.4 %collective-permute-done.65 = bf16[352,1024]{1,0:T(8,128)(2,1)} collective-permute-done((bf16[352,1024]{1,0:T(8,128)(2,1)}, bf16[352,1024]{1,0:T(8,128)(2,1)}, u32[]{:S(2)}, u32[]{:S(2)}) %collective-permute-start.65) | collective-permute-done | bytes 720928 | tf_op jit(solution)/shard_map/ppermute | solution.py:229
  201.8 14.5 %collective-permute-done.75 = bf16[352,1024]{1,0:T(8,128)(2,1)} collective-permute-done((bf16[352,1024]{1,0:T(8,128)(2,1)}, bf16[352,1024]{1,0:T(8,128)(2,1)}, u32[]{:S(2)}, u32[]{:S(2)}) %collective-permute-start.75) | collective-permute-done | bytes 720928 | tf_op jit(solution)/shard_map/ppermute | solution.py:229
  216.3 4.9 %multiply_convert_fusion.3 = (bf16[352,1024]{1,0:T(8,128)(2,1)}, bf16[352,1024]{1,0:T(8,128)(2,1)}, bf16[352,1024]{1,0:T(8,128)(2,1)}) fusion(bf16[352,1024]{1,0:T(8,128)(2,1)} %collective-permute-done.75, bf16[352,1024]{1,0:T(8,128)(2,1)} %fusion.44, bf16[352,1024]{1,0:T(8,128)(2,1)} %collective-permute-done.63, bf16[352,1024]{1,0:T(8,128)(2,1)} %fusion.42, ...), kind=kLoop, calls=%fused_computation.59 | loop fusion | flops 8650752 | bytes 6488064 | tf_op jit(solution)/shard_map/convert_element_type | solution.py:285
  225.6 4.3 %fusion.7 = f32[1024,512]{1,0:T(8,128)} fusion(bf16[2,512,1408]{2,1,0:T(8,128)(2,1)S(1)} %copy-done, s32[]{:T(128)S(6)} %select_n.148, s32[1024]{0:T(1024)S(1)} %fusion.99, f32[512]{0:T(512)S(1)} %select_reduce_fusion, bf16[256,1408]{1,0:T(8,128)(2,1)} %get-tuple-element.146, bf16[256,1408]{1,0:T(8,128)(2,1)} %collective-permute-done.53), kind=kOutput, calls=%fused_computation.16 | convolution fusion | flops 1279000576 | bytes 4986884 | tf_op jit(solution)/shard_map/dot_general | solution.py:15
  240.4 5.4 %collective-permute-done.69 = bf16[128,512]{1,0:T(8,128)(2,1)S(1)} collective-permute-done((bf16[128,512]{1,0:T(8,128)(2,1)S(1)}, bf16[128,512]{1,0:T(8,128)(2,1)S(1)}, u32[]{:S(2)}, u32[]{:S(2)}) %collective-permute-start.69) | collective-permute-done | bytes 131104 | tf_op jit(solution)/shard_map/ppermute | solution.py:47
  249.2 4.9 %collective-permute-done.72 = bf16[128,512]{1,0:T(8,128)(2,1)S(1)} collective-permute-done((bf16[128,512]{1,0:T(8,128)(2,1)S(1)}, bf16[128,512]{1,0:T(8,128)(2,1)S(1)}, u32[]{:S(2)}, u32[]{:S(2)}) %collective-permute-start.72) | collective-permute-done | bytes 131104 | tf_op jit(solution)/shard_map/ppermute | solution.py:53
  256.1 16.1 %conditional.18 = (bf16[704,512]{1,0:T(8,128)(2,1)}) conditional(s32[]{:T(128)} %clamp.2, bf16[704,512]{1,0:T(8,128)(2,1)S(1)} %convolution_convert_fusion.3.first_ref, bf16[704,512]{1,0:T(8,128)(2,1)S(1)} %convolution_convert_fusion.3.first_ref, ...), branch_computations={%region_37.38_spmd, %region_38.39_spmd, %region_39.40_spmd, %regio... | conditional | bytes 2883632 | solution.py:27
  256.6 15.5 %collective-permute-done.35 = bf16[704,512]{1,0:T(8,128)(2,1)} collective-permute-done((bf16[704,512]{1,0:T(8,128)(2,1)S(1)}, bf16[704,512]{1,0:T(8,128)(2,1)}, u32[]{:S(2)}, u32[]{:S(2)}) %collective-permute-start.35) | collective-permute-done | bytes 720928 | tf_op jit(solution)/shard_map/cond/branch_0_fun/ppermute | solution.py:27
  272.2 28.9 %conditional.17 = (bf16[704,512]{1,0:T(8,128)(2,1)}, bf16[704,512]{1,0:T(8,128)(2,1)}) conditional(s32[]{:T(128)} %clamp.2, (bf16[704,512]{1,0:T(8,128)(2,1)}, bf16[704,512]{1,0:T(8,128)(2,1)}) %tuple.217, (bf16[704,512]{1,0:T(8,128)(2,1)}, bf16[704,512]{1,0:T(8,128)(2,1)}) %tuple.217, (bf16[704,512]{1,0:T(8,128)(2,1)}, ...), branch_computations={%region_30.31_spmd, %region_31.32_spmd, %region_32.33_spmd, %regio... | conditional | bytes 5767264 | solution.py:27
  274.2 17.4 %collective-permute-done.21 = bf16[704,512]{1,0:T(8,128)(2,1)} collective-permute-done((bf16[704,512]{1,0:T(8,128)(2,1)}, bf16[704,512]{1,0:T(8,128)(2,1)}, u32[]{:S(2)}, u32[]{:S(2)}) %collective-permute-start.21) | collective-permute-done | bytes 720928 | tf_op jit(solution)/shard_map/cond/branch_0_fun/ppermute | solution.py:27
  291.6 9.5 %collective-permute-done.22 = bf16[704,512]{1,0:T(8,128)(2,1)} collective-permute-done((bf16[704,512]{1,0:T(8,128)(2,1)}, bf16[704,512]{1,0:T(8,128)(2,1)}, u32[]{:S(2)}, u32[]{:S(2)}) %collective-permute-start.22) | collective-permute-done | bytes 720928 | tf_op jit(solution)/shard_map/cond/branch_0_fun/ppermute | solution.py:27
  (197 shorter events, 114.0 us)
Async XLA Ops:
  3.3 21.7 %collective-permute-start.42 = (bf16[128,640]{1,0:T(8,128)(2,1)S(1)}, bf16[128,640]{1,0:T(8,128)(2,1)S(1)}, u32[]{:S(2)}, u32[]{:S(2)}) collective-permute-start(bf16[128,640]{1,0:T(8,128)(2,1)S(1)} %get-tuple-element.160), channel_id=1, source_target_pairs={{0,4},{4,0},{8,12},{12,8},{16,20},{20,16},{24,28},{28,24},{1,5},{5... | collective-permute-start | bytes 491528 | tf_op jit(solution)/shard_map/ppermute | solution.py:36
  6.2 18.1 %collective-permute-start.43 = (bf16[128,640]{1,0:T(8,128)(2,1)S(1)}, bf16[128,640]{1,0:T(8,128)(2,1)S(1)}, u32[]{:S(2)}, u32[]{:S(2)}) collective-permute-start(bf16[128,640]{1,0:T(8,128)(2,1)S(1)} %get-tuple-element.160), channel_id=1, source_target_pairs={{0,8},{4,12},{8,16},{12,20},{16,24},{20,28},{24,0},{28,4},{1,9},{5... | collective-permute-start | bytes 491528 | tf_op jit(solution)/shard_map/ppermute | solution.py:35
  7.8 12.4 %collective-permute-start.55 = (bf16[128,512]{1,0:T(8,128)(2,1)}, bf16[128,512]{1,0:T(8,128)(2,1)S(1)}, u32[]{:S(2)}, u32[]{:S(2)}) collective-permute-start(bf16[128,512]{1,0:T(8,128)(2,1)} %param.46), channel_id=1, source_target_pairs={{0,8},{4,12},{8,16},{12,20},{16,24},{20,28},{24,0},{28,4},{1,9},{5... | collective-permute-start | bytes 393224 | tf_op jit(solution)/shard_map/ppermute | solution.py:35
  9.4 14.0 %collective-permute-start.54 = (bf16[128,512]{1,0:T(8,128)(2,1)}, bf16[128,512]{1,0:T(8,128)(2,1)}, u32[]{:S(2)}, u32[]{:S(2)}) collective-permute-start(bf16[128,512]{1,0:T(8,128)(2,1)} %param.46), channel_id=1, source_target_pairs={{0,4},{4,0},{8,12},{12,8},{16,20},{20,16},{24,28},{28,24},{1,5},{5... | collective-permute-start | bytes 393224 | tf_op jit(solution)/shard_map/ppermute | solution.py:36
  20.2 10.0 %collective-permute-start.56 = (bf16[128,512]{1,0:T(8,128)(2,1)S(1)}, bf16[128,512]{1,0:T(8,128)(2,1)S(1)}, u32[]{:S(2)}, u32[]{:S(2)}) collective-permute-start(bf16[128,512]{1,0:T(8,128)(2,1)S(1)} %collective-permute-done.55), channel_id=1, source_target_pairs={{0,4},{4,0},{8,12},{12,8},{16,20},{20,16},{24,28},{28,24},{1,5},{5... | collective-permute-start | bytes 393224 | tf_op jit(solution)/shard_map/ppermute | solution.py:36
  24.3 10.6 %collective-permute-start.44 = (bf16[128,640]{1,0:T(8,128)(2,1)S(1)}, bf16[128,640]{1,0:T(8,128)(2,1)S(1)}, u32[]{:S(2)}, u32[]{:S(2)}) collective-permute-start(bf16[128,640]{1,0:T(8,128)(2,1)S(1)} %collective-permute-done.43), channel_id=1, source_target_pairs={{0,4},{4,0},{8,12},{12,8},{16,20},{20,16},{24,28},{28,24},{1,5},{5... | collective-permute-start | bytes 491528 | tf_op jit(solution)/shard_map/ppermute | solution.py:36
  60.3 18.3 %collective-permute-start = (bf16[704,512]{1,0:T(8,128)(2,1)S(1)}, bf16[704,512]{1,0:T(8,128)(2,1)}, u32[]{:S(2)}, u32[]{:S(2)}) collective-permute-start(bf16[704,512]{1,0:T(8,128)(2,1)S(1)} %param), channel_id=1, source_target_pairs={{0,4},{4,0},{8,12},{12,8},{16,20},{20,16},{24,28},{28,24},{1,5},{5... | collective-permute-start | bytes 2162696 | tf_op jit(solution)/shard_map/cond/branch_0_fun/ppermute | solution.py:27
  88.5 18.6 %collective-permute-start.7 = (bf16[704,512]{1,0:T(8,128)(2,1)S(1)}, bf16[704,512]{1,0:T(8,128)(2,1)}, u32[]{:S(2)}, u32[]{:S(2)}) collective-permute-start(bf16[704,512]{1,0:T(8,128)(2,1)S(1)} %param.7), channel_id=1, source_target_pairs={{0,4},{4,0},{8,12},{12,8},{16,20},{20,16},{24,28},{28,24},{1,5},{5... | collective-permute-start | bytes 2162696 | tf_op jit(solution)/shard_map/cond/branch_0_fun/ppermute | solution.py:27
  112.1 26.2 %collective-permute-start.52 = (bf16[256,1408]{1,0:T(8,128)(2,1)}, bf16[256,1408]{1,0:T(8,128)(2,1)}, u32[]{:S(2)}, u32[]{:S(2)}) collective-permute-start(bf16[256,1408]{1,0:T(8,128)(2,1)} %add_convert_fusion.2), channel_id=1, source_target_pairs={{0,2},{1,3},{2,0},{3,1},{4,6},{5,7},{6,4},{7,5},{8,10},{9,11},{10,... | collective-permute-start | bytes 2162696 | tf_op jit(solution)/shard_map/ppermute | solution.py:229
  113.7 33.2 %collective-permute-start.50 = (bf16[256,1408]{1,0:T(8,128)(2,1)}, bf16[256,1408]{1,0:T(8,128)(2,1)}, u32[]{:S(2)}, u32[]{:S(2)}) collective-permute-start(bf16[256,1408]{1,0:T(8,128)(2,1)} %add_convert_fusion.3), channel_id=1, source_target_pairs={{0,2},{1,3},{2,0},{3,1},{4,6},{5,7},{6,4},{7,5},{8,10},{9,11},{10,... | collective-permute-start | bytes 2162696 | tf_op jit(solution)/shard_map/ppermute | solution.py:229
  114.2 47.7 %collective-permute-start.78 = (bf16[256,1408]{1,0:T(8,128)(2,1)}, bf16[256,1408]{1,0:T(8,128)(2,1)}, u32[]{:S(2)}, u32[]{:S(2)}) collective-permute-start(bf16[256,1408]{1,0:T(8,128)(2,1)} %add_convert_fusion.1), channel_id=1, source_target_pairs={{0,2},{1,3},{2,0},{3,1},{4,6},{5,7},{6,4},{7,5},{8,10},{9,11},{10,... | collective-permute-start | bytes 2162696 | tf_op jit(solution)/shard_map/ppermute | solution.py:229
  117.2 17.8 %collective-permute-start.14 = (bf16[704,512]{1,0:T(8,128)(2,1)S(1)}, bf16[704,512]{1,0:T(8,128)(2,1)}, u32[]{:S(2)}, u32[]{:S(2)}) collective-permute-start(bf16[704,512]{1,0:T(8,128)(2,1)S(1)} %param.14), channel_id=1, source_target_pairs={{0,4},{4,0},{8,12},{12,8},{16,20},{20,16},{24,28},{28,24},{1,5},{5... | collective-permute-start | bytes 2162696 | tf_op jit(solution)/shard_map/cond/branch_0_fun/ppermute | solution.py:27
  138.2 30.9 %collective-permute-start.74 = (bf16[352,1024]{1,0:T(8,128)(2,1)S(1)}, bf16[352,1024]{1,0:T(8,128)(2,1)S(1)}, u32[]{:S(2)}, u32[]{:S(2)}) collective-permute-start(bf16[352,1024]{1,0:T(8,128)(2,1)S(1)} %convolution_convert_fusion.4), channel_id=1, source_target_pairs={{0,1},{1,0},{2,3},{3,2},{4,5},{5,4},{6,7},{7,6},{8,9},{9,8},{10,11... | collective-permute-start | bytes 2162696 | tf_op jit(solution)/shard_map/ppermute | solution.py:221
  167.1 19.3 %collective-permute-start.63 = (bf16[352,1024]{1,0:T(8,128)(2,1)}, bf16[352,1024]{1,0:T(8,128)(2,1)}, u32[]{:S(2)}, u32[]{:S(2)}) collective-permute-start(bf16[352,1024]{1,0:T(8,128)(2,1)} %fusion.42), channel_id=1, source_target_pairs={{0,2},{1,3},{2,0},{3,1},{4,6},{5,7},{6,4},{7,5},{8,10},{9,11},{10,... | collective-permute-start | bytes 2162696 | tf_op jit(solution)/shard_map/ppermute | solution.py:229
  168.6 33.3 %collective-permute-start.65 = (bf16[352,1024]{1,0:T(8,128)(2,1)}, bf16[352,1024]{1,0:T(8,128)(2,1)}, u32[]{:S(2)}, u32[]{:S(2)}) collective-permute-start(bf16[352,1024]{1,0:T(8,128)(2,1)} %fusion.43), channel_id=1, source_target_pairs={{0,2},{1,3},{2,0},{3,1},{4,6},{5,7},{6,4},{7,5},{8,10},{9,11},{10,... | collective-permute-start | bytes 2162696 | tf_op jit(solution)/shard_map/ppermute | solution.py:229
  170.6 45.7 %collective-permute-start.75 = (bf16[352,1024]{1,0:T(8,128)(2,1)}, bf16[352,1024]{1,0:T(8,128)(2,1)}, u32[]{:S(2)}, u32[]{:S(2)}) collective-permute-start(bf16[352,1024]{1,0:T(8,128)(2,1)} %fusion.44), channel_id=1, source_target_pairs={{0,2},{1,3},{2,0},{3,1},{4,6},{5,7},{6,4},{7,5},{8,10},{9,11},{10,... | collective-permute-start | bytes 2162696 | tf_op jit(solution)/shard_map/ppermute | solution.py:229
  172.8 50.6 %collective-permute-start.79 = (bf16[256,1408]{1,0:T(8,128)(2,1)}, bf16[256,1408]{1,0:T(8,128)(2,1)S(1)}, u32[]{:S(2)}, u32[]{:S(2)}) collective-permute-start(bf16[256,1408]{1,0:T(8,128)(2,1)} %get-tuple-element.145), channel_id=1, source_target_pairs={{0,1},{1,0},{2,3},{3,2},{4,5},{5,4},{6,7},{7,6},{8,9},{9,8},{10,11... | collective-permute-start | bytes 2162696 | tf_op jit(solution)/shard_map/ppermute | solution.py:234
  229.9 10.4 %collective-permute-start.77 = (bf16[352,1024]{1,0:T(8,128)(2,1)}, bf16[352,1024]{1,0:T(8,128)(2,1)S(1)}, u32[]{:S(2)}, u32[]{:S(2)}) collective-permute-start(bf16[352,1024]{1,0:T(8,128)(2,1)} %get-tuple-element.147), channel_id=1, source_target_pairs={{0,1},{1,0},{2,3},{3,2},{4,5},{5,4},{6,7},{7,6},{8,9},{9,8},{10,11... | collective-permute-start | bytes 2162696 | tf_op jit(solution)/shard_map/ppermute | solution.py:234
  234.4 74.3 %collective-permute-start.67 = (bf16[128,512]{1,0:T(8,128)(2,1)S(1)}, bf16[128,512]{1,0:T(8,128)(2,1)S(1)}, u32[]{:S(2)}, u32[]{:S(2)}) collective-permute-start(bf16[128,512]{1,0:T(8,128)(2,1)S(1)} %get-tuple-element.156), channel_id=1, source_target_pairs={{0,4},{4,0},{8,12},{12,8},{16,20},{20,16},{24,28},{28,24},{1,5},{5... | collective-permute-start | bytes 393224 | tf_op jit(solution)/shard_map/ppermute | solution.py:47
  238.1 11.1 %collective-permute-start.68 = (bf16[128,512]{1,0:T(8,128)(2,1)S(1)}, bf16[128,512]{1,0:T(8,128)(2,1)S(1)}, u32[]{:S(2)}, u32[]{:S(2)}) collective-permute-start(bf16[128,512]{1,0:T(8,128)(2,1)S(1)} %get-tuple-element.159), channel_id=1, source_target_pairs={{0,4},{4,0},{8,12},{12,8},{16,20},{20,16},{24,28},{28,24},{1,5},{5... | collective-permute-start | bytes 393224 | tf_op jit(solution)/shard_map/ppermute | solution.py:47
  254.2 54.4 %collective-permute-start.73 = (bf16[128,512]{1,0:T(8,128)(2,1)S(1)}, bf16[128,512]{1,0:T(8,128)(2,1)S(1)}, u32[]{:S(2)}, u32[]{:S(2)}) collective-permute-start(bf16[128,512]{1,0:T(8,128)(2,1)S(1)} %add_convert_fusion.5), channel_id=1, source_target_pairs={{0,8},{4,12},{8,16},{12,20},{16,24},{20,28},{24,0},{28,4},{1,9},{5... | collective-permute-start | bytes 393224 | tf_op jit(solution)/shard_map/ppermute | solution.py:53
  256.1 16.1 %collective-permute-start.35 = (bf16[704,512]{1,0:T(8,128)(2,1)S(1)}, bf16[704,512]{1,0:T(8,128)(2,1)}, u32[]{:S(2)}, u32[]{:S(2)}) collective-permute-start(bf16[704,512]{1,0:T(8,128)(2,1)S(1)} %param.28), channel_id=1, source_target_pairs={{0,4},{4,0},{8,12},{12,8},{16,20},{20,16},{24,28},{28,24},{1,5},{5... | collective-permute-start | bytes 2162696 | tf_op jit(solution)/shard_map/cond/branch_0_fun/ppermute | solution.py:27
  272.2 19.4 %collective-permute-start.21 = (bf16[704,512]{1,0:T(8,128)(2,1)}, bf16[704,512]{1,0:T(8,128)(2,1)}, u32[]{:S(2)}, u32[]{:S(2)}) collective-permute-start(bf16[704,512]{1,0:T(8,128)(2,1)} %get-tuple-element.106), channel_id=1, source_target_pairs={{0,4},{4,0},{8,12},{12,8},{16,20},{20,16},{24,28},{28,24},{1,5},{5... | collective-permute-start | bytes 2162696 | tf_op jit(solution)/shard_map/cond/branch_0_fun/ppermute | solution.py:27
  272.7 28.3 %collective-permute-start.22 = (bf16[704,512]{1,0:T(8,128)(2,1)}, bf16[704,512]{1,0:T(8,128)(2,1)}, u32[]{:S(2)}, u32[]{:S(2)}) collective-permute-start(bf16[704,512]{1,0:T(8,128)(2,1)} %get-tuple-element.107), channel_id=1, source_target_pairs={{0,4},{4,0},{8,12},{12,8},{16,20},{20,16},{24,28},{28,24},{1,5},{5... | collective-permute-start | bytes 2162696 | tf_op jit(solution)/shard_map/cond/branch_0_fun/ppermute | solution.py:27
  (46 other events, 329.0 us)

commit v4 on v3

--- a/solution.py
+++ b/solution.py
@@ -19,25 +19,30 @@
     return [(i, i ^ bits) for i in range(count)]
 
 
-def with_partner(count, apart, value):
-    branches = [
-        functools.partial(lax.ppermute, axis_name="expert", perm=xor_pairs(count, bits))
-        for bits in range(1, count)
-    ]
-    return lax.switch(apart - 1, branches, value)
-
-
-def ring_gather(value, count):
+def with_partner(count, apart, values, far=None, parts=()):
+    def run(bits, values, parts):
+        there = [lax.ppermute(v, "expert", xor_pairs(count, bits)) for v in values]
+        return there, [far(part) for part in parts]
+
+    branches = [functools.partial(run, bits) for bits in range(1, count)]
+    return lax.switch(apart - 1, branches, list(values), list(parts))
+
+
+def after(value, *others):
+    return lax.optimization_barrier((value, *others))[0]
+
+
+def ring_gather(value, count, beside):
     ring = [(i, (i + 2) % count) for i in range(count)]
     blocks = []
     for step in range(count // 2):
         if step > 0:
-            value = lax.ppermute(value, "expert", ring)
+            value = after(lax.ppermute(value, "expert", ring), *beside[step - 1 :: count // 2 - 1])
         blocks += [value, lax.ppermute(value, "expert", xor_pairs(count, 1))]
     return jnp.concatenate(blocks, axis=0)
 
 
-def ring_scatter(partial, count):
+def ring_scatter(partial, count, later):
     rows = partial.shape[0] // count
     ring = [(i, (i + 2) % count) for i in range(count)]
     steps = count // 2
@@ -51,12 +56,8 @@
         own = partial[at : at + rows].astype(F32) + twins[step].astype(F32)
         if step > 0:
             own = own + lax.ppermute(total, "expert", ring).astype(F32)
-        total = own.astype(BF16)
+        total = own.astype(BF16) if step > 0 else after(own.astype(BF16), later)
     return total
-
-
-def after(value, *others):
-    return lax.optimization_barrier((value, *others))[0]
 
 
 def tile_of(extent, most):
@@ -92,12 +93,18 @@
     )(slot.reshape(1), left, right)
 
 
-def slot_place(slot, keep, first, second, into):
+def slot_place(slot, keep, swap, first, second, into):
     half, width = first.shape
+    quarter = half // 2
     tile = tile_of(width, 256)
 
-    def kernel(slot_ref, keep_ref, first_ref, second_ref, into_ref, out_ref):
-        whole = jnp.concatenate([first_ref[...], second_ref[...]], axis=0).astype(F32)
+    def kernel(slot_ref, keep_ref, swap_ref, first_ref, second_ref, into_ref, out_ref):
+        swap = swap_ref[0] > 0
+        parts = []
+        for ref in (first_ref, second_ref):
+            one, two = ref[:quarter].astype(F32), ref[quarter:].astype(F32)
+            parts += [jnp.where(swap, two, one), jnp.where(swap, one, two)]
+        whole = jnp.concatenate(parts, axis=0)
         whole = jnp.where(keep_ref[0] > 0, whole, 0.0)
         out_ref[0] = whole.T.astype(BF16)
 
@@ -105,21 +112,21 @@
         kernel,
         out_shape=jax.ShapeDtypeStruct(into.shape, BF16),
         grid_spec=pltpu.PrefetchScalarGridSpec(
-            num_scalar_prefetch=2,
+            num_scalar_prefetch=3,
             grid=(width // tile,),
             in_specs=[
-                pl.BlockSpec((half, tile), lambda i, s, k: (0, i)),
-                pl.BlockSpec((half, tile), lambda i, s, k: (0, i)),
+                pl.BlockSpec((half, tile), lambda i, s, k, w: (0, i)),
+                pl.BlockSpec((half, tile), lambda i, s, k, w: (0, i)),
                 pl.BlockSpec(memory_space=pl.ANY),
             ],
-            out_specs=pl.BlockSpec((1, tile, 2 * half), lambda i, s, k: (s[0], i, 0)),
-        ),
-        input_output_aliases={4: 0},
+            out_specs=pl.BlockSpec((1, tile, 2 * half), lambda i, s, k, w: (s[0], i, 0)),
+        ),
+        input_output_aliases={5: 0},
         compiler_params=pltpu.CompilerParams(vmem_limit_bytes=32 << 20),
         cost_estimate=pl.CostEstimate(
             flops=0, bytes_accessed=8 * half * width, transcendentals=0
         ),
-    )(slot.reshape(1), keep.reshape(1), first, second, into)
+    )(slot.reshape(1), keep.reshape(1), swap.reshape(1), first, second, into)
 
 
 def activations(gate_sum, up_sum, back_sum):
@@ -181,13 +188,11 @@
     low = route - high - middle
     pieces = jnp.concatenate([high, middle, low], axis=1).astype(BF16)
     pad = -pieces.shape[1] % 128
-    payload = jnp.concatenate([tokens, jnp.pad(pieces, ((0, 0), (0, pad)))], axis=1)
-    gathered = ring_gather(payload, devices_n)
-    inputs_c = ring_gather(cotangent, devices_n)
-
     order = jnp.where(am_target, jnp.arange(neurons, dtype=jnp.int32), perm)
-    keep_order = jnp.where(am_target, order[:half], order[half:])
-    send_order = jnp.where(am_target, order[half:], order[:half])
+    order = order.reshape(2, 2, half // 2)
+    order = jnp.where(low_bit == 0, order, order[:, ::-1]).reshape(2, half)
+    keep_order = jnp.where(am_target, order[0], order[1])
+    send_order = jnp.where(am_target, order[1], order[0])
     columns = jnp.arange(neurons, dtype=jnp.int32)
     keep_hot = (keep_order[:, None] == columns[None, :]).astype(BF16)
     send_hot = (send_order[:, None] == columns[None, :]).astype(BF16)
@@ -196,8 +201,11 @@
     sends = [dot(send_hot, w, 1, 1).astype(BF16) for w in chosen]
     keeps = [dot(keep_hot, w, 1, 1).astype(BF16) for w in chosen]
 
+    payload = jnp.concatenate([tokens, cotangent, jnp.pad(pieces, ((0, 0), (0, pad)))], axis=1)
+    gathered = ring_gather(payload, devices_n, sends + keeps)
     inputs_x = gathered[:, :width]
-    parts = gathered[:, width : width + 3 * experts].astype(F32)
+    inputs_c = gathered[:, width : 2 * width]
+    parts = gathered[:, 2 * width : 2 * width + 3 * experts].astype(F32)
     route_all = parts[:, :experts] + parts[:, experts : 2 * experts] + parts[:, 2 * experts :]
     merged_hit = (expert_ids == source_e) | (expert_ids == target_e)
     merged_p = jnp.sum(jnp.where(merged_hit, route_all, 0.0), axis=1)
@@ -221,14 +229,24 @@
         arrived = lax.ppermute(send_part.astype(BF16), "hidden", xor_pairs(hidden_n, 1))
         return (keep_part + arrived.astype(F32)).astype(BF16)
 
-    def far_sum(part):
-        total, bit = part.astype(F32), 2
-        while bit < hidden_n:
-            if bit > 2:
-                part = total.astype(BF16)
+    last_bit = 2
+    while last_bit * 2 < hidden_n:
+        last_bit *= 2
+
+    def near_sum(part):
+        bit = 2
+        while bit < last_bit:
             arrived = lax.ppermute(part, "hidden", xor_pairs(hidden_n, bit))
-            total, bit = part.astype(F32) + arrived.astype(F32), bit * 2
-        return total
+            part, bit = (part.astype(F32) + arrived.astype(F32)).astype(BF16), bit * 2
+        return part
+
+    def far(part):
+        if last_bit < hidden_n:
+            return lax.ppermute(part, "hidden", xor_pairs(hidden_n, last_bit))
+        return jnp.zeros_like(part)
+
+    def added(one, two):
+        return one.astype(F32) + two.astype(F32)
 
     def swapped(value):
         return lax.ppermute(value, "hidden", xor_pairs(hidden_n, 1))
@@ -238,25 +256,23 @@
     apart = me ^ partner
 
     other_parts = [
-        core_sum(dot(value[:slots_half], w, 1, 0), dot(value[slots_half:], w, 1, 0))
+        near_sum(core_sum(dot(value[:slots_half], w, 1, 0), dot(value[slots_half:], w, 1, 0)))
         for value, w in zip((other_x, other_x, other_dy), others)
     ]
-    other_sums = [far_sum(part) for part in other_parts]
-
-    last = other_parts
-    merged, merged_sums = [], []
-    for value, send, keep in zip((inputs_x, inputs_x, merged_dy), sends, keeps):
-        arrived = with_partner(devices_n, apart, after(send, *last))
-        w = (0.5 * (keep.astype(F32) + arrived.astype(F32))).astype(BF16)
-        merged.append(w)
-        w_send = lax.dynamic_slice_in_dim(w, (1 - low_bit) * quarter, quarter, 0)
-        w_keep = lax.dynamic_slice_in_dim(w, low_bit * quarter, quarter, 0)
-        part = core_sum(dot(w_send, value, 1, 1), dot(w_keep, value, 1, 1))
-        merged_sums.append(far_sum(part))
-        last = [part]
+
+    arrived, other_far = with_partner(devices_n, apart, sends, far, other_parts)
+    merged = [
+        (0.5 * (k.astype(F32) + a.astype(F32))).astype(BF16) for k, a in zip(keeps, arrived)
+    ]
+    w_down = merged[2]
+    merged_sums = []
+    for value, w in zip((inputs_x, inputs_x, merged_dy), merged):
+        part = near_sum(core_sum(dot(w[quarter:], value, 1, 1), dot(w[:quarter], value, 1, 1)))
+        merged_sums.append((part, far(part)))
 
     other_h, other_dg, other_du = [
-        jnp.concatenate([swapped(a), a], axis=0) for a in activations(*other_sums)
+        jnp.concatenate([swapped(a), a], axis=0)
+        for a in activations(*map(added, other_parts, other_far))
     ]
     other_y = (dot(other_h, others[2], 1, 1) * slot_p[:, None]).astype(BF16)
     other_mixed = dot(slot_hot, other_y, 0, 0)
@@ -265,31 +281,30 @@
         for value, a in ((other_x, other_dg), (other_x, other_du), (other_dy, other_h))
     ]
 
-    def ordered(a):
-        b = swapped(a)
-        return jnp.concatenate(
-            [jnp.where(low_bit == 0, a, b), jnp.where(low_bit == 0, b, a)], axis=0
-        )
-
-    gate_sum, up_sum, back_sum = merged_sums
+    def joined(a):
+        a = a.astype(BF16)
+        return jnp.concatenate([a, swapped(a)], axis=0)
+
+    gate_sum, up_sum = added(*merged_sums[0]), added(*merged_sums[1])
     sigma = jax.nn.sigmoid(gate_sum)
     active = gate_sum * sigma
     inner = up_sum * sigma * (1.0 + gate_sum * (1.0 - sigma))
-    merged_h = ordered((active * up_sum).astype(BF16))
-    mixed = other_mixed + merged_p[:, None] * dot(merged_h, merged[2], 0, 0)
-    mixed = mixed.astype(BF16)
+    merged_h = joined(active * up_sum)
+    mixed = (other_mixed + merged_p[:, None] * dot(merged_h, w_down, 0, 0)).astype(BF16)
     down_half = dot(merged_h, merged_dy, 1, 0).astype(BF16)
-    far_down = with_partner(devices_n, apart, after(down_half, mixed))
-    mixed = ring_scatter(mixed, devices_n)
-    gate_half = dot(ordered((back_sum * inner).astype(BF16)), inputs_x, 1, 0).astype(BF16)
-    up_half = dot(ordered((back_sum * active).astype(BF16)), inputs_x, 1, 0).astype(BF16)
-    far_gate, far_up = with_partner(devices_n, apart, (gate_half, up_half))
+    (far_down,), _ = with_partner(devices_n, apart, [after(down_half, mixed)])
+    mixed = ring_scatter(mixed, devices_n, far_down)
+    back_sum = added(after(merged_sums[2][0], down_half), merged_sums[2][1])
+    gate_half = dot(joined(back_sum * inner), inputs_x, 1, 0).astype(BF16)
+    up_half = dot(joined(back_sum * active), inputs_x, 1, 0).astype(BF16)
+    (far_gate, far_up), _ = with_partner(devices_n, apart, [gate_half, up_half])
 
     keep_flag = am_target.astype(jnp.int32)
     outs = [
         slot_place(
             merged_slot,
             keep_flag,
+            low_bit,
             own,
             far,
             into,

time: 312 us -> 281 us (0.901)
  waiting for transfers between devices: 185 us -> 142 us
  matrix products: 39.8 us -> 50.8 us
  other arithmetic: 27.3 us -> 36.2 us
  starting transfers between devices: 32.2 us -> 26.2 us
    ppermute x18 -> x15, waiting for transfers between devices: 169 us -> 131 us  [the longest x6 92.4 us: run(): there = [lax.ppermute(v, 'expert', xor_pairs(count, bits)) for v in values]]
    dot_general x26, matrix products: 39.8 us -> 50.8 us  [dot(): lax.dot_general(a, b, (((ca,), (cb,)), ((), ())), preferred_element_type=...]
    convert_element_type x6 -> x10, other arithmetic: 7.74 us -> 15.6 us  [the longest x2 6.71 us: joined(): a = a.astype(BF16)]
    ppermute x4, waiting for transfers between devices: 6.47 us -> 0.01 us  [ring_scatter(): lax.ppermute(partial[at:at + rows], 'expert', xor_pairs(count, 1))]
    ppermute x8 -> x4, starting transfers between devices: 9.15 us -> 4.48 us  [ring_gather(): blocks += [value, lax.ppermute(value, 'expert', xor_pairs(count, 1))]]
    unnamed x64 -> x74, local copies, waits for them, and re-layouts: 7.14 us -> 4.38 us
    ppermute x18 -> x15, starting transfers between devices: 16.4 us -> 16.1 us  [the longest x6 7.03 us: far(): return lax.ppermute(part, 'hidden', xor_pairs(hidden_n, last_bit))]
  transfers between devices with their start and end apart: 45 -> 38, of which waited for: 20 -> 14; matrix products, arithmetic and copies ran while one was open for 17% -> 26% of each run, Pallas kernels for 5% -> 3%
where the time goes in v4:
time: 281 us; the launch traced here: 280 us
  waiting for transfers between devices  142 us (51%)
  matrix products  50.8 us (18%)
  other arithmetic  36.2 us (13%)
  starting transfers between devices  26.2 us (9%)
  Pallas kernels  14.4 us (5%)
  local copies, waits for them, and re-layouts  5.76 us (2%)
  between operations  4.64 us (2%)
    ppermute x6, waiting for transfers between devices, run(): there = [lax.ppermute(v, 'expert', xor_pairs(count, bits)) for v in values]  92.4 us
    dot_general x26, matrix products, dot(): lax.dot_general(a, b, (((ca,), (cb,)), ((), ())), preferred_element_type=...  50.8 us
    ppermute x6, waiting for transfers between devices, far(): return lax.ppermute(part, 'hidden', xor_pairs(hidden_n, last_bit))  22.9 us
    ppermute x3, waiting for transfers between devices, ring_gather(): lax.ppermute(value, 'expert', ring)  15.3 us
    pallas_call x3, Pallas kernels, slot_place(): pl.pallas_call(kernel, out_shape=jax.ShapeDtypeStruct(into.shape, BF16),...  8.01 us
    ppermute x6, starting transfers between devices, far(): return lax.ppermute(part, 'hidden', xor_pairs(hidden_n, last_bit))  7.03 us
    convert_element_type x2, other arithmetic, joined(): a = a.astype(BF16)  6.71 us
    pallas_call x3, Pallas kernels, slot_matmul(): pl.pallas_call(kernel, out_shape=jax.ShapeDtypeStruct((slots, width, neur...  6.41 us
  transfers between devices with their start and end apart: 38, of which 14 were waited for; matrix products, arithmetic and copies ran while one was open for 26% of the time, Pallas kernels for 3%

profile of v4, /device:TPU:0, one launch (start us, length us, event | category | flops | bytes accessed | tf_op | source)
XLA Modules:
  0.0 280.1 jit_solution(3185068392553325347)
XLA Ops:
  3.4 3.0 %collective-permute-start.63 = (bf16[128,1152]{1,0:T(8,128)(2,1)S(1)}, bf16[128,1152]{1,0:T(8,128)(2,1)}, u32[]{:S(2)}, u32[]{:S(2)}) collective-permute-start(bf16[128,1152]{1,0:T(8,128)(2,1)S(1)} %get-tuple-element.286), channel_id=1, source_target_pairs={{0,4},{4,0},{8,12},{12,8},{16,20},{20,16},{24,28},{28,24},{1,5},{5... | collective-permute-start | bytes 884744 | tf_op jit(solution)/shard_map/ppermute | solution.py:41
  26.9 3.6 %fusion.50 = bf16[704,512]{1,0:T(8,128)(2,1)} fusion(s32[704]{0:T(1024)S(1)} %select_n.137, bf16[2,512,1408]{2,1,0:T(8,128)(2,1)} %param.33, s32[]{:T(128)S(6)} %select_n.138), kind=kOutput, calls=%fused_computation.86 | convolution fusion | flops 1016373248 | bytes 2165508 | tf_op jit(solution)/shard_map/dot_general | solution.py:15
  30.5 3.7 %fusion.59 = bf16[704,512]{1,0:T(8,128)(2,1)} fusion(s32[704]{0:T(1024)S(1)} %select_n.140, bf16[2,512,1408]{2,1,0:T(8,128)(2,1)} %param.33, s32[]{:T(128)S(6)} %select_n.138), kind=kOutput, calls=%fused_computation.89 | convolution fusion | flops 1016373248 | bytes 2165508 | tf_op jit(solution)/shard_map/dot_general | solution.py:15
  37.4 6.9 %collective-permute-done.66 = bf16[128,1152]{1,0:T(8,128)(2,1)S(1)} collective-permute-done((bf16[128,1152]{1,0:T(8,128)(2,1)S(1)}, bf16[128,1152]{1,0:T(8,128)(2,1)S(1)}, u32[]{:S(2)}, u32[]{:S(2)}) %collective-permute-start.66) | collective-permute-done | bytes 294944 | tf_op jit(solution)/shard_map/ppermute | solution.py:40
  44.8 8.5 %collective-permute-done.68 = bf16[128,1152]{1,0:T(8,128)(2,1)S(1)} collective-permute-done((bf16[128,1152]{1,0:T(8,128)(2,1)S(1)}, bf16[128,1152]{1,0:T(8,128)(2,1)S(1)}, u32[]{:S(2)}, u32[]{:S(2)}) %collective-permute-start.68) | collective-permute-done | bytes 294944 | tf_op jit(solution)/shard_map/ppermute | solution.py:40
  53.9 6.1 %collective-permute-done.69 = bf16[128,1152]{1,0:T(8,128)(2,1)S(1)} collective-permute-done((bf16[128,1152]{1,0:T(8,128)(2,1)S(1)}, bf16[128,1152]{1,0:T(8,128)(2,1)S(1)}, u32[]{:S(2)}, u32[]{:S(2)}) %collective-permute-start.69) | collective-permute-done | bytes 294944 | tf_op jit(solution)/shard_map/ppermute | solution.py:41
  74.6 2.8 %add_convert_fusion.2 = bf16[256,1408]{1,0:T(8,128)(2,1)} fusion(bf16[256,1408]{1,0:T(8,128)(2,1)} %collective-permute-done.72, bf16[2,512,1408]{2,1,0:T(8,128)(2,1)S(1)} %copy-done, s32[]{:T(128)S(6)} %select_n.144, bf16[512,512]{1,0:T(8,128)(2,1)S(1)} %copy-done.4), kind=kOutput, calls=%fused_computation.81 | convolution fusion | flops 370180096 | bytes 3145732 | tf_op jit(solution)/shard_map/dot_general | solution.py:15
  77.5 51.3 %conditional.8 = (bf16[256,1408]{1,0:T(8,128)(2,1)}, bf16[256,1408]{1,0:T(8,128)(2,1)}, bf16[704,512]{1,0:T(8,128)(2,1)}, bf16[704,512]{1,0:T(8,128)(2,1)}, bf16...) conditional(s32[]{:T(128)} %clamp.2, (bf16[704,512]{1,0:T(8,128)(2,1)S(1)}, ...), branch_computations={%region_8.9_spmd, %region_9.10_spmd, %region_10.11_spmd, %region_1... | conditional | bytes 17301792
  82.1 14.5 %collective-permute-done = bf16[704,512]{1,0:T(8,128)(2,1)} collective-permute-done((bf16[704,512]{1,0:T(8,128)(2,1)S(1)}, bf16[704,512]{1,0:T(8,128)(2,1)}, u32[]{:S(2)}, u32[]{:S(2)}) %collective-permute-start) | collective-permute-done | bytes 720928 | tf_op jit(solution)/shard_map/cond/branch_0_fun/ppermute | solution.py:24
  98.1 14.0 %collective-permute-done.1 = bf16[704,512]{1,0:T(8,128)(2,1)} collective-permute-done((bf16[704,512]{1,0:T(8,128)(2,1)S(1)}, bf16[704,512]{1,0:T(8,128)(2,1)}, u32[]{:S(2)}, u32[]{:S(2)}) %collective-permute-start.1) | collective-permute-done | bytes 720928 | tf_op jit(solution)/shard_map/cond/branch_0_fun/ppermute | solution.py:24
  112.0 15.0 %collective-permute-done.2 = bf16[704,512]{1,0:T(8,128)(2,1)} collective-permute-done((bf16[704,512]{1,0:T(8,128)(2,1)S(1)}, bf16[704,512]{1,0:T(8,128)(2,1)}, u32[]{:S(2)}, u32[]{:S(2)}) %collective-permute-start.2) | collective-permute-done | bytes 720928 | tf_op jit(solution)/shard_map/cond/branch_0_fun/ppermute | solution.py:24
  141.6 4.1 %multiply_convert_fusion.1 = (bf16[256,1408]{1,0:T(8,128)(2,1)}, bf16[256,1408]{1,0:T(8,128)(2,1)}, bf16[256,1408]{1,0:T(8,128)(2,1)}) fusion(bf16[256,1408]{1,0:T(8,128)(2,1)} %get-tuple-element.268, bf16[256,1408]{1,0:T(8,128)(2,1)} %add_convert_fusion.2, bf16[256,1408]{1,0:T(8,128)(2,1)} %get-tuple-element.263, bf16[256,1408]{1,0:T(8,128)(2,1)S(1)} %copy-done.7, ...), kind=kLoop, calls=%fused_computation.67 | loop fusion | flops 8650752 | bytes 6488064 | tf_op jit(solution)/shard_map/convert_element_type | solution.py:139
  147.0 3.1 %add_convert_fusion.1 = bf16[352,1024]{1,0:T(8,128)(2,1)} fusion(bf16[352,1024]{1,0:T(8,128)(2,1)} %collective-permute-done.86, bf16[704,512]{1,0:T(8,128)(2,1)} %copy-done.19, f32[1024]{0:T(1024)S(1)} %get-tuple-element.269, bf16[1024,1152]{1,0:T(8,128)(2,1)} %copy-done.26), kind=kOutput, calls=%fused_computation.72 | convolution fusion | flops 371752960 | bytes 2854912 | tf_op jit(solution)/shard_map/dot_general | solution.py:15
  150.1 7.2 %collective-permute-done.75 = bf16[352,1024]{1,0:T(8,128)(2,1)} collective-permute-done((bf16[352,1024]{1,0:T(8,128)(2,1)}, bf16[352,1024]{1,0:T(8,128)(2,1)}, u32[]{:S(2)}, u32[]{:S(2)}) %collective-permute-start.75) | collective-permute-done | bytes 720928 | tf_op jit(solution)/shard_map/ppermute | solution.py:245
  158.8 14.0 %collective-permute-done.77 = bf16[352,1024]{1,0:T(8,128)(2,1)} collective-permute-done((bf16[352,1024]{1,0:T(8,128)(2,1)}, bf16[352,1024]{1,0:T(8,128)(2,1)}, u32[]{:S(2)}, u32[]{:S(2)}) %collective-permute-start.77) | collective-permute-done | bytes 720928 | tf_op jit(solution)/shard_map/ppermute | solution.py:245
  172.8 3.3 %multiply_convert_fusion.5 = bf16[352,1024]{1,0:T(8,128)(2,1)} fusion(bf16[352,1024]{1,0:T(8,128)(2,1)} %collective-permute-done.77, bf16[352,1024]{1,0:T(8,128)(2,1)} %fusion.49, bf16[352,1024]{1,0:T(8,128)(2,1)} %collective-permute-done.75, bf16[352,1024]{1,0:T(8,128)(2,1)} %fusion.48), kind=kLoop, calls=%fused_computation.73 | loop fusion | flops 4325376 | bytes 3604480 | tf_op jit(solution)/shard_map/convert_element_type | solution.py:285
  180.8 4.3 %fusion.6 = f32[1024,512]{1,0:T(8,128)} fusion(bf16[2,512,1408]{2,1,0:T(8,128)(2,1)S(1)} %copy-done, s32[]{:T(128)S(6)} %select_n.144, s32[1024]{0:T(1024)S(1)} %fusion.100, f32[512]{0:T(512)S(1)} %select_reduce_fusion, bf16[256,1408]{1,0:T(8,128)(2,1)} %get-tuple-element.279, bf16[256,1408]{1,0:T(8,128)(2,1)} %copy-done.24), kind=kOutput, calls=%fused_computation.15 | convolution fusion | flops 1279000576 | bytes 4986884 | tf_op jit(solution)/shard_map/dot_general | solution.py:15
  185.1 3.3 %add_convert_fusion = bf16[1024,512]{1,0:T(8,128)(2,1)S(1)} fusion(f32[1024,512]{1,0:T(8,128)} %fusion.6, bf16[704,512]{1,0:T(8,128)(2,1)} %copy-done.19, f32[1024]{0:T(1024)S(1)} %get-tuple-element.269, bf16[352,1024]{1,0:T(8,128)(2,1)} %collective-permute-done.78, bf16[352,1024]{1,0:T(8,128)(2,1)} %multiply_convert_fusion.5), kind=kOutput, calls=%fused_computation.12 | convolution fusion | flops 742653952 | bytes 5312512 | tf_op jit(solution)/shard_map/dot_general | solution.py:15
  194.3 20.6 %conditional.6 = (bf16[704,512]{1,0:T(8,128)(2,1)}) conditional(s32[]{:T(128)} %clamp.2, bf16[704,512]{1,0:T(8,128)(2,1)S(1)} %convolution_convert_fusion.4.first_ref, bf16[704,512]{1,0:T(8,128)(2,1)S(1)} %convolution_convert_fusion.4.first_ref, bf16[704,512]{1,0:T(8,128)(2,1)S(1)} %convolution_convert_fusion.4.first_ref, ...), branch_computations={%region_16.17_spmd, %region_17.18_spmd, %region_18.19_spmd, %regio... | conditional | bytes 2883632 | solution.py:28
  195.5 19.3 %collective-permute-done.42 = bf16[704,512]{1,0:T(8,128)(2,1)} collective-permute-done((bf16[704,512]{1,0:T(8,128)(2,1)S(1)}, bf16[704,512]{1,0:T(8,128)(2,1)}, u32[]{:S(2)}, u32[]{:S(2)}) %collective-permute-start.42) | collective-permute-done | bytes 720928 | tf_op jit(solution)/shard_map/cond/branch_0_fun/ppermute | solution.py:24
  215.9 3.4 %multiply_convert_fusion.3 = (bf16[352,1024]{1,0:T(8,128)(2,1)S(1)}, bf16[352,1024]{1,0:T(8,128)(2,1)S(1)}) fusion(bf16[352,1024]{1,0:T(8,128)(2,1)} %collective-permute-done.87, bf16[352,1024]{1,0:T(8,128)(2,1)} %add_convert_fusion.1, bf16[352,1024]{1,0:T(8,128)(2,1)} %collective-permute-done.75, bf16[352,1024]{1,0:T(8,128)(2,1)} %fusion.48, ...), kind=kLoop, calls=%fused_computation.69 | loop fusion | flops 7929856 | bytes 5767168 | tf_op jit(solution)/shard_map/convert_element_type | solution.py:285
  243.1 31.6 %conditional.7 = (bf16[704,512]{1,0:T(8,128)(2,1)}, bf16[704,512]{1,0:T(8,128)(2,1)}) conditional(s32[]{:T(128)} %clamp.2, (bf16[704,512]{1,0:T(8,128)(2,1)}, bf16[704,512]{1,0:T(8,128)(2,1)S(1)}) %tuple.198, (bf16[704,512]{1,0:T(8,128)(2,1)}, bf16[704,512]{1,0:T(8,128)(2,1)S(1)}) %tuple.198, ...), branch_computations={%region_23.24_spmd, %region_24.25_spmd, %region_25.26_spmd, %regio... | conditional | bytes 5767264 | solution.py:28
  245.2 17.4 %collective-permute-done.49 = bf16[704,512]{1,0:T(8,128)(2,1)} collective-permute-done((bf16[704,512]{1,0:T(8,128)(2,1)}, bf16[704,512]{1,0:T(8,128)(2,1)}, u32[]{:S(2)}, u32[]{:S(2)}) %collective-permute-start.49) | collective-permute-done | bytes 720928 | tf_op jit(solution)/shard_map/cond/branch_0_fun/ppermute | solution.py:24
  262.5 12.2 %collective-permute-done.50 = bf16[704,512]{1,0:T(8,128)(2,1)} collective-permute-done((bf16[704,512]{1,0:T(8,128)(2,1)S(1)}, bf16[704,512]{1,0:T(8,128)(2,1)}, u32[]{:S(2)}, u32[]{:S(2)}) %collective-permute-start.50) | collective-permute-done | bytes 720928 | tf_op jit(solution)/shard_map/cond/branch_0_fun/ppermute | solution.py:24
  (197 shorter events, 105.8 us)
Async XLA Ops:
  3.4 32.9 %collective-permute-start.63 = (bf16[128,1152]{1,0:T(8,128)(2,1)S(1)}, bf16[128,1152]{1,0:T(8,128)(2,1)}, u32[]{:S(2)}, u32[]{:S(2)}) collective-permute-start(bf16[128,1152]{1,0:T(8,128)(2,1)S(1)} %get-tuple-element.286), channel_id=1, source_target_pairs={{0,4},{4,0},{8,12},{12,8},{16,20},{20,16},{24,28},{28,24},{1,5},{5... | collective-permute-start | bytes 884744 | tf_op jit(solution)/shard_map/ppermute | solution.py:41
  6.4 27.9 %collective-permute-start.64 = (bf16[128,1152]{1,0:T(8,128)(2,1)S(1)}, bf16[128,1152]{1,0:T(8,128)(2,1)S(1)}, u32[]{:S(2)}, u32[]{:S(2)}) collective-permute-start(bf16[128,1152]{1,0:T(8,128)(2,1)S(1)} %get-tuple-element.286), channel_id=1, source_target_pairs={{0,8},{4,12},{8,16},{12,20},{16,24},{20,28},{24,0},{28,4},{1,9},{5... | collective-permute-start | bytes 884744 | tf_op jit(solution)/shard_map/ppermute | solution.py:40
  34.2 10.0 %collective-permute-start.66 = (bf16[128,1152]{1,0:T(8,128)(2,1)S(1)}, bf16[128,1152]{1,0:T(8,128)(2,1)S(1)}, u32[]{:S(2)}, u32[]{:S(2)}) collective-permute-start(bf16[128,1152]{1,0:T(8,128)(2,1)S(1)} %collective-permute-done.64), channel_id=1, source_target_pairs={{0,8},{4,12},{8,16},{12,20},{16,24},{20,28},{24,0},{28,4},{1,9},{5... | collective-permute-start | bytes 884744 | tf_op jit(solution)/shard_map/ppermute | solution.py:40
  77.5 19.1 %collective-permute-start = (bf16[704,512]{1,0:T(8,128)(2,1)S(1)}, bf16[704,512]{1,0:T(8,128)(2,1)}, u32[]{:S(2)}, u32[]{:S(2)}) collective-permute-start(bf16[704,512]{1,0:T(8,128)(2,1)S(1)} %get-tuple-element.163), channel_id=1, source_target_pairs={{0,4},{4,0},{8,12},{12,8},{16,20},{20,16},{24,28},{28,24},{1,5},{5... | collective-permute-start | bytes 2162696 | tf_op jit(solution)/shard_map/cond/branch_0_fun/ppermute | solution.py:24
  78.0 34.0 %collective-permute-start.1 = (bf16[704,512]{1,0:T(8,128)(2,1)S(1)}, bf16[704,512]{1,0:T(8,128)(2,1)}, u32[]{:S(2)}, u32[]{:S(2)}) collective-permute-start(bf16[704,512]{1,0:T(8,128)(2,1)S(1)} %get-tuple-element.164), channel_id=1, source_target_pairs={{0,4},{4,0},{8,12},{12,8},{16,20},{20,16},{24,28},{28,24},{1,5},{5... | collective-permute-start | bytes 2162696 | tf_op jit(solution)/shard_map/cond/branch_0_fun/ppermute | solution.py:24
  79.6 47.5 %collective-permute-start.2 = (bf16[704,512]{1,0:T(8,128)(2,1)S(1)}, bf16[704,512]{1,0:T(8,128)(2,1)}, u32[]{:S(2)}, u32[]{:S(2)}) collective-permute-start(bf16[704,512]{1,0:T(8,128)(2,1)S(1)} %get-tuple-element.165), channel_id=1, source_target_pairs={{0,4},{4,0},{8,12},{12,8},{16,20},{20,16},{24,28},{28,24},{1,5},{5... | collective-permute-start | bytes 2162696 | tf_op jit(solution)/shard_map/cond/branch_0_fun/ppermute | solution.py:24
  80.1 47.0 %collective-permute-start.3 = (bf16[256,1408]{1,0:T(8,128)(2,1)S(1)}, bf16[256,1408]{1,0:T(8,128)(2,1)}, u32[]{:S(2)}, u32[]{:S(2)}) collective-permute-start(bf16[256,1408]{1,0:T(8,128)(2,1)S(1)} %get-tuple-element.166), channel_id=1, source_target_pairs={{0,2},{1,3},{2,0},{3,1},{4,6},{5,7},{6,4},{7,5},{8,10},{9,11},{10,... | collective-permute-start | bytes 2162696 | tf_op jit(solution)/shard_map/cond/branch_0_fun/ppermute | solution.py:245
  81.6 45.5 %collective-permute-start.4 = (bf16[256,1408]{1,0:T(8,128)(2,1)S(1)}, bf16[256,1408]{1,0:T(8,128)(2,1)}, u32[]{:S(2)}, u32[]{:S(2)}) collective-permute-start(bf16[256,1408]{1,0:T(8,128)(2,1)S(1)} %get-tuple-element.167), channel_id=1, source_target_pairs={{0,2},{1,3},{2,0},{3,1},{4,6},{5,7},{6,4},{7,5},{8,10},{9,11},{10,... | collective-permute-start | bytes 2162696 | tf_op jit(solution)/shard_map/cond/branch_0_fun/ppermute | solution.py:245
  96.6 32.2 %collective-permute-start.5 = (bf16[256,1408]{1,0:T(8,128)(2,1)}, bf16[256,1408]{1,0:T(8,128)(2,1)}, u32[]{:S(2)}, u32[]{:S(2)}) collective-permute-start(bf16[256,1408]{1,0:T(8,128)(2,1)} %get-tuple-element.168), channel_id=1, source_target_pairs={{0,2},{1,3},{2,0},{3,1},{4,6},{5,7},{6,4},{7,5},{8,10},{9,11},{10,... | collective-permute-start | bytes 2162696 | tf_op jit(solution)/shard_map/cond/branch_0_fun/ppermute | solution.py:245
  136.6 10.4 %collective-permute-start.86 = (bf16[352,1024]{1,0:T(8,128)(2,1)}, bf16[352,1024]{1,0:T(8,128)(2,1)}, u32[]{:S(2)}, u32[]{:S(2)}) collective-permute-start(bf16[352,1024]{1,0:T(8,128)(2,1)} %convolution_convert_fusion.3), channel_id=1, source_target_pairs={{0,1},{1,0},{2,3},{3,2},{4,5},{5,4},{6,7},{7,6},{8,9},{9,8},{10,11... | collective-permute-start | bytes 2162696 | tf_op jit(solution)/shard_map/ppermute | solution.py:229
  138.1 19.2 %collective-permute-start.75 = (bf16[352,1024]{1,0:T(8,128)(2,1)}, bf16[352,1024]{1,0:T(8,128)(2,1)}, u32[]{:S(2)}, u32[]{:S(2)}) collective-permute-start(bf16[352,1024]{1,0:T(8,128)(2,1)} %fusion.48), channel_id=1, source_target_pairs={{0,2},{1,3},{2,0},{3,1},{4,6},{5,7},{6,4},{7,5},{8,10},{9,11},{10,... | collective-permute-start | bytes 2162696 | tf_op jit(solution)/shard_map/ppermute | solution.py:245
  141.0 31.8 %collective-permute-start.77 = (bf16[352,1024]{1,0:T(8,128)(2,1)}, bf16[352,1024]{1,0:T(8,128)(2,1)}, u32[]{:S(2)}, u32[]{:S(2)}) collective-permute-start(bf16[352,1024]{1,0:T(8,128)(2,1)} %fusion.49), channel_id=1, source_target_pairs={{0,2},{1,3},{2,0},{3,1},{4,6},{5,7},{6,4},{7,5},{8,10},{9,11},{10,... | collective-permute-start | bytes 2162696 | tf_op jit(solution)/shard_map/ppermute | solution.py:245
  145.7 30.4 %collective-permute-start.91 = (bf16[256,1408]{1,0:T(8,128)(2,1)}, bf16[256,1408]{1,0:T(8,128)(2,1)}, u32[]{:S(2)}, u32[]{:S(2)}) collective-permute-start(bf16[256,1408]{1,0:T(8,128)(2,1)} %get-tuple-element.277), channel_id=1, source_target_pairs={{0,1},{1,0},{2,3},{3,2},{4,5},{5,4},{6,7},{7,6},{8,9},{9,8},{10,11... | collective-permute-start | bytes 2162696 | tf_op jit(solution)/shard_map/ppermute | solution.py:252
  146.4 77.6 %collective-permute-start.90 = (bf16[256,1408]{1,0:T(8,128)(2,1)}, bf16[256,1408]{1,0:T(8,128)(2,1)}, u32[]{:S(2)}, u32[]{:S(2)}) collective-permute-start(bf16[256,1408]{1,0:T(8,128)(2,1)} %get-tuple-element.278), channel_id=1, source_target_pairs={{0,1},{1,0},{2,3},{3,2},{4,5},{5,4},{6,7},{7,6},{8,9},{9,8},{10,11... | collective-permute-start | bytes 2162696 | tf_op jit(solution)/shard_map/ppermute | solution.py:252
  146.9 31.8 %collective-permute-start.73 = (bf16[256,1408]{1,0:T(8,128)(2,1)}, bf16[256,1408]{1,0:T(8,128)(2,1)S(1)}, u32[]{:S(2)}, u32[]{:S(2)}) collective-permute-start(bf16[256,1408]{1,0:T(8,128)(2,1)} %get-tuple-element.279), channel_id=1, source_target_pairs={{0,1},{1,0},{2,3},{3,2},{4,5},{5,4},{6,7},{7,6},{8,9},{9,8},{10,11... | collective-permute-start | bytes 2162696 | tf_op jit(solution)/shard_map/ppermute | solution.py:252
  157.3 58.5 %collective-permute-start.87 = (bf16[352,1024]{1,0:T(8,128)(2,1)}, bf16[352,1024]{1,0:T(8,128)(2,1)}, u32[]{:S(2)}, u32[]{:S(2)}) collective-permute-start(bf16[352,1024]{1,0:T(8,128)(2,1)} %add_convert_fusion.1), channel_id=1, source_target_pairs={{0,2},{1,3},{2,0},{3,1},{4,6},{5,7},{6,4},{7,5},{8,10},{9,11},{10,... | collective-permute-start | bytes 2162696 | tf_op jit(solution)/shard_map/ppermute | solution.py:245
  189.3 25.6 %collective-permute-start.82 = (bf16[128,512]{1,0:T(8,128)(2,1)}, bf16[128,512]{1,0:T(8,128)(2,1)S(1)}, u32[]{:S(2)}, u32[]{:S(2)}) collective-permute-start(bf16[128,512]{1,0:T(8,128)(2,1)} %get-tuple-element.283), channel_id=1, source_target_pairs={{0,4},{4,0},{8,12},{12,8},{16,20},{20,16},{24,28},{28,24},{1,5},{5... | collective-permute-start | bytes 393224 | tf_op jit(solution)/shard_map/ppermute | solution.py:52
  193.4 26.5 %collective-permute-start.81 = (bf16[128,512]{1,0:T(8,128)(2,1)}, bf16[128,512]{1,0:T(8,128)(2,1)}, u32[]{:S(2)}, u32[]{:S(2)}) collective-permute-start(bf16[128,512]{1,0:T(8,128)(2,1)} %get-tuple-element.284), channel_id=1, source_target_pairs={{0,4},{4,0},{8,12},{12,8},{16,20},{20,16},{24,28},{28,24},{1,5},{5... | collective-permute-start | bytes 393224 | tf_op jit(solution)/shard_map/ppermute | solution.py:52
  194.3 20.6 %collective-permute-start.42 = (bf16[704,512]{1,0:T(8,128)(2,1)S(1)}, bf16[704,512]{1,0:T(8,128)(2,1)}, u32[]{:S(2)}, u32[]{:S(2)}) collective-permute-start(bf16[704,512]{1,0:T(8,128)(2,1)S(1)} %param.7), channel_id=1, source_target_pairs={{0,4},{4,0},{8,12},{12,8},{16,20},{20,16},{24,28},{28,24},{1,5},{5... | collective-permute-start | bytes 2162696 | tf_op jit(solution)/shard_map/cond/branch_0_fun/ppermute | solution.py:24
  219.3 21.1 %collective-permute-start.89 = (bf16[352,1024]{1,0:T(8,128)(2,1)S(1)}, bf16[352,1024]{1,0:T(8,128)(2,1)S(1)}, u32[]{:S(2)}, u32[]{:S(2)}) collective-permute-start(bf16[352,1024]{1,0:T(8,128)(2,1)S(1)} %get-tuple-element.280), channel_id=1, source_target_pairs={{0,1},{1,0},{2,3},{3,2},{4,5},{5,4},{6,7},{7,6},{8,9},{9,8},{10,11... | collective-permute-start | bytes 2162696 | tf_op jit(solution)/shard_map/ppermute | solution.py:252
  227.6 13.8 %collective-permute-start.88 = (bf16[352,1024]{1,0:T(8,128)(2,1)S(1)}, bf16[352,1024]{1,0:T(8,128)(2,1)S(1)}, u32[]{:S(2)}, u32[]{:S(2)}) collective-permute-start(bf16[352,1024]{1,0:T(8,128)(2,1)S(1)} %get-tuple-element.281), channel_id=1, source_target_pairs={{0,1},{1,0},{2,3},{3,2},{4,5},{5,4},{6,7},{7,6},{8,9},{9,8},{10,11... | collective-permute-start | bytes 2162696 | tf_op jit(solution)/shard_map/ppermute | solution.py:252
  227.6 11.2 %collective-permute-start.79 = (bf16[128,512]{1,0:T(8,128)(2,1)S(1)}, bf16[128,512]{1,0:T(8,128)(2,1)S(1)}, u32[]{:S(2)}, u32[]{:S(2)}) collective-permute-start(bf16[128,512]{1,0:T(8,128)(2,1)S(1)} %copy-done.29), channel_id=1, source_target_pairs={{0,4},{4,0},{8,12},{12,8},{16,20},{20,16},{24,28},{28,24},{1,5},{5... | collective-permute-start | bytes 393224 | tf_op jit(solution)/shard_map/ppermute | solution.py:52
  243.2 19.4 %collective-permute-start.49 = (bf16[704,512]{1,0:T(8,128)(2,1)}, bf16[704,512]{1,0:T(8,128)(2,1)}, u32[]{:S(2)}, u32[]{:S(2)}) collective-permute-start(bf16[704,512]{1,0:T(8,128)(2,1)} %get-tuple-element.205), channel_id=1, source_target_pairs={{0,4},{4,0},{8,12},{12,8},{16,20},{20,16},{24,28},{28,24},{1,5},{5... | collective-permute-start | bytes 2162696 | tf_op jit(solution)/shard_map/cond/branch_0_fun/ppermute | solution.py:24
  243.7 31.1 %collective-permute-start.50 = (bf16[704,512]{1,0:T(8,128)(2,1)S(1)}, bf16[704,512]{1,0:T(8,128)(2,1)}, u32[]{:S(2)}, u32[]{:S(2)}) collective-permute-start(bf16[704,512]{1,0:T(8,128)(2,1)S(1)} %get-tuple-element.206), channel_id=1, source_target_pairs={{0,4},{4,0},{8,12},{12,8},{16,20},{20,16},{24,28},{28,24},{1,5},{5... | collective-permute-start | bytes 2162696 | tf_op jit(solution)/shard_map/cond/branch_0_fun/ppermute | solution.py:24
  (48 other events, 213.9 us)

commit v5 on v4

--- a/solution.py
+++ b/solution.py
@@ -19,30 +19,29 @@
     return [(i, i ^ bits) for i in range(count)]
 
 
-def with_partner(count, apart, values, far=None, parts=()):
-    def run(bits, values, parts):
-        there = [lax.ppermute(v, "expert", xor_pairs(count, bits)) for v in values]
-        return there, [far(part) for part in parts]
+def with_partner(count, apart, values, use, *others):
+    def run(bits, values, *others):
+        return use([lax.ppermute(v, "expert", xor_pairs(count, bits)) for v in values], *others)
 
     branches = [functools.partial(run, bits) for bits in range(1, count)]
-    return lax.switch(apart - 1, branches, list(values), list(parts))
+    return lax.switch(apart - 1, branches, list(values), *others)
 
 
 def after(value, *others):
     return lax.optimization_barrier((value, *others))[0]
 
 
-def ring_gather(value, count, beside):
+def ring_gather(value, count):
     ring = [(i, (i + 2) % count) for i in range(count)]
     blocks = []
     for step in range(count // 2):
         if step > 0:
-            value = after(lax.ppermute(value, "expert", ring), *beside[step - 1 :: count // 2 - 1])
+            value = lax.ppermute(value, "expert", ring)
         blocks += [value, lax.ppermute(value, "expert", xor_pairs(count, 1))]
-    return jnp.concatenate(blocks, axis=0)
-
-
-def ring_scatter(partial, count, later):
+    return jnp.concatenate(blocks, axis=0), blocks[2::2]
+
+
+def ring_scatter(partial, count):
     rows = partial.shape[0] // count
     ring = [(i, (i + 2) % count) for i in range(count)]
     steps = count // 2
@@ -56,7 +55,7 @@
         own = partial[at : at + rows].astype(F32) + twins[step].astype(F32)
         if step > 0:
             own = own + lax.ppermute(total, "expert", ring).astype(F32)
-        total = own.astype(BF16) if step > 0 else after(own.astype(BF16), later)
+        total = own.astype(BF16)
     return total
 
 
@@ -69,12 +68,16 @@
     neurons = right.shape[1]
     tile = tile_of(width, 256)
 
-    def kernel(slot_ref, left_ref, right_ref, out_ref):
+    def kernel(slot_ref, left_ref, right_ref, out_ref, done_ref):
         out_ref[0] = dot(left_ref[...], right_ref[...], 0, 0).astype(BF16)
+        done_ref[...] = jnp.zeros_like(done_ref)
 
     return pl.pallas_call(
         kernel,
-        out_shape=jax.ShapeDtypeStruct((slots, width, neurons), BF16),
+        out_shape=[
+            jax.ShapeDtypeStruct((slots, width, neurons), BF16),
+            jax.ShapeDtypeStruct((8, 128), F32),
+        ],
         grid_spec=pltpu.PrefetchScalarGridSpec(
             num_scalar_prefetch=1,
             grid=(width // tile,),
@@ -82,7 +85,10 @@
                 pl.BlockSpec((rows, tile), lambda i, s: (0, i)),
                 pl.BlockSpec((rows, neurons), lambda i, s: (0, 0)),
             ],
-            out_specs=pl.BlockSpec((1, tile, neurons), lambda i, s: (s[0], i, 0)),
+            out_specs=[
+                pl.BlockSpec((1, tile, neurons), lambda i, s: (s[0], i, 0)),
+                pl.BlockSpec((8, 128), lambda i, s: (0, 0)),
+            ],
         ),
         compiler_params=pltpu.CompilerParams(vmem_limit_bytes=32 << 20),
         cost_estimate=pl.CostEstimate(
@@ -102,11 +108,11 @@
         swap = swap_ref[0] > 0
         parts = []
         for ref in (first_ref, second_ref):
-            one, two = ref[:quarter].astype(F32), ref[quarter:].astype(F32)
+            one, two = ref[:quarter], ref[quarter:]
             parts += [jnp.where(swap, two, one), jnp.where(swap, one, two)]
         whole = jnp.concatenate(parts, axis=0)
-        whole = jnp.where(keep_ref[0] > 0, whole, 0.0)
-        out_ref[0] = whole.T.astype(BF16)
+        whole = jnp.where(keep_ref[0] > 0, whole, jnp.zeros((), BF16))
+        out_ref[0] = whole.T
 
     return pl.pallas_call(
         kernel,
@@ -129,15 +135,54 @@
     )(slot.reshape(1), keep.reshape(1), swap.reshape(1), first, second, into)
 
 
-def activations(gate_sum, up_sum, back_sum):
+def hidden_units(gate_sum, up_sum):
+    return (gate_sum * jax.nn.sigmoid(gate_sum) * up_sum,)
+
+
+def hidden_gradients(gate_sum, up_sum, back_sum):
     sigma = jax.nn.sigmoid(gate_sum)
-    active = gate_sum * sigma
     slope = sigma * (1.0 + gate_sum * (1.0 - sigma))
-    return (
-        (active * up_sum).astype(BF16),
-        (back_sum * up_sum * slope).astype(BF16),
-        (back_sum * active).astype(BF16),
-    )
+    return back_sum * up_sum * slope, back_sum * (gate_sum * sigma)
+
+
+def units_and_gradients(*sums):
+    return *hidden_units(*sums[:2]), *hidden_gradients(*sums)
+
+
+def elementwise(function, count, pairs, before=()):
+    rows, cols = pairs[0][0].shape
+    tile = max(t for t in range(16, 193, 16) if rows % t == 0)
+    values = [value for pair in pairs for value in pair]
+
+    def kernel(*refs):
+        outs = refs[len(values) + len(before) :]
+
+        def strip(i, carry):
+            at = pl.ds(pl.multiple_of(i * 16, 16), 16)
+            sums = [
+                refs[2 * j][at, :].astype(F32) + refs[2 * j + 1][at, :].astype(F32)
+                for j in range(len(pairs))
+            ]
+            for ref, result in zip(outs, function(*sums)):
+                ref[at, :] = result.astype(BF16)
+            return carry
+
+        lax.fori_loop(0, tile // 16, strip, 0)
+
+    spec = pl.BlockSpec((tile, cols), lambda i: (i, 0))
+    return pl.pallas_call(
+        kernel,
+        out_shape=[jax.ShapeDtypeStruct((rows, cols), BF16)] * count,
+        grid=(rows // tile,),
+        in_specs=[spec] * len(values) + [pl.BlockSpec(memory_space=pl.ANY)] * len(before),
+        out_specs=[spec] * count,
+        compiler_params=pltpu.CompilerParams(vmem_limit_bytes=32 << 20),
+        cost_estimate=pl.CostEstimate(
+            flops=20 * rows * cols,
+            bytes_accessed=2 * rows * cols * (len(values) + count),
+            transcendentals=rows * cols,
+        ),
+    )(*values, *before)
 
 
 def shards(
@@ -188,12 +233,17 @@
     low = route - high - middle
     pieces = jnp.concatenate([high, middle, low], axis=1).astype(BF16)
     pad = -pieces.shape[1] % 128
+    payload = jnp.concatenate([tokens, cotangent, jnp.pad(pieces, ((0, 0), (0, pad)))], axis=1)
+    gathered, hops = ring_gather(payload, devices_n)
+
     order = jnp.where(am_target, jnp.arange(neurons, dtype=jnp.int32), perm)
     order = order.reshape(2, 2, half // 2)
     order = jnp.where(low_bit == 0, order, order[:, ::-1]).reshape(2, half)
     keep_order = jnp.where(am_target, order[0], order[1])
     send_order = jnp.where(am_target, order[1], order[0])
     columns = jnp.arange(neurons, dtype=jnp.int32)
+    send_order = after(send_order, *hops[:1])
+    keep_order = after(keep_order, *hops[1:2])
     keep_hot = (keep_order[:, None] == columns[None, :]).astype(BF16)
     send_hot = (send_order[:, None] == columns[None, :]).astype(BF16)
     chosen = [lax.dynamic_index_in_dim(w, merged_slot, 0, keepdims=False) for w in weights]
@@ -201,8 +251,6 @@
     sends = [dot(send_hot, w, 1, 1).astype(BF16) for w in chosen]
     keeps = [dot(keep_hot, w, 1, 1).astype(BF16) for w in chosen]
 
-    payload = jnp.concatenate([tokens, cotangent, jnp.pad(pieces, ((0, 0), (0, pad)))], axis=1)
-    gathered = ring_gather(payload, devices_n, sends + keeps)
     inputs_x = gathered[:, :width]
     inputs_c = gathered[:, width : 2 * width]
     parts = gathered[:, 2 * width : 2 * width + 3 * experts].astype(F32)
@@ -245,25 +293,25 @@
             return lax.ppermute(part, "hidden", xor_pairs(hidden_n, last_bit))
         return jnp.zeros_like(part)
 
-    def added(one, two):
-        return one.astype(F32) + two.astype(F32)
-
     def swapped(value):
         return lax.ppermute(value, "hidden", xor_pairs(hidden_n, 1))
 
     slots_half = slots // 2
     quarter = half // 2
-    apart = me ^ partner
 
     other_parts = [
         near_sum(core_sum(dot(value[:slots_half], w, 1, 0), dot(value[slots_half:], w, 1, 0)))
         for value, w in zip((other_x, other_x, other_dy), others)
     ]
 
-    arrived, other_far = with_partner(devices_n, apart, sends, far, other_parts)
-    merged = [
-        (0.5 * (k.astype(F32) + a.astype(F32))).astype(BF16) for k, a in zip(keeps, arrived)
-    ]
+    def blend(arrived, keeps, parts):
+        crossed = [far(part) for part in parts]
+        merged = [
+            (0.5 * (k.astype(F32) + a.astype(F32))).astype(BF16) for k, a in zip(keeps, arrived)
+        ]
+        return merged, crossed
+
+    merged, other_far = with_partner(devices_n, me ^ partner, sends, blend, keeps, other_parts)
     w_down = merged[2]
     merged_sums = []
     for value, w in zip((inputs_x, inputs_x, merged_dy), merged):
@@ -272,32 +320,31 @@
 
     other_h, other_dg, other_du = [
         jnp.concatenate([swapped(a), a], axis=0)
-        for a in activations(*map(added, other_parts, other_far))
+        for a in elementwise(units_and_gradients, 3, list(zip(other_parts, other_far)))
     ]
     other_y = (dot(other_h, others[2], 1, 1) * slot_p[:, None]).astype(BF16)
     other_mixed = dot(slot_hot, other_y, 0, 0)
-    other_grads = [
+    other_grads, other_done = zip(*[
         slot_matmul(other_slot, value, a, exp_local)
         for value, a in ((other_x, other_dg), (other_x, other_du), (other_dy, other_h))
-    ]
+    ])
 
     def joined(a):
-        a = a.astype(BF16)
         return jnp.concatenate([a, swapped(a)], axis=0)
 
-    gate_sum, up_sum = added(*merged_sums[0]), added(*merged_sums[1])
-    sigma = jax.nn.sigmoid(gate_sum)
-    active = gate_sum * sigma
-    inner = up_sum * sigma * (1.0 + gate_sum * (1.0 - sigma))
-    merged_h = joined(active * up_sum)
+    (merged_h,) = elementwise(
+        hidden_units, 1, merged_sums[:2], before=(other_mixed, merged_sums[2][0], *other_done)
+    )
+    merged_h = joined(merged_h)
     mixed = (other_mixed + merged_p[:, None] * dot(merged_h, w_down, 0, 0)).astype(BF16)
     down_half = dot(merged_h, merged_dy, 1, 0).astype(BF16)
-    (far_down,), _ = with_partner(devices_n, apart, [after(down_half, mixed)])
-    mixed = ring_scatter(mixed, devices_n, far_down)
-    back_sum = added(after(merged_sums[2][0], down_half), merged_sums[2][1])
-    gate_half = dot(joined(back_sum * inner), inputs_x, 1, 0).astype(BF16)
-    up_half = dot(joined(back_sum * active), inputs_x, 1, 0).astype(BF16)
-    (far_gate, far_up), _ = with_partner(devices_n, apart, [gate_half, up_half])
+    mixed = ring_scatter(mixed, devices_n)
+    merged_dg, merged_du = elementwise(hidden_gradients, 2, merged_sums)
+    gate_half = dot(joined(merged_dg), inputs_x, 1, 0).astype(BF16)
+    up_half = dot(joined(merged_du), inputs_x, 1, 0).astype(BF16)
+    far_gate, far_up, far_down = with_partner(
+        devices_n, me ^ partner, [gate_half, up_half, down_half], list
+    )
 
     keep_flag = am_target.astype(jnp.int32)
     outs = [

time: 281 us -> 258 us (0.918)
  matrix products: 50.8 us -> 31.8 us
  other arithmetic: 36.2 us -> 23.9 us
  Pallas kernels: 14.4 us -> 21.3 us
    dot_general x26, matrix products: 50.8 us -> 31.8 us  [dot(): lax.dot_general(a, b, (((ca,), (cb,)), ((), ())), preferred_element_type=...]
    ppermute x9, waiting for transfers between devices: 108 us -> 94 us  [the longest x6 84.4 us: run(): lax.ppermute(v, 'expert', xor_pairs(count, bits))]
    ppermute x6, waiting for transfers between devices: 22.9 us -> 31.1 us  [far(): return lax.ppermute(part, 'hidden', xor_pairs(hidden_n, last_bit))]
    pallas_call x3 -> x6, Pallas kernels: 6.41 us -> 13.9 us  [the longest x3 7.47 us: elementwise(): pl.pallas_call(kernel, out_shape=[jax.ShapeDtypeStruct((rows, cols), BF16...]
    convert_element_type x10 -> x8, other arithmetic: 19.7 us -> 12.7 us  [the longest x4 4.46 us: ring_scatter(): total = own.astype(BF16)]
    ppermute x4, waiting for transfers between devices: 0.01 us -> 5.72 us  [ring_scatter(): lax.ppermute(partial[at:at + rows], 'expert', xor_pairs(count, 1))]
    concatenate x3 -> x2, other arithmetic: 5.21 us -> 0.22 us  [shards(): jnp.concatenate([swapped(a), a], axis=0)]
  transfers between devices with their start and end apart: 38 -> 38, of which waited for: 14 -> 17; matrix products, arithmetic and copies ran while one was open for 26% -> 17% of each run, Pallas kernels for 3% -> 7%
where the time goes in v5:
time: 258 us; the launch traced here: 257 us
  waiting for transfers between devices  143 us (55%)
  matrix products  31.8 us (12%)
  starting transfers between devices  26.3 us (10%)
  other arithmetic  23.9 us (9%)
  Pallas kernels  21.3 us (8%)
  local copies, waits for them, and re-layouts  6.5 us (3%)
  between operations  4.55 us (2%)
    ppermute x6, waiting for transfers between devices, run(): lax.ppermute(v, 'expert', xor_pairs(count, bits))  84.4 us
    dot_general x26, matrix products, dot(): lax.dot_general(a, b, (((ca,), (cb,)), ((), ())), preferred_element_type=...  31.8 us
    ppermute x6, waiting for transfers between devices, far(): return lax.ppermute(part, 'hidden', xor_pairs(hidden_n, last_bit))  31.1 us
    ppermute x3, waiting for transfers between devices, ring_gather(): value = lax.ppermute(value, 'expert', ring)  9.57 us
    pallas_call x3, Pallas kernels, elementwise(): pl.pallas_call(kernel, out_shape=[jax.ShapeDtypeStruct((rows, cols), BF16...  7.47 us
    pallas_call x3, Pallas kernels, slot_place(): pl.pallas_call(kernel, out_shape=jax.ShapeDtypeStruct(into.shape, BF16),...  7.39 us
    ppermute x6, starting transfers between devices, far(): return lax.ppermute(part, 'hidden', xor_pairs(hidden_n, last_bit))  7.13 us
    pallas_call x3, Pallas kernels, slot_matmul(): pl.pallas_call(kernel, out_shape=[jax.ShapeDtypeStruct((slots, width, neu...  6.41 us
  transfers between devices with their start and end apart: 38, of which 17 were waited for; matrix products, arithmetic and copies ran while one was open for 17% of the time, Pallas kernels for 7%

profile of v5, /device:TPU:0, one launch (start us, length us, event | category | flops | bytes accessed | tf_op | source)
XLA Modules:
  0.0 257.4 jit_solution(18211087632415229431)
XLA Ops:
  3.4 3.0 %collective-permute-start.63 = (bf16[128,1152]{1,0:T(8,128)(2,1)S(1)}, bf16[128,1152]{1,0:T(8,128)(2,1)}, u32[]{:S(2)}, u32[]{:S(2)}) collective-permute-start(bf16[128,1152]{1,0:T(8,128)(2,1)S(1)} %get-tuple-element.377), channel_id=1, source_target_pairs={{0,4},{4,0},{8,12},{12,8},{16,20},{20,16},{24,28},{28,24},{1,5},{5... | collective-permute-start | bytes 884744 | tf_op jit(solution)/shard_map/ppermute | solution.py:40
  26.0 5.5 %collective-permute-done.66 = bf16[128,1152]{1,0:T(8,128)(2,1)S(1)} collective-permute-done((bf16[128,1152]{1,0:T(8,128)(2,1)S(1)}, bf16[128,1152]{1,0:T(8,128)(2,1)S(1)}, u32[]{:S(2)}, u32[]{:S(2)}) %collective-permute-start.66) | collective-permute-done | bytes 294944 | tf_op jit(solution)/shard_map/ppermute | solution.py:39
  36.5 4.1 %collective-permute-done.68 = bf16[128,1152]{1,0:T(8,128)(2,1)S(1)} collective-permute-done((bf16[128,1152]{1,0:T(8,128)(2,1)S(1)}, bf16[128,1152]{1,0:T(8,128)(2,1)S(1)}, u32[]{:S(2)}, u32[]{:S(2)}) %collective-permute-start.68) | collective-permute-done | bytes 294944 | tf_op jit(solution)/shard_map/ppermute | solution.py:39
  41.1 6.1 %collective-permute-done.69 = bf16[128,1152]{1,0:T(8,128)(2,1)S(1)} collective-permute-done((bf16[128,1152]{1,0:T(8,128)(2,1)S(1)}, bf16[128,1152]{1,0:T(8,128)(2,1)S(1)}, u32[]{:S(2)}, u32[]{:S(2)}) %collective-permute-start.69) | collective-permute-done | bytes 294944 | tf_op jit(solution)/shard_map/ppermute | solution.py:40
  57.3 52.4 %conditional.6 = (bf16[256,1408]{1,0:T(8,128)(2,1)}, bf16[256,1408]{1,0:T(8,128)(2,1)}, bf16[256,1408]{1,0:T(8,128)(2,1)}, f32[704,512]{1,0:T(8,128)S(1)}, f32[7...) conditional(s32[]{:T(128)} %clamp.4, ...), branch_computations={%region_8.9_spmd, %region_9.10_spmd, %region_10.11_spmd, %region_1... | conditional | flops 1081344 | bytes 26673488
  61.8 14.4 %collective-permute-done.3 = bf16[704,512]{1,0:T(8,128)(2,1)S(1)} collective-permute-done((bf16[704,512]{1,0:T(8,128)(2,1)S(1)}, bf16[704,512]{1,0:T(8,128)(2,1)S(1)}, u32[]{:S(2)}, u32[]{:S(2)}) %collective-permute-start.3) | collective-permute-done | bytes 720928 | tf_op jit(solution)/shard_map/cond/branch_0_fun/ppermute | solution.py:24
  79.0 12.6 %collective-permute-done.4 = bf16[704,512]{1,0:T(8,128)(2,1)S(1)} collective-permute-done((bf16[704,512]{1,0:T(8,128)(2,1)S(1)}, bf16[704,512]{1,0:T(8,128)(2,1)S(1)}, u32[]{:S(2)}, u32[]{:S(2)}) %collective-permute-start.4) | collective-permute-done | bytes 720928 | tf_op jit(solution)/shard_map/cond/branch_0_fun/ppermute | solution.py:24
  93.0 13.7 %collective-permute-done.5 = bf16[704,512]{1,0:T(8,128)(2,1)S(1)} collective-permute-done((bf16[704,512]{1,0:T(8,128)(2,1)S(1)}, bf16[704,512]{1,0:T(8,128)(2,1)S(1)}, u32[]{:S(2)}, u32[]{:S(2)}) %collective-permute-start.5) | collective-permute-done | bytes 720928 | tf_op jit(solution)/shard_map/cond/branch_0_fun/ppermute | solution.py:24
  109.7 4.3 %multiply_convert_fusion.2 = (bf16[704,512]{1,0:T(8,128)(2,1)S(1)}, bf16[704,512]{1,0:T(8,128)(2,1)S(1)}, bf16[704,512]{1,0:T(8,128)(2,1)S(1)}) fusion(f32[704,512]{1,0:T(8,128)} %get-tuple-element.327, f32[704,512]{1,0:T(8,128)} %get-tuple-element.360, bf16[704,512]{1,0:T(8,128)(2,1)} %get-tuple-element.328, f32[704,512]{1,0:T(8,128)} %get-tuple-element.359, ...), kind=kLoop, calls=%fused_computation.56 | loop fusion | flops 4325376 | bytes 10092544 | tf_op jit(solution)/shard_map/cond/branch_0_fun/convert_element_type | solution.py:310
  115.9 2.5 shard_map.129
  133.6 4.3 %fusion.6.refs_4_ = f32[1024,512]{1,0:T(8,128)} fusion(bf16[512,1408]{1,0:T(8,128)(2,1)} %copy-done.6, bf16[2,512,1408]{2,1,0:T(8,128)(2,1)S(1)} %copy-done, s32[]{:T(128)S(6)} %select_n.125, s32[1024]{0:T(1024)S(1)} %fusion.92, f32[512]{0:T(512)S(1)} %select_reduce_fusion), kind=kOutput, calls=%fused_computation.15 | convolution fusion | flops 1276116992 | bytes 4986884 | tf_op jit(solution)/shard_map/dot_general | solution.py:15
  137.9 3.2 %collective-permute-done.75.refs_1_ = bf16[352,1024]{1,0:T(8,128)(2,1)} collective-permute-done((bf16[352,1024]{1,0:T(8,128)(2,1)}, bf16[352,1024]{1,0:T(8,128)(2,1)}, u32[]{:S(2)}, u32[]{:S(2)}) %collective-permute-start.75) | collective-permute-done | bytes 720928 | tf_op jit(solution)/shard_map/ppermute | solution.py:293
  141.1 14.6 %collective-permute-done.77.refs_3_ = bf16[352,1024]{1,0:T(8,128)(2,1)} collective-permute-done((bf16[352,1024]{1,0:T(8,128)(2,1)}, bf16[352,1024]{1,0:T(8,128)(2,1)}, u32[]{:S(2)}, u32[]{:S(2)}) %collective-permute-start.77) | collective-permute-done | bytes 720928 | tf_op jit(solution)/shard_map/ppermute | solution.py:293
  165.1 13.4 %collective-permute-done.89.refs_5_ = bf16[352,1024]{1,0:T(8,128)(2,1)} collective-permute-done((bf16[352,1024]{1,0:T(8,128)(2,1)}, bf16[352,1024]{1,0:T(8,128)(2,1)}, u32[]{:S(2)}, u32[]{:S(2)}) %collective-permute-start.89) | collective-permute-done | bytes 720928 | tf_op jit(solution)/shard_map/ppermute | solution.py:293
  178.4 2.8 %shard_map.134 = (bf16[352,1024]{1,0:T(8,128)(2,1)S(1)}, bf16[352,1024]{1,0:T(8,128)(2,1)S(1)}) custom-call(bf16[352,1024]{1,0:T(8,128)(2,1)} %fusion.40.refs_0_, bf16[352,1024]{1,0:T(8,128)(2,1)} %collective-permute-done.75.refs_1_, bf16[352,1024]{1,0:T(8,128)(2,1)} %fusion.41.refs_2_, bf16[352,1024]{1,0:T(8,128)(2,1)} %collective-permute-done.77.refs_3_, ...), custom_call_target="tpu_custom_call" | custom-call | flops 7208960 | bytes 5767168 | tf_op jit(solution)/shard_map/pallas_call | solution.py:173
  185.9 4.2 %collective-permute-done.84 = bf16[128,512]{1,0:T(8,128)(2,1)S(1)} collective-permute-done((bf16[128,512]{1,0:T(8,128)(2,1)S(1)}, bf16[128,512]{1,0:T(8,128)(2,1)S(1)}, u32[]{:S(2)}, u32[]{:S(2)}) %collective-permute-start.84) | collective-permute-done | bytes 131104 | tf_op jit(solution)/shard_map/ppermute | solution.py:51
  195.0 4.3 %collective-permute-done.87 = bf16[128,512]{1,0:T(8,128)(2,1)S(1)} collective-permute-done((bf16[128,512]{1,0:T(8,128)(2,1)S(1)}, bf16[128,512]{1,0:T(8,128)(2,1)S(1)}, u32[]{:S(2)}, u32[]{:S(2)}) %collective-permute-start.87) | collective-permute-done | bytes 131104 | tf_op jit(solution)/shard_map/ppermute | solution.py:57
  202.2 46.3 %conditional.5 = (bf16[704,512]{1,0:T(8,128)(2,1)}, bf16[704,512]{1,0:T(8,128)(2,1)}, bf16[704,512]{1,0:T(8,128)(2,1)}) conditional(s32[]{:T(128)} %clamp.4, (bf16[704,512]{1,0:T(8,128)(2,1)S(1)}, bf16[704,512]{1,0:T(8,128)(2,1)}, bf16[704,512]{1,0:T(8,128)(2,1)S(1)}) %tuple.114, (bf16[704,512]{1,0:T(8,128)(2,1)S(1)}, ...), branch_computations={%region_16.17_spmd, %region_17.18_spmd, %region_18.19_spmd, %regio... | conditional | bytes 8650896 | solution.py:27
  204.7 16.6 %collective-permute-done.42 = bf16[704,512]{1,0:T(8,128)(2,1)} collective-permute-done((bf16[704,512]{1,0:T(8,128)(2,1)S(1)}, bf16[704,512]{1,0:T(8,128)(2,1)}, u32[]{:S(2)}, u32[]{:S(2)}) %collective-permute-start.42) | collective-permute-done | bytes 720928 | tf_op jit(solution)/shard_map/cond/branch_0_fun/ppermute | solution.py:24
  221.3 15.4 %collective-permute-done.43 = bf16[704,512]{1,0:T(8,128)(2,1)} collective-permute-done((bf16[704,512]{1,0:T(8,128)(2,1)}, bf16[704,512]{1,0:T(8,128)(2,1)}, u32[]{:S(2)}, u32[]{:S(2)}) %collective-permute-start.43) | collective-permute-done | bytes 720928 | tf_op jit(solution)/shard_map/cond/branch_0_fun/ppermute | solution.py:24
  236.8 11.6 %collective-permute-done.44 = bf16[704,512]{1,0:T(8,128)(2,1)} collective-permute-done((bf16[704,512]{1,0:T(8,128)(2,1)S(1)}, bf16[704,512]{1,0:T(8,128)(2,1)}, u32[]{:S(2)}, u32[]{:S(2)}) %collective-permute-start.44) | collective-permute-done | bytes 720928 | tf_op jit(solution)/shard_map/cond/branch_0_fun/ppermute | solution.py:24
  248.4 2.5 shard_map.137
  251.0 2.4 shard_map.135
  253.3 2.5 shard_map.136
  (182 shorter events, 88.6 us)
Async XLA Ops:
  3.4 21.5 %collective-permute-start.63 = (bf16[128,1152]{1,0:T(8,128)(2,1)S(1)}, bf16[128,1152]{1,0:T(8,128)(2,1)}, u32[]{:S(2)}, u32[]{:S(2)}) collective-permute-start(bf16[128,1152]{1,0:T(8,128)(2,1)S(1)} %get-tuple-element.377), channel_id=1, source_target_pairs={{0,4},{4,0},{8,12},{12,8},{16,20},{20,16},{24,28},{28,24},{1,5},{5... | collective-permute-start | bytes 884744 | tf_op jit(solution)/shard_map/ppermute | solution.py:40
  6.4 11.9 %collective-permute-start.64 = (bf16[128,1152]{1,0:T(8,128)(2,1)S(1)}, bf16[128,1152]{1,0:T(8,128)(2,1)S(1)}, u32[]{:S(2)}, u32[]{:S(2)}) collective-permute-start(bf16[128,1152]{1,0:T(8,128)(2,1)S(1)} %get-tuple-element.377), channel_id=1, source_target_pairs={{0,8},{4,12},{8,16},{12,20},{16,24},{20,28},{24,0},{28,4},{1,9},{5... | collective-permute-start | bytes 884744 | tf_op jit(solution)/shard_map/ppermute | solution.py:39
  21.4 10.0 %collective-permute-start.66 = (bf16[128,1152]{1,0:T(8,128)(2,1)S(1)}, bf16[128,1152]{1,0:T(8,128)(2,1)S(1)}, u32[]{:S(2)}, u32[]{:S(2)}) collective-permute-start(bf16[128,1152]{1,0:T(8,128)(2,1)S(1)} %collective-permute-done.64), channel_id=1, source_target_pairs={{0,8},{4,12},{8,16},{12,20},{16,24},{20,28},{24,0},{28,4},{1,9},{5... | collective-permute-start | bytes 884744 | tf_op jit(solution)/shard_map/ppermute | solution.py:39
  23.1 11.1 %collective-permute-start.65 = (bf16[128,1152]{1,0:T(8,128)(2,1)S(1)}, bf16[128,1152]{1,0:T(8,128)(2,1)S(1)}, u32[]{:S(2)}, u32[]{:S(2)}) collective-permute-start(bf16[128,1152]{1,0:T(8,128)(2,1)S(1)} %collective-permute-done.64), channel_id=1, source_target_pairs={{0,4},{4,0},{8,12},{12,8},{16,20},{20,16},{24,28},{28,24},{1,5},{5... | collective-permute-start | bytes 884744 | tf_op jit(solution)/shard_map/ppermute | solution.py:40
  31.5 9.1 %collective-permute-start.68 = (bf16[128,1152]{1,0:T(8,128)(2,1)S(1)}, bf16[128,1152]{1,0:T(8,128)(2,1)S(1)}, u32[]{:S(2)}, u32[]{:S(2)}) collective-permute-start(bf16[128,1152]{1,0:T(8,128)(2,1)S(1)} %collective-permute-done.66), channel_id=1, source_target_pairs={{0,8},{4,12},{8,16},{12,20},{16,24},{20,28},{24,0},{28,4},{1,9},{5... | collective-permute-start | bytes 884744 | tf_op jit(solution)/shard_map/ppermute | solution.py:39
  31.5 9.6 %collective-permute-start.67 = (bf16[128,1152]{1,0:T(8,128)(2,1)S(1)}, bf16[128,1152]{1,0:T(8,128)(2,1)S(1)}, u32[]{:S(2)}, u32[]{:S(2)}) collective-permute-start(bf16[128,1152]{1,0:T(8,128)(2,1)S(1)} %collective-permute-done.66), channel_id=1, source_target_pairs={{0,4},{4,0},{8,12},{12,8},{16,20},{20,16},{24,28},{28,24},{1,5},{5... | collective-permute-start | bytes 884744 | tf_op jit(solution)/shard_map/ppermute | solution.py:40
  57.3 18.9 %collective-permute-start.3 = (bf16[704,512]{1,0:T(8,128)(2,1)S(1)}, bf16[704,512]{1,0:T(8,128)(2,1)S(1)}, u32[]{:S(2)}, u32[]{:S(2)}) collective-permute-start(bf16[704,512]{1,0:T(8,128)(2,1)S(1)} %get-tuple-element.211), channel_id=1, source_target_pairs={{0,4},{4,0},{8,12},{12,8},{16,20},{20,16},{24,28},{28,24},{1,5},{5... | collective-permute-start | bytes 2162696 | tf_op jit(solution)/shard_map/cond/branch_0_fun/ppermute | solution.py:24
  57.8 50.2 %collective-permute-start = (bf16[256,1408]{1,0:T(8,128)(2,1)S(1)}, bf16[256,1408]{1,0:T(8,128)(2,1)}, u32[]{:S(2)}, u32[]{:S(2)}) collective-permute-start(bf16[256,1408]{1,0:T(8,128)(2,1)S(1)} %get-tuple-element.205), channel_id=1, source_target_pairs={{0,2},{1,3},{2,0},{3,1},{4,6},{5,7},{6,4},{7,5},{8,10},{9,11},{10,... | collective-permute-start | bytes 2162696 | tf_op jit(solution)/shard_map/cond/branch_0_fun/ppermute | solution.py:293
  59.3 32.4 %collective-permute-start.4 = (bf16[704,512]{1,0:T(8,128)(2,1)S(1)}, bf16[704,512]{1,0:T(8,128)(2,1)S(1)}, u32[]{:S(2)}, u32[]{:S(2)}) collective-permute-start(bf16[704,512]{1,0:T(8,128)(2,1)S(1)} %get-tuple-element.212), channel_id=1, source_target_pairs={{0,4},{4,0},{8,12},{12,8},{16,20},{20,16},{24,28},{28,24},{1,5},{5... | collective-permute-start | bytes 2162696 | tf_op jit(solution)/shard_map/cond/branch_0_fun/ppermute | solution.py:24
  60.8 45.9 %collective-permute-start.5 = (bf16[704,512]{1,0:T(8,128)(2,1)S(1)}, bf16[704,512]{1,0:T(8,128)(2,1)S(1)}, u32[]{:S(2)}, u32[]{:S(2)}) collective-permute-start(bf16[704,512]{1,0:T(8,128)(2,1)S(1)} %get-tuple-element.213), channel_id=1, source_target_pairs={{0,4},{4,0},{8,12},{12,8},{16,20},{20,16},{24,28},{28,24},{1,5},{5... | collective-permute-start | bytes 2162696 | tf_op jit(solution)/shard_map/cond/branch_0_fun/ppermute | solution.py:24
  61.3 46.7 %collective-permute-start.1 = (bf16[256,1408]{1,0:T(8,128)(2,1)S(1)}, bf16[256,1408]{1,0:T(8,128)(2,1)}, u32[]{:S(2)}, u32[]{:S(2)}) collective-permute-start(bf16[256,1408]{1,0:T(8,128)(2,1)S(1)} %get-tuple-element.206), channel_id=1, source_target_pairs={{0,2},{1,3},{2,0},{3,1},{4,6},{5,7},{6,4},{7,5},{8,10},{9,11},{10,... | collective-permute-start | bytes 2162696 | tf_op jit(solution)/shard_map/cond/branch_0_fun/ppermute | solution.py:293
  76.2 31.8 %collective-permute-start.2 = (bf16[256,1408]{1,0:T(8,128)(2,1)}, bf16[256,1408]{1,0:T(8,128)(2,1)}, u32[]{:S(2)}, u32[]{:S(2)}) collective-permute-start(bf16[256,1408]{1,0:T(8,128)(2,1)} %get-tuple-element.207), channel_id=1, source_target_pairs={{0,2},{1,3},{2,0},{3,1},{4,6},{5,7},{6,4},{7,5},{8,10},{9,11},{10,... | collective-permute-start | bytes 2162696 | tf_op jit(solution)/shard_map/cond/branch_0_fun/ppermute | solution.py:293
  119.2 12.9 %collective-permute-start.78 = (bf16[352,1024]{1,0:T(8,128)(2,1)S(1)}, bf16[352,1024]{1,0:T(8,128)(2,1)S(1)}, u32[]{:S(2)}, u32[]{:S(2)}) collective-permute-start(bf16[352,1024]{1,0:T(8,128)(2,1)S(1)} %convolution_convert_fusion.4), channel_id=1, source_target_pairs={{0,1},{1,0},{2,3},{3,2},{4,5},{5,4},{6,7},{7,6},{8,9},{9,8},{10,11... | collective-permute-start | bytes 2162696 | tf_op jit(solution)/shard_map/ppermute | solution.py:277
  121.8 19.3 %collective-permute-start.75 = (bf16[352,1024]{1,0:T(8,128)(2,1)}, bf16[352,1024]{1,0:T(8,128)(2,1)}, u32[]{:S(2)}, u32[]{:S(2)}) collective-permute-start(bf16[352,1024]{1,0:T(8,128)(2,1)} %fusion.40.refs_0_), channel_id=1, source_target_pairs={{0,2},{1,3},{2,0},{3,1},{4,6},{5,7},{6,4},{7,5},{8,10},{9,11},{10,... | collective-permute-start | bytes 2162696 | tf_op jit(solution)/shard_map/ppermute | solution.py:293
  124.7 31.0 %collective-permute-start.77 = (bf16[352,1024]{1,0:T(8,128)(2,1)}, bf16[352,1024]{1,0:T(8,128)(2,1)}, u32[]{:S(2)}, u32[]{:S(2)}) collective-permute-start(bf16[352,1024]{1,0:T(8,128)(2,1)} %fusion.41.refs_2_), channel_id=1, source_target_pairs={{0,2},{1,3},{2,0},{3,1},{4,6},{5,7},{6,4},{7,5},{8,10},{9,11},{10,... | collective-permute-start | bytes 2162696 | tf_op jit(solution)/shard_map/ppermute | solution.py:293
  159.6 18.9 %collective-permute-start.89 = (bf16[352,1024]{1,0:T(8,128)(2,1)}, bf16[352,1024]{1,0:T(8,128)(2,1)}, u32[]{:S(2)}, u32[]{:S(2)}) collective-permute-start(bf16[352,1024]{1,0:T(8,128)(2,1)} %add_convert_fusion.1.refs_5_.refs_4_), channel_id=1, source_target_pairs={{0,2},{1,3},{2,0},{3,1},{4,6},{5,7},{6,4},{7,5},{8,10},{9,11},{10,... | collective-permute-start | bytes 2162696 | tf_op jit(solution)/shard_map/ppermute | solution.py:293
  163.8 20.0 %collective-permute-start.85 = (bf16[128,512]{1,0:T(8,128)(2,1)}, bf16[128,512]{1,0:T(8,128)(2,1)S(1)}, u32[]{:S(2)}, u32[]{:S(2)}) collective-permute-start(bf16[128,512]{1,0:T(8,128)(2,1)} %get-tuple-element.374), channel_id=1, source_target_pairs={{0,4},{4,0},{8,12},{12,8},{16,20},{20,16},{24,28},{28,24},{1,5},{5... | collective-permute-start | bytes 393224 | tf_op jit(solution)/shard_map/ppermute | solution.py:51
  181.2 11.4 %collective-permute-start.90 = (bf16[352,1024]{1,0:T(8,128)(2,1)S(1)}, bf16[352,1024]{1,0:T(8,128)(2,1)S(1)}, u32[]{:S(2)}, u32[]{:S(2)}) collective-permute-start(bf16[352,1024]{1,0:T(8,128)(2,1)S(1)} %get-tuple-element.337), channel_id=1, source_target_pairs={{0,1},{1,0},{2,3},{3,2},{4,5},{5,4},{6,7},{7,6},{8,9},{9,8},{10,11... | collective-permute-start | bytes 2162696 | tf_op jit(solution)/shard_map/ppermute | solution.py:297
  181.3 19.1 %collective-permute-start.91 = (bf16[352,1024]{1,0:T(8,128)(2,1)S(1)}, bf16[352,1024]{1,0:T(8,128)(2,1)S(1)}, u32[]{:S(2)}, u32[]{:S(2)}) collective-permute-start(bf16[352,1024]{1,0:T(8,128)(2,1)S(1)} %get-tuple-element.338), channel_id=1, source_target_pairs={{0,1},{1,0},{2,3},{3,2},{4,5},{5,4},{6,7},{7,6},{8,9},{9,8},{10,11... | collective-permute-start | bytes 2162696 | tf_op jit(solution)/shard_map/ppermute | solution.py:297
  181.8 74.0 %collective-permute-start.82 = (bf16[128,512]{1,0:T(8,128)(2,1)S(1)}, bf16[128,512]{1,0:T(8,128)(2,1)S(1)}, u32[]{:S(2)}, u32[]{:S(2)}) collective-permute-start(bf16[128,512]{1,0:T(8,128)(2,1)S(1)} %get-tuple-element.373), channel_id=1, source_target_pairs={{0,4},{4,0},{8,12},{12,8},{16,20},{20,16},{24,28},{28,24},{1,5},{5... | collective-permute-start | bytes 393224 | tf_op jit(solution)/shard_map/ppermute | solution.py:51
  200.3 55.5 %collective-permute-start.88 = (bf16[128,512]{1,0:T(8,128)(2,1)S(1)}, bf16[128,512]{1,0:T(8,128)(2,1)S(1)}, u32[]{:S(2)}, u32[]{:S(2)}) collective-permute-start(bf16[128,512]{1,0:T(8,128)(2,1)S(1)} %add_convert_fusion.6), channel_id=1, source_target_pairs={{0,8},{4,12},{8,16},{12,20},{16,24},{20,28},{24,0},{28,4},{1,9},{5... | collective-permute-start | bytes 393224 | tf_op jit(solution)/shard_map/ppermute | solution.py:57
  202.2 19.2 %collective-permute-start.42 = (bf16[704,512]{1,0:T(8,128)(2,1)S(1)}, bf16[704,512]{1,0:T(8,128)(2,1)}, u32[]{:S(2)}, u32[]{:S(2)}) collective-permute-start(bf16[704,512]{1,0:T(8,128)(2,1)S(1)} %get-tuple-element.268), channel_id=1, source_target_pairs={{0,4},{4,0},{8,12},{12,8},{16,20},{20,16},{24,28},{28,24},{1,5},{5... | collective-permute-start | bytes 2162696 | tf_op jit(solution)/shard_map/cond/branch_0_fun/ppermute | solution.py:24
  202.7 34.1 %collective-permute-start.43 = (bf16[704,512]{1,0:T(8,128)(2,1)}, bf16[704,512]{1,0:T(8,128)(2,1)}, u32[]{:S(2)}, u32[]{:S(2)}) collective-permute-start(bf16[704,512]{1,0:T(8,128)(2,1)} %get-tuple-element.269), channel_id=1, source_target_pairs={{0,4},{4,0},{8,12},{12,8},{16,20},{20,16},{24,28},{28,24},{1,5},{5... | collective-permute-start | bytes 2162696 | tf_op jit(solution)/shard_map/cond/branch_0_fun/ppermute | solution.py:24
  204.2 44.2 %collective-permute-start.44 = (bf16[704,512]{1,0:T(8,128)(2,1)S(1)}, bf16[704,512]{1,0:T(8,128)(2,1)}, u32[]{:S(2)}, u32[]{:S(2)}) collective-permute-start(bf16[704,512]{1,0:T(8,128)(2,1)S(1)} %get-tuple-element.270), channel_id=1, source_target_pairs={{0,4},{4,0},{8,12},{12,8},{16,20},{20,16},{24,28},{28,24},{1,5},{5... | collective-permute-start | bytes 2162696 | tf_op jit(solution)/shard_map/cond/branch_0_fun/ppermute | solution.py:24
  (39 other events, 244.9 us)

commit v6 on v5

--- a/solution.py
+++ b/solution.py
@@ -27,8 +27,8 @@
     return lax.switch(apart - 1, branches, list(values), *others)
 
 
-def after(value, *others):
-    return lax.optimization_barrier((value, *others))[0]
+def never(value):
+    return (value[0, 0] > 1e30).astype(jnp.int32)
 
 
 def ring_gather(value, count):
@@ -38,10 +38,10 @@
         if step > 0:
             value = lax.ppermute(value, "expert", ring)
         blocks += [value, lax.ppermute(value, "expert", xor_pairs(count, 1))]
-    return jnp.concatenate(blocks, axis=0), blocks[2::2]
-
-
-def ring_scatter(partial, count):
+    return jnp.concatenate(blocks, axis=0), blocks[2::2] or blocks[:1]
+
+
+def ring_scatter(partial, count, later):
     rows = partial.shape[0] // count
     ring = [(i, (i + 2) % count) for i in range(count)]
     steps = count // 2
@@ -55,6 +55,8 @@
         own = partial[at : at + rows].astype(F32) + twins[step].astype(F32)
         if step > 0:
             own = own + lax.ppermute(total, "expert", ring).astype(F32)
+        if step == 1:
+            own = own + never(later)
         total = own.astype(BF16)
     return total
 
@@ -133,6 +135,10 @@
             flops=0, bytes_accessed=8 * half * width, transcendentals=0
         ),
     )(slot.reshape(1), keep.reshape(1), swap.reshape(1), first, second, into)
+
+
+def mean(total):
+    return (0.5 * total,)
 
 
 def hidden_units(gate_sum, up_sum):
@@ -210,6 +216,19 @@
     half = neurons // 2
     weights = (gate_weight, up_weight, down_weight)
 
+    expert_ids = jnp.arange(experts, dtype=jnp.int32)
+    route = jnp.sum(
+        jnp.where(routing[:, :, None] == expert_ids, route_weight[:, :, None], 0.0), axis=1
+    )
+    high = lax.reduce_precision(route, 8, 7)
+    middle = lax.reduce_precision(route - high, 8, 7)
+    low = route - high - middle
+    pieces = jnp.concatenate([high, middle, low], axis=1).astype(BF16)
+    pad = -pieces.shape[1] % 128
+    payload = jnp.concatenate([tokens, cotangent, jnp.pad(pieces, ((0, 0), (0, pad)))], axis=1)
+    gathered, hops = ring_gather(payload, devices_n)
+
+    merge_source = merge_source + never(hops[0])
     source_dev = merge_source // exp_local
     target_dev = merge_target // exp_local
     is_source = source_dev == me
@@ -224,26 +243,12 @@
     other_e = me * exp_local + other_slot
     perm = jnp.sum(jnp.where(mine[:, None], neuron_perm, 0), axis=0)
 
-    expert_ids = jnp.arange(experts, dtype=jnp.int32)
-    route = jnp.sum(
-        jnp.where(routing[:, :, None] == expert_ids, route_weight[:, :, None], 0.0), axis=1
-    )
-    high = lax.reduce_precision(route, 8, 7)
-    middle = lax.reduce_precision(route - high, 8, 7)
-    low = route - high - middle
-    pieces = jnp.concatenate([high, middle, low], axis=1).astype(BF16)
-    pad = -pieces.shape[1] % 128
-    payload = jnp.concatenate([tokens, cotangent, jnp.pad(pieces, ((0, 0), (0, pad)))], axis=1)
-    gathered, hops = ring_gather(payload, devices_n)
-
     order = jnp.where(am_target, jnp.arange(neurons, dtype=jnp.int32), perm)
     order = order.reshape(2, 2, half // 2)
     order = jnp.where(low_bit == 0, order, order[:, ::-1]).reshape(2, half)
     keep_order = jnp.where(am_target, order[0], order[1])
     send_order = jnp.where(am_target, order[1], order[0])
     columns = jnp.arange(neurons, dtype=jnp.int32)
-    send_order = after(send_order, *hops[:1])
-    keep_order = after(keep_order, *hops[1:2])
     keep_hot = (keep_order[:, None] == columns[None, :]).astype(BF16)
     send_hot = (send_order[:, None] == columns[None, :]).astype(BF16)
     chosen = [lax.dynamic_index_in_dim(w, merged_slot, 0, keepdims=False) for w in weights]
@@ -306,9 +311,7 @@
 
     def blend(arrived, keeps, parts):
         crossed = [far(part) for part in parts]
-        merged = [
-            (0.5 * (k.astype(F32) + a.astype(F32))).astype(BF16) for k, a in zip(keeps, arrived)
-        ]
+        merged = [elementwise(mean, 1, [pair])[0] for pair in zip(keeps, arrived)]
         return merged, crossed
 
     merged, other_far = with_partner(devices_n, me ^ partner, sends, blend, keeps, other_parts)
@@ -332,19 +335,17 @@
     def joined(a):
         return jnp.concatenate([a, swapped(a)], axis=0)
 
-    (merged_h,) = elementwise(
-        hidden_units, 1, merged_sums[:2], before=(other_mixed, merged_sums[2][0], *other_done)
+    merged_h, merged_dg, merged_du = map(
+        joined,
+        elementwise(units_and_gradients, 3, merged_sums, before=(other_mixed, *other_done)),
     )
-    merged_h = joined(merged_h)
     mixed = (other_mixed + merged_p[:, None] * dot(merged_h, w_down, 0, 0)).astype(BF16)
-    down_half = dot(merged_h, merged_dy, 1, 0).astype(BF16)
-    mixed = ring_scatter(mixed, devices_n)
-    merged_dg, merged_du = elementwise(hidden_gradients, 2, merged_sums)
-    gate_half = dot(joined(merged_dg), inputs_x, 1, 0).astype(BF16)
-    up_half = dot(joined(merged_du), inputs_x, 1, 0).astype(BF16)
-    far_gate, far_up, far_down = with_partner(
-        devices_n, me ^ partner, [gate_half, up_half, down_half], list
-    )
+    halves = [
+        dot(a, value, 1, 0).astype(BF16)
+        for a, value in ((merged_dg, inputs_x), (merged_du, inputs_x), (merged_h, merged_dy))
+    ]
+    far_halves = with_partner(devices_n, me ^ partner, halves, list)
+    mixed = ring_scatter(mixed, devices_n, far_halves[0])
 
     keep_flag = am_target.astype(jnp.int32)
     outs = [
@@ -357,7 +358,7 @@
             into,
         )
         for into, own, far in zip(
-            other_grads, (gate_half, up_half, down_half), (far_gate, far_up, far_down)
+            other_grads, halves, far_halves
         )
     ]
     return (mixed, *outs)

time: 258 us -> 271 us (1.050)
  other arithmetic: 23.9 us -> 14.8 us
  starting transfers between devices: 26.3 us -> 34.7 us
  matrix products: 31.8 us -> 37.9 us
  local copies, waits for them, and re-layouts: 6.5 us -> 12.1 us
    convert_element_type x4 -> x0, other arithmetic: 8.22 us -> none  [the longest x1 4.33 us: blend(): (0.5 * (k.astype(F32) + a.astype(F32))).astype(BF16)]
    dot_general x26, matrix products: 31.8 us -> 37.9 us  [dot(): lax.dot_general(a, b, (((ca,), (cb,)), ((), ())), preferred_element_type=...]
    ppermute x3, starting transfers between devices: 0.18 us -> 5.82 us  [ring_scatter(): own = own + lax.ppermute(total, 'expert', ring).astype(F32)]
    unnamed x57 -> x56, local copies, waits for them, and re-layouts: 3.69 us -> 8.97 us
    ppermute x3, waiting for transfers between devices: 9.57 us -> 13.4 us  [ring_gather(): value = lax.ppermute(value, 'expert', ring)]
    ppermute x4, waiting for transfers between devices: 5.72 us -> 2.37 us  [ring_scatter(): lax.ppermute(partial[at:at + rows], 'expert', xor_pairs(count, 1))]
    pallas_call x3 -> x5, Pallas kernels: 7.47 us -> 6.98 us  [elementwise(): pl.pallas_call(kernel, out_shape=[jax.ShapeDtypeStruct((rows, cols), BF16...]
  transfers between devices with their start and end apart: 38 -> 38, of which waited for: 17 -> 16; matrix products, arithmetic and copies ran while one was open for 17% -> 18% of each run, Pallas kernels for 7% -> 7%
where the time goes in v6:
time: 271 us
  waiting for transfers between devices  145 us (54%)
  matrix products  37.9 us (14%)
  starting transfers between devices  34.7 us (13%)
  Pallas kernels  20.8 us (8%)
  other arithmetic  14.8 us (5%)
  local copies, waits for them, and re-layouts  12.1 us (4%)
  between operations  5.63 us (2%)
    ppermute x6, waiting for transfers between devices, run(): lax.ppermute(v, 'expert', xor_pairs(count, bits))  85.8 us
    dot_general x26, matrix products, dot(): lax.dot_general(a, b, (((ca,), (cb,)), ((), ())), preferred_element_type=...  37.9 us
    ppermute x6, waiting for transfers between devices, far(): return lax.ppermute(part, 'hidden', xor_pairs(hidden_n, last_bit))  32.9 us
    ppermute x3, waiting for transfers between devices, ring_gather(): value = lax.ppermute(value, 'expert', ring)  13.4 us
    unnamed x56, local copies, waits for them, and re-layouts  8.97 us
    pallas_call x3, Pallas kernels, slot_place(): pl.pallas_call(kernel, out_shape=jax.ShapeDtypeStruct(into.shape, BF16),...  7.41 us
    pallas_call x5, Pallas kernels, elementwise(): pl.pallas_call(kernel, out_shape=[jax.ShapeDtypeStruct((rows, cols), BF16...  6.98 us
    ppermute x6, starting transfers between devices, far(): return lax.ppermute(part, 'hidden', xor_pairs(hidden_n, last_bit))  6.53 us
  transfers between devices with their start and end apart: 38, of which 16 were waited for; matrix products, arithmetic and copies ran while one was open for 18% of the time, Pallas kernels for 7%

profile of v6, /device:TPU:0, one launch (start us, length us, event | category | flops | bytes accessed | tf_op | source)
XLA Modules:
  0.0 271.3 jit_solution(2554930704182707880)
XLA Ops:
  3.4 3.0 %collective-permute-start.63 = (bf16[128,1152]{1,0:T(8,128)(2,1)S(1)}, bf16[128,1152]{1,0:T(8,128)(2,1)S(1)}, u32[]{:S(2)}, u32[]{:S(2)}) collective-permute-start(bf16[128,1152]{1,0:T(8,128)(2,1)S(1)} %get-tuple-element.311), channel_id=1, source_target_pairs={{0,8},{4,12},{8,16},{12,20},{16,24},{20,28},{24,0},{28,4},{1,9},{5... | collective-permute-start | bytes 884744 | tf_op jit(solution)/shard_map/ppermute | solution.py:39
  8.0 7.5 %collective-permute-done.63 = bf16[128,1152]{1,0:T(8,128)(2,1)S(1)} collective-permute-done((bf16[128,1152]{1,0:T(8,128)(2,1)S(1)}, bf16[128,1152]{1,0:T(8,128)(2,1)S(1)}, u32[]{:S(2)}, u32[]{:S(2)}) %collective-permute-start.63) | collective-permute-done | bytes 294944 | tf_op jit(solution)/shard_map/ppermute | solution.py:39
  33.1 3.5 %fusion.54 = bf16[704,512]{1,0:T(8,128)(2,1)} fusion(s32[704]{0:T(1024)S(1)} %select_n.146, bf16[2,512,1408]{2,1,0:T(8,128)(2,1)} %param.27, s32[]{:T(128)S(6)} %select_n.144), kind=kOutput, calls=%fused_computation.63 | convolution fusion | flops 1016373248 | bytes 2165508 | tf_op jit(solution)/shard_map/dot_general | solution.py:15
  41.0 2.8 %fusion.42 = bf16[704,512]{1,0:T(8,128)(2,1)S(1)} fusion(s32[704]{0:T(1024)S(1)} %select_n.143, bf16[2,512,1408]{2,1,0:T(8,128)(2,1)} %param.26, s32[]{:T(128)S(6)} %select_n.144), kind=kOutput, calls=%fused_computation.59 | convolution fusion | flops 1016373248 | bytes 2165508 | tf_op jit(solution)/shard_map/dot_general | solution.py:15
  47.9 5.9 %collective-permute-done.68 = bf16[128,1152]{1,0:T(8,128)(2,1)S(1)} collective-permute-done((bf16[128,1152]{1,0:T(8,128)(2,1)}, bf16[128,1152]{1,0:T(8,128)(2,1)S(1)}, u32[]{:S(2)}, u32[]{:S(2)}) %collective-permute-start.68) | collective-permute-done | bytes 294944 | tf_op jit(solution)/shard_map/ppermute | solution.py:39
  54.6 5.9 %collective-permute-done.69 = bf16[128,1152]{1,0:T(8,128)(2,1)S(1)} collective-permute-done((bf16[128,1152]{1,0:T(8,128)(2,1)S(1)}, bf16[128,1152]{1,0:T(8,128)(2,1)S(1)}, u32[]{:S(2)}, u32[]{:S(2)}) %collective-permute-start.69) | collective-permute-done | bytes 294944 | tf_op jit(solution)/shard_map/ppermute | solution.py:40
  72.2 51.7 %conditional.2 = (bf16[704,512]{1,0:T(8,128)(2,1)S(1)}, bf16[704,512]{1,0:T(8,128)(2,1)S(1)}, bf16[704,512]{1,0:T(8,128)(2,1)S(1)}, bf16[256,1408]{1,0:T(8,128)(...) conditional(s32[]{:T(128)} %clamp.4, ...), branch_computations={%region_8.9_spmd, %region_9.10_spmd, %region_10.11_spmd, %region_1... | conditional | flops 21626880 | bytes 23789856 | solution.py:27
  77.3 13.9 %collective-permute-done.refs_1_ = bf16[704,512]{1,0:T(8,128)(2,1)S(1)} collective-permute-done((bf16[704,512]{1,0:T(8,128)(2,1)S(1)}, bf16[704,512]{1,0:T(8,128)(2,1)S(1)}, u32[]{:S(2)}, u32[]{:S(2)}) %collective-permute-start) | collective-permute-done | bytes 720928 | tf_op jit(solution)/shard_map/cond/branch_0_fun/ppermute | solution.py:24
  93.2 13.4 %collective-permute-done.1.refs_1_ = bf16[704,512]{1,0:T(8,128)(2,1)S(1)} collective-permute-done((bf16[704,512]{1,0:T(8,128)(2,1)S(1)}, bf16[704,512]{1,0:T(8,128)(2,1)S(1)}, u32[]{:S(2)}, u32[]{:S(2)}) %collective-permute-start.1) | collective-permute-done | bytes 720928 | tf_op jit(solution)/shard_map/cond/branch_0_fun/ppermute | solution.py:24
  107.1 14.5 %collective-permute-done.2.refs_1_ = bf16[704,512]{1,0:T(8,128)(2,1)S(1)} collective-permute-done((bf16[704,512]{1,0:T(8,128)(2,1)S(1)}, bf16[704,512]{1,0:T(8,128)(2,1)S(1)}, u32[]{:S(2)}, u32[]{:S(2)}) %collective-permute-start.2) | collective-permute-done | bytes 720928 | tf_op jit(solution)/shard_map/cond/branch_0_fun/ppermute | solution.py:24
  128.0 2.7 shard_map.129
  147.1 4.3 %fusion.6.refs_6_ = f32[1024,512]{1,0:T(8,128)} fusion(bf16[512,1408]{1,0:T(8,128)(2,1)} %copy-done.4, bf16[2,512,1408]{2,1,0:T(8,128)(2,1)S(1)} %copy-done, s32[]{:T(128)S(6)} %select_n.133, s32[1024]{0:T(1024)S(1)} %fusion.92, f32[512]{0:T(512)S(1)} %select_reduce_fusion), kind=kOutput, calls=%fused_computation.15 | convolution fusion | flops 1276116992 | bytes 4986884 | tf_op jit(solution)/shard_map/dot_general | solution.py:15
  152.6 15.4 %collective-permute-done.77.refs_3_ = bf16[352,1024]{1,0:T(8,128)(2,1)} collective-permute-done((bf16[352,1024]{1,0:T(8,128)(2,1)}, bf16[352,1024]{1,0:T(8,128)(2,1)}, u32[]{:S(2)}, u32[]{:S(2)}) %collective-permute-start.77) | collective-permute-done | bytes 720928 | tf_op jit(solution)/shard_map/ppermute | solution.py:298
  168.0 14.6 %collective-permute-done.75.refs_1_ = bf16[352,1024]{1,0:T(8,128)(2,1)} collective-permute-done((bf16[352,1024]{1,0:T(8,128)(2,1)}, bf16[352,1024]{1,0:T(8,128)(2,1)}, u32[]{:S(2)}, u32[]{:S(2)}) %collective-permute-start.75) | collective-permute-done | bytes 720928 | tf_op jit(solution)/shard_map/ppermute | solution.py:298
  184.2 2.8 %shard_map.133 = (bf16[352,1024]{1,0:T(8,128)(2,1)S(1)}, bf16[352,1024]{1,0:T(8,128)(2,1)S(1)}, bf16[352,1024]{1,0:T(8,128)(2,1)S(1)}) custom-call(bf16[352,1024]{1,0:T(8,128)(2,1)} %fusion.40.refs_0_, bf16[352,1024]{1,0:T(8,128)(2,1)} %collective-permute-done.75.refs_1_, bf16[352,1024]{1,0:T(8,128)(2,1)} %fusion.41.refs_2_, ...), custom_call_target="tpu_custom_call" | custom-call | flops 7208960 | bytes 6488064 | tf_op jit(solution)/shard_map/pallas_call | solution.py:179
  201.6 47.3 %conditional.3 = (bf16[704,512]{1,0:T(8,128)(2,1)}, bf16[704,512]{1,0:T(8,128)(2,1)}, bf16[704,512]{1,0:T(8,128)(2,1)}) conditional(s32[]{:T(128)} %clamp.4, (bf16[704,512]{1,0:T(8,128)(2,1)S(1)}, bf16[704,512]{1,0:T(8,128)(2,1)}, bf16[704,512]{1,0:T(8,128)(2,1)S(1)}) %tuple.65, (bf16[704,512]{1,0:T(8,128)(2,1)S(1)}, ...), branch_computations={%region_16.17_spmd, %region_17.18_spmd, %region_18.19_spmd, %regio... | conditional | bytes 8650896 | solution.py:27
  204.9 15.9 %collective-permute-done.42 = bf16[704,512]{1,0:T(8,128)(2,1)} collective-permute-done((bf16[704,512]{1,0:T(8,128)(2,1)S(1)}, bf16[704,512]{1,0:T(8,128)(2,1)}, u32[]{:S(2)}, u32[]{:S(2)}) %collective-permute-start.42) | collective-permute-done | bytes 720928 | tf_op jit(solution)/shard_map/cond/branch_0_fun/ppermute | solution.py:24
  220.8 15.4 %collective-permute-done.43 = bf16[704,512]{1,0:T(8,128)(2,1)} collective-permute-done((bf16[704,512]{1,0:T(8,128)(2,1)}, bf16[704,512]{1,0:T(8,128)(2,1)}, u32[]{:S(2)}, u32[]{:S(2)}) %collective-permute-start.43) | collective-permute-done | bytes 720928 | tf_op jit(solution)/shard_map/cond/branch_0_fun/ppermute | solution.py:24
  236.3 12.7 %collective-permute-done.44 = bf16[704,512]{1,0:T(8,128)(2,1)} collective-permute-done((bf16[704,512]{1,0:T(8,128)(2,1)S(1)}, bf16[704,512]{1,0:T(8,128)(2,1)}, u32[]{:S(2)}, u32[]{:S(2)}) %collective-permute-start.44) | collective-permute-done | bytes 720928 | tf_op jit(solution)/shard_map/cond/branch_0_fun/ppermute | solution.py:24
  253.0 2.7 collective-permute-start.90
  256.5 3.4 %collective-permute-done.90 = bf16[128,512]{1,0:T(8,128)(2,1)S(1)} collective-permute-done((bf16[128,512]{1,0:T(8,128)(2,1)S(1)}, bf16[128,512]{1,0:T(8,128)(2,1)S(1)}, u32[]{:S(2)}, u32[]{:S(2)}) %collective-permute-start.90) | collective-permute-done | bytes 131104 | tf_op jit(solution)/shard_map/ppermute | solution.py:57
  262.3 2.5 shard_map.134
  264.8 2.5 shard_map.135
  267.3 2.4 shard_map.136
  (180 shorter events, 97.9 us)
Async XLA Ops:
  3.4 12.1 %collective-permute-start.63 = (bf16[128,1152]{1,0:T(8,128)(2,1)S(1)}, bf16[128,1152]{1,0:T(8,128)(2,1)S(1)}, u32[]{:S(2)}, u32[]{:S(2)}) collective-permute-start(bf16[128,1152]{1,0:T(8,128)(2,1)S(1)} %get-tuple-element.311), channel_id=1, source_target_pairs={{0,8},{4,12},{8,16},{12,20},{16,24},{20,28},{24,0},{28,4},{1,9},{5... | collective-permute-start | bytes 884744 | tf_op jit(solution)/shard_map/ppermute | solution.py:39
  6.4 30.2 %collective-permute-start.64 = (bf16[128,1152]{1,0:T(8,128)(2,1)S(1)}, bf16[128,1152]{1,0:T(8,128)(2,1)}, u32[]{:S(2)}, u32[]{:S(2)}) collective-permute-start(bf16[128,1152]{1,0:T(8,128)(2,1)S(1)} %get-tuple-element.311), channel_id=1, source_target_pairs={{0,4},{4,0},{8,12},{12,8},{16,20},{20,16},{24,28},{28,24},{1,5},{5... | collective-permute-start | bytes 884744 | tf_op jit(solution)/shard_map/ppermute | solution.py:40
  31.6 12.3 %collective-permute-start.66 = (bf16[128,1152]{1,0:T(8,128)(2,1)S(1)}, bf16[128,1152]{1,0:T(8,128)(2,1)}, u32[]{:S(2)}, u32[]{:S(2)}) collective-permute-start(bf16[128,1152]{1,0:T(8,128)(2,1)S(1)} %collective-permute-done.63), channel_id=1, source_target_pairs={{0,8},{4,12},{8,16},{12,20},{16,24},{20,28},{24,0},{28,4},{1,9},{5... | collective-permute-start | bytes 884744 | tf_op jit(solution)/shard_map/ppermute | solution.py:39
  31.6 14.4 %collective-permute-start.65 = (bf16[128,1152]{1,0:T(8,128)(2,1)S(1)}, bf16[128,1152]{1,0:T(8,128)(2,1)}, u32[]{:S(2)}, u32[]{:S(2)}) collective-permute-start(bf16[128,1152]{1,0:T(8,128)(2,1)S(1)} %collective-permute-done.63), channel_id=1, source_target_pairs={{0,4},{4,0},{8,12},{12,8},{16,20},{20,16},{24,28},{28,24},{1,5},{5... | collective-permute-start | bytes 884744 | tf_op jit(solution)/shard_map/ppermute | solution.py:40
  43.9 9.9 %collective-permute-start.68 = (bf16[128,1152]{1,0:T(8,128)(2,1)}, bf16[128,1152]{1,0:T(8,128)(2,1)S(1)}, u32[]{:S(2)}, u32[]{:S(2)}) collective-permute-start(bf16[128,1152]{1,0:T(8,128)(2,1)} %collective-permute-done.66), channel_id=1, source_target_pairs={{0,8},{4,12},{8,16},{12,20},{16,24},{20,28},{24,0},{28,4},{1,9},{5... | collective-permute-start | bytes 884744 | tf_op jit(solution)/shard_map/ppermute | solution.py:39
  45.4 9.1 %collective-permute-start.67 = (bf16[128,1152]{1,0:T(8,128)(2,1)}, bf16[128,1152]{1,0:T(8,128)(2,1)S(1)}, u32[]{:S(2)}, u32[]{:S(2)}) collective-permute-start(bf16[128,1152]{1,0:T(8,128)(2,1)} %collective-permute-done.66), channel_id=1, source_target_pairs={{0,4},{4,0},{8,12},{12,8},{16,20},{20,16},{24,28},{28,24},{1,5},{5... | collective-permute-start | bytes 884744 | tf_op jit(solution)/shard_map/ppermute | solution.py:40
  72.2 18.9 %collective-permute-start = (bf16[704,512]{1,0:T(8,128)(2,1)S(1)}, bf16[704,512]{1,0:T(8,128)(2,1)S(1)}, u32[]{:S(2)}, u32[]{:S(2)}) collective-permute-start(bf16[704,512]{1,0:T(8,128)(2,1)S(1)} %get-tuple-element.169), channel_id=1, source_target_pairs={{0,4},{4,0},{8,12},{12,8},{16,20},{20,16},{24,28},{28,24},{1,5},{5... | collective-permute-start | bytes 2162696 | tf_op jit(solution)/shard_map/cond/branch_0_fun/ppermute | solution.py:24
  73.2 33.4 %collective-permute-start.1 = (bf16[704,512]{1,0:T(8,128)(2,1)S(1)}, bf16[704,512]{1,0:T(8,128)(2,1)S(1)}, u32[]{:S(2)}, u32[]{:S(2)}) collective-permute-start(bf16[704,512]{1,0:T(8,128)(2,1)S(1)} %get-tuple-element.171), channel_id=1, source_target_pairs={{0,4},{4,0},{8,12},{12,8},{16,20},{20,16},{24,28},{28,24},{1,5},{5... | collective-permute-start | bytes 2162696 | tf_op jit(solution)/shard_map/cond/branch_0_fun/ppermute | solution.py:24
  74.3 47.4 %collective-permute-start.2 = (bf16[704,512]{1,0:T(8,128)(2,1)S(1)}, bf16[704,512]{1,0:T(8,128)(2,1)S(1)}, u32[]{:S(2)}, u32[]{:S(2)}) collective-permute-start(bf16[704,512]{1,0:T(8,128)(2,1)S(1)} %get-tuple-element.173), channel_id=1, source_target_pairs={{0,4},{4,0},{8,12},{12,8},{16,20},{20,16},{24,28},{28,24},{1,5},{5... | collective-permute-start | bytes 2162696 | tf_op jit(solution)/shard_map/cond/branch_0_fun/ppermute | solution.py:24
  75.3 46.9 %collective-permute-start.3 = (bf16[256,1408]{1,0:T(8,128)(2,1)S(1)}, bf16[256,1408]{1,0:T(8,128)(2,1)}, u32[]{:S(2)}, u32[]{:S(2)}) collective-permute-start(bf16[256,1408]{1,0:T(8,128)(2,1)S(1)} %get-tuple-element.174), channel_id=1, source_target_pairs={{0,2},{1,3},{2,0},{3,1},{4,6},{5,7},{6,4},{7,5},{8,10},{9,11},{10,... | collective-permute-start | bytes 2162696 | tf_op jit(solution)/shard_map/cond/branch_0_fun/ppermute | solution.py:298
  76.3 45.9 %collective-permute-start.4 = (bf16[256,1408]{1,0:T(8,128)(2,1)}, bf16[256,1408]{1,0:T(8,128)(2,1)}, u32[]{:S(2)}, u32[]{:S(2)}) collective-permute-start(bf16[256,1408]{1,0:T(8,128)(2,1)} %get-tuple-element.175), channel_id=1, source_target_pairs={{0,2},{1,3},{2,0},{3,1},{4,6},{5,7},{6,4},{7,5},{8,10},{9,11},{10,... | collective-permute-start | bytes 2162696 | tf_op jit(solution)/shard_map/cond/branch_0_fun/ppermute | solution.py:298
  91.2 32.7 %collective-permute-start.5 = (bf16[256,1408]{1,0:T(8,128)(2,1)}, bf16[256,1408]{1,0:T(8,128)(2,1)}, u32[]{:S(2)}, u32[]{:S(2)}) collective-permute-start(bf16[256,1408]{1,0:T(8,128)(2,1)} %get-tuple-element.176), channel_id=1, source_target_pairs={{0,2},{1,3},{2,0},{3,1},{4,6},{5,7},{6,4},{7,5},{8,10},{9,11},{10,... | collective-permute-start | bytes 2162696 | tf_op jit(solution)/shard_map/cond/branch_0_fun/ppermute | solution.py:298
  130.7 10.8 %collective-permute-start.73 = (bf16[256,1408]{1,0:T(8,128)(2,1)S(1)}, bf16[256,1408]{1,0:T(8,128)(2,1)S(1)}, u32[]{:S(2)}, u32[]{:S(2)}) collective-permute-start(bf16[256,1408]{1,0:T(8,128)(2,1)S(1)} %get-tuple-element.280), channel_id=1, source_target_pairs={{0,1},{1,0},{2,3},{3,2},{4,5},{5,4},{6,7},{7,6},{8,9},{9,8},{10,11... | collective-permute-start | bytes 2162696 | tf_op jit(solution)/shard_map/ppermute | solution.py:302
  131.2 10.3 %collective-permute-start.80 = (bf16[256,1408]{1,0:T(8,128)(2,1)S(1)}, bf16[256,1408]{1,0:T(8,128)(2,1)S(1)}, u32[]{:S(2)}, u32[]{:S(2)}) collective-permute-start(bf16[256,1408]{1,0:T(8,128)(2,1)S(1)} %get-tuple-element.284), channel_id=1, source_target_pairs={{0,1},{1,0},{2,3},{3,2},{4,5},{5,4},{6,7},{7,6},{8,9},{9,8},{10,11... | collective-permute-start | bytes 2162696 | tf_op jit(solution)/shard_map/ppermute | solution.py:302
  133.3 19.3 %collective-permute-start.79 = (bf16[352,1024]{1,0:T(8,128)(2,1)}, bf16[352,1024]{1,0:T(8,128)(2,1)}, u32[]{:S(2)}, u32[]{:S(2)}) collective-permute-start(bf16[352,1024]{1,0:T(8,128)(2,1)} %add_convert_fusion.1.refs_4_), channel_id=1, source_target_pairs={{0,2},{1,3},{2,0},{3,1},{4,6},{5,7},{6,4},{7,5},{8,10},{9,11},{10,... | collective-permute-start | bytes 2162696 | tf_op jit(solution)/shard_map/ppermute | solution.py:298
  135.7 32.3 %collective-permute-start.77 = (bf16[352,1024]{1,0:T(8,128)(2,1)}, bf16[352,1024]{1,0:T(8,128)(2,1)}, u32[]{:S(2)}, u32[]{:S(2)}) collective-permute-start(bf16[352,1024]{1,0:T(8,128)(2,1)} %fusion.41.refs_2_), channel_id=1, source_target_pairs={{0,2},{1,3},{2,0},{3,1},{4,6},{5,7},{6,4},{7,5},{8,10},{9,11},{10,... | collective-permute-start | bytes 2162696 | tf_op jit(solution)/shard_map/ppermute | solution.py:298
  138.2 44.4 %collective-permute-start.75 = (bf16[352,1024]{1,0:T(8,128)(2,1)}, bf16[352,1024]{1,0:T(8,128)(2,1)}, u32[]{:S(2)}, u32[]{:S(2)}) collective-permute-start(bf16[352,1024]{1,0:T(8,128)(2,1)} %fusion.40.refs_0_), channel_id=1, source_target_pairs={{0,2},{1,3},{2,0},{3,1},{4,6},{5,7},{6,4},{7,5},{8,10},{9,11},{10,... | collective-permute-start | bytes 2162696 | tf_op jit(solution)/shard_map/ppermute | solution.py:298
  187.6 12.3 %collective-permute-start.89 = (bf16[352,1024]{1,0:T(8,128)(2,1)S(1)}, bf16[352,1024]{1,0:T(8,128)(2,1)S(1)}, u32[]{:S(2)}, u32[]{:S(2)}) collective-permute-start(bf16[352,1024]{1,0:T(8,128)(2,1)S(1)} %get-tuple-element.291), channel_id=1, source_target_pairs={{0,1},{1,0},{2,3},{3,2},{4,5},{5,4},{6,7},{7,6},{8,9},{9,8},{10,11... | collective-permute-start | bytes 2162696 | tf_op jit(solution)/shard_map/ppermute | solution.py:302
  192.2 59.9 %collective-permute-start.85 = (bf16[128,512]{1,0:T(8,128)(2,1)}, bf16[128,512]{1,0:T(8,128)(2,1)S(1)}, u32[]{:S(2)}, u32[]{:S(2)}) collective-permute-start(bf16[128,512]{1,0:T(8,128)(2,1)} %get-tuple-element.308), channel_id=1, source_target_pairs={{0,4},{4,0},{8,12},{12,8},{16,20},{20,16},{24,28},{28,24},{1,5},{5... | collective-permute-start | bytes 393224 | tf_op jit(solution)/shard_map/ppermute | solution.py:51
  197.5 54.5 %collective-permute-start.87 = (bf16[128,512]{1,0:T(8,128)(2,1)S(1)}, bf16[128,512]{1,0:T(8,128)(2,1)S(1)}, u32[]{:S(2)}, u32[]{:S(2)}) collective-permute-start(bf16[128,512]{1,0:T(8,128)(2,1)S(1)} %add_convert_fusion.8), channel_id=1, source_target_pairs={{0,8},{4,12},{8,16},{12,20},{16,24},{20,28},{24,0},{28,4},{1,9},{5... | collective-permute-start | bytes 393224 | tf_op jit(solution)/shard_map/ppermute | solution.py:57
  201.6 19.2 %collective-permute-start.42 = (bf16[704,512]{1,0:T(8,128)(2,1)S(1)}, bf16[704,512]{1,0:T(8,128)(2,1)}, u32[]{:S(2)}, u32[]{:S(2)}) collective-permute-start(bf16[704,512]{1,0:T(8,128)(2,1)S(1)} %get-tuple-element.231), channel_id=1, source_target_pairs={{0,4},{4,0},{8,12},{12,8},{16,20},{20,16},{24,28},{28,24},{1,5},{5... | collective-permute-start | bytes 2162696 | tf_op jit(solution)/shard_map/cond/branch_0_fun/ppermute | solution.py:24
  202.9 33.4 %collective-permute-start.43 = (bf16[704,512]{1,0:T(8,128)(2,1)}, bf16[704,512]{1,0:T(8,128)(2,1)}, u32[]{:S(2)}, u32[]{:S(2)}) collective-permute-start(bf16[704,512]{1,0:T(8,128)(2,1)} %get-tuple-element.232), channel_id=1, source_target_pairs={{0,4},{4,0},{8,12},{12,8},{16,20},{20,16},{24,28},{28,24},{1,5},{5... | collective-permute-start | bytes 2162696 | tf_op jit(solution)/shard_map/cond/branch_0_fun/ppermute | solution.py:24
  203.7 45.3 %collective-permute-start.44 = (bf16[704,512]{1,0:T(8,128)(2,1)S(1)}, bf16[704,512]{1,0:T(8,128)(2,1)}, u32[]{:S(2)}, u32[]{:S(2)}) collective-permute-start(bf16[704,512]{1,0:T(8,128)(2,1)S(1)} %get-tuple-element.233), channel_id=1, source_target_pairs={{0,4},{4,0},{8,12},{12,8},{16,20},{20,16},{24,28},{28,24},{1,5},{5... | collective-permute-start | bytes 2162696 | tf_op jit(solution)/shard_map/cond/branch_0_fun/ppermute | solution.py:24
  255.7 14.0 %collective-permute-start.83 = (bf16[128,512]{1,0:T(8,128)(2,1)S(1)}, bf16[128,512]{1,0:T(8,128)(2,1)S(1)}, u32[]{:S(2)}, u32[]{:S(2)}) collective-permute-start(bf16[128,512]{1,0:T(8,128)(2,1)S(1)} %get-tuple-element.306), channel_id=1, source_target_pairs={{0,4},{4,0},{8,12},{12,8},{16,20},{20,16},{24,28},{28,24},{1,5},{5... | collective-permute-start | bytes 393224 | tf_op jit(solution)/shard_map/ppermute | solution.py:51
  (38 other events, 185.1 us)

commit v7 on v6

--- a/solution.py
+++ b/solution.py
@@ -25,10 +25,6 @@
 
     branches = [functools.partial(run, bits) for bits in range(1, count)]
     return lax.switch(apart - 1, branches, list(values), *others)
-
-
-def never(value):
-    return (value[0, 0] > 1e30).astype(jnp.int32)
 
 
 def ring_gather(value, count):
@@ -38,10 +34,10 @@
         if step > 0:
             value = lax.ppermute(value, "expert", ring)
         blocks += [value, lax.ppermute(value, "expert", xor_pairs(count, 1))]
-    return jnp.concatenate(blocks, axis=0), blocks[2::2] or blocks[:1]
-
-
-def ring_scatter(partial, count, later):
+    return jnp.concatenate(blocks, axis=0)
+
+
+def ring_scatter(partial, count):
     rows = partial.shape[0] // count
     ring = [(i, (i + 2) % count) for i in range(count)]
     steps = count // 2
@@ -49,16 +45,14 @@
     for step in range(steps):
         at = ((step + 1) % steps * 2 + 1) * rows
         twins.append(lax.ppermute(partial[at : at + rows], "expert", xor_pairs(count, 1)))
-    total = None
+    totals = []
     for step in range(steps):
         at = (step + 1) % steps * 2 * rows
         own = partial[at : at + rows].astype(F32) + twins[step].astype(F32)
         if step > 0:
-            own = own + lax.ppermute(total, "expert", ring).astype(F32)
-        if step == 1:
-            own = own + never(later)
-        total = own.astype(BF16)
-    return total
+            own = own + lax.ppermute(totals[-1], "expert", ring).astype(F32)
+        totals.append(own.astype(BF16))
+    return totals[-1], totals
 
 
 def tile_of(extent, most):
@@ -226,9 +220,8 @@
     pieces = jnp.concatenate([high, middle, low], axis=1).astype(BF16)
     pad = -pieces.shape[1] % 128
     payload = jnp.concatenate([tokens, cotangent, jnp.pad(pieces, ((0, 0), (0, pad)))], axis=1)
-    gathered, hops = ring_gather(payload, devices_n)
-
-    merge_source = merge_source + never(hops[0])
+    gathered = ring_gather(payload, devices_n)
+
     source_dev = merge_source // exp_local
     target_dev = merge_target // exp_local
     is_source = source_dev == me
@@ -335,17 +328,23 @@
     def joined(a):
         return jnp.concatenate([a, swapped(a)], axis=0)
 
-    merged_h, merged_dg, merged_du = map(
-        joined,
-        elementwise(units_and_gradients, 3, merged_sums, before=(other_mixed, *other_done)),
-    )
+    (merged_h,) = elementwise(
+        hidden_units,
+        1,
+        merged_sums[:2],
+        before=(other_mixed, merged_sums[2][0], *other_done),
+    )
+    merged_h = joined(merged_h)
     mixed = (other_mixed + merged_p[:, None] * dot(merged_h, w_down, 0, 0)).astype(BF16)
+    mixed, passed = ring_scatter(mixed, devices_n)
+    merged_dg, merged_du = map(
+        joined, elementwise(hidden_gradients, 2, merged_sums, before=passed[1:2])
+    )
     halves = [
         dot(a, value, 1, 0).astype(BF16)
         for a, value in ((merged_dg, inputs_x), (merged_du, inputs_x), (merged_h, merged_dy))
     ]
     far_halves = with_partner(devices_n, me ^ partner, halves, list)
-    mixed = ring_scatter(mixed, devices_n, far_halves[0])
 
     keep_flag = am_target.astype(jnp.int32)
     outs = [

time: 271 us -> 263 us (0.970)
  local copies, waits for them, and re-layouts: 12.1 us -> 5.41 us
  starting transfers between devices: 34.7 us -> 30.4 us
  waiting for transfers between devices: 145 us -> 148 us
    ppermute x6, waiting for transfers between devices: 32.9 us -> 23.2 us  [far(): return lax.ppermute(part, 'hidden', xor_pairs(hidden_n, last_bit))]
    ppermute x3, waiting for transfers between devices: 3.39 us -> 9.78 us  [ring_scatter(): own = own + lax.ppermute(totals[-1], 'expert', ring).astype(F32)]
    ppermute x3, starting transfers between devices: 5.82 us -> 0.18 us  [ring_scatter(): own = own + lax.ppermute(totals[-1], 'expert', ring).astype(F32)]
    unnamed x56 -> x63, local copies, waits for them, and re-layouts: 8.97 us -> 4.79 us
    pallas_call x5 -> x6, Pallas kernels: 6.98 us -> 9.1 us  [elementwise(): pl.pallas_call(kernel, out_shape=[jax.ShapeDtypeStruct((rows, cols), BF16...]
  transfers between devices with their start and end apart: 38 -> 38, of which waited for: 16 -> 18; matrix products, arithmetic and copies ran while one was open for 18% -> 16% of each run, Pallas kernels for 7% -> 5%
where the time goes in v7:
time: 263 us
  waiting for transfers between devices  148 us (56%)
  matrix products  37.4 us (14%)
  starting transfers between devices  30.4 us (12%)
  Pallas kernels  22.9 us (9%)
  other arithmetic  13.8 us (5%)
  local copies, waits for them, and re-layouts  5.41 us (2%)
  between operations  4.42 us (2%)
    ppermute x6, waiting for transfers between devices, run(): lax.ppermute(v, 'expert', xor_pairs(count, bits))  88.3 us
    dot_general x26, matrix products, dot(): lax.dot_general(a, b, (((ca,), (cb,)), ((), ())), preferred_element_type=...  37.4 us
    ppermute x6, waiting for transfers between devices, far(): return lax.ppermute(part, 'hidden', xor_pairs(hidden_n, last_bit))  23.2 us
    ppermute x3, waiting for transfers between devices, ring_gather(): value = lax.ppermute(value, 'expert', ring)  15.5 us
    ppermute x3, waiting for transfers between devices, ring_scatter(): own = own + lax.ppermute(totals[-1], 'expert', ring).astype(F32)  9.78 us
    pallas_call x6, Pallas kernels, elementwise(): pl.pallas_call(kernel, out_shape=[jax.ShapeDtypeStruct((rows, cols), BF16...  9.1 us
    pallas_call x3, Pallas kernels, slot_place(): pl.pallas_call(kernel, out_shape=jax.ShapeDtypeStruct(into.shape, BF16),...  7.39 us
    ppermute x6, starting transfers between devices, far(): return lax.ppermute(part, 'hidden', xor_pairs(hidden_n, last_bit))  7.05 us
  transfers between devices with their start and end apart: 38, of which 18 were waited for; matrix products, arithmetic and copies ran while one was open for 16% of the time, Pallas kernels for 5%

profile of v7, /device:TPU:0, one launch (start us, length us, event | category | flops | bytes accessed | tf_op | source)
XLA Modules:
  0.0 262.9 jit_solution(6120813964334505303)
XLA Ops:
  3.4 3.0 %collective-permute-start.63 = (bf16[128,1152]{1,0:T(8,128)(2,1)S(1)}, bf16[128,1152]{1,0:T(8,128)(2,1)}, u32[]{:S(2)}, u32[]{:S(2)}) collective-permute-start(bf16[128,1152]{1,0:T(8,128)(2,1)S(1)} %get-tuple-element.308), channel_id=1, source_target_pairs={{0,4},{4,0},{8,12},{12,8},{16,20},{20,16},{24,28},{28,24},{1,5},{5... | collective-permute-start | bytes 884744 | tf_op jit(solution)/shard_map/ppermute | solution.py:36
  16.3 3.7 %fusion.42 = bf16[704,512]{1,0:T(8,128)(2,1)} fusion(s32[704]{0:T(1024)S(1)} %select_n.143, bf16[2,512,1408]{2,1,0:T(8,128)(2,1)} %param.26, s32[]{:T(128)S(6)} %select_n.144), kind=kOutput, calls=%fused_computation.60 | convolution fusion | flops 1016373248 | bytes 2165508 | tf_op jit(solution)/shard_map/dot_general | solution.py:15
  33.0 7.1 %collective-permute-done.66 = bf16[128,1152]{1,0:T(8,128)(2,1)S(1)} collective-permute-done((bf16[128,1152]{1,0:T(8,128)(2,1)S(1)}, bf16[128,1152]{1,0:T(8,128)(2,1)S(1)}, u32[]{:S(2)}, u32[]{:S(2)}) %collective-permute-start.66) | collective-permute-done | bytes 294944 | tf_op jit(solution)/shard_map/ppermute | solution.py:35
  41.7 8.4 %collective-permute-done.68 = bf16[128,1152]{1,0:T(8,128)(2,1)S(1)} collective-permute-done((bf16[128,1152]{1,0:T(8,128)(2,1)S(1)}, bf16[128,1152]{1,0:T(8,128)(2,1)S(1)}, u32[]{:S(2)}, u32[]{:S(2)}) %collective-permute-start.68) | collective-permute-done | bytes 294944 | tf_op jit(solution)/shard_map/ppermute | solution.py:35
  50.8 6.1 %collective-permute-done.69 = bf16[128,1152]{1,0:T(8,128)(2,1)S(1)} collective-permute-done((bf16[128,1152]{1,0:T(8,128)(2,1)S(1)}, bf16[128,1152]{1,0:T(8,128)(2,1)S(1)}, u32[]{:S(2)}, u32[]{:S(2)}) %collective-permute-start.69) | collective-permute-done | bytes 294944 | tf_op jit(solution)/shard_map/ppermute | solution.py:36
  68.8 51.2 %conditional.2 = (bf16[704,512]{1,0:T(8,128)(2,1)S(1)}, bf16[704,512]{1,0:T(8,128)(2,1)S(1)}, bf16[704,512]{1,0:T(8,128)(2,1)S(1)}, bf16[256,1408]{1,0:T(8,128)(...) conditional(s32[]{:T(128)} %clamp.4, ...), branch_computations={%region_8.9_spmd, %region_9.10_spmd, %region_10.11_spmd, %region_1... | conditional | flops 21626880 | bytes 23789856 | solution.py:27
  73.4 14.4 %collective-permute-done.refs_1_ = bf16[704,512]{1,0:T(8,128)(2,1)S(1)} collective-permute-done((bf16[704,512]{1,0:T(8,128)(2,1)S(1)}, bf16[704,512]{1,0:T(8,128)(2,1)S(1)}, u32[]{:S(2)}, u32[]{:S(2)}) %collective-permute-start) | collective-permute-done | bytes 720928 | tf_op jit(solution)/shard_map/cond/branch_0_fun/ppermute | solution.py:24
  89.8 13.4 %collective-permute-done.1.refs_1_ = bf16[704,512]{1,0:T(8,128)(2,1)S(1)} collective-permute-done((bf16[704,512]{1,0:T(8,128)(2,1)S(1)}, bf16[704,512]{1,0:T(8,128)(2,1)S(1)}, u32[]{:S(2)}, u32[]{:S(2)}) %collective-permute-start.1) | collective-permute-done | bytes 720928 | tf_op jit(solution)/shard_map/cond/branch_0_fun/ppermute | solution.py:24
  103.7 14.5 %collective-permute-done.2.refs_1_ = bf16[704,512]{1,0:T(8,128)(2,1)S(1)} collective-permute-done((bf16[704,512]{1,0:T(8,128)(2,1)S(1)}, bf16[704,512]{1,0:T(8,128)(2,1)S(1)}, u32[]{:S(2)}, u32[]{:S(2)}) %collective-permute-start.2) | collective-permute-done | bytes 720928 | tf_op jit(solution)/shard_map/cond/branch_0_fun/ppermute | solution.py:24
  123.3 2.6 %shard_map.129 = (bf16[256,1408]{1,0:T(8,128)(2,1)S(1)}, bf16[256,1408]{1,0:T(8,128)(2,1)S(1)}, bf16[256,1408]{1,0:T(8,128)(2,1)S(1)}) custom-call(bf16[256,1408]{1,0:T(8,128)(2,1)S(1)} %copy-done.14, bf16[256,1408]{1,0:T(8,128)(2,1)} %get-tuple-element.276.refs_1_, bf16[256,1408]{1,0:T(8,128)(2,1)} %add_convert_fusion.3.refs_2_, ...), custom_call_target="tpu_custom_call" | custom-call | flops 7208960 | bytes 6488064 | tf_op jit(solution)/shard_map/pallas_call | solution.py:173
  141.1 4.3 %fusion.6.refs_4_ = f32[1024,512]{1,0:T(8,128)} fusion(bf16[512,1408]{1,0:T(8,128)(2,1)} %copy-done.6, bf16[2,512,1408]{2,1,0:T(8,128)(2,1)S(1)} %copy-done, s32[]{:T(128)S(6)} %select_n.133, s32[1024]{0:T(1024)S(1)} %fusion.92, f32[512]{0:T(512)S(1)} %select_reduce_fusion), kind=kOutput, calls=%fused_computation.15 | convolution fusion | flops 1276116992 | bytes 4986884 | tf_op jit(solution)/shard_map/dot_general | solution.py:15
  145.5 3.2 %collective-permute-done.75.refs_1_ = bf16[352,1024]{1,0:T(8,128)(2,1)} collective-permute-done((bf16[352,1024]{1,0:T(8,128)(2,1)}, bf16[352,1024]{1,0:T(8,128)(2,1)}, u32[]{:S(2)}, u32[]{:S(2)}) %collective-permute-start.75) | collective-permute-done | bytes 720928 | tf_op jit(solution)/shard_map/ppermute | solution.py:291
  148.6 14.6 %collective-permute-done.77.refs_3_ = bf16[352,1024]{1,0:T(8,128)(2,1)} collective-permute-done((bf16[352,1024]{1,0:T(8,128)(2,1)}, bf16[352,1024]{1,0:T(8,128)(2,1)}, u32[]{:S(2)}, u32[]{:S(2)}) %collective-permute-start.77) | collective-permute-done | bytes 720928 | tf_op jit(solution)/shard_map/ppermute | solution.py:291
  179.5 3.6 %collective-permute-done.86 = bf16[128,512]{1,0:T(8,128)(2,1)S(1)} collective-permute-done((bf16[128,512]{1,0:T(8,128)(2,1)S(1)}, bf16[128,512]{1,0:T(8,128)(2,1)S(1)}, u32[]{:S(2)}, u32[]{:S(2)}) %collective-permute-start.86) | collective-permute-done | bytes 131104 | tf_op jit(solution)/shard_map/ppermute | solution.py:53
  186.0 4.2 %collective-permute-done.89.refs_5_ = bf16[352,1024]{1,0:T(8,128)(2,1)} collective-permute-done((bf16[352,1024]{1,0:T(8,128)(2,1)}, bf16[352,1024]{1,0:T(8,128)(2,1)}, u32[]{:S(2)}, u32[]{:S(2)}) %collective-permute-start.89) | collective-permute-done | bytes 720928 | tf_op jit(solution)/shard_map/ppermute | solution.py:291
  190.2 2.8 %shard_map.134 = (bf16[352,1024]{1,0:T(8,128)(2,1)S(1)}, bf16[352,1024]{1,0:T(8,128)(2,1)S(1)}) custom-call(bf16[352,1024]{1,0:T(8,128)(2,1)} %fusion.40.refs_0_, bf16[352,1024]{1,0:T(8,128)(2,1)} %collective-permute-done.75.refs_1_, bf16[352,1024]{1,0:T(8,128)(2,1)} %fusion.41.refs_2_, bf16[352,1024]{1,0:T(8,128)(2,1)} %collective-permute-done.77.refs_3_, ...), custom_call_target="tpu_custom_call" | custom-call | flops 7208960 | bytes 5767168 | tf_op jit(solution)/shard_map/pallas_call | solution.py:173
  195.6 6.2 %collective-permute-done.88 = bf16[128,512]{1,0:T(8,128)(2,1)S(1)} collective-permute-done((bf16[128,512]{1,0:T(8,128)(2,1)S(1)}, bf16[128,512]{1,0:T(8,128)(2,1)S(1)}, u32[]{:S(2)}, u32[]{:S(2)}) %collective-permute-start.88) | collective-permute-done | bytes 131104 | tf_op jit(solution)/shard_map/ppermute | solution.py:53
  207.0 48.5 %conditional.3 = (bf16[704,512]{1,0:T(8,128)(2,1)}, bf16[704,512]{1,0:T(8,128)(2,1)}, bf16[704,512]{1,0:T(8,128)(2,1)}) conditional(s32[]{:T(128)} %clamp.4, (bf16[704,512]{1,0:T(8,128)(2,1)}, bf16[704,512]{1,0:T(8,128)(2,1)}, bf16[704,512]{1,0:T(8,128)(2,1)S(1)}) %tuple.65, (bf16[704,512]{1,0:T(8,128)(2,1)}, ...), branch_computations={%region_16.17_spmd, %region_17.18_spmd, %region_18.19_spmd, %regio... | conditional | bytes 8650896 | solution.py:27
  209.5 16.9 %collective-permute-done.42 = bf16[704,512]{1,0:T(8,128)(2,1)} collective-permute-done((bf16[704,512]{1,0:T(8,128)(2,1)}, bf16[704,512]{1,0:T(8,128)(2,1)}, u32[]{:S(2)}, u32[]{:S(2)}) %collective-permute-start.42) | collective-permute-done | bytes 720928 | tf_op jit(solution)/shard_map/cond/branch_0_fun/ppermute | solution.py:24
  226.4 15.4 %collective-permute-done.43 = bf16[704,512]{1,0:T(8,128)(2,1)} collective-permute-done((bf16[704,512]{1,0:T(8,128)(2,1)}, bf16[704,512]{1,0:T(8,128)(2,1)}, u32[]{:S(2)}, u32[]{:S(2)}) %collective-permute-start.43) | collective-permute-done | bytes 720928 | tf_op jit(solution)/shard_map/cond/branch_0_fun/ppermute | solution.py:24
  241.8 13.7 %collective-permute-done.44 = bf16[704,512]{1,0:T(8,128)(2,1)} collective-permute-done((bf16[704,512]{1,0:T(8,128)(2,1)S(1)}, bf16[704,512]{1,0:T(8,128)(2,1)}, u32[]{:S(2)}, u32[]{:S(2)}) %collective-permute-start.44) | collective-permute-done | bytes 720928 | tf_op jit(solution)/shard_map/cond/branch_0_fun/ppermute | solution.py:24
  255.5 2.5 shard_map.135
  257.9 2.5 shard_map.136
  260.5 2.4 shard_map.137
  (185 shorter events, 93.0 us)
Async XLA Ops:
  3.4 28.6 %collective-permute-start.63 = (bf16[128,1152]{1,0:T(8,128)(2,1)S(1)}, bf16[128,1152]{1,0:T(8,128)(2,1)}, u32[]{:S(2)}, u32[]{:S(2)}) collective-permute-start(bf16[128,1152]{1,0:T(8,128)(2,1)S(1)} %get-tuple-element.308), channel_id=1, source_target_pairs={{0,4},{4,0},{8,12},{12,8},{16,20},{20,16},{24,28},{28,24},{1,5},{5... | collective-permute-start | bytes 884744 | tf_op jit(solution)/shard_map/ppermute | solution.py:36
  6.4 23.5 %collective-permute-start.64 = (bf16[128,1152]{1,0:T(8,128)(2,1)S(1)}, bf16[128,1152]{1,0:T(8,128)(2,1)S(1)}, u32[]{:S(2)}, u32[]{:S(2)}) collective-permute-start(bf16[128,1152]{1,0:T(8,128)(2,1)S(1)} %get-tuple-element.308), channel_id=1, source_target_pairs={{0,8},{4,12},{8,16},{12,20},{16,24},{20,28},{24,0},{28,4},{1,9},{5... | collective-permute-start | bytes 884744 | tf_op jit(solution)/shard_map/ppermute | solution.py:35
  29.8 11.8 %collective-permute-start.65 = (bf16[128,1152]{1,0:T(8,128)(2,1)S(1)}, bf16[128,1152]{1,0:T(8,128)(2,1)S(1)}, u32[]{:S(2)}, u32[]{:S(2)}) collective-permute-start(bf16[128,1152]{1,0:T(8,128)(2,1)S(1)} %collective-permute-done.64), channel_id=1, source_target_pairs={{0,4},{4,0},{8,12},{12,8},{16,20},{20,16},{24,28},{28,24},{1,5},{5... | collective-permute-start | bytes 884744 | tf_op jit(solution)/shard_map/ppermute | solution.py:36
  30.4 9.7 %collective-permute-start.66 = (bf16[128,1152]{1,0:T(8,128)(2,1)S(1)}, bf16[128,1152]{1,0:T(8,128)(2,1)S(1)}, u32[]{:S(2)}, u32[]{:S(2)}) collective-permute-start(bf16[128,1152]{1,0:T(8,128)(2,1)S(1)} %collective-permute-done.64), channel_id=1, source_target_pairs={{0,8},{4,12},{8,16},{12,20},{16,24},{20,28},{24,0},{28,4},{1,9},{5... | collective-permute-start | bytes 884744 | tf_op jit(solution)/shard_map/ppermute | solution.py:35
  40.1 10.6 %collective-permute-start.67 = (bf16[128,1152]{1,0:T(8,128)(2,1)S(1)}, bf16[128,1152]{1,0:T(8,128)(2,1)S(1)}, u32[]{:S(2)}, u32[]{:S(2)}) collective-permute-start(bf16[128,1152]{1,0:T(8,128)(2,1)S(1)} %collective-permute-done.66), channel_id=1, source_target_pairs={{0,4},{4,0},{8,12},{12,8},{16,20},{20,16},{24,28},{28,24},{1,5},{5... | collective-permute-start | bytes 884744 | tf_op jit(solution)/shard_map/ppermute | solution.py:36
  41.7 8.5 %collective-permute-start.68 = (bf16[128,1152]{1,0:T(8,128)(2,1)S(1)}, bf16[128,1152]{1,0:T(8,128)(2,1)S(1)}, u32[]{:S(2)}, u32[]{:S(2)}) collective-permute-start(bf16[128,1152]{1,0:T(8,128)(2,1)S(1)} %collective-permute-done.66), channel_id=1, source_target_pairs={{0,8},{4,12},{8,16},{12,20},{16,24},{20,28},{24,0},{28,4},{1,9},{5... | collective-permute-start | bytes 884744 | tf_op jit(solution)/shard_map/ppermute | solution.py:35
  68.8 18.9 %collective-permute-start = (bf16[704,512]{1,0:T(8,128)(2,1)S(1)}, bf16[704,512]{1,0:T(8,128)(2,1)S(1)}, u32[]{:S(2)}, u32[]{:S(2)}) collective-permute-start(bf16[704,512]{1,0:T(8,128)(2,1)S(1)} %get-tuple-element.169), channel_id=1, source_target_pairs={{0,4},{4,0},{8,12},{12,8},{16,20},{20,16},{24,28},{28,24},{1,5},{5... | collective-permute-start | bytes 2162696 | tf_op jit(solution)/shard_map/cond/branch_0_fun/ppermute | solution.py:24
  69.3 33.9 %collective-permute-start.1 = (bf16[704,512]{1,0:T(8,128)(2,1)S(1)}, bf16[704,512]{1,0:T(8,128)(2,1)S(1)}, u32[]{:S(2)}, u32[]{:S(2)}) collective-permute-start(bf16[704,512]{1,0:T(8,128)(2,1)S(1)} %get-tuple-element.171), channel_id=1, source_target_pairs={{0,4},{4,0},{8,12},{12,8},{16,20},{20,16},{24,28},{28,24},{1,5},{5... | collective-permute-start | bytes 2162696 | tf_op jit(solution)/shard_map/cond/branch_0_fun/ppermute | solution.py:24
  70.9 47.3 %collective-permute-start.2 = (bf16[704,512]{1,0:T(8,128)(2,1)S(1)}, bf16[704,512]{1,0:T(8,128)(2,1)S(1)}, u32[]{:S(2)}, u32[]{:S(2)}) collective-permute-start(bf16[704,512]{1,0:T(8,128)(2,1)S(1)} %get-tuple-element.173), channel_id=1, source_target_pairs={{0,4},{4,0},{8,12},{12,8},{16,20},{20,16},{24,28},{28,24},{1,5},{5... | collective-permute-start | bytes 2162696 | tf_op jit(solution)/shard_map/cond/branch_0_fun/ppermute | solution.py:24
  71.3 47.4 %collective-permute-start.3 = (bf16[256,1408]{1,0:T(8,128)(2,1)S(1)}, bf16[256,1408]{1,0:T(8,128)(2,1)}, u32[]{:S(2)}, u32[]{:S(2)}) collective-permute-start(bf16[256,1408]{1,0:T(8,128)(2,1)S(1)} %get-tuple-element.174), channel_id=1, source_target_pairs={{0,2},{1,3},{2,0},{3,1},{4,6},{5,7},{6,4},{7,5},{8,10},{9,11},{10,... | collective-permute-start | bytes 2162696 | tf_op jit(solution)/shard_map/cond/branch_0_fun/ppermute | solution.py:291
  72.8 45.9 %collective-permute-start.4 = (bf16[256,1408]{1,0:T(8,128)(2,1)}, bf16[256,1408]{1,0:T(8,128)(2,1)}, u32[]{:S(2)}, u32[]{:S(2)}) collective-permute-start(bf16[256,1408]{1,0:T(8,128)(2,1)} %get-tuple-element.175), channel_id=1, source_target_pairs={{0,2},{1,3},{2,0},{3,1},{4,6},{5,7},{6,4},{7,5},{8,10},{9,11},{10,... | collective-permute-start | bytes 2162696 | tf_op jit(solution)/shard_map/cond/branch_0_fun/ppermute | solution.py:291
  87.8 32.2 %collective-permute-start.5 = (bf16[256,1408]{1,0:T(8,128)(2,1)}, bf16[256,1408]{1,0:T(8,128)(2,1)}, u32[]{:S(2)}, u32[]{:S(2)}) collective-permute-start(bf16[256,1408]{1,0:T(8,128)(2,1)} %get-tuple-element.176), channel_id=1, source_target_pairs={{0,2},{1,3},{2,0},{3,1},{4,6},{5,7},{6,4},{7,5},{8,10},{9,11},{10,... | collective-permute-start | bytes 2162696 | tf_op jit(solution)/shard_map/cond/branch_0_fun/ppermute | solution.py:291
  126.8 12.8 %collective-permute-start.78 = (bf16[352,1024]{1,0:T(8,128)(2,1)S(1)}, bf16[352,1024]{1,0:T(8,128)(2,1)S(1)}, u32[]{:S(2)}, u32[]{:S(2)}) collective-permute-start(bf16[352,1024]{1,0:T(8,128)(2,1)S(1)} %convolution_convert_fusion.4), channel_id=1, source_target_pairs={{0,1},{1,0},{2,3},{3,2},{4,5},{5,4},{6,7},{7,6},{8,9},{9,8},{10,11... | collective-permute-start | bytes 2162696 | tf_op jit(solution)/shard_map/ppermute | solution.py:275
  129.3 19.3 %collective-permute-start.75 = (bf16[352,1024]{1,0:T(8,128)(2,1)}, bf16[352,1024]{1,0:T(8,128)(2,1)}, u32[]{:S(2)}, u32[]{:S(2)}) collective-permute-start(bf16[352,1024]{1,0:T(8,128)(2,1)} %fusion.40.refs_0_), channel_id=1, source_target_pairs={{0,2},{1,3},{2,0},{3,1},{4,6},{5,7},{6,4},{7,5},{8,10},{9,11},{10,... | collective-permute-start | bytes 2162696 | tf_op jit(solution)/shard_map/ppermute | solution.py:291
  132.2 31.0 %collective-permute-start.77 = (bf16[352,1024]{1,0:T(8,128)(2,1)}, bf16[352,1024]{1,0:T(8,128)(2,1)}, u32[]{:S(2)}, u32[]{:S(2)}) collective-permute-start(bf16[352,1024]{1,0:T(8,128)(2,1)} %fusion.41.refs_2_), channel_id=1, source_target_pairs={{0,2},{1,3},{2,0},{3,1},{4,6},{5,7},{6,4},{7,5},{8,10},{9,11},{10,... | collective-permute-start | bytes 2162696 | tf_op jit(solution)/shard_map/ppermute | solution.py:291
  171.9 18.2 %collective-permute-start.89 = (bf16[352,1024]{1,0:T(8,128)(2,1)}, bf16[352,1024]{1,0:T(8,128)(2,1)}, u32[]{:S(2)}, u32[]{:S(2)}) collective-permute-start(bf16[352,1024]{1,0:T(8,128)(2,1)} %add_convert_fusion.1.refs_5_.refs_4_), channel_id=1, source_target_pairs={{0,2},{1,3},{2,0},{3,1},{4,6},{5,7},{6,4},{7,5},{8,10},{9,11},{10,... | collective-permute-start | bytes 2162696 | tf_op jit(solution)/shard_map/ppermute | solution.py:291
  176.3 17.2 %collective-permute-start.83 = (bf16[128,512]{1,0:T(8,128)(2,1)S(1)}, bf16[128,512]{1,0:T(8,128)(2,1)S(1)}, u32[]{:S(2)}, u32[]{:S(2)}) collective-permute-start(bf16[128,512]{1,0:T(8,128)(2,1)S(1)} %get-tuple-element.307), channel_id=1, source_target_pairs={{0,4},{4,0},{8,12},{12,8},{16,20},{20,16},{24,28},{28,24},{1,5},{5... | collective-permute-start | bytes 393224 | tf_op jit(solution)/shard_map/ppermute | solution.py:47
  183.1 10.3 %collective-permute-start.87 = (bf16[128,512]{1,0:T(8,128)(2,1)S(1)}, bf16[128,512]{1,0:T(8,128)(2,1)S(1)}, u32[]{:S(2)}, u32[]{:S(2)}) collective-permute-start(bf16[128,512]{1,0:T(8,128)(2,1)S(1)} %add_convert_fusion.7.refs_6_), channel_id=1, source_target_pairs={{0,8},{4,12},{8,16},{12,20},{16,24},{20,28},{24,0},{28,4},{1,9},{5... | collective-permute-start | bytes 393224 | tf_op jit(solution)/shard_map/ppermute | solution.py:53
  183.9 11.7 %collective-permute-start.82 = (bf16[128,512]{1,0:T(8,128)(2,1)S(1)}, bf16[128,512]{1,0:T(8,128)(2,1)S(1)}, u32[]{:S(2)}, u32[]{:S(2)}) collective-permute-start(bf16[128,512]{1,0:T(8,128)(2,1)S(1)} %get-tuple-element.304), channel_id=1, source_target_pairs={{0,4},{4,0},{8,12},{12,8},{16,20},{20,16},{24,28},{28,24},{1,5},{5... | collective-permute-start | bytes 393224 | tf_op jit(solution)/shard_map/ppermute | solution.py:47
  192.9 10.5 %collective-permute-start.90 = (bf16[352,1024]{1,0:T(8,128)(2,1)S(1)}, bf16[352,1024]{1,0:T(8,128)(2,1)S(1)}, u32[]{:S(2)}, u32[]{:S(2)}) collective-permute-start(bf16[352,1024]{1,0:T(8,128)(2,1)S(1)} %get-tuple-element.288), channel_id=1, source_target_pairs={{0,1},{1,0},{2,3},{3,2},{4,5},{5,4},{6,7},{7,6},{8,9},{9,8},{10,11... | collective-permute-start | bytes 2162696 | tf_op jit(solution)/shard_map/ppermute | solution.py:295
  193.0 12.2 %collective-permute-start.91 = (bf16[352,1024]{1,0:T(8,128)(2,1)S(1)}, bf16[352,1024]{1,0:T(8,128)(2,1)S(1)}, u32[]{:S(2)}, u32[]{:S(2)}) collective-permute-start(bf16[352,1024]{1,0:T(8,128)(2,1)S(1)} %get-tuple-element.289), channel_id=1, source_target_pairs={{0,1},{1,0},{2,3},{3,2},{4,5},{5,4},{6,7},{7,6},{8,9},{9,8},{10,11... | collective-permute-start | bytes 2162696 | tf_op jit(solution)/shard_map/ppermute | solution.py:295
  207.0 19.4 %collective-permute-start.42 = (bf16[704,512]{1,0:T(8,128)(2,1)}, bf16[704,512]{1,0:T(8,128)(2,1)}, u32[]{:S(2)}, u32[]{:S(2)}) collective-permute-start(bf16[704,512]{1,0:T(8,128)(2,1)} %get-tuple-element.231), channel_id=1, source_target_pairs={{0,4},{4,0},{8,12},{12,8},{16,20},{20,16},{24,28},{28,24},{1,5},{5... | collective-permute-start | bytes 2162696 | tf_op jit(solution)/shard_map/cond/branch_0_fun/ppermute | solution.py:24
  207.5 34.3 %collective-permute-start.43 = (bf16[704,512]{1,0:T(8,128)(2,1)}, bf16[704,512]{1,0:T(8,128)(2,1)}, u32[]{:S(2)}, u32[]{:S(2)}) collective-permute-start(bf16[704,512]{1,0:T(8,128)(2,1)} %get-tuple-element.232), channel_id=1, source_target_pairs={{0,4},{4,0},{8,12},{12,8},{16,20},{20,16},{24,28},{28,24},{1,5},{5... | collective-permute-start | bytes 2162696 | tf_op jit(solution)/shard_map/cond/branch_0_fun/ppermute | solution.py:24
  209.0 46.5 %collective-permute-start.44 = (bf16[704,512]{1,0:T(8,128)(2,1)S(1)}, bf16[704,512]{1,0:T(8,128)(2,1)}, u32[]{:S(2)}, u32[]{:S(2)}) collective-permute-start(bf16[704,512]{1,0:T(8,128)(2,1)S(1)} %get-tuple-element.233), channel_id=1, source_target_pairs={{0,4},{4,0},{8,12},{12,8},{16,20},{20,16},{24,28},{28,24},{1,5},{5... | collective-permute-start | bytes 2162696 | tf_op jit(solution)/shard_map/cond/branch_0_fun/ppermute | solution.py:24
  (42 other events, 238.2 us)

commit v8 on v7

--- a/solution.py
+++ b/solution.py
@@ -25,6 +25,10 @@
 
     branches = [functools.partial(run, bits) for bits in range(1, count)]
     return lax.switch(apart - 1, branches, list(values), *others)
+
+
+def never(value):
+    return (value[0, 0] > 1e30).astype(jnp.int32)
 
 
 def ring_gather(value, count):
@@ -34,7 +38,7 @@
         if step > 0:
             value = lax.ppermute(value, "expert", ring)
         blocks += [value, lax.ppermute(value, "expert", xor_pairs(count, 1))]
-    return jnp.concatenate(blocks, axis=0)
+    return jnp.concatenate(blocks, axis=0), blocks[3::2] or blocks[1:]
 
 
 def ring_scatter(partial, count):
@@ -45,18 +49,55 @@
     for step in range(steps):
         at = ((step + 1) % steps * 2 + 1) * rows
         twins.append(lax.ppermute(partial[at : at + rows], "expert", xor_pairs(count, 1)))
-    totals = []
+    terms, first = [], None
     for step in range(steps):
+        if step > 0:
+            total = sum(term.astype(F32) for term in terms).astype(BF16)
+            first = total if first is None else first
+            terms = [lax.ppermute(total, "expert", ring)]
+        else:
+            terms = []
         at = (step + 1) % steps * 2 * rows
-        own = partial[at : at + rows].astype(F32) + twins[step].astype(F32)
-        if step > 0:
-            own = own + lax.ppermute(totals[-1], "expert", ring).astype(F32)
-        totals.append(own.astype(BF16))
-    return totals[-1], totals
+        terms += [partial[at : at + rows], twins[step]]
+    return terms, first
 
 
 def tile_of(extent, most):
     return max(t for t in range(128, most + 1, 128) if extent % t == 0)
+
+
+def slot_select(slot, send_order, keep_order, weight, before):
+    slots, width, neurons = weight.shape
+    half = send_order.shape[0]
+    tile = max(t for t in range(16, 193, 16) if half % t == 0)
+
+    def kernel(slot_ref, send_ref, keep_ref, weight_ref, before_ref, sent_ref, kept_ref):
+        columns = lax.broadcasted_iota(jnp.int32, (tile, neurons), 1)
+        for order_ref, out_ref in ((send_ref, sent_ref), (keep_ref, kept_ref)):
+            hot = jnp.where(order_ref[...] == columns, 1.0, 0.0).astype(BF16)
+            out_ref[...] = dot(hot, weight_ref[0], 1, 1).astype(BF16)
+
+    return pl.pallas_call(
+        kernel,
+        out_shape=[jax.ShapeDtypeStruct((half, width), BF16)] * 2,
+        grid_spec=pltpu.PrefetchScalarGridSpec(
+            num_scalar_prefetch=1,
+            grid=(half // tile,),
+            in_specs=[
+                pl.BlockSpec((tile, 1), lambda i, s: (i, 0)),
+                pl.BlockSpec((tile, 1), lambda i, s: (i, 0)),
+                pl.BlockSpec((1, width, neurons), lambda i, s: (s[0], 0, 0)),
+                pl.BlockSpec(memory_space=pl.ANY),
+            ],
+            out_specs=[pl.BlockSpec((tile, width), lambda i, s: (i, 0))] * 2,
+        ),
+        compiler_params=pltpu.CompilerParams(vmem_limit_bytes=32 << 20),
+        cost_estimate=pl.CostEstimate(
+            flops=4 * half * width * neurons,
+            bytes_accessed=2 * (width * neurons + 2 * half * width),
+            transcendentals=0,
+        ),
+    )(slot.reshape(1), send_order[:, None], keep_order[:, None], weight, before)
 
 
 def slot_matmul(slot, left, right, slots):
@@ -220,7 +261,7 @@
     pieces = jnp.concatenate([high, middle, low], axis=1).astype(BF16)
     pad = -pieces.shape[1] % 128
     payload = jnp.concatenate([tokens, cotangent, jnp.pad(pieces, ((0, 0), (0, pad)))], axis=1)
-    gathered = ring_gather(payload, devices_n)
+    gathered, twins = ring_gather(payload, devices_n)
 
     source_dev = merge_source // exp_local
     target_dev = merge_target // exp_local
@@ -241,13 +282,11 @@
     order = jnp.where(low_bit == 0, order, order[:, ::-1]).reshape(2, half)
     keep_order = jnp.where(am_target, order[0], order[1])
     send_order = jnp.where(am_target, order[1], order[0])
-    columns = jnp.arange(neurons, dtype=jnp.int32)
-    keep_hot = (keep_order[:, None] == columns[None, :]).astype(BF16)
-    send_hot = (send_order[:, None] == columns[None, :]).astype(BF16)
-    chosen = [lax.dynamic_index_in_dim(w, merged_slot, 0, keepdims=False) for w in weights]
+    sends, keeps = zip(*[
+        slot_select(merged_slot, send_order, keep_order, w, twins[min(i, len(twins) - 1)])
+        for i, w in enumerate(weights)
+    ])
     others = [lax.dynamic_index_in_dim(w, other_slot, 0, keepdims=False) for w in weights]
-    sends = [dot(send_hot, w, 1, 1).astype(BF16) for w in chosen]
-    keeps = [dot(keep_hot, w, 1, 1).astype(BF16) for w in chosen]
 
     inputs_x = gathered[:, :width]
     inputs_c = gathered[:, width : 2 * width]
@@ -336,15 +375,18 @@
     )
     merged_h = joined(merged_h)
     mixed = (other_mixed + merged_p[:, None] * dot(merged_h, w_down, 0, 0)).astype(BF16)
-    mixed, passed = ring_scatter(mixed, devices_n)
+    mixed_terms, first_sum = ring_scatter(mixed, devices_n)
     merged_dg, merged_du = map(
-        joined, elementwise(hidden_gradients, 2, merged_sums, before=passed[1:2])
+        joined, elementwise(hidden_gradients, 2, merged_sums, before=(first_sum,))
     )
     halves = [
         dot(a, value, 1, 0).astype(BF16)
         for a, value in ((merged_dg, inputs_x), (merged_du, inputs_x), (merged_h, merged_dy))
     ]
     far_halves = with_partner(devices_n, me ^ partner, halves, list)
+
+    mixed = sum((t.astype(F32) for t in mixed_terms), never(far_halves[0]).astype(F32))
+    mixed = mixed.astype(BF16)
 
     keep_flag = am_target.astype(jnp.int32)
     outs = [

time: 263 us -> 248 us (0.943)
  waiting for transfers between devices: 148 us -> 129 us
  matrix products: 37.4 us -> 20.9 us
  Pallas kernels: 22.9 us -> 36.4 us
  local copies, waits for them, and re-layouts: 5.41 us -> 13.6 us
    dot_general x26 -> x20, matrix products: 37.4 us -> 20.9 us  [dot(): lax.dot_general(a, b, (((ca,), (cb,)), ((), ())), preferred_element_type=...]
    pallas_call x0 -> x3, Pallas kernels: none -> 14 us  [slot_select(): pl.pallas_call(kernel, out_shape=[jax.ShapeDtypeStruct((half, width), BF1...]
    ppermute x3, waiting for transfers between devices: 15.5 us -> 7 us  [ring_gather(): value = lax.ppermute(value, 'expert', ring)]
    unnamed x63 -> x53, local copies, waits for them, and re-layouts: 4.79 us -> 10 us
    ppermute x4, waiting for transfers between devices: 6.15 us -> 1.43 us  [ring_gather(): blocks += [value, lax.ppermute(value, 'expert', xor_pairs(count, 1))]]
    ppermute x3, waiting for transfers between devices: 9.78 us -> 6.24 us  [ring_scatter(): terms = [lax.ppermute(total, 'expert', ring)]]
  transfers between devices with their start and end apart: 38 -> 38, of which waited for: 18 -> 16; matrix products, arithmetic and copies ran while one was open for 16% -> 13% of each run, Pallas kernels for 5% -> 14%
where the time goes in v8:
time: 248 us
  waiting for transfers between devices  129 us (52%)
  Pallas kernels  36.4 us (15%)
  starting transfers between devices  29.3 us (12%)
  matrix products  20.9 us (8%)
  local copies, waits for them, and re-layouts  13.6 us (5%)
  other arithmetic  12.9 us (5%)
  between operations  5.08 us (2%)
    ppermute x6, waiting for transfers between devices, run(): lax.ppermute(v, 'expert', xor_pairs(count, bits))  86.5 us
    ppermute x6, waiting for transfers between devices, far(): return lax.ppermute(part, 'hidden', xor_pairs(hidden_n, last_bit))  23.2 us
    dot_general x20, matrix products, dot(): lax.dot_general(a, b, (((ca,), (cb,)), ((), ())), preferred_element_type=...  20.9 us
    pallas_call x3, Pallas kernels, slot_select(): pl.pallas_call(kernel, out_shape=[jax.ShapeDtypeStruct((half, width), BF1...  14 us
    unnamed x53, local copies, waits for them, and re-layouts  10 us
    pallas_call x6, Pallas kernels, elementwise(): pl.pallas_call(kernel, out_shape=[jax.ShapeDtypeStruct((rows, cols), BF16...  8.77 us
    pallas_call x3, Pallas kernels, slot_place(): pl.pallas_call(kernel, out_shape=jax.ShapeDtypeStruct(into.shape, BF16),...  7.16 us
    ppermute x6, starting transfers between devices, far(): return lax.ppermute(part, 'hidden', xor_pairs(hidden_n, last_bit))  7.08 us
  transfers between devices with their start and end apart: 38, of which 16 were waited for; matrix products, arithmetic and copies ran while one was open for 13% of the time, Pallas kernels for 14%

profile of v8, /device:TPU:0, one launch (start us, length us, event | category | flops | bytes accessed | tf_op | source)
XLA Modules:
  0.0 247.6 jit_solution(16504402945882977323)
XLA Ops:
  3.5 3.0 %collective-permute-start.69 = (bf16[128,1152]{1,0:T(8,128)(2,1)}, bf16[128,1152]{1,0:T(8,128)(2,1)}, u32[]{:S(2)}, u32[]{:S(2)}) collective-permute-start(bf16[128,1152]{1,0:T(8,128)(2,1)} %get-tuple-element.320), channel_id=1, source_target_pairs={{0,4},{4,0},{8,12},{12,8},{16,20},{20,16},{24,28},{28,24},{1,5},{5... | collective-permute-start | bytes 884744 | tf_op jit(solution)/shard_map/ppermute | solution.py:40
  25.1 4.9 %collective-permute-done.65 = bf16[128,1152]{1,0:T(8,128)(2,1)S(1)} collective-permute-done((bf16[128,1152]{1,0:T(8,128)(2,1)}, bf16[128,1152]{1,0:T(8,128)(2,1)S(1)}, u32[]{:S(2)}, u32[]{:S(2)}) %collective-permute-start.65) | collective-permute-done | bytes 294944 | tf_op jit(solution)/shard_map/ppermute | solution.py:39
  33.3 4.7 %shard_map.129 = (bf16[704,512]{1,0:T(8,128)(2,1)S(1)}, bf16[704,512]{1,0:T(8,128)(2,1)S(1)}) custom-call(s32[1]{0:T(128)} %bitcast.slot_ref, s32[704,1]{1,0:T(8,128)S(1)} %select_n.149.send_ref, s32[704,1]{1,0:T(8,128)S(1)} %copy-done.10, bf16[2,512,1408]{2,1,0:T(8,128)(2,1)S(1)} %copy-done, bf16[128,1152]{1,0:T(8,128)(2,1)S(1)} %collective-permute-done.64.before_ref), custom_call_target="tpu_custom_call" | custom-call | flops 2030043136 | bytes 2883584 | tf_op jit(solution)/shard_map/pallas_call | solution.py:80
  40.7 4.7 %shard_map.130 = (bf16[704,512]{1,0:T(8,128)(2,1)S(1)}, bf16[704,512]{1,0:T(8,128)(2,1)S(1)}) custom-call(s32[1]{0:T(128)} %bitcast.slot_ref, s32[704,1]{1,0:T(8,128)S(1)} %select_n.149.send_ref, s32[704,1]{1,0:T(8,128)S(1)} %copy-done.10, bf16[2,512,1408]{2,1,0:T(8,128)(2,1)S(1)} %copy-done.1, bf16[128,1152]{1,0:T(8,128)(2,1)S(1)} %collective-permute-done.66.before_ref), custom_call_target="tpu_custom_call" | custom-call | flops 2030043136 | bytes 2883584 | tf_op jit(solution)/shard_map/pallas_call | solution.py:80
  52.7 4.7 %shard_map.131 = (bf16[704,512]{1,0:T(8,128)(2,1)S(1)}, bf16[704,512]{1,0:T(8,128)(2,1)S(1)}) custom-call(s32[1]{0:T(128)} %bitcast.slot_ref, s32[704,1]{1,0:T(8,128)S(1)} %copy-done.9, s32[704,1]{1,0:T(8,128)S(1)} %copy-done.11, bf16[2,512,1408]{2,1,0:T(8,128)(2,1)S(1)} %copy-done.2, bf16[128,1152]{1,0:T(8,128)(2,1)S(1)} %collective-permute-done.68.before_ref), custom_call_target="tpu_custom_call" | custom-call | flops 2030043136 | bytes 2883584 | tf_op jit(solution)/shard_map/pallas_call | solution.py:80
  59.3 50.7 %conditional.2 = (bf16[704,512]{1,0:T(8,128)(2,1)S(1)}, bf16[704,512]{1,0:T(8,128)(2,1)S(1)}, bf16[704,512]{1,0:T(8,128)(2,1)S(1)}, bf16[256,1408]{1,0:T(8,128)(...) conditional(s32[]{:T(128)} %clamp.4, ...), branch_computations={%region_8.9_spmd, %region_9.10_spmd, %region_10.11_spmd, %region_1... | conditional | flops 21626880 | bytes 23789856 | solution.py:27
  63.9 14.5 %collective-permute-done.refs_1_ = bf16[704,512]{1,0:T(8,128)(2,1)S(1)} collective-permute-done((bf16[704,512]{1,0:T(8,128)(2,1)S(1)}, bf16[704,512]{1,0:T(8,128)(2,1)S(1)}, u32[]{:S(2)}, u32[]{:S(2)}) %collective-permute-start) | collective-permute-done | bytes 720928 | tf_op jit(solution)/shard_map/cond/branch_0_fun/ppermute | solution.py:24
  80.4 13.5 %collective-permute-done.1.refs_1_ = bf16[704,512]{1,0:T(8,128)(2,1)S(1)} collective-permute-done((bf16[704,512]{1,0:T(8,128)(2,1)S(1)}, bf16[704,512]{1,0:T(8,128)(2,1)S(1)}, u32[]{:S(2)}, u32[]{:S(2)}) %collective-permute-start.1) | collective-permute-done | bytes 720928 | tf_op jit(solution)/shard_map/cond/branch_0_fun/ppermute | solution.py:24
  94.3 13.8 %collective-permute-done.2.refs_1_ = bf16[704,512]{1,0:T(8,128)(2,1)S(1)} collective-permute-done((bf16[704,512]{1,0:T(8,128)(2,1)S(1)}, bf16[704,512]{1,0:T(8,128)(2,1)S(1)}, u32[]{:S(2)}, u32[]{:S(2)}) %collective-permute-start.2) | collective-permute-done | bytes 720928 | tf_op jit(solution)/shard_map/cond/branch_0_fun/ppermute | solution.py:24
  114.0 2.5 %shard_map.132 = (bf16[256,1408]{1,0:T(8,128)(2,1)S(1)}, bf16[256,1408]{1,0:T(8,128)(2,1)S(1)}, bf16[256,1408]{1,0:T(8,128)(2,1)S(1)}) custom-call(bf16[256,1408]{1,0:T(8,128)(2,1)S(1)} %copy-done.13, bf16[256,1408]{1,0:T(8,128)(2,1)} %get-tuple-element.291.refs_1_, bf16[256,1408]{1,0:T(8,128)(2,1)S(1)} %add_convert_fusion.3.refs_2_, ...), custom_call_target="tpu_custom_call" | custom-call | flops 7208960 | bytes 6488064 | tf_op jit(solution)/shard_map/pallas_call | solution.py:214
  132.2 4.3 %fusion.refs_4_ = f32[1024,512]{1,0:T(8,128)} fusion(bf16[512,1408]{1,0:T(8,128)(2,1)} %copy-done.7, bf16[2,512,1408]{2,1,0:T(8,128)(2,1)S(1)} %copy-done.3, s32[]{:T(128)S(6)} %select_n.146, s32[1024]{0:T(1024)S(1)} %fusion.50, f32[512]{0:T(512)S(1)} %select_reduce_fusion), kind=kOutput, calls=%fused_computation.7 | convolution fusion | flops 1276116992 | bytes 4986884 | tf_op jit(solution)/shard_map/dot_general | solution.py:15
  136.6 2.6 %collective-permute-done.74.refs_1_ = bf16[352,1024]{1,0:T(8,128)(2,1)} collective-permute-done((bf16[352,1024]{1,0:T(8,128)(2,1)}, bf16[352,1024]{1,0:T(8,128)(2,1)}, u32[]{:S(2)}, u32[]{:S(2)}) %collective-permute-start.74) | collective-permute-done | bytes 720928 | tf_op jit(solution)/shard_map/ppermute | solution.py:330
  139.2 14.6 %collective-permute-done.76.refs_3_ = bf16[352,1024]{1,0:T(8,128)(2,1)} collective-permute-done((bf16[352,1024]{1,0:T(8,128)(2,1)}, bf16[352,1024]{1,0:T(8,128)(2,1)}, u32[]{:S(2)}, u32[]{:S(2)}) %collective-permute-start.76) | collective-permute-done | bytes 720928 | tf_op jit(solution)/shard_map/ppermute | solution.py:330
  164.4 4.3 %collective-permute-done.83 = bf16[128,512]{1,0:T(8,128)(2,1)S(1)} collective-permute-done((bf16[128,512]{1,0:T(8,128)(2,1)S(1)}, bf16[128,512]{1,0:T(8,128)(2,1)S(1)}, u32[]{:S(2)}, u32[]{:S(2)}) %collective-permute-start.83) | collective-permute-done | bytes 131104 | tf_op jit(solution)/shard_map/ppermute | solution.py:51
  171.6 4.8 %collective-permute-done.78.refs_5_ = bf16[352,1024]{1,0:T(8,128)(2,1)S(1)} collective-permute-done((bf16[352,1024]{1,0:T(8,128)(2,1)}, bf16[352,1024]{1,0:T(8,128)(2,1)S(1)}, u32[]{:S(2)}, u32[]{:S(2)}) %collective-permute-start.78) | collective-permute-done | bytes 720928 | tf_op jit(solution)/shard_map/ppermute | solution.py:330
  176.4 2.6 %shard_map.137 = (bf16[352,1024]{1,0:T(8,128)(2,1)S(1)}, bf16[352,1024]{1,0:T(8,128)(2,1)S(1)}) custom-call(bf16[352,1024]{1,0:T(8,128)(2,1)} %fusion.22.refs_0_, bf16[352,1024]{1,0:T(8,128)(2,1)} %collective-permute-done.74.refs_1_, bf16[352,1024]{1,0:T(8,128)(2,1)} %fusion.23.refs_2_, bf16[352,1024]{1,0:T(8,128)(2,1)} %collective-permute-done.76.refs_3_, ...), custom_call_target="tpu_custom_call" | custom-call | flops 7208960 | bytes 5767168 | tf_op jit(solution)/shard_map/pallas_call | solution.py:214
  180.7 6.2 %collective-permute-done.88 = bf16[128,512]{1,0:T(8,128)(2,1)S(1)} collective-permute-done((bf16[128,512]{1,0:T(8,128)(2,1)S(1)}, bf16[128,512]{1,0:T(8,128)(2,1)S(1)}, u32[]{:S(2)}, u32[]{:S(2)}) %collective-permute-start.88) | collective-permute-done | bytes 131104 | tf_op jit(solution)/shard_map/ppermute | solution.py:57
  189.5 48.4 %conditional.3 = (bf16[704,512]{1,0:T(8,128)(2,1)}, bf16[704,512]{1,0:T(8,128)(2,1)}, bf16[704,512]{1,0:T(8,128)(2,1)}) conditional(s32[]{:T(128)} %clamp.4, (bf16[704,512]{1,0:T(8,128)(2,1)S(1)}, bf16[704,512]{1,0:T(8,128)(2,1)S(1)}, bf16[704,512]{1,0:T(8,128)(2,1)S(1)}) %tuple.65, (bf16[704,512]{1,0:T(8,128)(2,1)S(1)}, ...), branch_computations={%region_16.17_spmd, %region_17.18_spmd, %region_18.19_spmd, %regio... | conditional | bytes 8650896 | solution.py:27
  193.1 15.7 %collective-permute-done.42 = bf16[704,512]{1,0:T(8,128)(2,1)} collective-permute-done((bf16[704,512]{1,0:T(8,128)(2,1)S(1)}, bf16[704,512]{1,0:T(8,128)(2,1)}, u32[]{:S(2)}, u32[]{:S(2)}) %collective-permute-start.42) | collective-permute-done | bytes 720928 | tf_op jit(solution)/shard_map/cond/branch_0_fun/ppermute | solution.py:24
  208.8 15.4 %collective-permute-done.43 = bf16[704,512]{1,0:T(8,128)(2,1)} collective-permute-done((bf16[704,512]{1,0:T(8,128)(2,1)S(1)}, bf16[704,512]{1,0:T(8,128)(2,1)}, u32[]{:S(2)}, u32[]{:S(2)}) %collective-permute-start.43) | collective-permute-done | bytes 720928 | tf_op jit(solution)/shard_map/cond/branch_0_fun/ppermute | solution.py:24
  224.2 13.7 %collective-permute-done.44 = bf16[704,512]{1,0:T(8,128)(2,1)} collective-permute-done((bf16[704,512]{1,0:T(8,128)(2,1)S(1)}, bf16[704,512]{1,0:T(8,128)(2,1)}, u32[]{:S(2)}, u32[]{:S(2)}) %collective-permute-start.44) | collective-permute-done | bytes 720928 | tf_op jit(solution)/shard_map/cond/branch_0_fun/ppermute | solution.py:24
  239.7 2.4 shard_map.138
  242.1 2.4 shard_map.139
  244.5 2.4 shard_map.140
  (173 shorter events, 84.9 us)
Async XLA Ops:
  3.5 18.2 %collective-permute-start.69 = (bf16[128,1152]{1,0:T(8,128)(2,1)}, bf16[128,1152]{1,0:T(8,128)(2,1)}, u32[]{:S(2)}, u32[]{:S(2)}) collective-permute-start(bf16[128,1152]{1,0:T(8,128)(2,1)} %get-tuple-element.320), channel_id=1, source_target_pairs={{0,4},{4,0},{8,12},{12,8},{16,20},{20,16},{24,28},{28,24},{1,5},{5... | collective-permute-start | bytes 884744 | tf_op jit(solution)/shard_map/ppermute | solution.py:40
  6.5 13.1 %collective-permute-start.63 = (bf16[128,1152]{1,0:T(8,128)(2,1)}, bf16[128,1152]{1,0:T(8,128)(2,1)}, u32[]{:S(2)}, u32[]{:S(2)}) collective-permute-start(bf16[128,1152]{1,0:T(8,128)(2,1)} %get-tuple-element.320), channel_id=1, source_target_pairs={{0,8},{4,12},{8,16},{12,20},{16,24},{20,28},{24,0},{28,4},{1,9},{5... | collective-permute-start | bytes 884744 | tf_op jit(solution)/shard_map/ppermute | solution.py:39
  19.6 12.0 %collective-permute-start.64 = (bf16[128,1152]{1,0:T(8,128)(2,1)}, bf16[128,1152]{1,0:T(8,128)(2,1)S(1)}, u32[]{:S(2)}, u32[]{:S(2)}) collective-permute-start(bf16[128,1152]{1,0:T(8,128)(2,1)} %collective-permute-done.63), channel_id=1, source_target_pairs={{0,4},{4,0},{8,12},{12,8},{16,20},{20,16},{24,28},{28,24},{1,5},{5... | collective-permute-start | bytes 884744 | tf_op jit(solution)/shard_map/ppermute | solution.py:40
  20.1 9.9 %collective-permute-start.65 = (bf16[128,1152]{1,0:T(8,128)(2,1)}, bf16[128,1152]{1,0:T(8,128)(2,1)S(1)}, u32[]{:S(2)}, u32[]{:S(2)}) collective-permute-start(bf16[128,1152]{1,0:T(8,128)(2,1)} %collective-permute-done.63), channel_id=1, source_target_pairs={{0,8},{4,12},{8,16},{12,20},{16,24},{20,28},{24,0},{28,4},{1,9},{5... | collective-permute-start | bytes 884744 | tf_op jit(solution)/shard_map/ppermute | solution.py:39
  30.0 10.6 %collective-permute-start.66 = (bf16[128,1152]{1,0:T(8,128)(2,1)S(1)}, bf16[128,1152]{1,0:T(8,128)(2,1)S(1)}, u32[]{:S(2)}, u32[]{:S(2)}) collective-permute-start(bf16[128,1152]{1,0:T(8,128)(2,1)S(1)} %collective-permute-done.65), channel_id=1, source_target_pairs={{0,4},{4,0},{8,12},{12,8},{16,20},{20,16},{24,28},{28,24},{1,5},{5... | collective-permute-start | bytes 884744 | tf_op jit(solution)/shard_map/ppermute | solution.py:40
  59.3 19.1 %collective-permute-start = (bf16[704,512]{1,0:T(8,128)(2,1)S(1)}, bf16[704,512]{1,0:T(8,128)(2,1)S(1)}, u32[]{:S(2)}, u32[]{:S(2)}) collective-permute-start(bf16[704,512]{1,0:T(8,128)(2,1)S(1)} %get-tuple-element.169), channel_id=1, source_target_pairs={{0,4},{4,0},{8,12},{12,8},{16,20},{20,16},{24,28},{28,24},{1,5},{5... | collective-permute-start | bytes 2162696 | tf_op jit(solution)/shard_map/cond/branch_0_fun/ppermute | solution.py:24
  59.9 34.0 %collective-permute-start.1 = (bf16[704,512]{1,0:T(8,128)(2,1)S(1)}, bf16[704,512]{1,0:T(8,128)(2,1)S(1)}, u32[]{:S(2)}, u32[]{:S(2)}) collective-permute-start(bf16[704,512]{1,0:T(8,128)(2,1)S(1)} %get-tuple-element.171), channel_id=1, source_target_pairs={{0,4},{4,0},{8,12},{12,8},{16,20},{20,16},{24,28},{28,24},{1,5},{5... | collective-permute-start | bytes 2162696 | tf_op jit(solution)/shard_map/cond/branch_0_fun/ppermute | solution.py:24
  61.4 46.8 %collective-permute-start.2 = (bf16[704,512]{1,0:T(8,128)(2,1)S(1)}, bf16[704,512]{1,0:T(8,128)(2,1)S(1)}, u32[]{:S(2)}, u32[]{:S(2)}) collective-permute-start(bf16[704,512]{1,0:T(8,128)(2,1)S(1)} %get-tuple-element.173), channel_id=1, source_target_pairs={{0,4},{4,0},{8,12},{12,8},{16,20},{20,16},{24,28},{28,24},{1,5},{5... | collective-permute-start | bytes 2162696 | tf_op jit(solution)/shard_map/cond/branch_0_fun/ppermute | solution.py:24
  61.9 46.8 %collective-permute-start.3 = (bf16[256,1408]{1,0:T(8,128)(2,1)S(1)}, bf16[256,1408]{1,0:T(8,128)(2,1)}, u32[]{:S(2)}, u32[]{:S(2)}) collective-permute-start(bf16[256,1408]{1,0:T(8,128)(2,1)S(1)} %get-tuple-element.174), channel_id=1, source_target_pairs={{0,2},{1,3},{2,0},{3,1},{4,6},{5,7},{6,4},{7,5},{8,10},{9,11},{10,... | collective-permute-start | bytes 2162696 | tf_op jit(solution)/shard_map/cond/branch_0_fun/ppermute | solution.py:330
  63.4 45.3 %collective-permute-start.4 = (bf16[256,1408]{1,0:T(8,128)(2,1)S(1)}, bf16[256,1408]{1,0:T(8,128)(2,1)}, u32[]{:S(2)}, u32[]{:S(2)}) collective-permute-start(bf16[256,1408]{1,0:T(8,128)(2,1)S(1)} %get-tuple-element.175), channel_id=1, source_target_pairs={{0,2},{1,3},{2,0},{3,1},{4,6},{5,7},{6,4},{7,5},{8,10},{9,11},{10,... | collective-permute-start | bytes 2162696 | tf_op jit(solution)/shard_map/cond/branch_0_fun/ppermute | solution.py:330
  78.4 31.6 %collective-permute-start.5 = (bf16[256,1408]{1,0:T(8,128)(2,1)S(1)}, bf16[256,1408]{1,0:T(8,128)(2,1)}, u32[]{:S(2)}, u32[]{:S(2)}) collective-permute-start(bf16[256,1408]{1,0:T(8,128)(2,1)S(1)} %get-tuple-element.176), channel_id=1, source_target_pairs={{0,2},{1,3},{2,0},{3,1},{4,6},{5,7},{6,4},{7,5},{8,10},{9,11},{10,... | collective-permute-start | bytes 2162696 | tf_op jit(solution)/shard_map/cond/branch_0_fun/ppermute | solution.py:330
  117.3 12.8 %collective-permute-start.77 = (bf16[352,1024]{1,0:T(8,128)(2,1)S(1)}, bf16[352,1024]{1,0:T(8,128)(2,1)S(1)}, u32[]{:S(2)}, u32[]{:S(2)}) collective-permute-start(bf16[352,1024]{1,0:T(8,128)(2,1)S(1)} %convolution_convert_fusion.4), channel_id=1, source_target_pairs={{0,1},{1,0},{2,3},{3,2},{4,5},{5,4},{6,7},{7,6},{8,9},{9,8},{10,11... | collective-permute-start | bytes 2162696 | tf_op jit(solution)/shard_map/ppermute | solution.py:314
  119.9 19.3 %collective-permute-start.74 = (bf16[352,1024]{1,0:T(8,128)(2,1)}, bf16[352,1024]{1,0:T(8,128)(2,1)}, u32[]{:S(2)}, u32[]{:S(2)}) collective-permute-start(bf16[352,1024]{1,0:T(8,128)(2,1)} %fusion.22.refs_0_), channel_id=1, source_target_pairs={{0,2},{1,3},{2,0},{3,1},{4,6},{5,7},{6,4},{7,5},{8,10},{9,11},{10,... | collective-permute-start | bytes 2162696 | tf_op jit(solution)/shard_map/ppermute | solution.py:330
  122.8 31.0 %collective-permute-start.76 = (bf16[352,1024]{1,0:T(8,128)(2,1)}, bf16[352,1024]{1,0:T(8,128)(2,1)}, u32[]{:S(2)}, u32[]{:S(2)}) collective-permute-start(bf16[352,1024]{1,0:T(8,128)(2,1)} %fusion.23.refs_2_), channel_id=1, source_target_pairs={{0,2},{1,3},{2,0},{3,1},{4,6},{5,7},{6,4},{7,5},{8,10},{9,11},{10,... | collective-permute-start | bytes 2162696 | tf_op jit(solution)/shard_map/ppermute | solution.py:330
  157.6 18.8 %collective-permute-start.78 = (bf16[352,1024]{1,0:T(8,128)(2,1)}, bf16[352,1024]{1,0:T(8,128)(2,1)S(1)}, u32[]{:S(2)}, u32[]{:S(2)}) collective-permute-start(bf16[352,1024]{1,0:T(8,128)(2,1)} %add_convert_fusion.1.refs_5_.refs_4_), channel_id=1, source_target_pairs={{0,2},{1,3},{2,0},{3,1},{4,6},{5,7},{6,4},{7,5},{8,10},{9,11},{10,... | collective-permute-start | bytes 2162696 | tf_op jit(solution)/shard_map/ppermute | solution.py:330
  163.9 15.1 %collective-permute-start.87 = (bf16[128,512]{1,0:T(8,128)(2,1)S(1)}, bf16[128,512]{1,0:T(8,128)(2,1)S(1)}, u32[]{:S(2)}, u32[]{:S(2)}) collective-permute-start(bf16[128,512]{1,0:T(8,128)(2,1)S(1)} %get-tuple-element.319), channel_id=1, source_target_pairs={{0,4},{4,0},{8,12},{12,8},{16,20},{20,16},{24,28},{28,24},{1,5},{5... | collective-permute-start | bytes 393224 | tf_op jit(solution)/shard_map/ppermute | solution.py:51
  168.8 10.7 %collective-permute-start.86 = (bf16[128,512]{1,0:T(8,128)(2,1)S(1)}, bf16[128,512]{1,0:T(8,128)(2,1)S(1)}, u32[]{:S(2)}, u32[]{:S(2)}) collective-permute-start(bf16[128,512]{1,0:T(8,128)(2,1)S(1)} %add_convert_fusion.8.refs_6_), channel_id=1, source_target_pairs={{0,8},{4,12},{8,16},{12,20},{16,24},{20,28},{24,0},{28,4},{1,9},{5... | collective-permute-start | bytes 393224 | tf_op jit(solution)/shard_map/ppermute | solution.py:57
  169.5 77.3 %collective-permute-start.91 = (bf16[128,512]{1,0:T(8,128)(2,1)}, bf16[128,512]{1,0:T(8,128)(2,1)S(1)}, u32[]{:S(2)}, u32[]{:S(2)}) collective-permute-start(bf16[128,512]{1,0:T(8,128)(2,1)} %get-tuple-element.317), channel_id=1, source_target_pairs={{0,4},{4,0},{8,12},{12,8},{16,20},{20,16},{24,28},{28,24},{1,5},{5... | collective-permute-start | bytes 393224 | tf_op jit(solution)/shard_map/ppermute | solution.py:51
  171.1 9.6 %collective-permute-start.89 = (bf16[128,512]{1,0:T(8,128)(2,1)S(1)}, bf16[128,512]{1,0:T(8,128)(2,1)S(1)}, u32[]{:S(2)}, u32[]{:S(2)}) collective-permute-start(bf16[128,512]{1,0:T(8,128)(2,1)S(1)} %get-tuple-element.318), channel_id=1, source_target_pairs={{0,4},{4,0},{8,12},{12,8},{16,20},{20,16},{24,28},{28,24},{1,5},{5... | collective-permute-start | bytes 393224 | tf_op jit(solution)/shard_map/ppermute | solution.py:51
  179.1 9.5 %collective-permute-start.85 = (bf16[352,1024]{1,0:T(8,128)(2,1)S(1)}, bf16[352,1024]{1,0:T(8,128)(2,1)S(1)}, u32[]{:S(2)}, u32[]{:S(2)}) collective-permute-start(bf16[352,1024]{1,0:T(8,128)(2,1)S(1)} %get-tuple-element.301), channel_id=1, source_target_pairs={{0,1},{1,0},{2,3},{3,2},{4,5},{5,4},{6,7},{7,6},{8,9},{9,8},{10,11... | collective-permute-start | bytes 2162696 | tf_op jit(solution)/shard_map/ppermute | solution.py:334
  187.6 59.2 %collective-permute-start.90 = (bf16[128,512]{1,0:T(8,128)(2,1)}, bf16[128,512]{1,0:T(8,128)(2,1)S(1)}, u32[]{:S(2)}, u32[]{:S(2)}) collective-permute-start(bf16[128,512]{1,0:T(8,128)(2,1)} %add_convert_fusion.6), channel_id=1, source_target_pairs={{0,8},{4,12},{8,16},{12,20},{16,24},{20,28},{24,0},{28,4},{1,9},{5... | collective-permute-start | bytes 393224 | tf_op jit(solution)/shard_map/ppermute | solution.py:57
  189.5 19.2 %collective-permute-start.42 = (bf16[704,512]{1,0:T(8,128)(2,1)S(1)}, bf16[704,512]{1,0:T(8,128)(2,1)}, u32[]{:S(2)}, u32[]{:S(2)}) collective-permute-start(bf16[704,512]{1,0:T(8,128)(2,1)S(1)} %get-tuple-element.231), channel_id=1, source_target_pairs={{0,4},{4,0},{8,12},{12,8},{16,20},{20,16},{24,28},{28,24},{1,5},{5... | collective-permute-start | bytes 2162696 | tf_op jit(solution)/shard_map/cond/branch_0_fun/ppermute | solution.py:24
  191.1 33.1 %collective-permute-start.43 = (bf16[704,512]{1,0:T(8,128)(2,1)S(1)}, bf16[704,512]{1,0:T(8,128)(2,1)}, u32[]{:S(2)}, u32[]{:S(2)}) collective-permute-start(bf16[704,512]{1,0:T(8,128)(2,1)S(1)} %get-tuple-element.232), channel_id=1, source_target_pairs={{0,4},{4,0},{8,12},{12,8},{16,20},{20,16},{24,28},{28,24},{1,5},{5... | collective-permute-start | bytes 2162696 | tf_op jit(solution)/shard_map/cond/branch_0_fun/ppermute | solution.py:24
  191.6 46.3 %collective-permute-start.44 = (bf16[704,512]{1,0:T(8,128)(2,1)S(1)}, bf16[704,512]{1,0:T(8,128)(2,1)}, u32[]{:S(2)}, u32[]{:S(2)}) collective-permute-start(bf16[704,512]{1,0:T(8,128)(2,1)S(1)} %get-tuple-element.233), channel_id=1, source_target_pairs={{0,4},{4,0},{8,12},{12,8},{16,20},{20,16},{24,28},{28,24},{1,5},{5... | collective-permute-start | bytes 2162696 | tf_op jit(solution)/shard_map/cond/branch_0_fun/ppermute | solution.py:24
  (37 other events, 218.1 us)

commit v9 on v8

--- a/solution.py
+++ b/solution.py
@@ -49,17 +49,32 @@
     for step in range(steps):
         at = ((step + 1) % steps * 2 + 1) * rows
         twins.append(lax.ppermute(partial[at : at + rows], "expert", xor_pairs(count, 1)))
-    terms, first = [], None
+    owns = []
     for step in range(steps):
-        if step > 0:
-            total = sum(term.astype(F32) for term in terms).astype(BF16)
-            first = total if first is None else first
-            terms = [lax.ppermute(total, "expert", ring)]
-        else:
-            terms = []
         at = (step + 1) % steps * 2 * rows
-        terms += [partial[at : at + rows], twins[step]]
-    return terms, first
+        owns.append((partial[at : at + rows], twins[step]))
+
+    def added(*terms):
+        return sum(term.astype(F32) for term in terms)
+
+    def hop(total):
+        return lax.ppermute(total, "expert", ring)
+
+    total = added(*owns[0]).astype(BF16)
+    held = max(1, steps - 2)
+    for own in owns[1:held]:
+        total = added(*own, hop(total)).astype(BF16)
+    arrived = [hop(total)] if steps > 1 else []
+
+    def end(later):
+        if steps == 1:
+            return total
+        result = added(*owns[held], *arrived, never(later))
+        for own in owns[held + 1 :]:
+            result = added(*own, hop(result.astype(BF16)))
+        return result.astype(BF16)
+
+    return end, total
 
 
 def tile_of(extent, most):
@@ -69,7 +84,7 @@
 def slot_select(slot, send_order, keep_order, weight, before):
     slots, width, neurons = weight.shape
     half = send_order.shape[0]
-    tile = max(t for t in range(16, 193, 16) if half % t == 0)
+    tile = max(t for t in range(16, 353, 16) if half % t == 0)
 
     def kernel(slot_ref, send_ref, keep_ref, weight_ref, before_ref, sent_ref, kept_ref):
         columns = lax.broadcasted_iota(jnp.int32, (tile, neurons), 1)
@@ -371,13 +386,13 @@
         hidden_units,
         1,
         merged_sums[:2],
-        before=(other_mixed, merged_sums[2][0], *other_done),
+        before=(other_mixed[:8, :128], merged_sums[2][0], *other_done),
     )
     merged_h = joined(merged_h)
     mixed = (other_mixed + merged_p[:, None] * dot(merged_h, w_down, 0, 0)).astype(BF16)
-    mixed_terms, first_sum = ring_scatter(mixed, devices_n)
+    end_ring, passed = ring_scatter(mixed, devices_n)
     merged_dg, merged_du = map(
-        joined, elementwise(hidden_gradients, 2, merged_sums, before=(first_sum,))
+        joined, elementwise(hidden_gradients, 2, merged_sums, before=(passed,))
     )
     halves = [
         dot(a, value, 1, 0).astype(BF16)
@@ -385,8 +400,7 @@
     ]
     far_halves = with_partner(devices_n, me ^ partner, halves, list)
 
-    mixed = sum((t.astype(F32) for t in mixed_terms), never(far_halves[0]).astype(F32))
-    mixed = mixed.astype(BF16)
+    mixed = end_ring(far_halves[0])
 
     keep_flag = am_target.astype(jnp.int32)
     outs = [

time: 248 us -> 248 us (level)
  Pallas kernels: 36.4 us -> 32.3 us
  other arithmetic: 12.9 us -> 16.5 us
    pallas_call x3, Pallas kernels: 14 us -> 7.99 us  [slot_select(): pl.pallas_call(kernel, out_shape=[jax.ShapeDtypeStruct((half, width), BF1...]
    ppermute x6, waiting for transfers between devices: 23.2 us -> 19.4 us  [far(): return lax.ppermute(part, 'hidden', xor_pairs(hidden_n, last_bit))]
    unnamed x53 -> x49, local copies, waits for them, and re-layouts: 10 us -> 7.02 us
    concatenate x2, other arithmetic: 0.22 us -> 3.17 us  [shards(): jnp.concatenate([swapped(a), a], axis=0)]
  transfers between devices with their start and end apart: 38 -> 38, of which waited for: 16 -> 18; matrix products, arithmetic and copies ran while one was open for 13% -> 15% of each run, Pallas kernels for 14% -> 11%
where the time goes in v9:
time: 248 us; the launch traced here: 247 us
  waiting for transfers between devices  131 us (53%)
  Pallas kernels  32.3 us (13%)
  starting transfers between devices  28.4 us (11%)
  matrix products  22.4 us (9%)
  other arithmetic  16.5 us (7%)
  local copies, waits for them, and re-layouts  11.4 us (5%)
  between operations  4.76 us (2%)
    ppermute x6, waiting for transfers between devices, run(): lax.ppermute(v, 'expert', xor_pairs(count, bits))  87.6 us
    dot_general x20, matrix products, dot(): lax.dot_general(a, b, (((ca,), (cb,)), ((), ())), preferred_element_type=...  22.4 us
    ppermute x6, waiting for transfers between devices, far(): return lax.ppermute(part, 'hidden', xor_pairs(hidden_n, last_bit))  19.4 us
    pallas_call x6, Pallas kernels, elementwise(): pl.pallas_call(kernel, out_shape=[jax.ShapeDtypeStruct((rows, cols), BF16...  9.37 us
    ppermute x3, waiting for transfers between devices, ring_gather(): value = lax.ppermute(value, 'expert', ring)  9.02 us
    pallas_call x3, Pallas kernels, slot_select(): pl.pallas_call(kernel, out_shape=[jax.ShapeDtypeStruct((half, width), BF1...  7.99 us
    pallas_call x3, Pallas kernels, slot_matmul(): pl.pallas_call(kernel, out_shape=[jax.ShapeDtypeStruct((slots, width, neu...  7.79 us
    pallas_call x3, Pallas kernels, slot_place(): pl.pallas_call(kernel, out_shape=jax.ShapeDtypeStruct(into.shape, BF16),...  7.16 us
  transfers between devices with their start and end apart: 38, of which 18 were waited for; matrix products, arithmetic and copies ran while one was open for 15% of the time, Pallas kernels for 11%

profile of v9, /device:TPU:0, one launch (start us, length us, event | category | flops | bytes accessed | tf_op | source)
XLA Modules:
  0.0 246.8 jit_solution(17742530708725781806)
XLA Ops:
  3.4 3.0 %collective-permute-start.63 = (bf16[128,1152]{1,0:T(8,128)(2,1)S(1)}, bf16[128,1152]{1,0:T(8,128)(2,1)}, u32[]{:S(2)}, u32[]{:S(2)}) collective-permute-start(bf16[128,1152]{1,0:T(8,128)(2,1)S(1)} %get-tuple-element.320), channel_id=1, source_target_pairs={{0,4},{4,0},{8,12},{12,8},{16,20},{20,16},{24,28},{28,24},{1,5},{5... | collective-permute-start | bytes 884744 | tf_op jit(solution)/shard_map/ppermute | solution.py:40
  24.4 4.9 %collective-permute-done.66 = bf16[128,1152]{1,0:T(8,128)(2,1)S(1)} collective-permute-done((bf16[128,1152]{1,0:T(8,128)(2,1)}, bf16[128,1152]{1,0:T(8,128)(2,1)S(1)}, u32[]{:S(2)}, u32[]{:S(2)}) %collective-permute-start.66) | collective-permute-done | bytes 294944 | tf_op jit(solution)/shard_map/ppermute | solution.py:39
  32.6 2.7 %shard_map.129 = (bf16[704,512]{1,0:T(8,128)(2,1)S(1)}, bf16[704,512]{1,0:T(8,128)(2,1)S(1)}) custom-call(s32[1]{0:T(128)} %bitcast.3.slot_ref, s32[704,1]{1,0:T(8,128)S(1)} %select_n.149.send_ref, s32[704,1]{1,0:T(8,128)S(1)} %copy-done.8, bf16[2,512,1408]{2,1,0:T(8,128)(2,1)S(1)} %copy-done, bf16[128,1152]{1,0:T(8,128)(2,1)S(1)} %collective-permute-done.65.before_ref), custom_call_target="tpu_custom_call" | custom-call | flops 2030043136 | bytes 2883584 | tf_op jit(solution)/shard_map/pallas_call | solution.py:95
  35.3 4.1 %collective-permute-done.68 = bf16[128,1152]{1,0:T(8,128)(2,1)S(1)} collective-permute-done((bf16[128,1152]{1,0:T(8,128)(2,1)S(1)}, bf16[128,1152]{1,0:T(8,128)(2,1)S(1)}, u32[]{:S(2)}, u32[]{:S(2)}) %collective-permute-start.68) | collective-permute-done | bytes 294944 | tf_op jit(solution)/shard_map/ppermute | solution.py:39
  40.0 2.7 %shard_map.130 = (bf16[704,512]{1,0:T(8,128)(2,1)S(1)}, bf16[704,512]{1,0:T(8,128)(2,1)S(1)}) custom-call(s32[1]{0:T(128)} %bitcast.3.slot_ref, s32[704,1]{1,0:T(8,128)S(1)} %select_n.149.send_ref, s32[704,1]{1,0:T(8,128)S(1)} %copy-done.8, bf16[2,512,1408]{2,1,0:T(8,128)(2,1)S(1)} %copy-done.1, bf16[128,1152]{1,0:T(8,128)(2,1)S(1)} %collective-permute-done.67.before_ref), custom_call_target="tpu_custom_call" | custom-call | flops 2030043136 | bytes 2883584 | tf_op jit(solution)/shard_map/pallas_call | solution.py:95
  42.7 3.4 %collective-permute-done.69.before_ref = bf16[128,1152]{1,0:T(8,128)(2,1)S(1)} collective-permute-done((bf16[128,1152]{1,0:T(8,128)(2,1)S(1)}, bf16[128,1152]{1,0:T(8,128)(2,1)S(1)}, u32[]{:S(2)}, u32[]{:S(2)}) %collective-permute-start.69) | collective-permute-done | bytes 294944 | tf_op jit(solution)/shard_map/ppermute | solution.py:40
  52.0 2.7 %shard_map.131 = (bf16[704,512]{1,0:T(8,128)(2,1)S(1)}, bf16[704,512]{1,0:T(8,128)(2,1)S(1)}) custom-call(s32[1]{0:T(128)} %bitcast.3.slot_ref, s32[704,1]{1,0:T(8,128)S(1)} %copy-done.7, s32[704,1]{1,0:T(8,128)S(1)} %copy-done.9, bf16[2,512,1408]{2,1,0:T(8,128)(2,1)S(1)} %copy-done.2, bf16[128,1152]{1,0:T(8,128)(2,1)S(1)} %collective-permute-done.69.before_ref), custom_call_target="tpu_custom_call" | custom-call | flops 2030043136 | bytes 2883584 | tf_op jit(solution)/shard_map/pallas_call | solution.py:95
  56.6 50.7 %conditional.2 = (bf16[704,512]{1,0:T(8,128)(2,1)S(1)}, bf16[704,512]{1,0:T(8,128)(2,1)S(1)}, bf16[704,512]{1,0:T(8,128)(2,1)S(1)}, bf16[256,1408]{1,0:T(8,128)(...) conditional(s32[]{:T(128)} %clamp.4, ...), branch_computations={%region_8.9_spmd, %region_9.10_spmd, %region_10.11_spmd, %region_1... | conditional | flops 21626880 | bytes 23789856 | solution.py:27
  61.2 14.5 %collective-permute-done.refs_1_ = bf16[704,512]{1,0:T(8,128)(2,1)S(1)} collective-permute-done((bf16[704,512]{1,0:T(8,128)(2,1)S(1)}, bf16[704,512]{1,0:T(8,128)(2,1)S(1)}, u32[]{:S(2)}, u32[]{:S(2)}) %collective-permute-start) | collective-permute-done | bytes 720928 | tf_op jit(solution)/shard_map/cond/branch_0_fun/ppermute | solution.py:24
  77.7 13.4 %collective-permute-done.1.refs_1_ = bf16[704,512]{1,0:T(8,128)(2,1)S(1)} collective-permute-done((bf16[704,512]{1,0:T(8,128)(2,1)S(1)}, bf16[704,512]{1,0:T(8,128)(2,1)S(1)}, u32[]{:S(2)}, u32[]{:S(2)}) %collective-permute-start.1) | collective-permute-done | bytes 720928 | tf_op jit(solution)/shard_map/cond/branch_0_fun/ppermute | solution.py:24
  91.6 13.8 %collective-permute-done.2.refs_1_ = bf16[704,512]{1,0:T(8,128)(2,1)S(1)} collective-permute-done((bf16[704,512]{1,0:T(8,128)(2,1)S(1)}, bf16[704,512]{1,0:T(8,128)(2,1)S(1)}, u32[]{:S(2)}, u32[]{:S(2)}) %collective-permute-start.2) | collective-permute-done | bytes 720928 | tf_op jit(solution)/shard_map/cond/branch_0_fun/ppermute | solution.py:24
  110.9 3.3 %shard_map.132 = (bf16[256,1408]{1,0:T(8,128)(2,1)S(1)}, bf16[256,1408]{1,0:T(8,128)(2,1)}, bf16[256,1408]{1,0:T(8,128)(2,1)}) custom-call(bf16[256,1408]{1,0:T(8,128)(2,1)S(1)} %copy-done.11, bf16[256,1408]{1,0:T(8,128)(2,1)} %get-tuple-element.288.refs_1_, bf16[256,1408]{1,0:T(8,128)(2,1)S(1)} %add_convert_fusion.3.refs_2_, ...), custom_call_target="tpu_custom_call" | custom-call | flops 7208960 | bytes 6488064 | tf_op jit(solution)/shard_map/pallas_call | solution.py:229
  123.6 4.3 %fusion = f32[1024,512]{1,0:T(8,128)} fusion(bf16[512,1408]{1,0:T(8,128)(2,1)} %constant_dynamic-update-slice_fusion.8.right_ref, bf16[2,512,1408]{2,1,0:T(8,128)(2,1)S(1)} %copy-done.3, s32[]{:T(128)S(6)} %select_n.134, s32[1024]{0:T(1024)S(1)} %fusion.50, f32[512]{0:T(512)S(1)} %select_reduce_fusion), kind=kOutput, calls=%fused_computation.7 | convolution fusion | flops 1276116992 | bytes 4986884 | tf_op jit(solution)/shard_map/dot_general | solution.py:15
  129.5 3.5 %shard_map.135 = (bf16[2,512,1408]{2,1,0:T(8,128)(2,1)}, f32[8,128]{1,0:T(8,128)S(1)}) custom-call(s32[1]{0:T(128)} %bitcast.6.slot_ref, bf16[512,512]{1,0:T(8,128)(2,1)S(1)} %copy-done.5, bf16[512,1408]{1,0:T(8,128)(2,1)} %constant_dynamic-update-slice_fusion.8.right_ref), custom_call_target="tpu_custom_call" | custom-call | flops 738197504 | bytes 3407872 | tf_op jit(solution)/shard_map/pallas_call | solution.py:127
  140.7 11.4 %collective-permute-done.77.refs_3_ = bf16[352,1024]{1,0:T(8,128)(2,1)} collective-permute-done((bf16[352,1024]{1,0:T(8,128)(2,1)}, bf16[352,1024]{1,0:T(8,128)(2,1)}, u32[]{:S(2)}, u32[]{:S(2)}) %collective-permute-start.77) | collective-permute-done | bytes 720928 | tf_op jit(solution)/shard_map/ppermute | solution.py:345
  164.2 2.4 collective-permute-done.84
  166.6 4.3 %collective-permute-done.86 = bf16[128,512]{1,0:T(8,128)(2,1)S(1)} collective-permute-done((bf16[128,512]{1,0:T(8,128)(2,1)S(1)}, bf16[128,512]{1,0:T(8,128)(2,1)S(1)}, u32[]{:S(2)}, u32[]{:S(2)}) %collective-permute-start.86) | collective-permute-done | bytes 131104 | tf_op jit(solution)/shard_map/ppermute | solution.py:61
  171.0 6.7 %collective-permute-done.88.refs_5_ = bf16[352,1024]{1,0:T(8,128)(2,1)S(1)} collective-permute-done((bf16[352,1024]{1,0:T(8,128)(2,1)S(1)}, bf16[352,1024]{1,0:T(8,128)(2,1)S(1)}, u32[]{:S(2)}, u32[]{:S(2)}) %collective-permute-start.88) | collective-permute-done | bytes 720928 | tf_op jit(solution)/shard_map/ppermute | solution.py:345
  177.7 2.5 shard_map.137
  184.3 49.3 %conditional.3 = (bf16[704,512]{1,0:T(8,128)(2,1)}, bf16[704,512]{1,0:T(8,128)(2,1)}, bf16[704,512]{1,0:T(8,128)(2,1)}) conditional(s32[]{:T(128)} %clamp.4, (bf16[704,512]{1,0:T(8,128)(2,1)S(1)}, bf16[704,512]{1,0:T(8,128)(2,1)S(1)}, bf16[704,512]{1,0:T(8,128)(2,1)S(1)}) %tuple.65, (bf16[704,512]{1,0:T(8,128)(2,1)S(1)}, ...), branch_computations={%region_16.17_spmd, %region_17.18_spmd, %region_18.19_spmd, %regio... | conditional | bytes 8650896 | solution.py:27
  187.8 15.7 %collective-permute-done.42 = bf16[704,512]{1,0:T(8,128)(2,1)} collective-permute-done((bf16[704,512]{1,0:T(8,128)(2,1)S(1)}, bf16[704,512]{1,0:T(8,128)(2,1)}, u32[]{:S(2)}, u32[]{:S(2)}) %collective-permute-start.42) | collective-permute-done | bytes 720928 | tf_op jit(solution)/shard_map/cond/branch_0_fun/ppermute | solution.py:24
  203.5 15.4 %collective-permute-done.43 = bf16[704,512]{1,0:T(8,128)(2,1)} collective-permute-done((bf16[704,512]{1,0:T(8,128)(2,1)S(1)}, bf16[704,512]{1,0:T(8,128)(2,1)}, u32[]{:S(2)}, u32[]{:S(2)}) %collective-permute-start.43) | collective-permute-done | bytes 720928 | tf_op jit(solution)/shard_map/cond/branch_0_fun/ppermute | solution.py:24
  218.9 14.6 %collective-permute-done.44 = bf16[704,512]{1,0:T(8,128)(2,1)} collective-permute-done((bf16[704,512]{1,0:T(8,128)(2,1)S(1)}, bf16[704,512]{1,0:T(8,128)(2,1)}, u32[]{:S(2)}, u32[]{:S(2)}) %collective-permute-start.44) | collective-permute-done | bytes 720928 | tf_op jit(solution)/shard_map/cond/branch_0_fun/ppermute | solution.py:24
  238.0 2.4 shard_map.138
  (170 shorter events, 90.2 us)
Async XLA Ops:
  3.4 17.6 %collective-permute-start.63 = (bf16[128,1152]{1,0:T(8,128)(2,1)S(1)}, bf16[128,1152]{1,0:T(8,128)(2,1)}, u32[]{:S(2)}, u32[]{:S(2)}) collective-permute-start(bf16[128,1152]{1,0:T(8,128)(2,1)S(1)} %get-tuple-element.320), channel_id=1, source_target_pairs={{0,4},{4,0},{8,12},{12,8},{16,20},{20,16},{24,28},{28,24},{1,5},{5... | collective-permute-start | bytes 884744 | tf_op jit(solution)/shard_map/ppermute | solution.py:40
  6.4 12.5 %collective-permute-start.64 = (bf16[128,1152]{1,0:T(8,128)(2,1)S(1)}, bf16[128,1152]{1,0:T(8,128)(2,1)}, u32[]{:S(2)}, u32[]{:S(2)}) collective-permute-start(bf16[128,1152]{1,0:T(8,128)(2,1)S(1)} %get-tuple-element.320), channel_id=1, source_target_pairs={{0,8},{4,12},{8,16},{12,20},{16,24},{20,28},{24,0},{28,4},{1,9},{5... | collective-permute-start | bytes 884744 | tf_op jit(solution)/shard_map/ppermute | solution.py:39
  18.9 12.0 %collective-permute-start.65 = (bf16[128,1152]{1,0:T(8,128)(2,1)}, bf16[128,1152]{1,0:T(8,128)(2,1)S(1)}, u32[]{:S(2)}, u32[]{:S(2)}) collective-permute-start(bf16[128,1152]{1,0:T(8,128)(2,1)} %collective-permute-done.64), channel_id=1, source_target_pairs={{0,4},{4,0},{8,12},{12,8},{16,20},{20,16},{24,28},{28,24},{1,5},{5... | collective-permute-start | bytes 884744 | tf_op jit(solution)/shard_map/ppermute | solution.py:40
  19.5 9.9 %collective-permute-start.66 = (bf16[128,1152]{1,0:T(8,128)(2,1)}, bf16[128,1152]{1,0:T(8,128)(2,1)S(1)}, u32[]{:S(2)}, u32[]{:S(2)}) collective-permute-start(bf16[128,1152]{1,0:T(8,128)(2,1)} %collective-permute-done.64), channel_id=1, source_target_pairs={{0,8},{4,12},{8,16},{12,20},{16,24},{20,28},{24,0},{28,4},{1,9},{5... | collective-permute-start | bytes 884744 | tf_op jit(solution)/shard_map/ppermute | solution.py:39
  29.4 10.6 %collective-permute-start.67 = (bf16[128,1152]{1,0:T(8,128)(2,1)S(1)}, bf16[128,1152]{1,0:T(8,128)(2,1)S(1)}, u32[]{:S(2)}, u32[]{:S(2)}) collective-permute-start(bf16[128,1152]{1,0:T(8,128)(2,1)S(1)} %collective-permute-done.66), channel_id=1, source_target_pairs={{0,4},{4,0},{8,12},{12,8},{16,20},{20,16},{24,28},{28,24},{1,5},{5... | collective-permute-start | bytes 884744 | tf_op jit(solution)/shard_map/ppermute | solution.py:40
  30.9 8.5 %collective-permute-start.68 = (bf16[128,1152]{1,0:T(8,128)(2,1)S(1)}, bf16[128,1152]{1,0:T(8,128)(2,1)S(1)}, u32[]{:S(2)}, u32[]{:S(2)}) collective-permute-start(bf16[128,1152]{1,0:T(8,128)(2,1)S(1)} %collective-permute-done.66), channel_id=1, source_target_pairs={{0,8},{4,12},{8,16},{12,20},{16,24},{20,28},{24,0},{28,4},{1,9},{5... | collective-permute-start | bytes 884744 | tf_op jit(solution)/shard_map/ppermute | solution.py:39
  56.6 19.1 %collective-permute-start = (bf16[704,512]{1,0:T(8,128)(2,1)S(1)}, bf16[704,512]{1,0:T(8,128)(2,1)S(1)}, u32[]{:S(2)}, u32[]{:S(2)}) collective-permute-start(bf16[704,512]{1,0:T(8,128)(2,1)S(1)} %get-tuple-element.169), channel_id=1, source_target_pairs={{0,4},{4,0},{8,12},{12,8},{16,20},{20,16},{24,28},{28,24},{1,5},{5... | collective-permute-start | bytes 2162696 | tf_op jit(solution)/shard_map/cond/branch_0_fun/ppermute | solution.py:24
  57.2 34.0 %collective-permute-start.1 = (bf16[704,512]{1,0:T(8,128)(2,1)S(1)}, bf16[704,512]{1,0:T(8,128)(2,1)S(1)}, u32[]{:S(2)}, u32[]{:S(2)}) collective-permute-start(bf16[704,512]{1,0:T(8,128)(2,1)S(1)} %get-tuple-element.171), channel_id=1, source_target_pairs={{0,4},{4,0},{8,12},{12,8},{16,20},{20,16},{24,28},{28,24},{1,5},{5... | collective-permute-start | bytes 2162696 | tf_op jit(solution)/shard_map/cond/branch_0_fun/ppermute | solution.py:24
  58.7 46.8 %collective-permute-start.2 = (bf16[704,512]{1,0:T(8,128)(2,1)S(1)}, bf16[704,512]{1,0:T(8,128)(2,1)S(1)}, u32[]{:S(2)}, u32[]{:S(2)}) collective-permute-start(bf16[704,512]{1,0:T(8,128)(2,1)S(1)} %get-tuple-element.173), channel_id=1, source_target_pairs={{0,4},{4,0},{8,12},{12,8},{16,20},{20,16},{24,28},{28,24},{1,5},{5... | collective-permute-start | bytes 2162696 | tf_op jit(solution)/shard_map/cond/branch_0_fun/ppermute | solution.py:24
  59.2 46.8 %collective-permute-start.3 = (bf16[256,1408]{1,0:T(8,128)(2,1)S(1)}, bf16[256,1408]{1,0:T(8,128)(2,1)}, u32[]{:S(2)}, u32[]{:S(2)}) collective-permute-start(bf16[256,1408]{1,0:T(8,128)(2,1)S(1)} %get-tuple-element.174), channel_id=1, source_target_pairs={{0,2},{1,3},{2,0},{3,1},{4,6},{5,7},{6,4},{7,5},{8,10},{9,11},{10,... | collective-permute-start | bytes 2162696 | tf_op jit(solution)/shard_map/cond/branch_0_fun/ppermute | solution.py:345
  60.7 45.3 %collective-permute-start.4 = (bf16[256,1408]{1,0:T(8,128)(2,1)S(1)}, bf16[256,1408]{1,0:T(8,128)(2,1)}, u32[]{:S(2)}, u32[]{:S(2)}) collective-permute-start(bf16[256,1408]{1,0:T(8,128)(2,1)S(1)} %get-tuple-element.175), channel_id=1, source_target_pairs={{0,2},{1,3},{2,0},{3,1},{4,6},{5,7},{6,4},{7,5},{8,10},{9,11},{10,... | collective-permute-start | bytes 2162696 | tf_op jit(solution)/shard_map/cond/branch_0_fun/ppermute | solution.py:345
  75.7 31.6 %collective-permute-start.5 = (bf16[256,1408]{1,0:T(8,128)(2,1)S(1)}, bf16[256,1408]{1,0:T(8,128)(2,1)}, u32[]{:S(2)}, u32[]{:S(2)}) collective-permute-start(bf16[256,1408]{1,0:T(8,128)(2,1)S(1)} %get-tuple-element.176), channel_id=1, source_target_pairs={{0,2},{1,3},{2,0},{3,1},{4,6},{5,7},{6,4},{7,5},{8,10},{9,11},{10,... | collective-permute-start | bytes 2162696 | tf_op jit(solution)/shard_map/cond/branch_0_fun/ppermute | solution.py:345
  115.8 23.1 %collective-permute-start.78 = (bf16[352,1024]{1,0:T(8,128)(2,1)}, bf16[352,1024]{1,0:T(8,128)(2,1)}, u32[]{:S(2)}, u32[]{:S(2)}) collective-permute-start(bf16[352,1024]{1,0:T(8,128)(2,1)} %convolution_convert_fusion.4), channel_id=1, source_target_pairs={{0,1},{1,0},{2,3},{3,2},{4,5},{5,4},{6,7},{7,6},{8,9},{9,8},{10,11... | collective-permute-start | bytes 2162696 | tf_op jit(solution)/shard_map/ppermute | solution.py:329
  116.3 11.6 %collective-permute-start.79 = (bf16[256,1408]{1,0:T(8,128)(2,1)}, bf16[256,1408]{1,0:T(8,128)(2,1)}, u32[]{:S(2)}, u32[]{:S(2)}) collective-permute-start(bf16[256,1408]{1,0:T(8,128)(2,1)} %get-tuple-element.295), channel_id=1, source_target_pairs={{0,1},{1,0},{2,3},{3,2},{4,5},{5,4},{6,7},{7,6},{8,9},{9,8},{10,11... | collective-permute-start | bytes 2162696 | tf_op jit(solution)/shard_map/ppermute | solution.py:349
  116.3 18.8 %collective-permute-start.80 = (bf16[256,1408]{1,0:T(8,128)(2,1)}, bf16[256,1408]{1,0:T(8,128)(2,1)}, u32[]{:S(2)}, u32[]{:S(2)}) collective-permute-start(bf16[256,1408]{1,0:T(8,128)(2,1)} %get-tuple-element.297), channel_id=1, source_target_pairs={{0,1},{1,0},{2,3},{3,2},{4,5},{5,4},{6,7},{7,6},{8,9},{9,8},{10,11... | collective-permute-start | bytes 2162696 | tf_op jit(solution)/shard_map/ppermute | solution.py:349
  118.2 22.4 %collective-permute-start.75 = (bf16[352,1024]{1,0:T(8,128)(2,1)}, bf16[352,1024]{1,0:T(8,128)(2,1)}, u32[]{:S(2)}, u32[]{:S(2)}) collective-permute-start(bf16[352,1024]{1,0:T(8,128)(2,1)} %fusion.22.refs_0_), channel_id=1, source_target_pairs={{0,2},{1,3},{2,0},{3,1},{4,6},{5,7},{6,4},{7,5},{8,10},{9,11},{10,... | collective-permute-start | bytes 2162696 | tf_op jit(solution)/shard_map/ppermute | solution.py:345
  121.2 30.9 %collective-permute-start.77 = (bf16[352,1024]{1,0:T(8,128)(2,1)}, bf16[352,1024]{1,0:T(8,128)(2,1)}, u32[]{:S(2)}, u32[]{:S(2)}) collective-permute-start(bf16[352,1024]{1,0:T(8,128)(2,1)} %fusion.23.refs_2_), channel_id=1, source_target_pairs={{0,2},{1,3},{2,0},{3,1},{4,6},{5,7},{6,4},{7,5},{8,10},{9,11},{10,... | collective-permute-start | bytes 2162696 | tf_op jit(solution)/shard_map/ppermute | solution.py:345
  159.7 17.9 %collective-permute-start.88 = (bf16[352,1024]{1,0:T(8,128)(2,1)S(1)}, bf16[352,1024]{1,0:T(8,128)(2,1)S(1)}, u32[]{:S(2)}, u32[]{:S(2)}) collective-permute-start(bf16[352,1024]{1,0:T(8,128)(2,1)S(1)} %add_convert_fusion.1.refs_5_.refs_4_), channel_id=1, source_target_pairs={{0,2},{1,3},{2,0},{3,1},{4,6},{5,7},{6,4},{7,5},{8,10},{9,11},{10,... | collective-permute-start | bytes 2162696 | tf_op jit(solution)/shard_map/ppermute | solution.py:345
  180.7 55.7 %collective-permute-start.83 = (bf16[128,512]{1,0:T(8,128)(2,1)}, bf16[128,512]{1,0:T(8,128)(2,1)S(1)}, u32[]{:S(2)}, u32[]{:S(2)}) collective-permute-start(bf16[128,512]{1,0:T(8,128)(2,1)} %get-tuple-element.319), channel_id=1, source_target_pairs={{0,4},{4,0},{8,12},{12,8},{16,20},{20,16},{24,28},{28,24},{1,5},{5... | collective-permute-start | bytes 393224 | tf_op jit(solution)/shard_map/ppermute | solution.py:51
  182.2 54.2 %collective-permute-start.87 = (bf16[128,512]{1,0:T(8,128)(2,1)S(1)}, bf16[128,512]{1,0:T(8,128)(2,1)}, u32[]{:S(2)}, u32[]{:S(2)}) collective-permute-start(bf16[128,512]{1,0:T(8,128)(2,1)S(1)} %add_convert_fusion.7.refs_6_), channel_id=1, source_target_pairs={{0,8},{4,12},{8,16},{12,20},{16,24},{20,28},{24,0},{28,4},{1,9},{5... | collective-permute-start | bytes 393224 | tf_op jit(solution)/shard_map/ppermute | solution.py:61
  184.3 19.2 %collective-permute-start.42 = (bf16[704,512]{1,0:T(8,128)(2,1)S(1)}, bf16[704,512]{1,0:T(8,128)(2,1)}, u32[]{:S(2)}, u32[]{:S(2)}) collective-permute-start(bf16[704,512]{1,0:T(8,128)(2,1)S(1)} %get-tuple-element.231), channel_id=1, source_target_pairs={{0,4},{4,0},{8,12},{12,8},{16,20},{20,16},{24,28},{28,24},{1,5},{5... | collective-permute-start | bytes 2162696 | tf_op jit(solution)/shard_map/cond/branch_0_fun/ppermute | solution.py:24
  185.7 33.2 %collective-permute-start.43 = (bf16[704,512]{1,0:T(8,128)(2,1)S(1)}, bf16[704,512]{1,0:T(8,128)(2,1)}, u32[]{:S(2)}, u32[]{:S(2)}) collective-permute-start(bf16[704,512]{1,0:T(8,128)(2,1)S(1)} %get-tuple-element.232), channel_id=1, source_target_pairs={{0,4},{4,0},{8,12},{12,8},{16,20},{20,16},{24,28},{28,24},{1,5},{5... | collective-permute-start | bytes 2162696 | tf_op jit(solution)/shard_map/cond/branch_0_fun/ppermute | solution.py:24
  186.4 47.2 %collective-permute-start.44 = (bf16[704,512]{1,0:T(8,128)(2,1)S(1)}, bf16[704,512]{1,0:T(8,128)(2,1)}, u32[]{:S(2)}, u32[]{:S(2)}) collective-permute-start(bf16[704,512]{1,0:T(8,128)(2,1)S(1)} %get-tuple-element.233), channel_id=1, source_target_pairs={{0,4},{4,0},{8,12},{12,8},{16,20},{20,16},{24,28},{28,24},{1,5},{5... | collective-permute-start | bytes 2162696 | tf_op jit(solution)/shard_map/cond/branch_0_fun/ppermute | solution.py:24
  233.6 11.6 %collective-permute-start.82 = (bf16[128,512]{1,0:T(8,128)(2,1)}, bf16[128,512]{1,0:T(8,128)(2,1)}, u32[]{:S(2)}, u32[]{:S(2)}) collective-permute-start(bf16[128,512]{1,0:T(8,128)(2,1)} %get-tuple-element.316), channel_id=1, source_target_pairs={{0,4},{4,0},{8,12},{12,8},{16,20},{20,16},{24,28},{28,24},{1,5},{5... | collective-permute-start | bytes 393224 | tf_op jit(solution)/shard_map/ppermute | solution.py:51
  (35 other events, 196.0 us)

commit v10 on v9

--- a/solution.py
+++ b/solution.py
@@ -41,7 +41,7 @@
     return jnp.concatenate(blocks, axis=0), blocks[3::2] or blocks[1:]
 
 
-def ring_scatter(partial, count):
+def ring_scatter(partial, count, later):
     rows = partial.shape[0] // count
     ring = [(i, (i + 2) % count) for i in range(count)]
     steps = count // 2
@@ -60,21 +60,12 @@
     def hop(total):
         return lax.ppermute(total, "expert", ring)
 
-    total = added(*owns[0]).astype(BF16)
-    held = max(1, steps - 2)
-    for own in owns[1:held]:
-        total = added(*own, hop(total)).astype(BF16)
-    arrived = [hop(total)] if steps > 1 else []
-
-    def end(later):
-        if steps == 1:
-            return total
-        result = added(*owns[held], *arrived, never(later))
-        for own in owns[held + 1 :]:
-            result = added(*own, hop(result.astype(BF16)))
-        return result.astype(BF16)
-
-    return end, total
+    total = added(*owns[0])
+    for step in range(1, steps):
+        total = added(*owns[step], hop(total.astype(BF16)))
+        if step == max(1, steps - 2):
+            total = total + never(later)
+    return total.astype(BF16)
 
 
 def tile_of(extent, most):
@@ -363,10 +354,11 @@
 
     merged, other_far = with_partner(devices_n, me ^ partner, sends, blend, keeps, other_parts)
     w_down = merged[2]
-    merged_sums = []
-    for value, w in zip((inputs_x, inputs_x, merged_dy), merged):
-        part = near_sum(core_sum(dot(w[quarter:], value, 1, 1), dot(w[:quarter], value, 1, 1)))
-        merged_sums.append((part, far(part)))
+    merged_parts = [
+        near_sum(core_sum(dot(w[quarter:], value, 1, 1), dot(w[:quarter], value, 1, 1)))
+        for value, w in zip((inputs_x, inputs_x, merged_dy), merged)
+    ]
+    merged_sums = [(part, far(part)) for part in merged_parts[:2]]
 
     other_h, other_dg, other_du = [
         jnp.concatenate([swapped(a), a], axis=0)
@@ -385,22 +377,29 @@
     (merged_h,) = elementwise(
         hidden_units,
         1,
-        merged_sums[:2],
-        before=(other_mixed[:8, :128], merged_sums[2][0], *other_done),
+        merged_sums,
+        before=(other_mixed[:8, :128], merged_parts[2], *other_done),
     )
     merged_h = joined(merged_h)
-    mixed = (other_mixed + merged_p[:, None] * dot(merged_h, w_down, 0, 0)).astype(BF16)
-    end_ring, passed = ring_scatter(mixed, devices_n)
-    merged_dg, merged_du = map(
-        joined, elementwise(hidden_gradients, 2, merged_sums, before=(passed,))
+
+    def with_back(arrived, part):
+        return arrived[0], far(part)
+
+    down_half = dot(merged_h, merged_dy, 1, 0).astype(BF16)
+    far_down, back = with_partner(
+        devices_n, me ^ partner, [down_half], with_back, merged_parts[2]
     )
+    merged_sums.append((merged_parts[2], back))
     halves = [
-        dot(a, value, 1, 0).astype(BF16)
-        for a, value in ((merged_dg, inputs_x), (merged_du, inputs_x), (merged_h, merged_dy))
+        dot(joined(a), inputs_x, 1, 0).astype(BF16)
+        for a in elementwise(hidden_gradients, 2, merged_sums)
     ]
     far_halves = with_partner(devices_n, me ^ partner, halves, list)
 
-    mixed = end_ring(far_halves[0])
+    mixed = other_mixed + merged_p[:, None] * dot(merged_h, w_down, 0, 0) + never(far_down)
+    mixed = ring_scatter(mixed.astype(BF16), devices_n, far_halves[0])
+    halves.append(down_half)
+    far_halves.append(far_down)
 
     keep_flag = am_target.astype(jnp.int32)
     outs = [

time: 248 us -> 243 us (0.980)
  waiting for transfers between devices: 131 us -> 121 us
  matrix products: 22.4 us -> 25.2 us
    ppermute x6, waiting for transfers between devices: 19.4 us -> 13.1 us  [far(): return lax.ppermute(part, 'hidden', xor_pairs(hidden_n, last_bit))]
    ppermute x3, waiting for transfers between devices: 4.35 us -> 1.51 us  [hop(): return lax.ppermute(total, 'expert', ring)]
    dot_general x20, matrix products: 22.4 us -> 25.2 us  [dot(): lax.dot_general(a, b, (((ca,), (cb,)), ((), ())), preferred_element_type=...]
    unnamed x49 -> x51, local copies, waits for them, and re-layouts: 7.02 us -> 6.92 us
  transfers between devices with their start and end apart: 38 -> 38, of which waited for: 18 -> 15; matrix products, arithmetic and copies ran while one was open for 15% -> 15% of each run, Pallas kernels for 11% -> 13%
where the time goes in v10:
time: 243 us; the launch traced here: 242 us
  waiting for transfers between devices  121 us (50%)
  Pallas kernels  32.6 us (13%)
  starting transfers between devices  29.6 us (12%)
  matrix products  25.2 us (10%)
  other arithmetic  14.7 us (6%)
  local copies, waits for them, and re-layouts  12.6 us (5%)
  between operations  5.58 us (2%)
    ppermute x6, waiting for transfers between devices, run(): lax.ppermute(v, 'expert', xor_pairs(count, bits))  88.4 us
    dot_general x20, matrix products, dot(): lax.dot_general(a, b, (((ca,), (cb,)), ((), ())), preferred_element_type=...  25.2 us
    ppermute x6, waiting for transfers between devices, far(): return lax.ppermute(part, 'hidden', xor_pairs(hidden_n, last_bit))  13.1 us
    pallas_call x6, Pallas kernels, elementwise(): pl.pallas_call(kernel, out_shape=[jax.ShapeDtypeStruct((rows, cols), BF16...  9.62 us
    ppermute x3, waiting for transfers between devices, ring_gather(): value = lax.ppermute(value, 'expert', ring)  8.81 us
    pallas_call x3, Pallas kernels, slot_select(): pl.pallas_call(kernel, out_shape=[jax.ShapeDtypeStruct((half, width), BF1...  7.99 us
    pallas_call x3, Pallas kernels, slot_matmul(): pl.pallas_call(kernel, out_shape=[jax.ShapeDtypeStruct((slots, width, neu...  7.79 us
    pallas_call x3, Pallas kernels, slot_place(): pl.pallas_call(kernel, out_shape=jax.ShapeDtypeStruct(into.shape, BF16),...  7.25 us
  transfers between devices with their start and end apart: 38, of which 15 were waited for; matrix products, arithmetic and copies ran while one was open for 15% of the time, Pallas kernels for 13%

profile of v10, /device:TPU:0, one launch (start us, length us, event | category | flops | bytes accessed | tf_op | source)
XLA Modules:
  0.0 241.8 jit_solution(8721989371468214764)
XLA Ops:
  3.4 3.0 %collective-permute-start.70 = (bf16[128,1152]{1,0:T(8,128)(2,1)S(1)}, bf16[128,1152]{1,0:T(8,128)(2,1)}, u32[]{:S(2)}, u32[]{:S(2)}) collective-permute-start(bf16[128,1152]{1,0:T(8,128)(2,1)S(1)} %get-tuple-element.343), channel_id=1, source_target_pairs={{0,4},{4,0},{8,12},{12,8},{16,20},{20,16},{24,28},{28,24},{1,5},{5... | collective-permute-start | bytes 884744 | tf_op jit(solution)/shard_map/ppermute | solution.py:40
  24.7 4.7 %collective-permute-done.73 = bf16[128,1152]{1,0:T(8,128)(2,1)S(1)} collective-permute-done((bf16[128,1152]{1,0:T(8,128)(2,1)}, bf16[128,1152]{1,0:T(8,128)(2,1)S(1)}, u32[]{:S(2)}, u32[]{:S(2)}) %collective-permute-start.73) | collective-permute-done | bytes 294944 | tf_op jit(solution)/shard_map/ppermute | solution.py:39
  31.7 2.7 %shard_map.129 = (bf16[704,512]{1,0:T(8,128)(2,1)S(1)}, bf16[704,512]{1,0:T(8,128)(2,1)S(1)}) custom-call(s32[1]{0:T(128)} %bitcast.3.slot_ref, s32[704,1]{1,0:T(8,128)S(1)} %copy-done.8, s32[704,1]{1,0:T(8,128)S(1)} %select_n.150.keep_ref, bf16[2,512,1408]{2,1,0:T(8,128)(2,1)S(1)} %copy-done, bf16[128,1152]{1,0:T(8,128)(2,1)S(1)} %collective-permute-done.72.before_ref), custom_call_target="tpu_custom_call" | custom-call | flops 2030043136 | bytes 2883584 | tf_op jit(solution)/shard_map/pallas_call | solution.py:86
  34.4 4.1 %collective-permute-done.75 = bf16[128,1152]{1,0:T(8,128)(2,1)S(1)} collective-permute-done((bf16[128,1152]{1,0:T(8,128)(2,1)S(1)}, bf16[128,1152]{1,0:T(8,128)(2,1)S(1)}, u32[]{:S(2)}, u32[]{:S(2)}) %collective-permute-start.75) | collective-permute-done | bytes 294944 | tf_op jit(solution)/shard_map/ppermute | solution.py:39
  39.1 2.7 %shard_map.130 = (bf16[704,512]{1,0:T(8,128)(2,1)S(1)}, bf16[704,512]{1,0:T(8,128)(2,1)S(1)}) custom-call(s32[1]{0:T(128)} %bitcast.3.slot_ref, s32[704,1]{1,0:T(8,128)S(1)} %copy-done.8, s32[704,1]{1,0:T(8,128)S(1)} %select_n.150.keep_ref, bf16[2,512,1408]{2,1,0:T(8,128)(2,1)S(1)} %copy-done.1, bf16[128,1152]{1,0:T(8,128)(2,1)S(1)} %collective-permute-done.74.before_ref), custom_call_target="tpu_custom_call" | custom-call | flops 2030043136 | bytes 2883584 | tf_op jit(solution)/shard_map/pallas_call | solution.py:86
  41.8 3.4 %collective-permute-done.76.before_ref = bf16[128,1152]{1,0:T(8,128)(2,1)S(1)} collective-permute-done((bf16[128,1152]{1,0:T(8,128)(2,1)S(1)}, bf16[128,1152]{1,0:T(8,128)(2,1)S(1)}, u32[]{:S(2)}, u32[]{:S(2)}) %collective-permute-start.76) | collective-permute-done | bytes 294944 | tf_op jit(solution)/shard_map/ppermute | solution.py:40
  51.0 2.7 %shard_map.131 = (bf16[704,512]{1,0:T(8,128)(2,1)S(1)}, bf16[704,512]{1,0:T(8,128)(2,1)S(1)}) custom-call(s32[1]{0:T(128)} %bitcast.3.slot_ref, s32[704,1]{1,0:T(8,128)S(1)} %copy-done.8, s32[704,1]{1,0:T(8,128)S(1)} %copy-done.7, bf16[2,512,1408]{2,1,0:T(8,128)(2,1)S(1)} %copy-done.2, bf16[128,1152]{1,0:T(8,128)(2,1)S(1)} %collective-permute-done.76.before_ref), custom_call_target="tpu_custom_call" | custom-call | flops 2030043136 | bytes 2883584 | tf_op jit(solution)/shard_map/pallas_call | solution.py:86
  55.5 50.8 %conditional.3 = (bf16[704,512]{1,0:T(8,128)(2,1)S(1)}, bf16[704,512]{1,0:T(8,128)(2,1)S(1)}, bf16[704,512]{1,0:T(8,128)(2,1)S(1)}, bf16[256,1408]{1,0:T(8,128)(...) conditional(s32[]{:T(128)} %clamp.2, ...), branch_computations={%region_8.9_spmd, %region_9.10_spmd, %region_10.11_spmd, %region_1... | conditional | flops 21626880 | bytes 23789856 | solution.py:27
  60.2 14.4 %collective-permute-done.refs_1_ = bf16[704,512]{1,0:T(8,128)(2,1)S(1)} collective-permute-done((bf16[704,512]{1,0:T(8,128)(2,1)S(1)}, bf16[704,512]{1,0:T(8,128)(2,1)S(1)}, u32[]{:S(2)}, u32[]{:S(2)}) %collective-permute-start) | collective-permute-done | bytes 720928 | tf_op jit(solution)/shard_map/cond/branch_0_fun/ppermute | solution.py:24
  76.6 13.4 %collective-permute-done.1.refs_1_ = bf16[704,512]{1,0:T(8,128)(2,1)S(1)} collective-permute-done((bf16[704,512]{1,0:T(8,128)(2,1)S(1)}, bf16[704,512]{1,0:T(8,128)(2,1)S(1)}, u32[]{:S(2)}, u32[]{:S(2)}) %collective-permute-start.1) | collective-permute-done | bytes 720928 | tf_op jit(solution)/shard_map/cond/branch_0_fun/ppermute | solution.py:24
  90.6 14.0 %collective-permute-done.2.refs_1_ = bf16[704,512]{1,0:T(8,128)(2,1)S(1)} collective-permute-done((bf16[704,512]{1,0:T(8,128)(2,1)S(1)}, bf16[704,512]{1,0:T(8,128)(2,1)S(1)}, u32[]{:S(2)}, u32[]{:S(2)}) %collective-permute-start.2) | collective-permute-done | bytes 720928 | tf_op jit(solution)/shard_map/cond/branch_0_fun/ppermute | solution.py:24
  110.0 3.3 %shard_map.132 = (bf16[256,1408]{1,0:T(8,128)(2,1)S(1)}, bf16[256,1408]{1,0:T(8,128)(2,1)}, bf16[256,1408]{1,0:T(8,128)(2,1)}) custom-call(bf16[256,1408]{1,0:T(8,128)(2,1)S(1)} %copy-done.10, bf16[256,1408]{1,0:T(8,128)(2,1)} %get-tuple-element.310.refs_1_, bf16[256,1408]{1,0:T(8,128)(2,1)S(1)} %add_convert_fusion.3.refs_2_, ...), custom_call_target="tpu_custom_call" | custom-call | flops 7208960 | bytes 6488064 | tf_op jit(solution)/shard_map/pallas_call | solution.py:220
  122.6 4.3 %fusion = f32[1024,512]{1,0:T(8,128)} fusion(bf16[512,1408]{1,0:T(8,128)(2,1)} %constant_dynamic-update-slice_fusion.8.right_ref, bf16[2,512,1408]{2,1,0:T(8,128)(2,1)S(1)} %copy-done.3, s32[]{:T(128)S(6)} %select_n.134, s32[1024]{0:T(1024)S(1)} %fusion.50, f32[512]{0:T(512)S(1)} %select_reduce_fusion), kind=kOutput, calls=%fused_computation.7 | convolution fusion | flops 1276116992 | bytes 4986884 | tf_op jit(solution)/shard_map/dot_general | solution.py:15
  128.4 3.5 %shard_map.135 = (bf16[2,512,1408]{2,1,0:T(8,128)(2,1)}, f32[8,128]{1,0:T(8,128)S(1)}) custom-call(s32[1]{0:T(128)} %bitcast.6.slot_ref, bf16[512,512]{1,0:T(8,128)(2,1)S(1)} %copy-done.5, bf16[512,1408]{1,0:T(8,128)(2,1)} %constant_dynamic-update-slice_fusion.8.right_ref), custom_call_target="tpu_custom_call" | custom-call | flops 738197504 | bytes 3407872 | tf_op jit(solution)/shard_map/pallas_call | solution.py:118
  140.3 10.8 %collective-permute-done.82.refs_1_ = bf16[352,1024]{1,0:T(8,128)(2,1)} collective-permute-done((bf16[352,1024]{1,0:T(8,128)(2,1)}, bf16[352,1024]{1,0:T(8,128)(2,1)}, u32[]{:S(2)}, u32[]{:S(2)}) %collective-permute-start.82) | collective-permute-done | bytes 720928 | tf_op jit(solution)/shard_map/ppermute | solution.py:336
  157.4 19.5 %conditional.4 = (bf16[704,512]{1,0:T(8,128)(2,1)}, bf16[352,1024]{1,0:T(8,128)(2,1)}) conditional(s32[]{:T(128)} %clamp.2, (bf16[704,512]{1,0:T(8,128)(2,1)}, bf16[352,1024]{1,0:T(8,128)(2,1)S(1)}) %tuple.93, (bf16[704,512]{1,0:T(8,128)(2,1)}, bf16[352,1024]{1,0:T(8,128)(2,1)S(1)}) %tuple.93, ...), branch_computations={%region_16.17_spmd, %region_17.18_spmd, %region_18.19_spmd, %regio... | conditional | bytes 5767264 | solution.py:27
  160.4 15.5 %collective-permute-done.42 = bf16[704,512]{1,0:T(8,128)(2,1)} collective-permute-done((bf16[704,512]{1,0:T(8,128)(2,1)}, bf16[704,512]{1,0:T(8,128)(2,1)}, u32[]{:S(2)}, u32[]{:S(2)}) %collective-permute-start.42) | collective-permute-done | bytes 720928 | tf_op jit(solution)/shard_map/cond/branch_0_fun/ppermute | solution.py:24
  178.9 2.9 %add_convert_fusion = bf16[1024,512]{1,0:T(8,128)(2,1)S(1)} fusion(f32[1024,512]{1,0:T(8,128)} %fusion, bf16[704,512]{1,0:T(8,128)(2,1)S(1)} %copy-done.15, f32[]{:T(128)} %bitcast.7, f32[1024]{0:T(1024)S(1)} %get-tuple-element.331, bf16[352,1024]{1,0:T(8,128)(2,1)} %copy-done.21, bf16[352,1024]{1,0:T(8,128)(2,1)S(1)} %shard_map.136), kind=kOutput, calls=%fused_computation.3 | convolution fusion | flops 743178240 | bytes 5312516 | tf_op jit(solution)/shard_map/dot_general | solution.py:15
  182.4 2.7 %shard_map.137 = (bf16[352,1024]{1,0:T(8,128)(2,1)S(1)}, bf16[352,1024]{1,0:T(8,128)(2,1)S(1)}) custom-call(bf16[352,1024]{1,0:T(8,128)(2,1)} %fusion.22.refs_0_, bf16[352,1024]{1,0:T(8,128)(2,1)} %collective-permute-done.82.refs_1_, bf16[352,1024]{1,0:T(8,128)(2,1)} %fusion.23.refs_2_, bf16[352,1024]{1,0:T(8,128)(2,1)} %collective-permute-done.84.refs_3_, ...), custom_call_target="tpu_custom_call" | custom-call | flops 7208960 | bytes 5767168 | tf_op jit(solution)/shard_map/pallas_call | solution.py:220
  187.6 3.9 %collective-permute-done.91 = bf16[128,512]{1,0:T(8,128)(2,1)S(1)} collective-permute-done((bf16[128,512]{1,0:T(8,128)(2,1)S(1)}, bf16[128,512]{1,0:T(8,128)(2,1)S(1)}, u32[]{:S(2)}, u32[]{:S(2)}) %collective-permute-start.91) | collective-permute-done | bytes 131104 | tf_op jit(solution)/shard_map/ppermute | solution.py:51
  196.6 33.2 %conditional.5 = (bf16[704,512]{1,0:T(8,128)(2,1)}, bf16[704,512]{1,0:T(8,128)(2,1)}) conditional(s32[]{:T(128)} %clamp.2, (bf16[704,512]{1,0:T(8,128)(2,1)S(1)}, bf16[704,512]{1,0:T(8,128)(2,1)S(1)}) %tuple.94, (bf16[704,512]{1,0:T(8,128)(2,1)S(1)}, bf16[704,512]{1,0:T(8,128)(2,1)S(1)}) %tuple.94, ...), branch_computations={%region_23.24_spmd, %region_24.25_spmd, %region_25.26_spmd, %regio... | conditional | bytes 5767264 | solution.py:27
  198.7 17.1 %collective-permute-done.56 = bf16[704,512]{1,0:T(8,128)(2,1)} collective-permute-done((bf16[704,512]{1,0:T(8,128)(2,1)S(1)}, bf16[704,512]{1,0:T(8,128)(2,1)}, u32[]{:S(2)}, u32[]{:S(2)}) %collective-permute-start.56) | collective-permute-done | bytes 720928 | tf_op jit(solution)/shard_map/cond/branch_0_fun/ppermute | solution.py:24
  215.8 14.0 %collective-permute-done.57 = bf16[704,512]{1,0:T(8,128)(2,1)} collective-permute-done((bf16[704,512]{1,0:T(8,128)(2,1)S(1)}, bf16[704,512]{1,0:T(8,128)(2,1)}, u32[]{:S(2)}, u32[]{:S(2)}) %collective-permute-start.57) | collective-permute-done | bytes 720928 | tf_op jit(solution)/shard_map/cond/branch_0_fun/ppermute | solution.py:24
  233.9 2.5 %shard_map.140 = bf16[2,512,1408]{2,1,0:T(8,128)(2,1)} custom-call(s32[1]{0:T(128)} %bitcast.3.slot_ref, s32[1]{0:T(128)} %bitcast.9.keep_ref, s32[1]{0:T(128)} %bitcast.10.swap_ref, bf16[704,512]{1,0:T(8,128)(2,1)} %convolution_convert_fusion.3.first_ref, bf16[704,512]{1,0:T(8,128)(2,1)} %get-tuple-element.322.second_ref, ...), custom_call_target="tpu_custom_call", output_to_operand_aliasing={{}: (5, {})} | custom-call | bytes 2883584 | tf_op jit(solution)/shard_map/pallas_call | solution.py:160
  (174 shorter events, 90.7 us)
Async XLA Ops:
  3.4 17.9 %collective-permute-start.70 = (bf16[128,1152]{1,0:T(8,128)(2,1)S(1)}, bf16[128,1152]{1,0:T(8,128)(2,1)}, u32[]{:S(2)}, u32[]{:S(2)}) collective-permute-start(bf16[128,1152]{1,0:T(8,128)(2,1)S(1)} %get-tuple-element.343), channel_id=1, source_target_pairs={{0,4},{4,0},{8,12},{12,8},{16,20},{20,16},{24,28},{28,24},{1,5},{5... | collective-permute-start | bytes 884744 | tf_op jit(solution)/shard_map/ppermute | solution.py:40
  6.4 12.8 %collective-permute-start.71 = (bf16[128,1152]{1,0:T(8,128)(2,1)S(1)}, bf16[128,1152]{1,0:T(8,128)(2,1)}, u32[]{:S(2)}, u32[]{:S(2)}) collective-permute-start(bf16[128,1152]{1,0:T(8,128)(2,1)S(1)} %get-tuple-element.343), channel_id=1, source_target_pairs={{0,8},{4,12},{8,16},{12,20},{16,24},{20,28},{24,0},{28,4},{1,9},{5... | collective-permute-start | bytes 884744 | tf_op jit(solution)/shard_map/ppermute | solution.py:39
  19.2 10.2 %collective-permute-start.73 = (bf16[128,1152]{1,0:T(8,128)(2,1)}, bf16[128,1152]{1,0:T(8,128)(2,1)S(1)}, u32[]{:S(2)}, u32[]{:S(2)}) collective-permute-start(bf16[128,1152]{1,0:T(8,128)(2,1)} %collective-permute-done.71), channel_id=1, source_target_pairs={{0,8},{4,12},{8,16},{12,20},{16,24},{20,28},{24,0},{28,4},{1,9},{5... | collective-permute-start | bytes 884744 | tf_op jit(solution)/shard_map/ppermute | solution.py:39
  29.4 9.6 %collective-permute-start.74 = (bf16[128,1152]{1,0:T(8,128)(2,1)S(1)}, bf16[128,1152]{1,0:T(8,128)(2,1)S(1)}, u32[]{:S(2)}, u32[]{:S(2)}) collective-permute-start(bf16[128,1152]{1,0:T(8,128)(2,1)S(1)} %collective-permute-done.73), channel_id=1, source_target_pairs={{0,4},{4,0},{8,12},{12,8},{16,20},{20,16},{24,28},{28,24},{1,5},{5... | collective-permute-start | bytes 884744 | tf_op jit(solution)/shard_map/ppermute | solution.py:40
  55.6 19.1 %collective-permute-start = (bf16[704,512]{1,0:T(8,128)(2,1)S(1)}, bf16[704,512]{1,0:T(8,128)(2,1)S(1)}, u32[]{:S(2)}, u32[]{:S(2)}) collective-permute-start(bf16[704,512]{1,0:T(8,128)(2,1)S(1)} %get-tuple-element.183), channel_id=1, source_target_pairs={{0,4},{4,0},{8,12},{12,8},{16,20},{20,16},{24,28},{28,24},{1,5},{5... | collective-permute-start | bytes 2162696 | tf_op jit(solution)/shard_map/cond/branch_0_fun/ppermute | solution.py:24
  56.1 33.9 %collective-permute-start.1 = (bf16[704,512]{1,0:T(8,128)(2,1)S(1)}, bf16[704,512]{1,0:T(8,128)(2,1)S(1)}, u32[]{:S(2)}, u32[]{:S(2)}) collective-permute-start(bf16[704,512]{1,0:T(8,128)(2,1)S(1)} %get-tuple-element.185), channel_id=1, source_target_pairs={{0,4},{4,0},{8,12},{12,8},{16,20},{20,16},{24,28},{28,24},{1,5},{5... | collective-permute-start | bytes 2162696 | tf_op jit(solution)/shard_map/cond/branch_0_fun/ppermute | solution.py:24
  57.6 46.9 %collective-permute-start.2 = (bf16[704,512]{1,0:T(8,128)(2,1)S(1)}, bf16[704,512]{1,0:T(8,128)(2,1)S(1)}, u32[]{:S(2)}, u32[]{:S(2)}) collective-permute-start(bf16[704,512]{1,0:T(8,128)(2,1)S(1)} %get-tuple-element.187), channel_id=1, source_target_pairs={{0,4},{4,0},{8,12},{12,8},{16,20},{20,16},{24,28},{28,24},{1,5},{5... | collective-permute-start | bytes 2162696 | tf_op jit(solution)/shard_map/cond/branch_0_fun/ppermute | solution.py:24
  58.2 46.9 %collective-permute-start.3 = (bf16[256,1408]{1,0:T(8,128)(2,1)S(1)}, bf16[256,1408]{1,0:T(8,128)(2,1)}, u32[]{:S(2)}, u32[]{:S(2)}) collective-permute-start(bf16[256,1408]{1,0:T(8,128)(2,1)S(1)} %get-tuple-element.188), channel_id=1, source_target_pairs={{0,2},{1,3},{2,0},{3,1},{4,6},{5,7},{6,4},{7,5},{8,10},{9,11},{10,... | collective-permute-start | bytes 2162696 | tf_op jit(solution)/shard_map/cond/branch_0_fun/ppermute | solution.py:336
  59.6 45.4 %collective-permute-start.4 = (bf16[256,1408]{1,0:T(8,128)(2,1)S(1)}, bf16[256,1408]{1,0:T(8,128)(2,1)}, u32[]{:S(2)}, u32[]{:S(2)}) collective-permute-start(bf16[256,1408]{1,0:T(8,128)(2,1)S(1)} %get-tuple-element.189), channel_id=1, source_target_pairs={{0,2},{1,3},{2,0},{3,1},{4,6},{5,7},{6,4},{7,5},{8,10},{9,11},{10,... | collective-permute-start | bytes 2162696 | tf_op jit(solution)/shard_map/cond/branch_0_fun/ppermute | solution.py:336
  74.6 31.7 %collective-permute-start.5 = (bf16[256,1408]{1,0:T(8,128)(2,1)S(1)}, bf16[256,1408]{1,0:T(8,128)(2,1)}, u32[]{:S(2)}, u32[]{:S(2)}) collective-permute-start(bf16[256,1408]{1,0:T(8,128)(2,1)S(1)} %get-tuple-element.190), channel_id=1, source_target_pairs={{0,2},{1,3},{2,0},{3,1},{4,6},{5,7},{6,4},{7,5},{8,10},{9,11},{10,... | collective-permute-start | bytes 2162696 | tf_op jit(solution)/shard_map/cond/branch_0_fun/ppermute | solution.py:336
  114.8 23.6 %collective-permute-start.85 = (bf16[352,1024]{1,0:T(8,128)(2,1)}, bf16[352,1024]{1,0:T(8,128)(2,1)}, u32[]{:S(2)}, u32[]{:S(2)}) collective-permute-start(bf16[352,1024]{1,0:T(8,128)(2,1)} %convolution_convert_fusion.4), channel_id=1, source_target_pairs={{0,1},{1,0},{2,3},{3,2},{4,5},{5,4},{6,7},{7,6},{8,9},{9,8},{10,11... | collective-permute-start | bytes 2162696 | tf_op jit(solution)/shard_map/ppermute | solution.py:320
  115.3 19.4 %collective-permute-start.86 = (bf16[256,1408]{1,0:T(8,128)(2,1)}, bf16[256,1408]{1,0:T(8,128)(2,1)}, u32[]{:S(2)}, u32[]{:S(2)}) collective-permute-start(bf16[256,1408]{1,0:T(8,128)(2,1)} %get-tuple-element.317), channel_id=1, source_target_pairs={{0,1},{1,0},{2,3},{3,2},{4,5},{5,4},{6,7},{7,6},{8,9},{9,8},{10,11... | collective-permute-start | bytes 2162696 | tf_op jit(solution)/shard_map/ppermute | solution.py:340
  115.4 11.5 %collective-permute-start.87 = (bf16[256,1408]{1,0:T(8,128)(2,1)}, bf16[256,1408]{1,0:T(8,128)(2,1)}, u32[]{:S(2)}, u32[]{:S(2)}) collective-permute-start(bf16[256,1408]{1,0:T(8,128)(2,1)} %get-tuple-element.319), channel_id=1, source_target_pairs={{0,1},{1,0},{2,3},{3,2},{4,5},{5,4},{6,7},{7,6},{8,9},{9,8},{10,11... | collective-permute-start | bytes 2162696 | tf_op jit(solution)/shard_map/ppermute | solution.py:340
  117.2 23.0 %collective-permute-start.84 = (bf16[352,1024]{1,0:T(8,128)(2,1)}, bf16[352,1024]{1,0:T(8,128)(2,1)}, u32[]{:S(2)}, u32[]{:S(2)}) collective-permute-start(bf16[352,1024]{1,0:T(8,128)(2,1)} %fusion.23.refs_2_), channel_id=1, source_target_pairs={{0,2},{1,3},{2,0},{3,1},{4,6},{5,7},{6,4},{7,5},{8,10},{9,11},{10,... | collective-permute-start | bytes 2162696 | tf_op jit(solution)/shard_map/ppermute | solution.py:336
  120.2 30.9 %collective-permute-start.82 = (bf16[352,1024]{1,0:T(8,128)(2,1)}, bf16[352,1024]{1,0:T(8,128)(2,1)}, u32[]{:S(2)}, u32[]{:S(2)}) collective-permute-start(bf16[352,1024]{1,0:T(8,128)(2,1)} %fusion.22.refs_0_), channel_id=1, source_target_pairs={{0,2},{1,3},{2,0},{3,1},{4,6},{5,7},{6,4},{7,5},{8,10},{9,11},{10,... | collective-permute-start | bytes 2162696 | tf_op jit(solution)/shard_map/ppermute | solution.py:336
  157.4 18.5 %collective-permute-start.42 = (bf16[704,512]{1,0:T(8,128)(2,1)}, bf16[704,512]{1,0:T(8,128)(2,1)}, u32[]{:S(2)}, u32[]{:S(2)}) collective-permute-start(bf16[704,512]{1,0:T(8,128)(2,1)} %get-tuple-element.245), channel_id=1, source_target_pairs={{0,4},{4,0},{8,12},{12,8},{16,20},{20,16},{24,28},{28,24},{1,5},{5... | collective-permute-start | bytes 2162696 | tf_op jit(solution)/shard_map/cond/branch_0_fun/ppermute | solution.py:24
  158.9 18.0 %collective-permute-start.43 = (bf16[352,1024]{1,0:T(8,128)(2,1)S(1)}, bf16[352,1024]{1,0:T(8,128)(2,1)}, u32[]{:S(2)}, u32[]{:S(2)}) collective-permute-start(bf16[352,1024]{1,0:T(8,128)(2,1)S(1)} %get-tuple-element.246), channel_id=1, source_target_pairs={{0,2},{1,3},{2,0},{3,1},{4,6},{5,7},{6,4},{7,5},{8,10},{9,11},{10,... | collective-permute-start | bytes 2162696 | tf_op jit(solution)/shard_map/cond/branch_0_fun/ppermute | solution.py:336
  185.1 9.6 %collective-permute-start.95 = (bf16[352,1024]{1,0:T(8,128)(2,1)S(1)}, bf16[352,1024]{1,0:T(8,128)(2,1)S(1)}, u32[]{:S(2)}, u32[]{:S(2)}) collective-permute-start(bf16[352,1024]{1,0:T(8,128)(2,1)S(1)} %get-tuple-element.324), channel_id=1, source_target_pairs={{0,1},{1,0},{2,3},{3,2},{4,5},{5,4},{6,7},{7,6},{8,9},{9,8},{10,11... | collective-permute-start | bytes 2162696 | tf_op jit(solution)/shard_map/ppermute | solution.py:340
  187.0 54.1 %collective-permute-start.89 = (bf16[128,512]{1,0:T(8,128)(2,1)S(1)}, bf16[128,512]{1,0:T(8,128)(2,1)S(1)}, u32[]{:S(2)}, u32[]{:S(2)}) collective-permute-start(bf16[128,512]{1,0:T(8,128)(2,1)S(1)} %get-tuple-element.339), channel_id=1, source_target_pairs={{0,4},{4,0},{8,12},{12,8},{16,20},{20,16},{24,28},{28,24},{1,5},{5... | collective-permute-start | bytes 393224 | tf_op jit(solution)/shard_map/ppermute | solution.py:51
  191.5 40.0 %collective-permute-start.90 = (bf16[128,512]{1,0:T(8,128)(2,1)S(1)}, bf16[128,512]{1,0:T(8,128)(2,1)S(1)}, u32[]{:S(2)}, u32[]{:S(2)}) collective-permute-start(bf16[128,512]{1,0:T(8,128)(2,1)S(1)} %get-tuple-element.342), channel_id=1, source_target_pairs={{0,4},{4,0},{8,12},{12,8},{16,20},{20,16},{24,28},{28,24},{1,5},{5... | collective-permute-start | bytes 393224 | tf_op jit(solution)/shard_map/ppermute | solution.py:51
  194.6 36.9 %collective-permute-start.94 = (bf16[128,512]{1,0:T(8,128)(2,1)S(1)}, bf16[128,512]{1,0:T(8,128)(2,1)S(1)}, u32[]{:S(2)}, u32[]{:S(2)}) collective-permute-start(bf16[128,512]{1,0:T(8,128)(2,1)S(1)} %add_convert_fusion.7), channel_id=1, source_target_pairs={{0,8},{4,12},{8,16},{12,20},{16,24},{20,28},{24,0},{28,4},{1,9},{5... | collective-permute-start | bytes 393224 | tf_op jit(solution)/shard_map/ppermute | solution.py:61
  196.6 19.2 %collective-permute-start.56 = (bf16[704,512]{1,0:T(8,128)(2,1)S(1)}, bf16[704,512]{1,0:T(8,128)(2,1)}, u32[]{:S(2)}, u32[]{:S(2)}) collective-permute-start(bf16[704,512]{1,0:T(8,128)(2,1)S(1)} %get-tuple-element.259), channel_id=1, source_target_pairs={{0,4},{4,0},{8,12},{12,8},{16,20},{20,16},{24,28},{28,24},{1,5},{5... | collective-permute-start | bytes 2162696 | tf_op jit(solution)/shard_map/cond/branch_0_fun/ppermute | solution.py:24
  197.2 32.6 %collective-permute-start.57 = (bf16[704,512]{1,0:T(8,128)(2,1)S(1)}, bf16[704,512]{1,0:T(8,128)(2,1)}, u32[]{:S(2)}, u32[]{:S(2)}) collective-permute-start(bf16[704,512]{1,0:T(8,128)(2,1)S(1)} %get-tuple-element.260), channel_id=1, source_target_pairs={{0,4},{4,0},{8,12},{12,8},{16,20},{20,16},{24,28},{28,24},{1,5},{5... | collective-permute-start | bytes 2162696 | tf_op jit(solution)/shard_map/cond/branch_0_fun/ppermute | solution.py:24
  231.6 9.5 %collective-permute-start.97 = (bf16[128,512]{1,0:T(8,128)(2,1)S(1)}, bf16[128,512]{1,0:T(8,128)(2,1)S(1)}, u32[]{:S(2)}, u32[]{:S(2)}) collective-permute-start(bf16[128,512]{1,0:T(8,128)(2,1)S(1)} %add_convert_fusion.6), channel_id=1, source_target_pairs={{0,8},{4,12},{8,16},{12,20},{16,24},{20,28},{24,0},{28,4},{1,9},{5... | collective-permute-start | bytes 393224 | tf_op jit(solution)/shard_map/ppermute | solution.py:61
  (36 other events, 263.3 us)
